TPU v7x, 32 devices: a whole 2x2x4 slice. The times are simulated.
32 devices in a mesh: runs: 2 (over y), box: 4 (over z), slab: 2 (over x), fld: 2 (over core).
Axes of the slice: x: 2, y: 2, z: 4, core: 2. Of those that a mesh axis runs over, the one named last changes fastest.
Arguments:
- boxes: float32 [3, 32, 24, 16, 256], P(None, ('runs', 'box'), 'fld', 'slab'), parts along dimension 1, may hold values from -6 to 6
- move_dest: int32 [32], P('runs'), parts along dimension 0, may hold values from 0 to 3, as said below
- parent: int32 [32], P('runs'), parts along dimension 0, may hold values from 0 to 31, as said below
- coarse: float32 [64, 24, 1000], P(('runs', 'box'), 'fld'), parts along dimension 0, may hold values from -6 to 6
- lap_mix: float32 [24, 24], replicated, may hold values from -0.3125 to 0.3125
- grad_mix: float32 [24, 24], replicated, may hold values from -1.25 to 1.25
- damp_mix: float32 [24, 24], replicated, may hold values from -1.25 to 1.25
Outputs:
- moved_levels: float32 [3, 64, 24, 16, 256], P(None, ('runs', 'box'), 'fld', 'slab'), parts along dimension 1
- slope: float32 [64, 24, 16, 256], P(('runs', 'box'), 'fld', 'slab'), parts along dimension 0
There are 2 independent parts, one for each index of `runs`. A program takes and returns all parts, laid end to end along the dimension named above; an argument that names none is the same for every part. Nothing has to cross between parts.
Inputs may be any that keep to these rules, and one draw needn't show every extreme that they name: `move_dest`: of the 4 boxes of one index of box, at most 2 share a destination; in every draw some destination receives exactly 2 boxes from every index of box, and every index of box is the destination of some box. `parent`: the boxes that one destination receives from one source have parents held by one index of box, and different sources give different such indices; so at most 2 boxes of one destination have parents on one index of box, and some destination reaches 2 from every index.
All inputs are finite; a program needn't handle non-finite values.
Results may differ from a plain program's by a relative error of at most 0.00007.
Values sent between devices are 32-bit elements; how exact they have to be, the bound alone decides.
No kernel may reach another device: no remote copies, remote signals or barrier semaphores. Data moves between devices by JAX's collectives and lax.ppermute only.
A program may use at most 128 MiB of HBM per device.

v0:
```python
import jax
import jax.numpy as jnp
from jax import lax
from jax.sharding import PartitionSpec as P


def with_halo(cells, sides, width):
    for axis, dim in sides:
        count = lax.axis_size(axis)
        ends = count - 1
        head = lax.slice_in_dim(cells, 0, width, axis=dim)
        tail = lax.slice_in_dim(cells, cells.shape[dim] - width, cells.shape[dim], axis=dim)
        cells = jnp.concatenate(
            [
                lax.ppermute(tail, axis, [(i, (i + 1) % count) for i in range(ends)]),
                cells,
                lax.ppermute(head, axis, [((i + 1) % count, i) for i in range(ends)]),
            ],
            axis=dim,
        )
    return cells


def prolong_block(values):
    for axis_pos in (-3, -2, -1):
        values = jnp.repeat(values, 2, axis=axis_pos)
    return values[..., 1:-1, 1:-1, 1:-1]


def stencil_terms(padded):
    centre = padded[..., 1:-1, 1:-1, 1:-1]
    x_after = padded[..., 2:, 1:-1, 1:-1]
    x_before = padded[..., :-2, 1:-1, 1:-1]
    y_after = padded[..., 1:-1, 2:, 1:-1]
    y_before = padded[..., 1:-1, :-2, 1:-1]
    z_after = padded[..., 1:-1, 1:-1, 2:]
    z_before = padded[..., 1:-1, 1:-1, :-2]
    laplace = x_after + x_before + y_after + y_before + z_after + z_before - 6.0 * centre
    slopes = 0.5 * (x_after - x_before + (y_after - y_before) + (z_after - z_before))
    return (laplace, slopes, centre)


def body(boxes, move_dest, parent, coarse, lap_mix, grad_mix, damp_mix):
    box_count = lax.axis_size("box")
    slab_count = lax.axis_size("slab")
    own_box = lax.axis_index("box")
    slab_index = lax.axis_index("slab")
    field_index = lax.axis_index("fld")
    level_count, per_device, own_fields, planes, cross = boxes.shape
    box_edge = planes * slab_count
    coarse_side = box_edge // 2 + 2
    coarse_planes = planes // 2
    all_fields = own_fields * lax.axis_size("fld")
    slot_count = 2 * box_count
    coarse_count = coarse.shape[0]
    total_boxes = move_dest.shape[0]
    dest_grid = move_dest.reshape(box_count, per_device)
    earlier = jnp.arange(per_device)[None, :] < jnp.arange(per_device)[:, None]
    matching = dest_grid[:, :, None] == dest_grid[:, None, :]
    box_rank = jnp.sum(matching & earlier[None], axis=2, dtype=jnp.int32)
    own_dest = lax.dynamic_index_in_dim(dest_grid, own_box, 0, keepdims=False)
    own_rank = lax.dynamic_index_in_dim(box_rank, own_box, 0, keepdims=False)
    send_slot = own_dest * 2 + own_rank
    outgoing = (
        jnp.zeros((level_count, slot_count, own_fields, planes, cross), jnp.float32)
        .at[:, send_slot]
        .set(boxes)
    )
    arrived = lax.all_to_all(outgoing, "box", split_axis=1, concat_axis=1, tiled=True)
    current = arrived[0]
    slot_match = (dest_grid == own_box)[:, None, :] & (
        box_rank[:, None, :] == jnp.arange(2)[None, :, None]
    )
    occupied = jnp.any(slot_match, axis=2).reshape(slot_count)
    owner_all = parent // coarse_count
    local_all = parent % coarse_count
    earlier_all = jnp.arange(total_boxes)[None, :] < jnp.arange(total_boxes)[:, None]
    face_match = (
        (owner_all[:, None] == owner_all[None, :])
        & (move_dest[:, None] == move_dest[None, :])
        & earlier_all
    )
    face_rank = jnp.sum(face_match, axis=1, dtype=jnp.int32)

    def pick_slot(values):
        grid_values = values.reshape(box_count, per_device)[:, None, :]
        return jnp.sum(jnp.where(slot_match, grid_values, 0), axis=2, dtype=jnp.int32).reshape(
            slot_count
        )

    slot_owner = pick_slot(owner_all)
    slot_face_rank = pick_slot(face_rank)
    coarse_grid = coarse.reshape(coarse_count, own_fields, coarse_side, coarse_side * coarse_side)
    shells = lax.dynamic_slice_in_dim(
        coarse_grid, slab_index * coarse_planes, coarse_planes + 2, axis=2
    )
    shells = shells.reshape(
        coarse_count, own_fields, (coarse_planes + 2) * coarse_side * coarse_side
    )
    target = jnp.where(owner_all == own_box, move_dest * 2 + face_rank, slot_count)
    outgoing_faces = (
        jnp.zeros((slot_count,) + shells.shape[1:], jnp.float32)
        .at[target]
        .set(shells[local_all], mode="drop")
    )
    arrived_faces = lax.all_to_all(outgoing_faces, "box", split_axis=0, concat_axis=0, tiled=True)
    faces = arrived_faces[slot_owner * 2 + slot_face_rank]
    block = min(8, slot_count)
    blocks = slot_count // block
    mixing = jnp.concatenate([lap_mix, grad_mix, damp_mix], axis=1)
    whole, faces_all = (
        lax.all_gather(current, "fld", axis=1, tiled=True),
        lax.all_gather(faces, "fld", axis=1, tiled=True),
    )
    rimmed = with_halo(whole, (("slab", 2),), 1)
    own_mixing = lax.dynamic_slice_in_dim(mixing, field_index * own_fields, own_fields, 0)
    fields_out = own_mixing.shape[0]

    def slope_block(block_items):
        rim_part, face_part = block_items
        coarse_part = face_part.reshape(
            block, all_fields, coarse_planes + 2, coarse_side, coarse_side
        )
        padded = prolong_block(coarse_part)
        inner = rim_part.reshape(block, all_fields, planes + 2, box_edge, box_edge)
        lower_plane = jnp.where(slab_index == 0, padded[:, :, 0, 1:-1, 1:-1], inner[:, :, 0])
        upper_plane = jnp.where(
            slab_index == slab_count - 1, padded[:, :, -1, 1:-1, 1:-1], inner[:, :, -1]
        )
        inner = jnp.concatenate(
            [lower_plane[:, :, None], inner[:, :, 1:-1], upper_plane[:, :, None]], axis=2
        )
        padded = padded.at[:, :, :, 1:-1, 1:-1].set(inner)
        stencil_all = jnp.concatenate(stencil_terms(padded), axis=-4)
        mixed_terms = jnp.einsum(
            "fg,bgxyz->bfxyz", own_mixing, stencil_all, precision=lax.Precision.HIGHEST
        )
        return mixed_terms.reshape(block, fields_out, planes, cross)

    result = lax.map(
        slope_block,
        (
            rimmed.reshape((blocks, block) + rimmed.shape[1:]),
            faces_all.reshape((blocks, block) + faces_all.shape[1:]),
        ),
    )
    slope_out = result.reshape(slot_count, fields_out, planes, cross)
    slope_out = slope_out * occupied[:, None, None, None].astype(jnp.float32)
    return (arrived, slope_out)


def solution(mesh):
    placed = (
        P(None, ("runs", "box"), "fld", "slab", None),
        P("runs"),
        P("runs"),
        P(("runs", "box"), "fld", None),
        P(),
        P(),
        P(),
    )
    return jax.shard_map(
        body,
        mesh=mesh,
        in_specs=placed,
        out_specs=(
            P(None, ("runs", "box"), "fld", "slab", None),
            P(("runs", "box"), "fld", "slab", None),
        ),
        check_vma=False,
    )
```

profile of v0, /device:TPU:0, one launch (start us, length us, event | category | flops | bytes accessed | tf_op | source)
XLA Modules:
  0.0 283.0 jit_solution(5891491023644665479)
XLA Ops:
  7.2 0.7 reshape.213
  7.9 1.4 copy.31
  9.3 0.2 convert_reduce_fusion.1
  9.6 0.2 broadcast_in_dim.70
  9.8 1.0 scatter_fusion
  10.8 1.6 copy.32
  12.4 6.3 %all-to-all-start = ((f32[3,8,12,8,256]{4,3,2,0,1:T(8,128)}), f32[3,8,12,8,256]{4,3,2,0,1:T(8,128)S(1)}, u32[]{:S(2)}, u32[]{:S(2)}) async-start(f32[3,8,12,8,256]{4,3,2,0,1:T(8,128)} %copy.32), calls=%async_computation | async-start | bytes 4718592 | tf_op jit(solution)/shard_map/all_to_all | solution.py:69
  18.7 0.5 reshape.215
  19.3 0.1 reshape.216
  19.5 0.6 gather_fusion
  20.1 52.4 %all-to-all-done = f32[3,8,12,8,256]{4,3,2,0,1:T(8,128)S(1)} async-done(((f32[3,8,12,8,256]{4,3,2,0,1:T(8,128)}), f32[3,8,12,8,256]{4,3,2,0,1:T(8,128)S(1)}, u32[]{:S(2)}, u32[]{:S(2)}) %all-to-all-start) | async-done | bytes 2359328 | tf_op jit(solution)/shard_map/all_to_all | solution.py:69
  72.6 1.0 slice.137
  73.6 0.2 convert_reduce_fusion
  73.7 0.7 broadcast_in_dim.71
  74.5 3.1 %scatter_fusion.1 = f32[8,12,600]{2,1,0:T(8,128)} fusion(f32[8,12,600]{2,1,0:T(8,128)} %broadcast_in_dim.71, s32[16]{0:T(128)S(1)} %compare_select_fusion.2, f32[16,12,600]{2,1,0:T(8,128)S(1)} %gather_fusion), kind=kCustom, calls=%fused_computation.3 | custom fusion | bytes 1382464 | tf_op jit(solution)/shard_map/scatter | solution.py:104
  77.6 3.5 %all-to-all-start.1 = ((f32[8,12,600]{2,1,0:T(8,128)}), f32[8,12,600]{2,1,0:T(8,128)S(1)}, u32[]{:S(2)}, u32[]{:S(2)}) async-start(f32[8,12,600]{2,1,0:T(8,128)} %scatter_fusion.1), calls=%async_computation.1 | async-start | bytes 655360 | tf_op jit(solution)/shard_map/all_to_all | solution.py:106
  81.1 0.1 broadcast_in_dim.77
  81.3 0.2 fusion.18
  81.4 0.2 select_reduce_fusion.1
  81.6 0.1 copy.41
  81.7 0.1 reshape.222
  81.8 0.1 copy.35
  81.9 0.1 add.116
  82.0 8.9 %all-to-all-done.1 = f32[8,12,600]{2,1,0:T(8,128)S(1)} async-done(((f32[8,12,600]{2,1,0:T(8,128)}), f32[8,12,600]{2,1,0:T(8,128)S(1)}, u32[]{:S(2)}, u32[]{:S(2)}) %all-to-all-start.1) | async-done | bytes 230432 | tf_op jit(solution)/shard_map/all_to_all | solution.py:106
  90.8 0.6 gather_fusion.1
  91.5 2.2 all-gather.1
  93.7 2.2 copy.37
  95.9 2.1 broadcast_in_dim.79
  98.0 0.8 broadcast_in_dim.80
  98.8 7.0 %broadcast_in_dim.81 = f32[8,24,12,20,10,2]{1,0,5,4,3,2:T(8,128)} broadcast(f32[8,24,12,20,10]{1,0,4,3,2:T(8,128)S(1)} %bitcast.31), dimensions={0,1,2,3,4} | broadcast | bytes 5529600 | tf_op jit(solution)/shard_map/while/body/eval_jaxpr/broadcast_in_dim | solution.py:26
  105.8 10.3 %slice.145 = f32[8,24,10,18,18]{1,0,4,3,2:T(8,128)} slice(f32[8,24,12,20,20]{1,0,4,3,2:T(8,128)} %bitcast.27), slice={[0:8], [0:24], [1:11], [1:19], [1:19]} | slice | bytes 4976640 | tf_op jit(solution)/shard_map/while/body/eval_jaxpr/slice | solution.py:27
  116.2 13.9 %copy.47 = f32[8,24,10,18,18]{1,4,3,2,0:T(8,128)} copy(f32[8,24,10,18,18]{1,0,4,3,2:T(8,128)} %slice.145) | data formatting | bytes 4976640
  130.0 2.3 fusion.21
  132.3 3.4 %collective-permute-start = (f32[8,24,1,256]{3,2,1,0:T(1,128)S(1)}, f32[8,24,1,256]{3,2,1,0:T(1,128)S(1)}, u32[]{:S(2)}, u32[]{:S(2)}) collective-permute-start(f32[8,24,1,256]{3,2,1,0:T(1,128)S(1)} %get-tuple-element.51), channel_id=1, source_target_pairs={{0,2},{1,3},{4,6},{5,7},{8,10},{9,11},{12,14},{13,15},{16,18},{17,... | collective-permute-start | bytes 589832 | tf_op jit(solution)/shard_map/ppermute | solution.py:15
  135.7 1.5 collective-permute-start.1
  137.2 3.1 %fusion.20 = (f32[8,24,1,16,16]{1,0,4,3,2:T(8,128)}, f32[8,24,1,16,16]{1,0,4,3,2:T(8,128)}) fusion(f32[8,24,12,20,20]{1,0,4,3,2:T(8,128)} %bitcast.28), kind=kLoop, calls=%fused_computation.58 | loop fusion | bytes 786432 | tf_op jit(solution)/shard_map/while/body/eval_jaxpr/slice | solution.py:126
  140.3 1.6 copy.43
  141.9 2.4 collective-permute-done.1
  144.3 0.6 pad_maximum_fusion.3
  144.9 6.7 %copy.33 = f32[8,24,10,256]{1,3,2,0:T(8,128)} copy(f32[8,24,10,256]{3,2,1,0:T(8,128)S(1)} %pad_maximum_fusion.3) | data formatting | bytes 3932160 | tf_op jit(solution)/shard_map/concatenate | solution.py:13
  151.6 4.5 %slice.140 = f32[8,24,8,16,16]{1,4,3,2,0:T(8,128)S(1)} slice(f32[8,24,10,16,16]{1,4,3,2,0:T(8,128)} %bitcast.29), slice={[0:8], [0:24], [1:9], [0:16], [0:16]} | slice | bytes 3145728 | tf_op jit(solution)/shard_map/while/body/eval_jaxpr/slice | solution.py:131
  156.2 3.6 %slice_select_fusion = (f32[8,24,1,16,16]{1,4,3,2,0:T(8,128)S(1)}, f32[8,24,1,16,16]{1,4,3,2,0:T(8,128)S(1)}) fusion(f32[8,24,10,16,16]{1,4,3,2,0:T(8,128)} %bitcast.30, f32[8,24,1,16,16]{1,0,4,3,2:T(8,128)S(1)} %copy-done.2, pred[]{:T(512)S(6)} %eq.95, f32[8,24,1,16,16]{1,0,4,3,2:T(8,128)S(1)} %copy-done.3, pred[]{:T(512)S(6)} %eq.81), kind=kLoop, calls=%fused_computation.16 | loop fusion | flops 98304 | bytes 1179650 | tf_op jit(solution)/shard_map/while/body/eval_jaxpr/jit(_where)/select_n | solution.py:126
  159.8 5.6 %pad_maximum_fusion = f32[8,24,10,16,16]{1,4,3,2,0:T(8,128)} fusion(f32[8,24,1,16,16]{1,4,3,2,0:T(8,128)S(1)} %get-tuple-element.50, f32[8,24,8,16,16]{1,4,3,2,0:T(8,128)S(1)} %slice.140, f32[8,24,1,16,16]{1,4,3,2,0:T(8,128)S(1)} %get-tuple-element.49), kind=kLoop, calls=%fused_computation.4 | loop fusion | flops 983040 | bytes 3932160 | tf_op jit(solution)/shard_map/while/body/eval_jaxpr/concatenate | solution.py:130
  165.4 61.1 %scatter.21 = f32[8,24,10,18,18]{1,4,3,2,0:T(8,128)} dynamic-update-slice(f32[8,24,10,18,18]{1,4,3,2,0:T(8,128)} %copy.47, f32[8,24,10,16,16]{1,4,3,2,0:T(8,128)} %pad_maximum_fusion, s32[]{:T(128)} %constant.106.clone.1, s32[]{:T(128)} %constant.106.clone.1, s32[]{:T(128)} %constant.106.clone.1, s32[]{:T(128)} %constant.111.clone.1, s32[]{:T(128)} %constant.111.clone.1) | dynamic-update-slice | bytes 3932164 | tf_op jit(solution)/shard_map/while/body/eval_jaxpr/scatter | solution.py:133
  226.6 29.4 %multiply_subtract_fusion = (f32[8,24,8,16,16]{1,4,3,2,0:T(8,128)}, f32[8,24,8,16,16]{1,4,3,2,0:T(8,128)}) fusion(f32[8,24,8,16,16]{1,4,3,2,0:T(8,128)} %copy-done, f32[8,24,10,18,18]{1,4,3,2,0:T(8,128)} %scatter.21, f32[8,24,1,16,16]{1,4,3,2,0:T(8,128)S(1)} %get-tuple-element.50, f32[8,24,1,16,16]{1,4,3,2,0:T(8,128)S(1)} %get-tuple-element.49), kind=kLoop, calls=%fused_computation.14 | loop fusion | flops 5898240 | bytes 11403264 | tf_op jit(solution)/shard_map/while/body/eval_jaxpr/sub | solution.py:38
  256.0 13.9 %fusion = f32[8,8,16,16,12]{4,3,2,1,0:T(8,128)} fusion(f32[8,24,8,16,16]{1,4,3,2,0:T(8,128)S(1)} %copy-done.1, f32[8,24,8,16,16]{1,4,3,2,0:T(8,128)} %get-tuple-element.46, f32[8,24,8,16,16]{1,4,3,2,0:T(8,128)} %get-tuple-element.45, s32[]{:T(128)S(6)} %select_n.95, f32[24,24]{1,0:T(8,128)S(1)} %copy-done.6, f32[24,24]{1,0:T(8,128)S(1)} %copy-done.7, ...), kind=kOutput, calls=%fused_computation.7 | convolution fusion | flops 172230336 | bytes 5511940 | tf_op jit(solution)/shard_map/while/body/eval_jaxpr/fg,bgxyz->bfxyz/dot_general | solution.py:135
  269.9 5.2 %copy.42 = f32[8,12,8,256]{3,2,1,0:T(8,128)S(1)} copy(f32[8,12,8,256]{1,3,2,0:T(8,128)} %bitcast.32) | data formatting | bytes 1572864 | tf_op jit(solution)/shard_map/reshape | solution.py:147
  275.2 1.0 broadcast_multiply_fusion
  (40 shorter events, 0.4 us)
Async XLA Ops:
  9.8 9.7 %copy-start.10 = (s32[16]{0:T(128)S(1)}, s32[16]{0:T(128)}, u32[]{:S(2)}) copy-start(s32[16]{0:T(128)} %param.11) | copy-start | bytes 196
  10.8 8.0 %copy-start.5 = (f32[8,12,1000]{2,0,1:T(8,128)S(1)}, f32[8,12,1000]{2,0,1:T(8,128)}, u32[]{:S(2)}) copy-start(f32[8,12,1000]{2,0,1:T(8,128)} %param.12) | copy-start | bytes 1152004
  10.8 62.7 %copy-start.9 = (s32[16]{0:T(128)S(1)}, s32[16]{0:T(128)}, u32[]{:S(2)}) copy-start(s32[16]{0:T(128)} %param.10) | copy-start | bytes 196
  12.4 60.1 %all-to-all-start = ((f32[3,8,12,8,256]{4,3,2,0,1:T(8,128)}), f32[3,8,12,8,256]{4,3,2,0,1:T(8,128)S(1)}, u32[]{:S(2)}, u32[]{:S(2)}) async-start(f32[3,8,12,8,256]{4,3,2,0,1:T(8,128)} %copy.32), calls=%async_computation | async-start | bytes 4718592 | tf_op jit(solution)/shard_map/all_to_all | solution.py:69
  18.7 111.3 %all-gather.4.cloned.1.call-start = ((), (), s32[]{:S(2)}) async-start(), calls=%async_computation.2 | async-start | bytes 2359296 | tf_op jit(solution)/shard_map/all_gather | solution.py:112
  77.6 13.2 %all-to-all-start.1 = ((f32[8,12,600]{2,1,0:T(8,128)}), f32[8,12,600]{2,1,0:T(8,128)S(1)}, u32[]{:S(2)}, u32[]{:S(2)}) async-start(f32[8,12,600]{2,1,0:T(8,128)} %scatter_fusion.1), calls=%async_computation.1 | async-start | bytes 655360 | tf_op jit(solution)/shard_map/all_to_all | solution.py:106
  130.0 14.3 %copy-start.4 = (f32[1,8,24,8,256]{4,3,2,0,1:T(8,128)S(1)}, f32[1,8,24,8,256]{4,3,2,0,1:T(8,128)}, u32[]{:S(2)}) copy-start(f32[1,8,24,8,256]{4,3,2,0,1:T(8,128)} %all-gather.4.cloned.1.call-done) | copy-start | bytes 4718596
  132.3 9.6 %collective-permute-start = (f32[8,24,1,256]{3,2,1,0:T(1,128)S(1)}, f32[8,24,1,256]{3,2,1,0:T(1,128)S(1)}, u32[]{:S(2)}, u32[]{:S(2)}) collective-permute-start(f32[8,24,1,256]{3,2,1,0:T(1,128)S(1)} %get-tuple-element.51), channel_id=1, source_target_pairs={{0,2},{1,3},{4,6},{5,7},{8,10},{9,11},{12,14},{13,15},{16,18},{17,... | collective-permute-start | bytes 589832 | tf_op jit(solution)/shard_map/ppermute | solution.py:15
  135.7 8.6 %collective-permute-start.1 = (f32[8,24,1,256]{3,2,1,0:T(1,128)S(1)}, f32[8,24,1,256]{3,2,1,0:T(1,128)S(1)}, u32[]{:S(2)}, u32[]{:S(2)}) collective-permute-start(f32[8,24,1,256]{3,2,1,0:T(1,128)S(1)} %get-tuple-element.52), channel_id=1, source_target_pairs={{2,0},{3,1},{6,4},{7,5},{10,8},{11,9},{14,12},{15,13},{18,16},{19,... | collective-permute-start | bytes 589832 | tf_op jit(solution)/shard_map/ppermute | solution.py:17
  151.6 4.5 %copy-start.2 = (f32[8,24,1,16,16]{1,0,4,3,2:T(8,128)S(1)}, f32[8,24,1,16,16]{1,0,4,3,2:T(8,128)}, u32[]{:S(2)}) copy-start(f32[8,24,1,16,16]{1,0,4,3,2:T(8,128)} %get-tuple-element.47) | copy-start | bytes 589828
  151.6 4.5 %copy-start.3 = (f32[8,24,1,16,16]{1,0,4,3,2:T(8,128)S(1)}, f32[8,24,1,16,16]{1,0,4,3,2:T(8,128)}, u32[]{:S(2)}) copy-start(f32[8,24,1,16,16]{1,0,4,3,2:T(8,128)} %get-tuple-element.48) | copy-start | bytes 589828
  156.1 3.6 %copy-start = (f32[8,24,8,16,16]{1,4,3,2,0:T(8,128)}, f32[8,24,8,16,16]{1,4,3,2,0:T(8,128)S(1)}, u32[]{:S(2)}) copy-start(f32[8,24,8,16,16]{1,4,3,2,0:T(8,128)S(1)} %slice.140) | copy-start | bytes 4718596
  226.6 29.4 %copy-start.1 = (f32[8,24,8,16,16]{1,4,3,2,0:T(8,128)S(1)}, f32[8,24,8,16,16]{1,4,3,2,0:T(8,128)}, u32[]{:S(2)}) copy-start(f32[8,24,8,16,16]{1,4,3,2,0:T(8,128)} %copy-done) | copy-start | bytes 4718596
  226.6 29.4 %copy-start.6 = (f32[24,24]{1,0:T(8,128)S(1)}, f32[24,24]{1,0:T(8,128)}, u32[]{:S(2)}) copy-start(f32[24,24]{1,0:T(8,128)} %param.13) | copy-start | bytes 6916
  226.6 29.4 %copy-start.7 = (f32[24,24]{1,0:T(8,128)S(1)}, f32[24,24]{1,0:T(8,128)}, u32[]{:S(2)}) copy-start(f32[24,24]{1,0:T(8,128)} %param.14) | copy-start | bytes 6916
  226.6 29.4 %copy-start.8 = (f32[24,24]{1,0:T(8,128)S(1)}, f32[24,24]{1,0:T(8,128)}, u32[]{:S(2)}) copy-start(f32[24,24]{1,0:T(8,128)} %param.15) | copy-start | bytes 6916
Sparse Core Ops, SparseCore 0:
  73.7 8.9 all-gather.3
where the time goes:
time: 285 us; the launch traced here: 283 us
  local copies, waits for them, and re-layouts  133 us (47%)
  waiting for transfers between devices  63.7 us (22%)
  other arithmetic  41 us (14%)
  starting transfers between devices  14.7 us (5%)
  between operations  14.4 us (5%)
  matrix products  13.9 us (5%)
    scatter x1, local copies, waits for them, and re-layouts, slope_block(): padded = padded.at[:, :, :, 1:-1, 1:-1].set(inner)  61.1 us
    all_to_all x1, waiting for transfers between devices, body(): lax.all_to_all(outgoing, 'box', split_axis=1, concat_axis=1, tiled=True)  52.4 us
    sub x1, other arithmetic, stencil_terms(): x_after + x_before + y_after + y_before + z_after + z_before - 6.0 * centre  29.4 us
    unnamed x25, local copies, waits for them, and re-layouts  16.9 us
    dot_general x1, matrix products, slope_block(): jnp.einsum('fg,bgxyz->bfxyz', own_mixing, stencil_all, precision=lax.Prec...  13.9 us
    slice x1, local copies, waits for them, and re-layouts, prolong_block(): return values[..., 1:-1, 1:-1, 1:-1]  10.3 us
    broadcast_in_dim x3, local copies, waits for them, and re-layouts, prolong_block(): values = jnp.repeat(values, 2, axis=axis_pos)  9.95 us
    all_to_all x1, waiting for transfers between devices, body(): lax.all_to_all(outgoing_faces, 'box', split_axis=0, concat_axis=0, tiled=...  8.86 us
  transfers between devices with their start and end apart: 5, of which 3 were waited for; matrix products, arithmetic and copies ran while one was open for 17% of the time, Pallas kernels for 0%

commit v1 on v0

v1 whole, which is shorter than its diff:
```python
import functools

import jax
import jax.numpy as jnp
import numpy as np
from jax import lax
from jax.experimental import pallas as pl
from jax.experimental.pallas import tpu as pltpu
from jax.sharding import PartitionSpec as P

HIGHEST = lax.Precision.HIGHEST
ROWS = 16


def round_up(value, unit):
    return -(-value // unit) * unit


def split_three(values):
    high = values.astype(jnp.bfloat16)
    rest = values - high.astype(jnp.float32)
    middle = rest.astype(jnp.bfloat16)
    low = (rest - middle.astype(jnp.float32)).astype(jnp.bfloat16)
    return high, middle, low


def pack_kernel(levels, per_device, slots, dest_ref, boxes_ref, *refs):
    outs, (table, zeros, sems) = refs[: len(levels)], refs[len(levels) :]
    own = lax.axis_index("box")
    zeros[...] = jnp.zeros_like(zeros)
    for slot in range(slots):
        table[slot] = -1

    def place(b, carry):
        slot = 2 * dest_ref[own * per_device + b]
        slot = jnp.where(table[slot] >= 0, slot + 1, slot)
        table[slot] = b
        return carry

    lax.fori_loop(0, per_device, place, 0)
    for n, level in enumerate(levels):
        for slot in range(slots):
            b = table[slot]

            @pl.when(b >= 0)
            def _():
                pltpu.make_async_copy(boxes_ref.at[level, b], outs[n].at[slot], sems.at[n, slot]).start()

            @pl.when(b < 0)
            def _():
                pltpu.make_async_copy(zeros, outs[n].at[slot], sems.at[n, slot]).start()

    for n in range(len(levels)):
        for slot in range(slots):
            pltpu.make_async_copy(zeros, outs[n].at[slot], sems.at[n, slot]).wait()


def pack_levels(levels, boxes, move_dest, slots):
    per_device = boxes.shape[1]
    item = boxes.shape[2:]
    size = int(np.prod(item)) * 4
    return pl.pallas_call(
        functools.partial(pack_kernel, levels, per_device, slots),
        out_shape=[jax.ShapeDtypeStruct((slots,) + item, jnp.float32)] * len(levels),
        in_specs=[pl.BlockSpec(memory_space=pltpu.SMEM), pl.BlockSpec(memory_space=pl.ANY)],
        out_specs=[pl.BlockSpec(memory_space=pl.ANY)] * len(levels),
        scratch_shapes=[
            pltpu.SMEM((slots,), jnp.int32),
            pltpu.VMEM(item, jnp.float32),
            pltpu.SemaphoreType.DMA((len(levels), slots)),
        ],
        cost_estimate=pl.CostEstimate(
            flops=0, bytes_accessed=2 * len(levels) * slots * size, transcendentals=0
        ),
    )(move_dest, boxes)


def face_tables(coarse_side, coarse_planes, slabs):
    half = coarse_side - 2
    square = coarse_side * coarse_side
    inner = np.arange(half) + 1
    sides = []
    for c in range(coarse_planes):
        base = (c + 1) * square
        sides += [base + inner, base + (coarse_side - 1) * coarse_side + inner]
        sides += [base + inner * coarse_side, base + inner * coarse_side + coarse_side - 1]
    yz = np.concatenate(sides)
    x = (inner[:, None] * coarse_side + inner[None, :]).reshape(-1)
    lanes = round_up(yz.size + x.size, 128)
    table = np.zeros((8, lanes), np.int32)
    table[0] = -(10 ** 6)
    table[0, : yz.size] = yz
    table[1, : yz.size] = coarse_planes * square
    table[0, yz.size : yz.size + x.size] = x
    table[2, yz.size : yz.size + x.size] = (coarse_side - 1) * square
    return table


def expand_table(coarse_planes, edge, lanes):
    half = edge // 2
    cross = edge * edge
    spread = np.zeros((lanes, (2 * coarse_planes + 1) * cross), np.float32)
    for c in range(coarse_planes):
        base = c * 4 * half
        forward, backward = 2 * c * cross, (2 * c + 1) * cross
        for m in range(edge):
            spread[base + m // 2, backward + m] += 1
            spread[base + half + m // 2, forward + (edge - 1) * edge + m] += 1
            spread[base + 2 * half + m // 2, backward + m * edge] += 1
            spread[base + 3 * half + m // 2, forward + m * edge + edge - 1] += 1
    base, to = coarse_planes * 4 * half, 2 * coarse_planes * cross
    for y in range(edge):
        for z in range(edge):
            spread[base + (y // 2) * half + z // 2, to + y * edge + z] = 1
    return spread


def faces_kernel(slots, total, dest_ref, parent_ref, coarse_ref, table_ref, out_ref, picked, table):
    coarse_count, fields, cells = coarse_ref.shape
    own, slab = lax.axis_index("box"), lax.axis_index("slab")
    picked[...] = jnp.zeros_like(picked)
    for slot in range(slots):
        table[slot] = -1

    def place(b, carry):
        slot = 2 * dest_ref[b]
        local = parent_ref[b] - own * coarse_count

        @pl.when(jnp.logical_and(local >= 0, local < coarse_count))
        def _():
            table[jnp.where(table[slot] >= 0, slot + 1, slot)] = local

        return carry

    lax.fori_loop(0, total, place, 0)
    for slot in range(slots):
        local = table[slot]

        @pl.when(local >= 0)
        def _():
            picked[slot * ROWS : slot * ROWS + fields, :cells] = coarse_ref[local]

    index = table_ref[0:1] + slab * table_ref[1:2] + jnp.where(slab > 0, table_ref[2:3], 0)
    cell = lax.broadcasted_iota(jnp.int32, (picked.shape[1], index.shape[1]), 0)
    chosen = (cell == index).astype(jnp.float32).astype(jnp.bfloat16)
    high, middle, low = (
        jnp.dot(part, chosen, preferred_element_type=jnp.float32) for part in split_three(picked[...])
    )
    out_ref[...] = (high + (middle + low)).reshape(out_ref.shape)


def pack_faces(coarse, move_dest, parent, slots, slabs, coarse_side, coarse_planes):
    table = face_tables(coarse_side, coarse_planes, slabs)
    lanes = table.shape[1]
    depth = round_up(coarse.shape[2], 128)
    smem, vmem = pl.BlockSpec(memory_space=pltpu.SMEM), pl.BlockSpec(memory_space=pltpu.VMEM)
    return pl.pallas_call(
        functools.partial(faces_kernel, slots, move_dest.shape[0]),
        out_shape=jax.ShapeDtypeStruct((slots, ROWS, lanes), jnp.float32),
        in_specs=[smem, smem, vmem, vmem],
        out_specs=vmem,
        scratch_shapes=[pltpu.VMEM((slots * ROWS, depth), jnp.float32), pltpu.SMEM((slots,), jnp.int32)],
        compiler_params=pltpu.CompilerParams(vmem_limit_bytes=32 * 2 ** 20),
        cost_estimate=pl.CostEstimate(
            flops=6 * slots * ROWS * depth * lanes, bytes_accessed=4 * coarse.size, transcendentals=0
        ),
    )(move_dest, parent, coarse, jnp.asarray(table))


def slope_columns(fields, planes, coarse_planes):
    column_field, forward, backward, centre = [], [], [], []
    p = np.arange(planes)

    def add(field, f, b, c):
        column_field.append(field)
        forward.append(f * np.ones(planes))
        backward.append(b * np.ones(planes))
        centre.append(c * np.ones(planes))

    for f, b, c in ((1, 0, 0), (0, 1, 0), (0, 0, 1)):
        for g in range(2 * fields):
            for q in range(planes):
                here = p == q
                add(g, f * here + c * (p + 1 == q), b * here + c * (p - 1 == q), c * here)
    rows = [g if g < fields else -1 for g in range(ROWS)]
    rows += [fields + g if g < fields else -1 for g in range(ROWS)]
    for g in rows:
        add(g, 0, p == 0, 0)
    for g in rows:
        add(g, p == planes - 1, 0, 0)
    for c in range(coarse_planes):
        for g in rows:
            add(g, p // 2 == c, 0, 0)
        for g in rows:
            add(g, 0, p // 2 == c, 0)
    width = round_up(len(column_field), 128)
    select = np.zeros((2 * fields, width), np.float32)
    masks = np.zeros((3, planes, width), np.float32)
    for k, g in enumerate(column_field):
        if g >= 0:
            select[g, k] = 1
        masks[0, :, k], masks[1, :, k], masks[2, :, k] = forward[k], backward[k], centre[k]
    return select, masks


def slope_kernel(
    edge, planes, fields, coarse_planes, per_device, total, coarse_count, slots, slabs,
    dest_ref, parent_ref, own_ref, other_ref, own_low, other_low, own_high, other_high,
    own_faces, other_faces, spread_ref, weight_ref, out_ref, stack, table, count,
):
    step = pl.program_id(0)
    cross = edge * edge
    rows = fields * planes
    own, slab = lax.axis_index("box"), lax.axis_index("slab")

    @pl.when(step == 0)
    def _():
        stack[...] = jnp.zeros_like(stack)
        for slot in range(slots):
            table[slot] = -1
            count[slot] = 0

        def place(b, carry):
            @pl.when(dest_ref[b] == own)
            def _():
                slot = 2 * (b // per_device)
                owner = parent_ref[b] // coarse_count
                table[jnp.where(table[slot] >= 0, slot + 1, slot)] = 2 * owner + count[owner]
                count[owner] = count[owner] + 1

            return carry

        lax.fori_loop(0, total, place, 0)

    face = table[step]

    @pl.when(face < 0)
    def _():
        out_ref[...] = jnp.zeros_like(out_ref)

    @pl.when(face >= 0)
    def _():
        lane = lax.broadcasted_iota(jnp.int32, (1, cross), 1)
        y, z = lane // edge, lane % edge
        if planes % 8:
            for n, ref in enumerate((own_ref, other_ref)):
                for f in range(fields):
                    at = 4 * rows + n * rows + f * planes
                    stack[at : at + planes] = ref[0, f]
        else:
            stack[4 * rows : 5 * rows] = own_ref[0].reshape(rows, cross)
            stack[5 * rows : 6 * rows] = other_ref[0].reshape(rows, cross)
        cells = stack[4 * rows : 6 * rows]
        stack[0 : 2 * rows] = jnp.where(y < edge - 1, pltpu.roll(cells, cross - edge, 1), 0.0) + jnp.where(
            z < edge - 1, pltpu.roll(cells, cross - 1, 1), 0.0
        )
        stack[2 * rows : 4 * rows] = jnp.where(y > 0, pltpu.roll(cells, edge, 1), 0.0) + jnp.where(
            z > 0, pltpu.roll(cells, 1, 1), 0.0
        )
        rim = jnp.concatenate([own_faces[face], other_faces[face]], axis=0)
        high, middle, low = (
            jnp.dot(part, spread_ref[...], preferred_element_type=jnp.float32) for part in split_three(rim)
        )
        ghosts = high + (middle + low)
        base = 6 * rows
        x_face = ghosts[:, 2 * coarse_planes * cross :]
        stack[base : base + 2 * ROWS] = x_face
        stack[base + 2 * ROWS : base + 4 * ROWS] = x_face

        @pl.when(slab > 0)
        def _():
            stack[base : base + fields] = own_low[0]
            stack[base + ROWS : base + ROWS + fields] = other_low[0]

        @pl.when(slab < slabs - 1)
        def _():
            stack[base + 2 * ROWS : base + 2 * ROWS + fields] = own_high[0]
            stack[base + 3 * ROWS : base + 3 * ROWS + fields] = other_high[0]

        base += 4 * ROWS
        for n in range(2 * coarse_planes):
            stack[base + 2 * ROWS * n : base + 2 * ROWS * (n + 1)] = ghosts[:, n * cross : (n + 1) * cross]
        mixed = jnp.dot(weight_ref[...], stack[...], precision=HIGHEST, preferred_element_type=jnp.float32)
        if planes % 8:
            for f in range(fields):
                out_ref[0, f] = mixed[f * planes : (f + 1) * planes]
        else:
            out_ref[0] = mixed.reshape(fields, planes, cross)


def body(boxes, move_dest, parent, coarse, lap_mix, grad_mix, damp_mix):
    box_count = lax.axis_size("box")
    slabs = lax.axis_size("slab")
    slab = lax.axis_index("slab")
    group = lax.axis_index("fld")
    levels, per_device, fields, planes, cross = boxes.shape
    edge = planes * slabs
    coarse_side = edge // 2 + 2
    coarse_planes = planes // 2
    slots = 2 * box_count
    total = move_dest.shape[0]
    coarse_count = coarse.shape[0]

    def exchange(values):
        return lax.all_to_all(values, "box", split_axis=0, concat_axis=0, tiled=True)

    (now,) = pack_levels((0,), boxes, move_dest, slots)
    now = exchange(now)
    faces = pack_faces(coarse, move_dest, parent, slots, slabs, coarse_side, coarse_planes)
    faces = exchange(faces)
    later = pack_levels(tuple(range(1, levels)), boxes, move_dest, slots)
    later = [exchange(values) for values in later]

    swap = [(0, 1), (1, 0)]
    now_other = lax.ppermute(now, "fld", swap)
    faces_other = lax.ppermute(faces, "fld", swap)

    def shifted(values, up):
        pairs = [(s, s + 1) if up else (s + 1, s) for s in range(slabs - 1)]
        crossed = [(2 * a + f, 2 * b + 1 - f) for a, b in pairs for f in range(2)]
        return lax.ppermute(values, "slab", pairs), lax.ppermute(values, ("slab", "fld"), crossed)

    first, last = now[:, :, 0], now[:, :, planes - 1]
    if slabs == 2:
        facing = jnp.where(slab == 0, last, first)
        pairs = [(0, 1), (1, 0)]
        crossed = [(0, 3), (3, 0), (1, 2), (2, 1)]
        low = high = (lax.ppermute(facing, "slab", pairs), lax.ppermute(facing, ("slab", "fld"), crossed))
    else:
        low, high = shifted(last, True), shifted(first, False)

    select, masks = slope_columns(fields, planes, coarse_planes)
    terms = jnp.stack([lap_mix + 0.5 * grad_mix, lap_mix - 0.5 * grad_mix, damp_mix - 6.0 * lap_mix])
    terms = lax.dynamic_slice_in_dim(terms, group * fields, fields, 1)
    terms = jnp.where(group == 0, terms, jnp.roll(terms, fields, axis=2))
    terms = jnp.einsum("tfg,gk->tfk", terms, jnp.asarray(select), precision=HIGHEST)
    width = select.shape[1]
    weight = jnp.sum(terms[:, :, None, :] * jnp.asarray(masks)[:, None], axis=0).reshape(fields * planes, width)
    spread = expand_table(coarse_planes, edge, faces.shape[2])
    spread = jnp.asarray(spread).astype(jnp.bfloat16)

    smem = pl.BlockSpec(memory_space=pltpu.SMEM)
    by_slot = pl.BlockSpec((1, fields, planes, cross), lambda n: (n, 0, 0, 0))
    rim_slot = pl.BlockSpec((1, fields, cross), lambda n: (n, 0, 0))
    whole_faces = pl.BlockSpec(faces.shape, lambda n: (0, 0, 0))
    slope = pl.pallas_call(
        functools.partial(
            slope_kernel, edge, planes, fields, coarse_planes, per_device, total, coarse_count, slots, slabs
        ),
        grid=(slots,),
        out_shape=jax.ShapeDtypeStruct(now.shape, jnp.float32),
        in_specs=[smem, smem, by_slot, by_slot, rim_slot, rim_slot, rim_slot, rim_slot, whole_faces, whole_faces]
        + [pl.BlockSpec(spread.shape, lambda n: (0, 0)), pl.BlockSpec(weight.shape, lambda n: (0, 0))],
        out_specs=by_slot,
        scratch_shapes=[
            pltpu.VMEM((width, cross), jnp.float32),
            pltpu.SMEM((slots,), jnp.int32),
            pltpu.SMEM((slots,), jnp.int32),
        ],
        compiler_params=pltpu.CompilerParams(vmem_limit_bytes=32 * 2 ** 20),
        cost_estimate=pl.CostEstimate(
            flops=12 * slots * weight.shape[0] * width * cross, bytes_accessed=12 * now.size, transcendentals=0
        ),
    )(move_dest, parent, now, now_other, low[0], low[1], high[0], high[1], faces, faces_other, spread, weight)
    return jnp.stack([now] + later), slope


def solution(mesh):
    placed = (
        P(None, ("runs", "box"), "fld", "slab", None),
        P("runs"),
        P("runs"),
        P(("runs", "box"), "fld", None),
        P(),
        P(),
        P(),
    )
    return jax.shard_map(
        body,
        mesh=mesh,
        in_specs=placed,
        out_specs=(
            P(None, ("runs", "box"), "fld", "slab", None),
            P(("runs", "box"), "fld", "slab", None),
        ),
        check_vma=False,
    )
```

time: 285 us -> 123 us (0.43)
  the two profiles are of different devices: /device:TPU:0 before, /device:TPU:4 now
where the time goes in v1:
time: 123 us; the launch traced here: 124 us
  Pallas kernels  59 us (48%)
  waiting for transfers between devices  35.6 us (29%)
  starting transfers between devices  21.6 us (18%)
  local copies, waits for them, and re-layouts  3.46 us (3%)
  other arithmetic  3 us (2%)
    pallas_call x2, Pallas kernels, pack_levels(): pl.pallas_call(functools.partial(pack_kernel, levels, per_device, slots),...  39.8 us
    all_to_all x4, waiting for transfers between devices, exchange(): lax.all_to_all(values, 'box', split_axis=0, concat_axis=0, tiled=True)  35.6 us
    all_to_all x4, starting transfers between devices, exchange(): lax.all_to_all(values, 'box', split_axis=0, concat_axis=0, tiled=True)  19.3 us
    pallas_call x1, Pallas kernels, body(): pl.pallas_call(functools.partial(slope_kernel, edge, planes, fields, coar...  17.2 us
    unnamed x23, local copies, waits for them, and re-layouts  3.27 us
    another operation x1, other arithmetic, body(): return (jnp.stack([now] + later), slope)  2.86 us
  transfers between devices with their start and end apart: 8, of which 2 were waited for; matrix products, arithmetic and copies ran while one was open for 3% of the time, Pallas kernels for 32%

profile of v1, /device:TPU:4, one launch (start us, length us, event | category | flops | bytes accessed | tf_op | source)
XLA Modules:
  0.0 123.8 jit_solution(2024410974892459611)
XLA Ops:
  0.6 1.2 copy.25.coarse_ref
  1.9 0.0 copy-start
  1.9 0.6 copy-done
  2.5 0.0 copy-start.2
  2.5 0.7 copy-done.2
  3.2 0.0 copy-start.5
  3.2 0.7 copy-done.5
  3.9 2.0 %shard_map.124 = f32[8,16,256]{2,1,0:T(8,128)} custom-call(s32[16]{0:T(128)S(1)} %copy-done, s32[16]{0:T(128)S(1)} %copy-done.2, f32[8,12,1000]{2,1,0:T(8,128)S(1)} %copy.25.coarse_ref, s32[8,256]{1,0:T(8,128)S(1)} %copy-done.5), custom_call_target="tpu_custom_call" | custom-call | flops 201326592 | bytes 384000 | tf_op jit(solution)/shard_map/pallas_call | solution.py:157
  5.8 4.9 %all-to-all-start.3 = ((f32[8,16,256]{2,1,0:T(8,128)}), f32[8,16,256]{2,1,0:T(8,128)S(1)}, u32[]{:S(2)}, u32[]{:S(2)}) async-start(f32[8,16,256]{2,1,0:T(8,128)} %shard_map.124), calls=%async_computation.3 | async-start | bytes 262144 | tf_op jit(solution)/shard_map/all_to_all | solution.py:305
  10.7 13.8 %shard_map.122 = f32[8,12,8,256]{3,2,1,0:T(8,128)} custom-call(s32[16]{0:T(128)} %dest_ref.7, f32[3,4,12,8,256]{4,3,2,1,0:T(8,128)} %boxes_ref.3), custom_call_target="tpu_custom_call" | custom-call | bytes 1572864 | tf_op jit(solution)/shard_map/pallas_call | solution.py:62
  24.5 0.0 copy-start.8
  24.5 0.0 copy-start.9
  24.6 0.0 copy-start.10
  24.6 0.0 all-to-all-done.3.own_faces
  24.6 5.1 %all-to-all-start = ((f32[8,12,8,256]{3,2,1,0:T(8,128)}), f32[8,12,8,256]{3,2,1,0:T(8,128)S(1)}, u32[]{:S(2)}, u32[]{:S(2)}) async-start(f32[8,12,8,256]{3,2,1,0:T(8,128)} %shard_map.122), calls=%async_computation | async-start | bytes 1572864 | tf_op jit(solution)/shard_map/all_to_all | solution.py:305
  29.7 0.0 copy-start.7
  29.7 0.0 copy-start.6
  29.7 25.9 %shard_map.123 = (f32[8,12,8,256]{3,2,1,0:T(8,128)}, f32[8,12,8,256]{3,2,1,0:T(8,128)}) custom-call(s32[16]{0:T(128)} %dest_ref.7, f32[3,4,12,8,256]{4,3,2,1,0:T(8,128)} %boxes_ref.3), custom_call_target="tpu_custom_call" | custom-call | bytes 3145728 | tf_op jit(solution)/shard_map/pallas_call | solution.py:62
  55.6 0.0 all-to-all-done.own_ref
  55.6 5.1 %all-to-all-start.1 = ((f32[8,12,8,256]{3,2,1,0:T(8,128)}), f32[8,12,8,256]{3,2,1,0:T(8,128)S(1)}, u32[]{:S(2)}, u32[]{:S(2)}) async-start(f32[8,12,8,256]{3,2,1,0:T(8,128)} %get-tuple-element.4), calls=%async_computation.1 | async-start | bytes 1572864 | tf_op jit(solution)/shard_map/all_to_all | solution.py:305
  60.7 0.0 copy-done.8
  60.7 0.0 copy-done.9
  60.8 0.0 copy-done.10
  60.8 19.0 %all-to-all-done.1 = f32[8,12,8,256]{3,2,1,0:T(8,128)S(1)} async-done(((f32[8,12,8,256]{3,2,1,0:T(8,128)}), f32[8,12,8,256]{3,2,1,0:T(8,128)S(1)}, u32[]{:S(2)}, u32[]{:S(2)}) %all-to-all-start.1) | async-done | bytes 786464 | tf_op jit(solution)/shard_map/all_to_all | solution.py:305
  79.7 4.2 %all-to-all-start.2 = ((f32[8,12,8,256]{3,2,1,0:T(8,128)}), f32[8,12,8,256]{3,2,1,0:T(8,128)}, u32[]{:S(2)}, u32[]{:S(2)}) async-start(f32[8,12,8,256]{3,2,1,0:T(8,128)} %get-tuple-element.5), calls=%async_computation.2 | async-start | bytes 1572864 | tf_op jit(solution)/shard_map/all_to_all | solution.py:305
  84.0 0.1 fusion.9
  84.0 0.0 copy-done.7
  84.0 0.4 fusion.3
  84.4 0.1 collective-permute-start
  84.5 0.0 copy-done.6
  84.5 0.1 multiply_reduce_fusion
  84.6 0.5 collective-permute-start.3
  85.1 0.1 fusion.8
  85.3 1.2 collective-permute-start.2
  86.5 0.5 collective-permute-start.1
  87.0 16.6 %all-to-all-done.2 = f32[8,12,8,256]{3,2,1,0:T(8,128)} async-done(((f32[8,12,8,256]{3,2,1,0:T(8,128)}), f32[8,12,8,256]{3,2,1,0:T(8,128)}, u32[]{:S(2)}, u32[]{:S(2)}) %all-to-all-start.2) | async-done | bytes 786464 | tf_op jit(solution)/shard_map/all_to_all | solution.py:305
  103.6 0.0 copy-start.1
  103.6 0.0 copy-start.3
  103.6 0.0 copy-start.4
  103.6 2.9 %pad_maximum_fusion = f32[3,8,12,8,256]{4,3,2,1,0:T(8,128)} fusion(f32[1,8,12,8,256]{4,3,2,1,0:T(8,128)} %bitcast.2, f32[1,8,12,8,256]{4,3,2,1,0:T(8,128)S(1)} %bitcast.16, f32[1,8,12,8,256]{4,3,2,1,0:T(8,128)S(1)} %bitcast.14), kind=kLoop, calls=%fused_computation | loop fusion | flops 1179648 | bytes 4718592 | tf_op jit(solution)/shard_map/stack | solution.py:365
  106.5 0.0 collective-permute-done.3.other_faces
  106.5 0.0 collective-permute-done.2.other_low.other_high
  106.5 0.0 collective-permute-done.1.own_low.own_high
  106.5 0.0 collective-permute-done.other_ref
  106.5 0.0 copy-done.1
  106.5 0.0 copy-done.3
  106.5 0.0 copy-done.4
  106.5 17.2 %shard_map.125 = f32[8,12,8,256]{3,2,1,0:T(8,128)} custom-call(s32[16]{0:T(128)S(1)} %copy-done.1, s32[16]{0:T(128)S(1)} %copy-done.3, f32[8,12,8,256]{3,2,1,0:T(8,128)S(1)} %all-to-all-done.own_ref, f32[8,12,8,256]{3,2,1,0:T(8,128)S(1)} %collective-permute-done.other_ref, f32[8,12,256]{2,1,0:T(8,128)S(1)} %collective-permute-done.1.own_low.own_high, ...), custom_call_target="tpu_custom_call" | custom-call | flops 2113929216 | bytes 2359296 | tf_op jit(solution)/shard_map/pallas_call | solution.py:346
  (3 shorter events, 0.1 us)
Async XLA Ops:
  1.9 0.7 copy-start
  2.5 0.7 copy-start.2
  3.2 0.7 copy-start.5
  5.8 18.7 %all-to-all-start.3 = ((f32[8,16,256]{2,1,0:T(8,128)}), f32[8,16,256]{2,1,0:T(8,128)S(1)}, u32[]{:S(2)}, u32[]{:S(2)}) async-start(f32[8,16,256]{2,1,0:T(8,128)} %shard_map.124), calls=%async_computation.3 | async-start | bytes 262144 | tf_op jit(solution)/shard_map/all_to_all | solution.py:305
  24.5 36.2 %copy-start.8 = (f32[24,24]{1,0:T(8,128)S(1)}, f32[24,24]{1,0:T(8,128)}, u32[]{:S(2)}) copy-start(f32[24,24]{1,0:T(8,128)} %param.15) | copy-start | bytes 6916
  24.5 36.2 %copy-start.9 = (f32[24,24]{1,0:T(8,128)S(1)}, f32[24,24]{1,0:T(8,128)}, u32[]{:S(2)}) copy-start(f32[24,24]{1,0:T(8,128)} %param.16) | copy-start | bytes 6916
  24.6 36.2 %copy-start.10 = (f32[24,24]{1,0:T(8,128)S(1)}, f32[24,24]{1,0:T(8,128)}, u32[]{:S(2)}) copy-start(f32[24,24]{1,0:T(8,128)} %param.17) | copy-start | bytes 6916
  24.6 31.1 %all-to-all-start = ((f32[8,12,8,256]{3,2,1,0:T(8,128)}), f32[8,12,8,256]{3,2,1,0:T(8,128)S(1)}, u32[]{:S(2)}, u32[]{:S(2)}) async-start(f32[8,12,8,256]{3,2,1,0:T(8,128)} %shard_map.122), calls=%async_computation | async-start | bytes 1572864 | tf_op jit(solution)/shard_map/all_to_all | solution.py:305
  29.7 54.4 %copy-start.7 = (f32[24,896,1]{1,0,2:T(8,128)S(1)}, f32[24,896,1]{1,0,2:T(8,128)}, u32[]{:S(2)}) copy-start(f32[24,896,1]{1,0,2:T(8,128)} %constant.32) | copy-start | bytes 258052
  29.7 54.8 %copy-start.6 = (f32[3,8,896]{2,1,0:T(8,128)S(1)}, f32[3,8,896]{2,1,0:T(8,128)}, u32[]{:S(2)}) copy-start(f32[3,8,896]{2,1,0:T(8,128)} %constant.28.clone) | copy-start | bytes 258052
  55.6 24.1 %all-to-all-start.1 = ((f32[8,12,8,256]{3,2,1,0:T(8,128)}), f32[8,12,8,256]{3,2,1,0:T(8,128)S(1)}, u32[]{:S(2)}, u32[]{:S(2)}) async-start(f32[8,12,8,256]{3,2,1,0:T(8,128)} %get-tuple-element.4), calls=%async_computation.1 | async-start | bytes 1572864 | tf_op jit(solution)/shard_map/all_to_all | solution.py:305
  79.7 23.9 %all-to-all-start.2 = ((f32[8,12,8,256]{3,2,1,0:T(8,128)}), f32[8,12,8,256]{3,2,1,0:T(8,128)}, u32[]{:S(2)}, u32[]{:S(2)}) async-start(f32[8,12,8,256]{3,2,1,0:T(8,128)} %get-tuple-element.5), calls=%async_computation.2 | async-start | bytes 1572864 | tf_op jit(solution)/shard_map/all_to_all | solution.py:305
  84.4 22.1 %collective-permute-start = (f32[8,12,8,256]{3,2,1,0:T(8,128)S(1)}, f32[8,12,8,256]{3,2,1,0:T(8,128)S(1)}, u32[]{:S(2)}, u32[]{:S(2)}) collective-permute-start(f32[8,12,8,256]{3,2,1,0:T(8,128)S(1)} %all-to-all-done.own_ref), channel_id=1, source_target_pairs={{0,1},{1,0},{2,3},{3,2},{4,5},{5,4},{6,7},{7,6},{8,9},{9,8},{10,11... | collective-permute-start | bytes 2359304 | tf_op jit(solution)/shard_map/ppermute | solution.py:315
  84.6 21.9 %collective-permute-start.3 = (f32[8,16,256]{2,1,0:T(8,128)S(1)}, f32[8,16,256]{2,1,0:T(8,128)S(1)}, u32[]{:S(2)}, u32[]{:S(2)}) collective-permute-start(f32[8,16,256]{2,1,0:T(8,128)S(1)} %all-to-all-done.3.own_faces), channel_id=1, source_target_pairs={{0,1},{1,0},{2,3},{3,2},{4,5},{5,4},{6,7},{7,6},{8,9},{9,8},{10,11... | collective-permute-start | bytes 393224 | tf_op jit(solution)/shard_map/ppermute | solution.py:316
  85.3 21.2 %collective-permute-start.2 = (f32[8,12,256]{2,1,0:T(8,128)S(1)}, f32[8,12,256]{2,1,0:T(8,128)S(1)}, u32[]{:S(2)}, u32[]{:S(2)}) collective-permute-start(f32[8,12,256]{2,1,0:T(8,128)S(1)} %fusion), channel_id=1, source_target_pairs={{0,3},{3,0},{1,2},{2,1},{4,7},{7,4},{5,6},{6,5},{8,11},{11,8},{9,1... | collective-permute-start | bytes 294920 | tf_op jit(solution)/shard_map/ppermute | solution.py:328
  86.5 20.0 %collective-permute-start.1 = (f32[8,12,256]{2,1,0:T(8,128)S(1)}, f32[8,12,256]{2,1,0:T(8,128)S(1)}, u32[]{:S(2)}, u32[]{:S(2)}) collective-permute-start(f32[8,12,256]{2,1,0:T(8,128)S(1)} %fusion), channel_id=1, source_target_pairs={{0,2},{2,0},{1,3},{3,1},{4,6},{6,4},{5,7},{7,5},{8,10},{10,8},{9,1... | collective-permute-start | bytes 294920 | tf_op jit(solution)/shard_map/ppermute | solution.py:328
  103.6 2.9 %copy-start.1 = (s32[16]{0:T(128)S(1)}, s32[16]{0:T(128)}, u32[]{:S(2)}) copy-start(s32[16]{0:T(128)} %dest_ref.7) | copy-start | bytes 196
  103.6 2.9 %copy-start.3 = (s32[16]{0:T(128)S(1)}, s32[16]{0:T(128)}, u32[]{:S(2)}) copy-start(s32[16]{0:T(128)} %parent_ref.3) | copy-start | bytes 196
  103.6 2.9 %copy-start.4 = (bf16[256,2304]{1,0:T(8,128)(2,1)S(1)}, bf16[256,2304]{1,0:T(8,128)(2,1)}, u32[]{:S(2)}) copy-start(bf16[256,2304]{1,0:T(8,128)(2,1)} %constant.31.spread_ref) | copy-start | bytes 3538948

commit v2 on v1

--- a/solution.py
+++ b/solution.py
@@ -24,11 +24,10 @@
     return high, middle, low
 
 
-def pack_kernel(levels, per_device, slots, dest_ref, boxes_ref, *refs):
-    outs, (table, zeros, sems) = refs[: len(levels)], refs[len(levels) :]
+def pack_kernel(per_device, box_count, dest_ref, boxes_ref, *refs):
+    outs, table = refs[:box_count], refs[box_count]
     own = lax.axis_index("box")
-    zeros[...] = jnp.zeros_like(zeros)
-    for slot in range(slots):
+    for slot in range(2 * box_count):
         table[slot] = -1
 
     def place(b, carry):
@@ -38,41 +37,109 @@
         return carry
 
     lax.fori_loop(0, per_device, place, 0)
-    for n, level in enumerate(levels):
-        for slot in range(slots):
-            b = table[slot]
-
-            @pl.when(b >= 0)
-            def _():
-                pltpu.make_async_copy(boxes_ref.at[level, b], outs[n].at[slot], sems.at[n, slot]).start()
-
-            @pl.when(b < 0)
-            def _():
-                pltpu.make_async_copy(zeros, outs[n].at[slot], sems.at[n, slot]).start()
-
-    for n in range(len(levels)):
-        for slot in range(slots):
-            pltpu.make_async_copy(zeros, outs[n].at[slot], sems.at[n, slot]).wait()
-
-
-def pack_levels(levels, boxes, move_dest, slots):
+    for shift in range(box_count):
+        target = lax.rem(own + shift, box_count)
+        for k in range(2):
+            b = table[2 * target + k]
+            values = boxes_ref[0, jnp.maximum(b, 0)]
+            outs[shift][k] = jnp.where(b >= 0, values, 0.0)
+
+
+def pack_level(level, boxes, move_dest, box_count):
     per_device = boxes.shape[1]
     item = boxes.shape[2:]
     size = int(np.prod(item)) * 4
+    zero = (0,) * 4
     return pl.pallas_call(
-        functools.partial(pack_kernel, levels, per_device, slots),
-        out_shape=[jax.ShapeDtypeStruct((slots,) + item, jnp.float32)] * len(levels),
-        in_specs=[pl.BlockSpec(memory_space=pltpu.SMEM), pl.BlockSpec(memory_space=pl.ANY)],
-        out_specs=[pl.BlockSpec(memory_space=pl.ANY)] * len(levels),
-        scratch_shapes=[
-            pltpu.SMEM((slots,), jnp.int32),
-            pltpu.VMEM(item, jnp.float32),
-            pltpu.SemaphoreType.DMA((len(levels), slots)),
+        functools.partial(pack_kernel, per_device, box_count),
+        grid=(1,),
+        out_shape=[jax.ShapeDtypeStruct((2,) + item, jnp.float32)] * box_count,
+        in_specs=[
+            pl.BlockSpec(memory_space=pltpu.SMEM),
+            pl.BlockSpec((1,) + boxes.shape[1:], lambda n: (level,) + zero),
         ],
+        out_specs=[pl.BlockSpec((2,) + item, lambda n: zero)] * box_count,
+        scratch_shapes=[pltpu.SMEM((2 * box_count,), jnp.int32)],
+        compiler_params=pltpu.CompilerParams(vmem_limit_bytes=32 * 2 ** 20),
         cost_estimate=pl.CostEstimate(
-            flops=0, bytes_accessed=2 * len(levels) * slots * size, transcendentals=0
+            flops=0, bytes_accessed=(per_device + 2 * box_count) * size, transcendentals=0
         ),
     )(move_dest, boxes)
+
+
+def settle_kernel(level, box_count, *refs):
+    pieces, out_ref, sems = refs[:box_count], refs[-2], refs[-1]
+    own = lax.axis_index("box")
+
+    def copy(shift):
+        source = lax.rem(own - shift + box_count, box_count)
+        return pltpu.make_async_copy(pieces[shift], out_ref.at[level, pl.ds(2 * source, 2)], sems.at[shift])
+
+    for shift in range(box_count):
+        copy(shift).start()
+    for shift in range(box_count):
+        copy(shift).wait()
+
+
+def settle(level, pieces, moved):
+    box_count = len(pieces)
+    vmem, anywhere = pl.BlockSpec(memory_space=pltpu.VMEM), pl.BlockSpec(memory_space=pl.ANY)
+    return pl.pallas_call(
+        functools.partial(settle_kernel, level, box_count),
+        out_shape=jax.ShapeDtypeStruct(moved.shape, jnp.float32),
+        in_specs=[vmem] * box_count + [anywhere],
+        out_specs=anywhere,
+        scratch_shapes=[pltpu.SemaphoreType.DMA((box_count,))],
+        input_output_aliases={box_count: 0},
+        compiler_params=pltpu.CompilerParams(vmem_limit_bytes=32 * 2 ** 20),
+        cost_estimate=pl.CostEstimate(
+            flops=0, bytes_accessed=8 * box_count * pieces[0].size, transcendentals=0
+        ),
+    )(*pieces, moved)
+
+
+def arrive_kernel(box_count, slabs, *refs):
+    pieces, edges, sems = refs[:box_count], refs[box_count + 2 : -1], refs[-1]
+    now_ref, moved_ref = refs[box_count : box_count + 2]
+    own, slab = lax.axis_index("box"), lax.axis_index("slab")
+    _, fields, planes, _ = now_ref.shape
+
+    def copy(shift):
+        source = lax.rem(own - shift + box_count, box_count)
+        return pltpu.make_async_copy(pieces[shift], moved_ref.at[0, pl.ds(2 * source, 2)], sems.at[shift])
+
+    for shift in range(box_count):
+        copy(shift).start()
+    faced = [jnp.where(slab == 0, planes - 1, 0)] if slabs == 2 else [0, planes - 1]
+    for shift in range(box_count):
+        source = lax.rem(own - shift + box_count, box_count)
+        for k in range(2):
+            now_ref[2 * source + k] = pieces[shift][k]
+            for edge_ref, plane in zip(edges, faced):
+                for f in range(fields):
+                    edge_ref[2 * source + k, f : f + 1] = pieces[shift][k, f, pl.ds(plane, 1)]
+    for shift in range(box_count):
+        copy(shift).wait()
+
+
+def arrive(pieces, levels, slabs):
+    box_count = len(pieces)
+    _, fields, planes, cross = pieces[0].shape
+    slots = 2 * box_count
+    sides = 1 if slabs == 2 else 2
+    vmem, anywhere = pl.BlockSpec(memory_space=pltpu.VMEM), pl.BlockSpec(memory_space=pl.ANY)
+    shapes = [(slots, fields, planes, cross), (levels, slots, fields, planes, cross)] + [(slots, fields, cross)] * sides
+    return pl.pallas_call(
+        functools.partial(arrive_kernel, box_count, slabs),
+        out_shape=[jax.ShapeDtypeStruct(shape, jnp.float32) for shape in shapes],
+        in_specs=[vmem] * box_count,
+        out_specs=[vmem, anywhere] + [vmem] * sides,
+        scratch_shapes=[pltpu.SemaphoreType.DMA((box_count,))],
+        compiler_params=pltpu.CompilerParams(vmem_limit_bytes=32 * 2 ** 20),
+        cost_estimate=pl.CostEstimate(
+            flops=0, bytes_accessed=12 * box_count * pieces[0].size, transcendentals=0
+        ),
+    )(*pieces)
 
 
 def face_tables(coarse_side, coarse_planes, slabs):
@@ -115,7 +182,9 @@
     return spread
 
 
-def faces_kernel(slots, total, dest_ref, parent_ref, coarse_ref, table_ref, out_ref, picked, table):
+def faces_kernel(box_count, total, dest_ref, parent_ref, coarse_ref, table_ref, *refs):
+    outs, picked, table = refs[:box_count], refs[-2], refs[-1]
+    slots = 2 * box_count
     coarse_count, fields, cells = coarse_ref.shape
     own, slab = lax.axis_index("box"), lax.axis_index("slab")
     picked[...] = jnp.zeros_like(picked)
@@ -134,7 +203,7 @@
 
     lax.fori_loop(0, total, place, 0)
     for slot in range(slots):
-        local = table[slot]
+        local = table[2 * lax.rem(own + slot // 2, box_count) + slot % 2]
 
         @pl.when(local >= 0)
         def _():
@@ -146,7 +215,11 @@
     high, middle, low = (
         jnp.dot(part, chosen, preferred_element_type=jnp.float32) for part in split_three(picked[...])
     )
-    out_ref[...] = (high + (middle + low)).reshape(out_ref.shape)
+    chosen_cells = high + (middle + low)
+    for shift in range(box_count):
+        for k in range(2):
+            at = (2 * shift + k) * ROWS
+            outs[shift][k] = chosen_cells[at : at + ROWS]
 
 
 def pack_faces(coarse, move_dest, parent, slots, slabs, coarse_side, coarse_planes):
@@ -155,10 +228,10 @@
     depth = round_up(coarse.shape[2], 128)
     smem, vmem = pl.BlockSpec(memory_space=pltpu.SMEM), pl.BlockSpec(memory_space=pltpu.VMEM)
     return pl.pallas_call(
-        functools.partial(faces_kernel, slots, move_dest.shape[0]),
-        out_shape=jax.ShapeDtypeStruct((slots, ROWS, lanes), jnp.float32),
+        functools.partial(faces_kernel, slots // 2, move_dest.shape[0]),
+        out_shape=[jax.ShapeDtypeStruct((2, ROWS, lanes), jnp.float32)] * (slots // 2),
         in_specs=[smem, smem, vmem, vmem],
-        out_specs=vmem,
+        out_specs=[vmem] * (slots // 2),
         scratch_shapes=[pltpu.VMEM((slots * ROWS, depth), jnp.float32), pltpu.SMEM((slots,), jnp.int32)],
         compiler_params=pltpu.CompilerParams(vmem_limit_bytes=32 * 2 ** 20),
         cost_estimate=pl.CostEstimate(
@@ -257,7 +330,8 @@
         stack[2 * rows : 4 * rows] = jnp.where(y > 0, pltpu.roll(cells, edge, 1), 0.0) + jnp.where(
             z > 0, pltpu.roll(cells, 1, 1), 0.0
         )
-        rim = jnp.concatenate([own_faces[face], other_faces[face]], axis=0)
+        shift = lax.rem(own - face // 2 + slots // 2, slots // 2)
+        rim = jnp.concatenate([own_faces[shift, face % 2], other_faces[shift, face % 2]], axis=0)
         high, middle, low = (
             jnp.dot(part, spread_ref[...], preferred_element_type=jnp.float32) for part in split_three(rim)
         )
@@ -291,7 +365,6 @@
 def body(boxes, move_dest, parent, coarse, lap_mix, grad_mix, damp_mix):
     box_count = lax.axis_size("box")
     slabs = lax.axis_size("slab")
-    slab = lax.axis_index("slab")
     group = lax.axis_index("fld")
     levels, per_device, fields, planes, cross = boxes.shape
     edge = planes * slabs
@@ -301,15 +374,15 @@
     total = move_dest.shape[0]
     coarse_count = coarse.shape[0]
 
-    def exchange(values):
-        return lax.all_to_all(values, "box", split_axis=0, concat_axis=0, tiled=True)
-
-    (now,) = pack_levels((0,), boxes, move_dest, slots)
-    now = exchange(now)
-    faces = pack_faces(coarse, move_dest, parent, slots, slabs, coarse_side, coarse_planes)
-    faces = exchange(faces)
-    later = pack_levels(tuple(range(1, levels)), boxes, move_dest, slots)
-    later = [exchange(values) for values in later]
+    def exchange(pieces):
+        around = [[(s, (s + shift) % box_count) for s in range(box_count)] for shift in range(box_count)]
+        return [pieces[0]] + [lax.ppermute(pieces[n], "box", around[n]) for n in range(1, box_count)]
+
+    arrived = exchange(pack_level(0, boxes, move_dest, box_count))
+    faces = exchange(pack_faces(coarse, move_dest, parent, slots, slabs, coarse_side, coarse_planes))
+    later = [exchange(pack_level(level, boxes, move_dest, box_count)) for level in range(1, levels)]
+    now, moved, *facing = arrive(arrived, levels, slabs)
+    faces = jnp.stack(faces)
 
     swap = [(0, 1), (1, 0)]
     now_other = lax.ppermute(now, "fld", swap)
@@ -320,14 +393,11 @@
         crossed = [(2 * a + f, 2 * b + 1 - f) for a, b in pairs for f in range(2)]
         return lax.ppermute(values, "slab", pairs), lax.ppermute(values, ("slab", "fld"), crossed)
 
-    first, last = now[:, :, 0], now[:, :, planes - 1]
     if slabs == 2:
-        facing = jnp.where(slab == 0, last, first)
-        pairs = [(0, 1), (1, 0)]
         crossed = [(0, 3), (3, 0), (1, 2), (2, 1)]
-        low = high = (lax.ppermute(facing, "slab", pairs), lax.ppermute(facing, ("slab", "fld"), crossed))
+        low = high = (lax.ppermute(facing[0], "slab", swap), lax.ppermute(facing[0], ("slab", "fld"), crossed))
     else:
-        low, high = shifted(last, True), shifted(first, False)
+        low, high = shifted(facing[1], True), shifted(facing[0], False)
 
     select, masks = slope_columns(fields, planes, coarse_planes)
     terms = jnp.stack([lap_mix + 0.5 * grad_mix, lap_mix - 0.5 * grad_mix, damp_mix - 6.0 * lap_mix])
@@ -336,13 +406,13 @@
     terms = jnp.einsum("tfg,gk->tfk", terms, jnp.asarray(select), precision=HIGHEST)
     width = select.shape[1]
     weight = jnp.sum(terms[:, :, None, :] * jnp.asarray(masks)[:, None], axis=0).reshape(fields * planes, width)
-    spread = expand_table(coarse_planes, edge, faces.shape[2])
+    spread = expand_table(coarse_planes, edge, faces.shape[3])
     spread = jnp.asarray(spread).astype(jnp.bfloat16)
 
     smem = pl.BlockSpec(memory_space=pltpu.SMEM)
     by_slot = pl.BlockSpec((1, fields, planes, cross), lambda n: (n, 0, 0, 0))
     rim_slot = pl.BlockSpec((1, fields, cross), lambda n: (n, 0, 0))
-    whole_faces = pl.BlockSpec(faces.shape, lambda n: (0, 0, 0))
+    whole_faces = pl.BlockSpec(faces.shape, lambda n: (0, 0, 0, 0))
     slope = pl.pallas_call(
         functools.partial(
             slope_kernel, edge, planes, fields, coarse_planes, per_device, total, coarse_count, slots, slabs
@@ -362,7 +432,9 @@
             flops=12 * slots * weight.shape[0] * width * cross, bytes_accessed=12 * now.size, transcendentals=0
         ),
     )(move_dest, parent, now, now_other, low[0], low[1], high[0], high[1], faces, faces_other, spread, weight)
-    return jnp.stack([now] + later), slope
+    for n, pieces in enumerate(later):
+        moved = settle(n + 1, pieces, moved)
+    return moved, slope
 
 
 def solution(mesh):

time: 123 us -> 87.4 us (0.71)
  the two profiles are of different devices: /device:TPU:4 before, /device:TPU:29 now
where the time goes in v2:
time: 87.4 us; the launch traced here: 86.9 us
  waiting for transfers between devices  33.4 us (38%)
  Pallas kernels  25.6 us (29%)
  starting transfers between devices  16.7 us (19%)
  local copies, waits for them, and re-layouts  6.69 us (8%)
  other arithmetic  2.42 us (3%)
  matrix products  1.28 us (1%)
    ppermute x12, waiting for transfers between devices, exchange(): lax.ppermute(pieces[n], 'box', around[n])  32.1 us
    pallas_call x1, Pallas kernels, body(): pl.pallas_call(functools.partial(slope_kernel, edge, planes, fields, coar...  17.3 us
    ppermute x12, starting transfers between devices, exchange(): lax.ppermute(pieces[n], 'box', around[n])  9.58 us
    unnamed x25, local copies, waits for them, and re-layouts  5.2 us
    pallas_call x3, Pallas kernels, pack_level(): pl.pallas_call(functools.partial(pack_kernel, per_device, box_count), gri...  3.55 us
    ppermute x1, starting transfers between devices, body(): now_other = lax.ppermute(now, 'fld', swap)  2.76 us
    pallas_call x1, Pallas kernels, pack_faces(): pl.pallas_call(functools.partial(faces_kernel, slots // 2, move_dest.shap...  1.93 us
    ppermute x1, starting transfers between devices, body(): lax.ppermute(facing[0], ('slab', 'fld'), crossed)  1.9 us
  transfers between devices with their start and end apart: 16, of which 4 were waited for; matrix products, arithmetic and copies ran while one was open for 7% of the time, Pallas kernels for 8%

profile of v2, /device:TPU:29, one launch (start us, length us, event | category | flops | bytes accessed | tf_op | source)
XLA Modules:
  0.0 86.9 jit_solution(16237790706900331706)
XLA Ops:
  0.6 1.3 %copy-done = f32[3,4,12,8,256]{4,3,2,1,0:T(8,128)S(1)} copy-done((f32[3,4,12,8,256]{4,3,2,1,0:T(8,128)S(1)}, f32[3,4,12,8,256]{4,3,2,1,0:T(8,128)}, u32[]{:S(2)}) %copy-start) | copy-done | bytes 1179672
  1.9 0.7 copy-done.2
  2.6 1.4 %shard_map.124 = (f32[2,12,8,256]{3,2,1,0:T(8,128)S(1)}, f32[2,12,8,256]{3,2,1,0:T(8,128)}, f32[2,12,8,256]{3,2,1,0:T(8,128)}, f32[2,12,8,256]{3,2,1,0:T(8,128)S(1)}) custom-call(s32[16]{0:T(128)S(1)} %copy-done.2, f32[3,4,12,8,256]{4,3,2,1,0:T(8,128)S(1)} %copy-done), custom_call_target="tpu_custom_call" | custom-call | bytes 1179648 | tf_op jit(solution)/shard_map/pallas_call | solution.py:53
  4.0 0.0 collective-permute-start.6
  4.0 1.3 %collective-permute-start.7 = (f32[2,12,8,256]{3,2,1,0:T(8,128)}, f32[2,12,8,256]{3,2,1,0:T(8,128)S(1)}, u32[]{:S(2)}, u32[]{:S(2)}) collective-permute-start(f32[2,12,8,256]{3,2,1,0:T(8,128)} %get-tuple-element.31), channel_id=1, source_target_pairs={{0,8},{4,12},{8,0},{12,4},{1,9},{5,13},{9,1},{13,5},{2,10},{6,14},... | collective-permute-start | bytes 589832 | tf_op jit(solution)/shard_map/ppermute | solution.py:379
  5.4 0.2 collective-permute-start.8
  5.5 1.2 %copy.16.coarse_ref = f32[8,12,1000]{2,1,0:T(8,128)S(1)} copy(f32[8,12,1000]{2,0,1:T(8,128)} %param.14) | data formatting | bytes 768000 | tf_op args[3]
  6.8 0.0 copy-start.5
  6.8 0.6 copy-done.5
  7.4 0.7 copy-done.8
  8.1 1.9 %shard_map.128 = (f32[2,16,256]{2,1,0:T(8,128)S(1)}, f32[2,16,256]{2,1,0:T(8,128)}, f32[2,16,256]{2,1,0:T(8,128)}, f32[2,16,256]{2,1,0:T(8,128)S(1)}) custom-call(s32[16]{0:T(128)S(1)} %copy-done.2, s32[16]{0:T(128)S(1)} %copy-done.5, f32[8,12,1000]{2,1,0:T(8,128)S(1)} %copy.16.coarse_ref, s32[8,256]{1,0:T(8,128)S(1)} %copy-done.8), custom_call_target="tpu_custom_call" | custom-call | flops 201326592 | bytes 384000 | tf_op jit(solution)/shard_map/pallas_call | solution.py:230
  10.1 3.1 %collective-permute-start.12 = (f32[2,16,256]{2,1,0:T(8,128)}, f32[2,16,256]{2,1,0:T(8,128)}, u32[]{:S(2)}, u32[]{:S(2)}) collective-permute-start(f32[2,16,256]{2,1,0:T(8,128)} %get-tuple-element.37), channel_id=1, source_target_pairs={{0,4},{4,8},{8,12},{12,0},{1,5},{5,9},{9,13},{13,1},{2,6},{6,10},{... | collective-permute-start | bytes 98312 | tf_op jit(solution)/shard_map/ppermute | solution.py:379
  13.2 0.0 collective-permute-start.13
  13.2 1.4 %shard_map.123 = (f32[2,12,8,256]{3,2,1,0:T(8,128)S(1)}, f32[2,12,8,256]{3,2,1,0:T(8,128)}, f32[2,12,8,256]{3,2,1,0:T(8,128)S(1)}, f32[2,12,8,256]{3,2,1,0:T(8,128)S(1)}) custom-call(s32[16]{0:T(128)S(1)} %copy-done.2, f32[3,4,12,8,256]{4,3,2,1,0:T(8,128)S(1)} %copy-done.1), custom_call_target="tpu_custom_call" | custom-call | bytes 1179648 | tf_op jit(solution)/shard_map/pallas_call | solution.py:53
  14.6 0.7 copy-done.4
  15.3 0.7 collective-permute-start.14
  16.0 7.9 %collective-permute-done.7.refs_2_ = f32[2,12,8,256]{3,2,1,0:T(8,128)S(1)} collective-permute-done((f32[2,12,8,256]{3,2,1,0:T(8,128)}, f32[2,12,8,256]{3,2,1,0:T(8,128)S(1)}, u32[]{:S(2)}, u32[]{:S(2)}) %collective-permute-start.7) | collective-permute-done | bytes 196640 | tf_op jit(solution)/shard_map/ppermute | solution.py:379
  23.9 0.9 %shard_map.125 = (f32[8,12,8,256]{3,2,1,0:T(8,128)S(1)}, f32[3,8,12,8,256]{4,3,2,1,0:T(8,128)}, f32[8,12,256]{2,1,0:T(8,128)S(1)}) custom-call(f32[2,12,8,256]{3,2,1,0:T(8,128)S(1)} %get-tuple-element.29.refs_0_, f32[2,12,8,256]{3,2,1,0:T(8,128)S(1)} %collective-permute-done.6.refs_1_, f32[2,12,8,256]{3,2,1,0:T(8,128)S(1)} %collective-permute-done.7.refs_2_, ...), custom_call_target="tpu_custom_call" | custom-call | bytes 2359296 | tf_op jit(solution)/shard_map/pallas_call | solution.py:132
  24.9 2.8 %collective-permute-start.9 = (f32[8,12,8,256]{3,2,1,0:T(8,128)S(1)}, f32[8,12,8,256]{3,2,1,0:T(8,128)S(1)}, u32[]{:S(2)}, u32[]{:S(2)}) collective-permute-start(f32[8,12,8,256]{3,2,1,0:T(8,128)S(1)} %get-tuple-element.34.own_ref), channel_id=1, source_target_pairs={{0,1},{1,0},{2,3},{3,2},{4,5},{5,4},{6,7},{7,6},{8,9},{9,8},{10,11... | collective-permute-start | bytes 2359304 | tf_op jit(solution)/shard_map/ppermute | solution.py:388
  27.6 0.6 fusion.1
  28.2 1.5 %fusion.7 = (f32[3,12,12]{2,1,0:T(8,128)}, f32[3,12,12]{2,1,0:T(8,128)}) fusion(f32[3,12,24]{2,1,0:T(8,128)} %fusion.1), kind=kLoop, calls=%fused_computation.16 | loop fusion | bytes 6912 | tf_op jit(solution)/shard_map/jit(_roll_static)/slice | solution.py:405
  29.7 0.7 shard_map.122
  30.4 0.0 collective-permute-done.12
  30.5 0.1 collective-permute-start.4
  30.5 0.0 collective-permute-done.13
  30.5 1.8 %collective-permute-start.5 = (f32[2,12,8,256]{3,2,1,0:T(8,128)S(1)}, f32[2,12,8,256]{3,2,1,0:T(8,128)S(1)}, u32[]{:S(2)}, u32[]{:S(2)}) collective-permute-start(f32[2,12,8,256]{3,2,1,0:T(8,128)S(1)} %get-tuple-element.28), channel_id=1, source_target_pairs={{0,12},{4,0},{8,4},{12,8},{1,13},{5,1},{9,5},{13,9},{2,14},{6,2},{... | collective-permute-start | bytes 589832 | tf_op jit(solution)/shard_map/ppermute | solution.py:379
  32.3 2.1 %collective-permute-start = (f32[2,12,8,256]{3,2,1,0:T(8,128)S(1)}, f32[2,12,8,256]{3,2,1,0:T(8,128)S(1)}, u32[]{:S(2)}, u32[]{:S(2)}) collective-permute-start(f32[2,12,8,256]{3,2,1,0:T(8,128)S(1)} %get-tuple-element.22), channel_id=1, source_target_pairs={{0,4},{4,8},{8,12},{12,0},{1,5},{5,9},{9,13},{13,1},{2,6},{6,10},{... | collective-permute-start | bytes 589832 | tf_op jit(solution)/shard_map/ppermute | solution.py:379
  34.4 0.0 collective-permute-done.3.refs_1_
  34.4 0.3 collective-permute-start.1
  34.7 1.3 %fusion.2 = f32[3,12,896]{2,1,0:T(8,128)S(1)} fusion(f32[24,896,1]{1,0,2:T(8,128)} %constant.30, f32[3,12,24]{2,1,0:T(8,128)} %fusion.1, f32[3,12,12]{2,1,0:T(8,128)} %get-tuple-element.41, f32[3,12,12]{2,1,0:T(8,128)} %get-tuple-element.40, pred[]{:T(512)S(6)} %eq.3), kind=kOutput, calls=%fused_computation.8 | convolution fusion | flops 9291456 | bytes 221953 | tf_op jit(solution)/shard_map/tfg,gk->tfk/dot_general | solution.py:406
  36.0 10.6 %collective-permute-done.4.refs_2_ = f32[2,12,8,256]{3,2,1,0:T(8,128)S(1)} collective-permute-done((f32[2,12,8,256]{3,2,1,0:T(8,128)}, f32[2,12,8,256]{3,2,1,0:T(8,128)S(1)}, u32[]{:S(2)}, u32[]{:S(2)}) %collective-permute-start.4) | collective-permute-done | bytes 196640 | tf_op jit(solution)/shard_map/ppermute | solution.py:379
  46.6 0.0 collective-permute-start.2
  46.6 0.8 pad_maximum_fusion.own_faces
  47.4 1.3 %collective-permute-start.15 = (f32[4,2,16,256]{3,2,1,0:T(8,128)S(1)}, f32[4,2,16,256]{3,2,1,0:T(8,128)S(1)}, u32[]{:S(2)}, u32[]{:S(2)}) collective-permute-start(f32[4,2,16,256]{3,2,1,0:T(8,128)S(1)} %pad_maximum_fusion.own_faces), channel_id=1, source_target_pairs={{0,1},{1,0},{2,3},{3,2},{4,5},{5,4},{6,7},{7,6},{8,9},{9,8},{10,11... | collective-permute-start | bytes 393224 | tf_op jit(solution)/shard_map/ppermute | solution.py:389
  48.7 0.0 collective-permute-done.refs_1_
  48.7 1.2 %collective-permute-start.10 = (f32[8,12,256]{2,1,0:T(8,128)S(1)}, f32[8,12,256]{2,1,0:T(8,128)S(1)}, u32[]{:S(2)}, u32[]{:S(2)}) collective-permute-start(f32[8,12,256]{2,1,0:T(8,128)S(1)} %get-tuple-element.35), channel_id=1, source_target_pairs={{0,2},{2,0},{1,3},{3,1},{4,6},{6,4},{5,7},{7,5},{8,10},{10,8},{9,1... | collective-permute-start | bytes 294920 | tf_op jit(solution)/shard_map/ppermute | solution.py:398
  49.9 13.5 %collective-permute-done.1.refs_2_ = f32[2,12,8,256]{3,2,1,0:T(8,128)S(1)} collective-permute-done((f32[2,12,8,256]{3,2,1,0:T(8,128)S(1)}, f32[2,12,8,256]{3,2,1,0:T(8,128)S(1)}, u32[]{:S(2)}, u32[]{:S(2)}) %collective-permute-start.1) | collective-permute-done | bytes 196640 | tf_op jit(solution)/shard_map/ppermute | solution.py:379
  63.4 1.9 %collective-permute-start.11 = (f32[8,12,256]{2,1,0:T(8,128)S(1)}, f32[8,12,256]{2,1,0:T(8,128)S(1)}, u32[]{:S(2)}, u32[]{:S(2)}) collective-permute-start(f32[8,12,256]{2,1,0:T(8,128)S(1)} %get-tuple-element.35), channel_id=1, source_target_pairs={{0,3},{3,0},{1,2},{2,1},{4,7},{7,4},{5,6},{6,5},{8,11},{11,8},{9,1... | collective-permute-start | bytes 294920 | tf_op jit(solution)/shard_map/ppermute | solution.py:398
  65.3 1.0 %multiply_reduce_fusion = f32[12,8,896]{2,1,0:T(8,128)S(1)} fusion(f32[3,8,896]{2,1,0:T(8,128)} %constant.26.clone, f32[3,12,896]{2,1,0:T(8,128)S(1)} %fusion.2), kind=kLoop, calls=%fused_computation | loop fusion | flops 430080 | bytes 559104 | tf_op jit(solution)/shard_map/reduce_sum | solution.py:408
  66.3 0.9 %shard_map.126.refs_4_ = f32[3,8,12,8,256]{4,3,2,1,0:T(8,128)} custom-call(f32[2,12,8,256]{3,2,1,0:T(8,128)S(1)} %get-tuple-element.25.refs_0_, f32[2,12,8,256]{3,2,1,0:T(8,128)S(1)} %collective-permute-done.3.refs_1_, f32[2,12,8,256]{3,2,1,0:T(8,128)S(1)} %collective-permute-done.4.refs_2_, ...), custom_call_target="tpu_custom_call", output_to_operand_aliasing={{}: (4, {})} | custom-call | bytes 1572864 | tf_op jit(solution)/shard_map/pallas_call | solution.py:87
  67.3 0.0 collective-permute-done.2.refs_3_
  67.3 0.0 copy-start.6
  67.3 0.0 copy-start.7
  67.3 0.9 %shard_map.127 = f32[3,8,12,8,256]{4,3,2,1,0:T(8,128)} custom-call(f32[2,12,8,256]{3,2,1,0:T(8,128)S(1)} %get-tuple-element.21.refs_0_, f32[2,12,8,256]{3,2,1,0:T(8,128)S(1)} %collective-permute-done.refs_1_, f32[2,12,8,256]{3,2,1,0:T(8,128)S(1)} %collective-permute-done.1.refs_2_, ...), custom_call_target="tpu_custom_call", output_to_operand_aliasing={{}: (4, {})} | custom-call | bytes 1572864 | tf_op jit(solution)/shard_map/pallas_call | solution.py:87
  68.2 0.0 collective-permute-done.15.other_faces
  68.2 1.3 %collective-permute-done.11.other_low.other_high = f32[8,12,256]{2,1,0:T(8,128)S(1)} collective-permute-done((f32[8,12,256]{2,1,0:T(8,128)S(1)}, f32[8,12,256]{2,1,0:T(8,128)S(1)}, u32[]{:S(2)}, u32[]{:S(2)}) %collective-permute-start.11) | collective-permute-done | bytes 98336 | tf_op jit(solution)/shard_map/ppermute | solution.py:398
  69.6 0.0 collective-permute-done.9.other_ref
  69.6 17.3 %shard_map.129 = f32[8,12,8,256]{3,2,1,0:T(8,128)} custom-call(s32[16]{0:T(128)S(1)} %copy-done.3, s32[16]{0:T(128)S(1)} %copy-done.6, f32[8,12,8,256]{3,2,1,0:T(8,128)S(1)} %get-tuple-element.34.own_ref, f32[8,12,8,256]{3,2,1,0:T(8,128)S(1)} %collective-permute-done.9.other_ref, f32[8,12,256]{2,1,0:T(8,128)S(1)} %collective-permute-done.10.own_low.own_high, ...), custom_call_target="tpu_custom_call" | custom-call | flops 2113929216 | bytes 2359296 | tf_op jit(solution)/shard_map/pallas_call | solution.py:416
  (23 shorter events, 0.1 us)
Async XLA Ops:
  0.6 1.3 %copy-start = (f32[3,4,12,8,256]{4,3,2,1,0:T(8,128)S(1)}, f32[3,4,12,8,256]{4,3,2,1,0:T(8,128)}, u32[]{:S(2)}) copy-start(f32[3,4,12,8,256]{4,3,2,1,0:T(8,128)} %boxes_ref.5) | copy-start | bytes 3538948
  1.9 0.7 copy-start.2
  2.6 10.6 %copy-start.1 = (f32[3,4,12,8,256]{4,3,2,1,0:T(8,128)S(1)}, f32[3,4,12,8,256]{4,3,2,1,0:T(8,128)}, u32[]{:S(2)}) copy-start(f32[3,4,12,8,256]{4,3,2,1,0:T(8,128)} %boxes_ref.5) | copy-start | bytes 3538948
  2.6 12.7 %copy-start.9 = (f32[24,24]{1,0:T(8,128)S(1)}, f32[24,24]{1,0:T(8,128)}, u32[]{:S(2)}) copy-start(f32[24,24]{1,0:T(8,128)} %param.15) | copy-start | bytes 6916
  2.6 12.7 %copy-start.10 = (f32[24,24]{1,0:T(8,128)S(1)}, f32[24,24]{1,0:T(8,128)}, u32[]{:S(2)}) copy-start(f32[24,24]{1,0:T(8,128)} %param.16) | copy-start | bytes 6916
  2.6 12.7 %copy-start.11 = (f32[24,24]{1,0:T(8,128)S(1)}, f32[24,24]{1,0:T(8,128)}, u32[]{:S(2)}) copy-start(f32[24,24]{1,0:T(8,128)} %param.17) | copy-start | bytes 6916
  2.6 27.1 %copy-start.3 = (s32[16]{0:T(128)S(1)}, s32[16]{0:T(128)}, u32[]{:S(2)}) copy-start(s32[16]{0:T(128)} %dest_ref.9) | copy-start | bytes 196
  4.0 11.2 %collective-permute-start.6 = (f32[2,12,8,256]{3,2,1,0:T(8,128)}, f32[2,12,8,256]{3,2,1,0:T(8,128)S(1)}, u32[]{:S(2)}, u32[]{:S(2)}) collective-permute-start(f32[2,12,8,256]{3,2,1,0:T(8,128)} %get-tuple-element.30), channel_id=1, source_target_pairs={{0,4},{4,8},{8,12},{12,0},{1,5},{5,9},{9,13},{13,1},{2,6},{6,10},{... | collective-permute-start | bytes 589832 | tf_op jit(solution)/shard_map/ppermute | solution.py:379
  4.0 19.9 %collective-permute-start.7 = (f32[2,12,8,256]{3,2,1,0:T(8,128)}, f32[2,12,8,256]{3,2,1,0:T(8,128)S(1)}, u32[]{:S(2)}, u32[]{:S(2)}) collective-permute-start(f32[2,12,8,256]{3,2,1,0:T(8,128)} %get-tuple-element.31), channel_id=1, source_target_pairs={{0,8},{4,12},{8,0},{12,4},{1,9},{5,13},{9,1},{13,5},{2,10},{6,14},... | collective-permute-start | bytes 589832 | tf_op jit(solution)/shard_map/ppermute | solution.py:379
  5.4 18.6 %collective-permute-start.8 = (f32[2,12,8,256]{3,2,1,0:T(8,128)S(1)}, f32[2,12,8,256]{3,2,1,0:T(8,128)S(1)}, u32[]{:S(2)}, u32[]{:S(2)}) collective-permute-start(f32[2,12,8,256]{3,2,1,0:T(8,128)S(1)} %get-tuple-element.32), channel_id=1, source_target_pairs={{0,12},{4,0},{8,4},{12,8},{1,13},{5,1},{9,5},{13,9},{2,14},{6,2},{... | collective-permute-start | bytes 589832 | tf_op jit(solution)/shard_map/ppermute | solution.py:379
  6.8 0.7 copy-start.5
  7.4 0.7 copy-start.8
  10.1 20.4 %collective-permute-start.12 = (f32[2,16,256]{2,1,0:T(8,128)}, f32[2,16,256]{2,1,0:T(8,128)}, u32[]{:S(2)}, u32[]{:S(2)}) collective-permute-start(f32[2,16,256]{2,1,0:T(8,128)} %get-tuple-element.37), channel_id=1, source_target_pairs={{0,4},{4,8},{8,12},{12,0},{1,5},{5,9},{9,13},{13,1},{2,6},{6,10},{... | collective-permute-start | bytes 98312 | tf_op jit(solution)/shard_map/ppermute | solution.py:379
  13.2 17.4 %collective-permute-start.13 = (f32[2,16,256]{2,1,0:T(8,128)}, f32[2,16,256]{2,1,0:T(8,128)}, u32[]{:S(2)}, u32[]{:S(2)}) collective-permute-start(f32[2,16,256]{2,1,0:T(8,128)} %get-tuple-element.38), channel_id=1, source_target_pairs={{0,8},{4,12},{8,0},{12,4},{1,9},{5,13},{9,1},{13,5},{2,10},{6,14},... | collective-permute-start | bytes 98312 | tf_op jit(solution)/shard_map/ppermute | solution.py:379
  14.6 0.7 copy-start.4
  15.3 17.1 %collective-permute-start.14 = (f32[2,16,256]{2,1,0:T(8,128)S(1)}, f32[2,16,256]{2,1,0:T(8,128)}, u32[]{:S(2)}, u32[]{:S(2)}) collective-permute-start(f32[2,16,256]{2,1,0:T(8,128)S(1)} %get-tuple-element.39), channel_id=1, source_target_pairs={{0,12},{4,0},{8,4},{12,8},{1,13},{5,1},{9,5},{13,9},{2,14},{6,2},{... | collective-permute-start | bytes 98312 | tf_op jit(solution)/shard_map/ppermute | solution.py:379
  23.9 10.5 %collective-permute-start.3 = (f32[2,12,8,256]{3,2,1,0:T(8,128)}, f32[2,12,8,256]{3,2,1,0:T(8,128)S(1)}, u32[]{:S(2)}, u32[]{:S(2)}) collective-permute-start(f32[2,12,8,256]{3,2,1,0:T(8,128)} %get-tuple-element.26), channel_id=1, source_target_pairs={{0,4},{4,8},{8,12},{12,0},{1,5},{5,9},{9,13},{13,1},{2,6},{6,10},{... | collective-permute-start | bytes 589832 | tf_op jit(solution)/shard_map/ppermute | solution.py:379
  24.9 44.7 %collective-permute-start.9 = (f32[8,12,8,256]{3,2,1,0:T(8,128)S(1)}, f32[8,12,8,256]{3,2,1,0:T(8,128)S(1)}, u32[]{:S(2)}, u32[]{:S(2)}) collective-permute-start(f32[8,12,8,256]{3,2,1,0:T(8,128)S(1)} %get-tuple-element.34.own_ref), channel_id=1, source_target_pairs={{0,1},{1,0},{2,3},{3,2},{4,5},{5,4},{6,7},{7,6},{8,9},{9,8},{10,11... | collective-permute-start | bytes 2359304 | tf_op jit(solution)/shard_map/ppermute | solution.py:388
  30.5 16.1 %collective-permute-start.4 = (f32[2,12,8,256]{3,2,1,0:T(8,128)}, f32[2,12,8,256]{3,2,1,0:T(8,128)S(1)}, u32[]{:S(2)}, u32[]{:S(2)}) collective-permute-start(f32[2,12,8,256]{3,2,1,0:T(8,128)} %copy-done.4), channel_id=1, source_target_pairs={{0,8},{4,12},{8,0},{12,4},{1,9},{5,13},{9,1},{13,5},{2,10},{6,14},... | collective-permute-start | bytes 589832 | tf_op jit(solution)/shard_map/ppermute | solution.py:379
  30.5 16.8 %collective-permute-start.5 = (f32[2,12,8,256]{3,2,1,0:T(8,128)S(1)}, f32[2,12,8,256]{3,2,1,0:T(8,128)S(1)}, u32[]{:S(2)}, u32[]{:S(2)}) collective-permute-start(f32[2,12,8,256]{3,2,1,0:T(8,128)S(1)} %get-tuple-element.28), channel_id=1, source_target_pairs={{0,12},{4,0},{8,4},{12,8},{1,13},{5,1},{9,5},{13,9},{2,14},{6,2},{... | collective-permute-start | bytes 589832 | tf_op jit(solution)/shard_map/ppermute | solution.py:379
  32.3 16.3 %collective-permute-start = (f32[2,12,8,256]{3,2,1,0:T(8,128)S(1)}, f32[2,12,8,256]{3,2,1,0:T(8,128)S(1)}, u32[]{:S(2)}, u32[]{:S(2)}) collective-permute-start(f32[2,12,8,256]{3,2,1,0:T(8,128)S(1)} %get-tuple-element.22), channel_id=1, source_target_pairs={{0,4},{4,8},{8,12},{12,0},{1,5},{5,9},{9,13},{13,1},{2,6},{6,10},{... | collective-permute-start | bytes 589832 | tf_op jit(solution)/shard_map/ppermute | solution.py:379
  34.4 29.0 %collective-permute-start.1 = (f32[2,12,8,256]{3,2,1,0:T(8,128)S(1)}, f32[2,12,8,256]{3,2,1,0:T(8,128)S(1)}, u32[]{:S(2)}, u32[]{:S(2)}) collective-permute-start(f32[2,12,8,256]{3,2,1,0:T(8,128)S(1)} %get-tuple-element.23), channel_id=1, source_target_pairs={{0,8},{4,12},{8,0},{12,4},{1,9},{5,13},{9,1},{13,5},{2,10},{6,14},... | collective-permute-start | bytes 589832 | tf_op jit(solution)/shard_map/ppermute | solution.py:379
  46.6 20.7 %collective-permute-start.2 = (f32[2,12,8,256]{3,2,1,0:T(8,128)S(1)}, f32[2,12,8,256]{3,2,1,0:T(8,128)S(1)}, u32[]{:S(2)}, u32[]{:S(2)}) collective-permute-start(f32[2,12,8,256]{3,2,1,0:T(8,128)S(1)} %get-tuple-element.24), channel_id=1, source_target_pairs={{0,12},{4,0},{8,4},{12,8},{1,13},{5,1},{9,5},{13,9},{2,14},{6,2},{... | collective-permute-start | bytes 589832 | tf_op jit(solution)/shard_map/ppermute | solution.py:379
  47.4 20.8 %collective-permute-start.15 = (f32[4,2,16,256]{3,2,1,0:T(8,128)S(1)}, f32[4,2,16,256]{3,2,1,0:T(8,128)S(1)}, u32[]{:S(2)}, u32[]{:S(2)}) collective-permute-start(f32[4,2,16,256]{3,2,1,0:T(8,128)S(1)} %pad_maximum_fusion.own_faces), channel_id=1, source_target_pairs={{0,1},{1,0},{2,3},{3,2},{4,5},{5,4},{6,7},{7,6},{8,9},{9,8},{10,11... | collective-permute-start | bytes 393224 | tf_op jit(solution)/shard_map/ppermute | solution.py:389
  48.7 19.6 %collective-permute-start.10 = (f32[8,12,256]{2,1,0:T(8,128)S(1)}, f32[8,12,256]{2,1,0:T(8,128)S(1)}, u32[]{:S(2)}, u32[]{:S(2)}) collective-permute-start(f32[8,12,256]{2,1,0:T(8,128)S(1)} %get-tuple-element.35), channel_id=1, source_target_pairs={{0,2},{2,0},{1,3},{3,1},{4,6},{6,4},{5,7},{7,5},{8,10},{10,8},{9,1... | collective-permute-start | bytes 294920 | tf_op jit(solution)/shard_map/ppermute | solution.py:398
  63.4 6.2 %collective-permute-start.11 = (f32[8,12,256]{2,1,0:T(8,128)S(1)}, f32[8,12,256]{2,1,0:T(8,128)S(1)}, u32[]{:S(2)}, u32[]{:S(2)}) collective-permute-start(f32[8,12,256]{2,1,0:T(8,128)S(1)} %get-tuple-element.35), channel_id=1, source_target_pairs={{0,3},{3,0},{1,2},{2,1},{4,7},{7,4},{5,6},{6,5},{8,11},{11,8},{9,1... | collective-permute-start | bytes 294920 | tf_op jit(solution)/shard_map/ppermute | solution.py:398
  67.3 2.3 %copy-start.6 = (s32[16]{0:T(128)S(1)}, s32[16]{0:T(128)}, u32[]{:S(2)}) copy-start(s32[16]{0:T(128)} %parent_ref.3) | copy-start | bytes 196
  67.3 2.3 %copy-start.7 = (bf16[256,2304]{1,0:T(8,128)(2,1)S(1)}, bf16[256,2304]{1,0:T(8,128)(2,1)}, u32[]{:S(2)}) copy-start(bf16[256,2304]{1,0:T(8,128)(2,1)} %constant.29.spread_ref) | copy-start | bytes 3538948

commit v3 on v2

v3 whole, which is shorter than its diff:
```python
import functools

import jax
import jax.numpy as jnp
import numpy as np
from jax import lax
from jax.experimental import pallas as pl
from jax.experimental.pallas import tpu as pltpu
from jax.sharding import PartitionSpec as P

HIGHEST = lax.Precision.HIGHEST
ROWS = 16


def round_up(value, unit):
    return -(-value // unit) * unit


def split_three(values):
    high = values.astype(jnp.bfloat16)
    rest = values - high.astype(jnp.float32)
    middle = rest.astype(jnp.bfloat16)
    low = (rest - middle.astype(jnp.float32)).astype(jnp.bfloat16)
    return high, middle, low


def place_boxes(per_device, box_count, dest_ref, table):
    own = lax.axis_index("box")
    for slot in range(2 * box_count):
        table[slot] = -1

    def place(b, carry):
        slot = 2 * dest_ref[own * per_device + b]
        table[jnp.where(table[slot] >= 0, slot + 1, slot)] = b
        return carry

    lax.fori_loop(0, per_device, place, 0)


def each_slot(box_count):
    own = lax.axis_index("box")
    for shift in range(box_count):
        for k in range(2):
            yield shift, k, 2 * lax.rem(own + shift, box_count) + k


def first_kernel(per_device, box_count, total, dest_ref, parent_ref, boxes_ref, coarse_ref, table_ref, *refs):
    outs, (chosen, box_table, face_table, sems) = refs[:box_count], refs[box_count:]
    fields, coarse_count, cells = coarse_ref.shape
    own, slab = lax.axis_index("box"), lax.axis_index("slab")
    place_boxes(per_device, box_count, dest_ref, box_table)

    def copy(shift, k, b):
        return pltpu.make_async_copy(
            boxes_ref.at[0, b], outs[shift].at[k, pl.ds(0, fields)], sems.at[shift, k]
        )

    for shift, k, slot in each_slot(box_count):
        b = box_table[slot]

        @pl.when(b >= 0)
        def _():
            copy(shift, k, b).start()

        @pl.when(b < 0)
        def _():
            outs[shift][k, :fields] = jnp.zeros((fields,) + outs[shift].shape[2:], jnp.float32)

    for slot in range(2 * box_count):
        face_table[slot] = -1

    def place(b, carry):
        slot = 2 * dest_ref[b]
        local = parent_ref[b] - own * coarse_count

        @pl.when(jnp.logical_and(local >= 0, local < coarse_count))
        def _():
            face_table[jnp.where(face_table[slot] >= 0, slot + 1, slot)] = local

        return carry

    lax.fori_loop(0, total, place, 0)
    index = table_ref[0:1] + slab * table_ref[1:2] + jnp.where(slab > 0, table_ref[2:3], 0)
    cell = lax.broadcasted_iota(jnp.int32, (cells, index.shape[1]), 0)
    one_hot = (cell == index).astype(jnp.float32).astype(jnp.bfloat16)
    high, middle, low = (
        jnp.dot(part, one_hot, preferred_element_type=jnp.float32)
        for part in split_three(coarse_ref[...].reshape(fields * coarse_count, cells))
    )
    chosen[...] = (high + (middle + low)).reshape(chosen.shape)
    planes = outs[0].shape[2]
    for shift, k, slot in each_slot(box_count):
        local = face_table[slot]
        for row in range(ROWS):
            to = fields + row // planes
            if row < fields:
                values = chosen[row, pl.ds(jnp.maximum(local, 0), 1)]
                values = jnp.where(local >= 0, values, 0.0)
            else:
                values = jnp.zeros((1, chosen.shape[2]), jnp.float32)
            outs[shift][k, to, row % planes : row % planes + 1] = values
    for shift, k, slot in each_slot(box_count):
        b = box_table[slot]

        @pl.when(b >= 0)
        def _():
            copy(shift, k, b).wait()


def pack_first(boxes, coarse, move_dest, parent, table, box_count):
    per_device, fields, planes, cross = boxes.shape[1:]
    coarse = jnp.transpose(coarse, (1, 0, 2))
    smem, vmem = pl.BlockSpec(memory_space=pltpu.SMEM), pl.BlockSpec(memory_space=pltpu.VMEM)
    item = (2, fields + ROWS // planes, planes, cross)
    return pl.pallas_call(
        functools.partial(first_kernel, per_device, box_count, move_dest.shape[0]),
        out_shape=[jax.ShapeDtypeStruct(item, jnp.float32)] * box_count,
        in_specs=[smem, smem, pl.BlockSpec(memory_space=pl.ANY), vmem, vmem],
        out_specs=[vmem] * box_count,
        scratch_shapes=[
            pltpu.VMEM(coarse.shape[:2] + (cross,), jnp.float32),
            pltpu.SMEM((2 * box_count,), jnp.int32),
            pltpu.SMEM((2 * box_count,), jnp.int32),
            pltpu.SemaphoreType.DMA((box_count, 2)),
        ],
        compiler_params=pltpu.CompilerParams(vmem_limit_bytes=48 * 2 ** 20),
        cost_estimate=pl.CostEstimate(
            flops=6 * coarse.size * cross, bytes_accessed=4 * (coarse.size + 2 * boxes.size), transcendentals=0
        ),
    )(move_dest, parent, boxes, coarse, table)


def later_kernel(per_device, box_count, levels, dest_ref, boxes_ref, *refs):
    outs, (table, sems) = refs[:box_count], refs[box_count:]
    place_boxes(per_device, box_count, dest_ref, table)

    def copy(shift, k, b, n):
        return pltpu.make_async_copy(boxes_ref.at[n + 1, b], outs[shift].at[n, k], sems.at[n, shift, k])

    for shift, k, slot in each_slot(box_count):
        b = table[slot]

        @pl.when(b >= 0)
        def _():
            for n in range(levels):
                copy(shift, k, b, n).start()

        @pl.when(b < 0)
        def _():
            for n in range(levels):
                outs[shift][n, k] = jnp.zeros(outs[shift].shape[2:], jnp.float32)

    for shift, k, slot in each_slot(box_count):
        b = table[slot]

        @pl.when(b >= 0)
        def _():
            for n in range(levels):
                copy(shift, k, b, n).wait()


def pack_later(boxes, move_dest, box_count):
    levels, per_device = boxes.shape[0] - 1, boxes.shape[1]
    return pl.pallas_call(
        functools.partial(later_kernel, per_device, box_count, levels),
        out_shape=[jax.ShapeDtypeStruct((levels, 2) + boxes.shape[2:], jnp.float32)] * box_count,
        in_specs=[pl.BlockSpec(memory_space=pltpu.SMEM), pl.BlockSpec(memory_space=pl.ANY)],
        out_specs=[pl.BlockSpec(memory_space=pltpu.VMEM)] * box_count,
        scratch_shapes=[
            pltpu.SMEM((2 * box_count,), jnp.int32),
            pltpu.SemaphoreType.DMA((levels, box_count, 2)),
        ],
        compiler_params=pltpu.CompilerParams(vmem_limit_bytes=48 * 2 ** 20),
        cost_estimate=pl.CostEstimate(flops=0, bytes_accessed=12 * boxes.size, transcendentals=0),
    )(move_dest, boxes)


def source_of(shift, box_count):
    return lax.rem(lax.axis_index("box") - shift + box_count, box_count)


def settle_kernel(levels, box_count, *refs):
    pieces, out_ref, sems = refs[: box_count - 1], refs[-2], refs[-1]

    def copy(shift):
        to = out_ref.at[pl.ds(1, levels), pl.ds(2 * source_of(shift, box_count), 2)]
        return pltpu.make_async_copy(pieces[shift - 1], to, sems.at[shift])

    for shift in range(1, box_count):
        copy(shift).start()
    for shift in range(1, box_count):
        copy(shift).wait()


def settle(pieces, moved, after):
    box_count = len(pieces) + 1
    levels = moved.shape[0] - 1
    vmem, anywhere = pl.BlockSpec(memory_space=pltpu.VMEM), pl.BlockSpec(memory_space=pl.ANY)
    return pl.pallas_call(
        functools.partial(settle_kernel, levels, box_count),
        out_shape=jax.ShapeDtypeStruct(moved.shape, jnp.float32),
        in_specs=[vmem] * (box_count - 1) + [anywhere] * 2,
        out_specs=anywhere,
        scratch_shapes=[pltpu.SemaphoreType.DMA((box_count,))],
        input_output_aliases={box_count - 1: 0},
        compiler_params=pltpu.CompilerParams(vmem_limit_bytes=48 * 2 ** 20),
        cost_estimate=pl.CostEstimate(
            flops=0, bytes_accessed=8 * (box_count - 1) * pieces[0].size, transcendentals=0
        ),
    )(*pieces, moved, after)


def arrive_kernel(box_count, slabs, levels, fields, *refs):
    pieces, own_later, (now_ref, moved_ref) = refs[:box_count], refs[box_count], refs[box_count + 1 : box_count + 3]
    edges, sems = refs[box_count + 3 : -1], refs[-1]
    slab = lax.axis_index("slab")
    planes = now_ref.shape[2]
    copies = []
    for shift in range(box_count):
        to = moved_ref.at[0, pl.ds(2 * source_of(shift, box_count), 2)]
        copies.append(pltpu.make_async_copy(pieces[shift].at[:, pl.ds(0, fields)], to, sems.at[shift]))
    to = moved_ref.at[pl.ds(1, levels - 1), pl.ds(2 * source_of(0, box_count), 2)]
    copies.append(pltpu.make_async_copy(own_later, to, sems.at[box_count]))
    for copy in copies:
        copy.start()
    faced = [jnp.where(slab == 0, planes - 1, 0)] if slabs == 2 else [0, planes - 1]
    for shift in range(box_count):
        source = source_of(shift, box_count)
        for k in range(2):
            now_ref[2 * source + k] = pieces[shift][k]
            for edge_ref, plane in zip(edges, faced):
                for f in range(fields):
                    edge_ref[2 * source + k, f : f + 1] = pieces[shift][k, f, pl.ds(plane, 1)]
    for copy in copies:
        copy.wait()


def arrive(pieces, own_later, slabs):
    box_count = len(pieces)
    _, blocks, planes, cross = pieces[0].shape
    levels, fields = own_later.shape[0] + 1, own_later.shape[2]
    slots = 2 * box_count
    sides = 1 if slabs == 2 else 2
    vmem, anywhere = pl.BlockSpec(memory_space=pltpu.VMEM), pl.BlockSpec(memory_space=pl.ANY)
    shapes = [(slots, blocks, planes, cross), (levels, slots, fields, planes, cross)]
    shapes += [(slots, fields, cross)] * sides
    return pl.pallas_call(
        functools.partial(arrive_kernel, box_count, slabs, levels, fields),
        out_shape=[jax.ShapeDtypeStruct(shape, jnp.float32) for shape in shapes],
        in_specs=[vmem] * (box_count + 1),
        out_specs=[vmem, anywhere] + [vmem] * sides,
        scratch_shapes=[pltpu.SemaphoreType.DMA((box_count + 1,))],
        compiler_params=pltpu.CompilerParams(vmem_limit_bytes=48 * 2 ** 20),
        cost_estimate=pl.CostEstimate(
            flops=0, bytes_accessed=12 * box_count * pieces[0].size, transcendentals=0
        ),
    )(*pieces, own_later)


def face_tables(coarse_side, coarse_planes, lanes):
    half = coarse_side - 2
    square = coarse_side * coarse_side
    inner = np.arange(half) + 1
    sides = []
    for c in range(coarse_planes):
        base = (c + 1) * square
        sides += [base + inner, base + (coarse_side - 1) * coarse_side + inner]
        sides += [base + inner * coarse_side, base + inner * coarse_side + coarse_side - 1]
    yz = np.concatenate(sides)
    x = (inner[:, None] * coarse_side + inner[None, :]).reshape(-1)
    table = np.zeros((8, lanes), np.int32)
    table[0] = -(10 ** 6)
    table[0, : yz.size] = yz
    table[1, : yz.size] = coarse_planes * square
    table[0, yz.size : yz.size + x.size] = x
    table[2, yz.size : yz.size + x.size] = (coarse_side - 1) * square
    return table


def expand_table(coarse_planes, edge, lanes):
    half = edge // 2
    cross = edge * edge
    spread = np.zeros((lanes, (2 * coarse_planes + 1) * cross), np.float32)
    for c in range(coarse_planes):
        base = c * 4 * half
        forward, backward = 2 * c * cross, (2 * c + 1) * cross
        for m in range(edge):
            spread[base + m // 2, backward + m] += 1
            spread[base + half + m // 2, forward + (edge - 1) * edge + m] += 1
            spread[base + 2 * half + m // 2, backward + m * edge] += 1
            spread[base + 3 * half + m // 2, forward + m * edge + edge - 1] += 1
    base, to = coarse_planes * 4 * half, 2 * coarse_planes * cross
    for y in range(edge):
        for z in range(edge):
            spread[base + (y // 2) * half + z // 2, to + y * edge + z] = 1
    return spread


def slope_columns(fields, planes, coarse_planes):
    column_field, forward, backward, centre = [], [], [], []
    p = np.arange(planes)

    def add(field, f, b, c):
        column_field.append(field)
        forward.append(f * np.ones(planes))
        backward.append(b * np.ones(planes))
        centre.append(c * np.ones(planes))

    for f, b, c in ((1, 0, 0), (0, 1, 0), (0, 0, 1)):
        for g in range(2 * fields):
            for q in range(planes):
                here = p == q
                add(g, f * here + c * (p + 1 == q), b * here + c * (p - 1 == q), c * here)
    rows = [g if g < fields else -1 for g in range(ROWS)]
    rows += [fields + g if g < fields else -1 for g in range(ROWS)]
    for g in rows:
        add(g, 0, p == 0, 0)
    for g in rows:
        add(g, p == planes - 1, 0, 0)
    for c in range(coarse_planes):
        for g in rows:
            add(g, p // 2 == c, 0, 0)
        for g in rows:
            add(g, 0, p // 2 == c, 0)
    width = round_up(len(column_field), 128)
    select = np.zeros((2 * fields, width), np.float32)
    masks = np.zeros((3, planes, width), np.float32)
    for k, g in enumerate(column_field):
        if g >= 0:
            select[g, k] = 1
        masks[0, :, k], masks[1, :, k], masks[2, :, k] = forward[k], backward[k], centre[k]
    return select, masks


def slope_kernel(
    edge, planes, fields, coarse_planes, per_device, total, coarse_count, slots, slabs,
    dest_ref, parent_ref, own_ref, other_ref, own_low, other_low, own_high, other_high,
    spread_ref, weight_ref, out_ref, stack, ghosts, table, count,
):
    step = pl.program_id(0)
    cross = edge * edge
    rows = fields * planes
    own, slab = lax.axis_index("box"), lax.axis_index("slab")

    @pl.when(step == 0)
    def _():
        stack[...] = jnp.zeros_like(stack)
        for slot in range(slots):
            table[slot] = -1
            count[slot] = 0

        def place(b, carry):
            @pl.when(dest_ref[b] == own)
            def _():
                slot = 2 * (b // per_device)
                owner = parent_ref[b] // coarse_count
                table[jnp.where(table[slot] >= 0, slot + 1, slot)] = 2 * owner + count[owner]
                count[owner] = count[owner] + 1

            return carry

        lax.fori_loop(0, total, place, 0)
        for slot in range(slots):
            for n, ref in enumerate((own_ref, other_ref)):
                at = (2 * slot + n) * ROWS
                for block in range(ROWS // planes):
                    ghosts[at + block * planes : at + (block + 1) * planes, :cross] = ref[slot, fields + block]
        high, middle, low = (
            jnp.dot(part, spread_ref[...], preferred_element_type=jnp.float32)
            for part in split_three(ghosts[:, :cross])
        )
        ghosts[...] = high + (middle + low)

    face = table[step]

    @pl.when(face < 0)
    def _():
        out_ref[...] = jnp.zeros_like(out_ref)

    @pl.when(face >= 0)
    def _():
        lane = lax.broadcasted_iota(jnp.int32, (1, cross), 1)
        y, z = lane // edge, lane % edge
        for n, ref in enumerate((own_ref, other_ref)):
            at = (4 + n) * rows
            if planes % 8:
                for f in range(fields):
                    stack[at + f * planes : at + (f + 1) * planes] = ref[step, f]
            else:
                stack[at : at + rows] = ref[step, :fields].reshape(rows, cross)
        cells = stack[4 * rows : 6 * rows]
        stack[0 : 2 * rows] = jnp.where(y < edge - 1, pltpu.roll(cells, cross - edge, 1), 0.0) + jnp.where(
            z < edge - 1, pltpu.roll(cells, cross - 1, 1), 0.0
        )
        stack[2 * rows : 4 * rows] = jnp.where(y > 0, pltpu.roll(cells, edge, 1), 0.0) + jnp.where(
            z > 0, pltpu.roll(cells, 1, 1), 0.0
        )
        rim = ghosts[pl.ds(pl.multiple_of(2 * ROWS * face, 2 * ROWS), 2 * ROWS)]
        base = 6 * rows
        x_face = rim[:, 2 * coarse_planes * cross :]
        stack[base : base + 2 * ROWS] = x_face
        stack[base + 2 * ROWS : base + 4 * ROWS] = x_face

        @pl.when(slab > 0)
        def _():
            stack[base : base + fields] = own_low[step]
            stack[base + ROWS : base + ROWS + fields] = other_low[step]

        @pl.when(slab < slabs - 1)
        def _():
            stack[base + 2 * ROWS : base + 2 * ROWS + fields] = own_high[step]
            stack[base + 3 * ROWS : base + 3 * ROWS + fields] = other_high[step]

        base += 4 * ROWS
        for n in range(2 * coarse_planes):
            stack[base + 2 * ROWS * n : base + 2 * ROWS * (n + 1)] = rim[:, n * cross : (n + 1) * cross]
        mixed = jnp.dot(weight_ref[...], stack[...], precision=HIGHEST, preferred_element_type=jnp.float32)
        if planes % 8:
            for f in range(fields):
                out_ref[0, f] = mixed[f * planes : (f + 1) * planes]
        else:
            out_ref[0] = mixed.reshape(fields, planes, cross)


def mixing_weights(mixes, group, fields, planes, coarse_planes):
    lap_mix, grad_mix, damp_mix = mixes
    select, masks = slope_columns(fields, planes, coarse_planes)
    terms = jnp.stack([lap_mix + 0.5 * grad_mix, lap_mix - 0.5 * grad_mix, damp_mix - 6.0 * lap_mix])
    terms = lax.dynamic_slice_in_dim(terms, group * fields, fields, 1)
    terms = jnp.where(group == 0, terms, jnp.roll(terms, fields, axis=2))
    terms = jnp.einsum("tfg,gk->tfk", terms, jnp.asarray(select), precision=HIGHEST)
    return jnp.sum(terms[:, :, None, :] * jnp.asarray(masks)[:, None], axis=0).reshape(fields * planes, -1)


def body(boxes, move_dest, parent, coarse, lap_mix, grad_mix, damp_mix):
    box_count = lax.axis_size("box")
    slabs = lax.axis_size("slab")
    group = lax.axis_index("fld")
    levels, per_device, fields, planes, cross = boxes.shape
    edge = planes * slabs
    coarse_side = edge // 2 + 2
    coarse_planes = planes // 2
    slots = 2 * box_count
    total = move_dest.shape[0]
    coarse_count = coarse.shape[0]

    def exchange(pieces):
        around = [[(s, (s + shift) % box_count) for s in range(box_count)] for shift in range(box_count)]
        return [lax.ppermute(pieces[n], "box", around[n]) for n in range(1, box_count)]

    table = jnp.asarray(face_tables(coarse_side, coarse_planes, cross))
    first = pack_first(boxes, coarse, move_dest, parent, table, box_count)
    later = pack_later(boxes, move_dest, box_count)
    arrived = [first[0]] + exchange(first)
    later_arrived = exchange(later)
    now, moved, *facing = arrive(arrived, later[0], slabs)

    swap = [(0, 1), (1, 0)]
    now_other = lax.ppermute(now, "fld", swap)

    def shifted(values, up):
        pairs = [(s, s + 1) if up else (s + 1, s) for s in range(slabs - 1)]
        crossed = [(2 * a + f, 2 * b + 1 - f) for a, b in pairs for f in range(2)]
        return lax.ppermute(values, "slab", pairs), lax.ppermute(values, ("slab", "fld"), crossed)

    if slabs == 2:
        crossed = [(0, 3), (3, 0), (1, 2), (2, 1)]
        low = high = (lax.ppermute(facing[0], "slab", swap), lax.ppermute(facing[0], ("slab", "fld"), crossed))
    else:
        low, high = shifted(facing[1], True), shifted(facing[0], False)

    weight = mixing_weights((lap_mix, grad_mix, damp_mix), group, fields, planes, coarse_planes)
    spread = jnp.asarray(expand_table(coarse_planes, edge, cross)).astype(jnp.bfloat16)
    smem, vmem = pl.BlockSpec(memory_space=pltpu.SMEM), pl.BlockSpec(memory_space=pltpu.VMEM)
    slope = pl.pallas_call(
        functools.partial(
            slope_kernel, edge, planes, fields, coarse_planes, per_device, total, coarse_count, slots, slabs
        ),
        grid=(slots,),
        out_shape=jax.ShapeDtypeStruct((slots, fields, planes, cross), jnp.float32),
        in_specs=[smem, smem] + [vmem] * 8,
        out_specs=pl.BlockSpec((1, fields, planes, cross), lambda n: (n, 0, 0, 0)),
        scratch_shapes=[
            pltpu.VMEM((weight.shape[1], cross), jnp.float32),
            pltpu.VMEM((2 * ROWS * slots, spread.shape[1]), jnp.float32),
            pltpu.SMEM((slots,), jnp.int32),
            pltpu.SMEM((slots,), jnp.int32),
        ],
        compiler_params=pltpu.CompilerParams(vmem_limit_bytes=48 * 2 ** 20),
        cost_estimate=pl.CostEstimate(
            flops=12 * slots * weight.size * cross, bytes_accessed=12 * now.size, transcendentals=0
        ),
    )(move_dest, parent, now, now_other, low[0], low[1], high[0], high[1], spread, weight)
    return settle(later_arrived, moved, slope), slope


def solution(mesh):
    placed = (
        P(None, ("runs", "box"), "fld", "slab", None),
        P("runs"),
        P("runs"),
        P(("runs", "box"), "fld", None),
        P(),
        P(),
        P(),
    )
    return jax.shard_map(
        body,
        mesh=mesh,
        in_specs=placed,
        out_specs=(
            P(None, ("runs", "box"), "fld", "slab", None),
            P(("runs", "box"), "fld", "slab", None),
        ),
        check_vma=False,
    )
```

time: 87.4 us -> 70.6 us (0.81)
  the two profiles are of different devices: /device:TPU:29 before, /device:TPU:21 now
where the time goes in v3:
time: 70.6 us; the launch traced here: 71.3 us
  waiting for transfers between devices  35.2 us (50%)
  Pallas kernels  17.4 us (25%)
  starting transfers between devices  10.2 us (14%)
  local copies, waits for them, and re-layouts  5.49 us (8%)
  matrix products  1.23 us (2%)
  other arithmetic  1.03 us (1%)
  between operations  0.74 us (1%)
    ppermute x6, waiting for transfers between devices, exchange(): lax.ppermute(pieces[n], 'box', around[n])  29.1 us
    pallas_call x1, Pallas kernels, body(): pl.pallas_call(functools.partial(slope_kernel, edge, planes, fields, coar...  10.5 us
    ppermute x6, starting transfers between devices, exchange(): lax.ppermute(pieces[n], 'box', around[n])  7.2 us
    unnamed x24, local copies, waits for them, and re-layouts  5.42 us
    ppermute x1, waiting for transfers between devices, body(): lax.ppermute(facing[0], ('slab', 'fld'), crossed)  3.06 us
    ppermute x1, waiting for transfers between devices, body(): lax.ppermute(facing[0], 'slab', swap)  3.05 us
    pallas_call x1, Pallas kernels, pack_first(): pl.pallas_call(functools.partial(first_kernel, per_device, box_count, mov...  2.85 us
    pallas_call x1, Pallas kernels, pack_later(): pl.pallas_call(functools.partial(later_kernel, per_device, box_count, lev...  1.96 us
  transfers between devices with their start and end apart: 9, of which 4 were waited for; matrix products, arithmetic and copies ran while one was open for 3% of the time, Pallas kernels for 19%

profile of v3, /device:TPU:21, one launch (start us, length us, event | category | flops | bytes accessed | tf_op | source)
XLA Modules:
  0.0 71.3 jit_solution(6882714427348069881)
XLA Ops:
  0.6 0.0 copy-start
  0.6 1.3 %copy-done = f32[3,4,12,8,256]{4,3,2,1,0:T(8,128)S(1)} copy-done((f32[3,4,12,8,256]{4,3,2,1,0:T(8,128)S(1)}, f32[3,4,12,8,256]{4,3,2,1,0:T(8,128)}, u32[]{:S(2)}) %copy-start) | copy-done | bytes 1179672
  1.9 0.0 copy-start.2
  1.9 1.0 %copy-done.2 = f32[8,12,1000]{2,0,1:T(8,128)S(1)} copy-done((f32[8,12,1000]{2,0,1:T(8,128)S(1)}, f32[8,12,1000]{2,0,1:T(8,128)}, u32[]{:S(2)}) %copy-start.2) | copy-done | bytes 384024
  2.9 0.0 copy-start.3
  2.9 0.7 copy-done.3
  3.6 0.0 copy-start.4
  3.6 0.7 copy-done.4
  4.3 0.0 copy-start.6
  4.3 0.7 copy-done.6
  4.9 0.0 copy-start.9
  4.9 0.0 copy-start.10
  4.9 0.0 copy-start.11
  4.9 0.0 copy-start.7
  4.9 2.8 %shard_map.123 = (f32[2,14,8,256]{3,2,1,0:T(8,128)S(1)}, f32[2,14,8,256]{3,2,1,0:T(8,128)}, f32[2,14,8,256]{3,2,1,0:T(8,128)}, f32[2,14,8,256]{3,2,1,0:T(8,128)S(1)}) custom-call(s32[16]{0:T(128)S(1)} %copy-done.4, s32[16]{0:T(128)S(1)} %copy-done.6, f32[3,4,12,8,256]{4,3,2,1,0:T(8,128)S(1)} %copy-done, f32[12,8,1000]{2,1,0:T(8,128)S(1)} %bitcast.10, ...), custom_call_target="tpu_custom_call" | custom-call | flops 147456000 | bytes 2743296 | tf_op jit(solution)/shard_map/pallas_call | solution.py:115
  7.8 1.3 %collective-permute-start.3 = (f32[2,14,8,256]{3,2,1,0:T(8,128)}, f32[2,14,8,256]{3,2,1,0:T(8,128)S(1)}, u32[]{:S(2)}, u32[]{:S(2)}) collective-permute-start(f32[2,14,8,256]{3,2,1,0:T(8,128)} %get-tuple-element.17), channel_id=1, source_target_pairs={{0,4},{4,8},{8,12},{12,0},{1,5},{5,9},{9,13},{13,1},{2,6},{6,10},{... | collective-permute-start | bytes 688136 | tf_op jit(solution)/shard_map/ppermute | solution.py:449
  9.1 0.1 collective-permute-start.4
  9.2 1.2 %collective-permute-start.5 = (f32[2,14,8,256]{3,2,1,0:T(8,128)S(1)}, f32[2,14,8,256]{3,2,1,0:T(8,128)S(1)}, u32[]{:S(2)}, u32[]{:S(2)}) collective-permute-start(f32[2,14,8,256]{3,2,1,0:T(8,128)S(1)} %get-tuple-element.19), channel_id=1, source_target_pairs={{0,12},{4,0},{8,4},{12,8},{1,13},{5,1},{9,5},{13,9},{2,14},{6,2},{... | collective-permute-start | bytes 688136 | tf_op jit(solution)/shard_map/ppermute | solution.py:449
  10.4 2.0 %shard_map.122 = (f32[2,2,12,8,256]{4,3,2,1,0:T(8,128)S(1)}, f32[2,2,12,8,256]{4,3,2,1,0:T(8,128)S(1)}, f32[2,2,12,8,256]{4,3,2,1,0:T(8,128)S(1)}, f32[2,2,12,8,256]{4,3,2,1,0:T(8,128)S(1)}) custom-call(s32[16]{0:T(128)S(1)} %copy-done.4, f32[3,4,12,8,256]{4,3,2,1,0:T(8,128)S(1)} %copy-done), custom_call_target="tpu_custom_call" | custom-call | bytes 3538944 | tf_op jit(solution)/shard_map/pallas_call | solution.py:164
  12.4 0.3 collective-permute-start
  12.7 2.3 %collective-permute-start.1 = (f32[2,2,12,8,256]{4,3,2,1,0:T(8,128)S(1)}, f32[2,2,12,8,256]{4,3,2,1,0:T(8,128)S(1)}, u32[]{:S(2)}, u32[]{:S(2)}) collective-permute-start(f32[2,2,12,8,256]{4,3,2,1,0:T(8,128)S(1)} %get-tuple-element.14), channel_id=1, source_target_pairs={{0,8},{4,12},{8,0},{12,4},{1,9},{5,13},{9,1},{13,5},{2,10},{6,14},... | collective-permute-start | bytes 1179656 | tf_op jit(solution)/shard_map/ppermute | solution.py:449
  15.0 0.0 collective-permute-done.3.refs_1_
  15.0 2.0 %collective-permute-start.2 = (f32[2,2,12,8,256]{4,3,2,1,0:T(8,128)S(1)}, f32[2,2,12,8,256]{4,3,2,1,0:T(8,128)S(1)}, u32[]{:S(2)}, u32[]{:S(2)}) collective-permute-start(f32[2,2,12,8,256]{4,3,2,1,0:T(8,128)S(1)} %get-tuple-element.15), channel_id=1, source_target_pairs={{0,12},{4,0},{8,4},{12,8},{1,13},{5,1},{9,5},{13,9},{2,14},{6,2},{... | collective-permute-start | bytes 1179656 | tf_op jit(solution)/shard_map/ppermute | solution.py:449
  17.0 7.9 %collective-permute-done.4.refs_2_ = f32[2,14,8,256]{3,2,1,0:T(8,128)S(1)} collective-permute-done((f32[2,14,8,256]{3,2,1,0:T(8,128)}, f32[2,14,8,256]{3,2,1,0:T(8,128)S(1)}, u32[]{:S(2)}, u32[]{:S(2)}) %collective-permute-start.4) | collective-permute-done | bytes 229408 | tf_op jit(solution)/shard_map/ppermute | solution.py:449
  24.9 21.2 %collective-permute-done.5.refs_3_ = f32[2,14,8,256]{3,2,1,0:T(8,128)S(1)} collective-permute-done((f32[2,14,8,256]{3,2,1,0:T(8,128)S(1)}, f32[2,14,8,256]{3,2,1,0:T(8,128)S(1)}, u32[]{:S(2)}, u32[]{:S(2)}) %collective-permute-start.5) | collective-permute-done | bytes 229408 | tf_op jit(solution)/shard_map/ppermute | solution.py:449
  46.1 1.1 %shard_map.124 = (f32[8,14,8,256]{3,2,1,0:T(8,128)S(1)}, f32[3,8,12,8,256]{4,3,2,1,0:T(8,128)}, f32[8,12,256]{2,1,0:T(8,128)S(1)}) custom-call(f32[2,14,8,256]{3,2,1,0:T(8,128)S(1)} %get-tuple-element.16.refs_0_, f32[2,14,8,256]{3,2,1,0:T(8,128)S(1)} %collective-permute-done.3.refs_1_, f32[2,14,8,256]{3,2,1,0:T(8,128)S(1)} %collective-permute-done.4.refs_2_, ...), custom_call_target="tpu_custom_call" | custom-call | bytes 2752512 | tf_op jit(solution)/shard_map/pallas_call | solution.py:247
  47.1 0.7 collective-permute-start.6
  47.8 0.0 copy-done.9
  47.8 0.0 copy-done.10
  47.8 0.0 copy-done.11
  47.8 0.1 fusion.7
  47.9 1.1 %collective-permute-start.8 = (f32[8,12,256]{2,1,0:T(8,128)S(1)}, f32[8,12,256]{2,1,0:T(8,128)S(1)}, u32[]{:S(2)}, u32[]{:S(2)}) collective-permute-start(f32[8,12,256]{2,1,0:T(8,128)S(1)} %get-tuple-element.23), channel_id=1, source_target_pairs={{0,3},{3,0},{1,2},{2,1},{4,7},{7,4},{5,6},{6,5},{8,11},{11,8},{9,1... | collective-permute-start | bytes 294920 | tf_op jit(solution)/shard_map/ppermute | solution.py:468
  49.1 1.2 %fusion.2 = f32[3,12,896]{2,1,0:T(8,128)S(1)} fusion(f32[24,896,1]{1,0,2:T(8,128)} %constant.30, f32[3,12,24]{2,1,0:T(8,128)S(1)} %fusion.1, f32[3,12,12]{2,1,0:T(8,128)S(1)} %get-tuple-element.25, f32[3,12,12]{2,1,0:T(8,128)S(1)} %get-tuple-element.24, pred[]{:T(512)S(6)} %eq.3), kind=kOutput, calls=%fused_computation.7 | convolution fusion | flops 9291456 | bytes 221953 | tf_op jit(solution)/shard_map/tfg,gk->tfk/dot_general | solution.py:431
  50.3 3.1 %collective-permute-done.8.other_low.other_high = f32[8,12,256]{2,1,0:T(8,128)S(1)} collective-permute-done((f32[8,12,256]{2,1,0:T(8,128)S(1)}, f32[8,12,256]{2,1,0:T(8,128)S(1)}, u32[]{:S(2)}, u32[]{:S(2)}) %collective-permute-start.8) | collective-permute-done | bytes 98336 | tf_op jit(solution)/shard_map/ppermute | solution.py:468
  53.4 1.2 %collective-permute-start.7 = (f32[8,12,256]{2,1,0:T(8,128)S(1)}, f32[8,12,256]{2,1,0:T(8,128)S(1)}, u32[]{:S(2)}, u32[]{:S(2)}) collective-permute-start(f32[8,12,256]{2,1,0:T(8,128)S(1)} %get-tuple-element.23), channel_id=1, source_target_pairs={{0,2},{2,0},{1,3},{3,1},{4,6},{6,4},{5,7},{7,5},{8,10},{10,8},{9,1... | collective-permute-start | bytes 294920 | tf_op jit(solution)/shard_map/ppermute | solution.py:468
  54.6 1.0 %multiply_reduce_fusion = f32[12,8,896]{2,1,0:T(8,128)S(1)} fusion(f32[3,8,896]{2,1,0:T(8,128)} %constant.26.clone, f32[3,12,896]{2,1,0:T(8,128)S(1)} %fusion.2), kind=kLoop, calls=%fused_computation | loop fusion | flops 430080 | bytes 559104 | tf_op jit(solution)/shard_map/reduce_sum | solution.py:432
  55.6 3.0 %collective-permute-done.7.own_low.own_high = f32[8,12,256]{2,1,0:T(8,128)S(1)} collective-permute-done((f32[8,12,256]{2,1,0:T(8,128)S(1)}, f32[8,12,256]{2,1,0:T(8,128)S(1)}, u32[]{:S(2)}, u32[]{:S(2)}) %collective-permute-start.7) | collective-permute-done | bytes 98336 | tf_op jit(solution)/shard_map/ppermute | solution.py:468
  58.6 0.0 collective-permute-done.6.other_ref
  58.6 0.0 copy-done.5
  58.6 0.0 copy-done.7
  58.6 0.0 copy-done.8
  58.7 10.5 %shard_map.125.refs_4_ = f32[8,12,8,256]{3,2,1,0:T(8,128)} custom-call(s32[16]{0:T(128)S(1)} %copy-done.5, s32[16]{0:T(128)S(1)} %copy-done.7, f32[8,14,8,256]{3,2,1,0:T(8,128)S(1)} %get-tuple-element.22.own_ref, f32[8,14,8,256]{3,2,1,0:T(8,128)S(1)} %collective-permute-done.6.other_ref, f32[8,12,256]{2,1,0:T(8,128)S(1)} %collective-permute-done.7.own_low.own_high, ...), custom_call_target="tpu_custom_call" | custom-call | flops 2113929216 | bytes 2752512 | tf_op jit(solution)/shard_map/pallas_call | solution.py:475
  69.1 0.0 collective-permute-done.refs_0_
  69.1 0.0 collective-permute-done.1.refs_1_
  69.1 0.0 collective-permute-done.2.refs_2_
  69.1 0.0 copy-start.1
  69.1 1.1 %copy-done.1 = f32[8,12,8,256]{3,2,1,0:T(8,128)S(1)} copy-done((f32[8,12,8,256]{3,2,1,0:T(8,128)S(1)}, f32[8,12,8,256]{3,2,1,0:T(8,128)}, u32[]{:S(2)}) %copy-start.1) | copy-done | bytes 786456
  70.3 1.0 %shard_map.126 = f32[3,8,12,8,256]{4,3,2,1,0:T(8,128)} custom-call(f32[2,2,12,8,256]{4,3,2,1,0:T(8,128)S(1)} %collective-permute-done.refs_0_, f32[2,2,12,8,256]{4,3,2,1,0:T(8,128)S(1)} %collective-permute-done.1.refs_1_, f32[2,2,12,8,256]{4,3,2,1,0:T(8,128)S(1)} %collective-permute-done.2.refs_2_, ...), custom_call_target="tpu_custom_call", output_to_operand_aliasing={{}: (3, {})} | custom-call | bytes 2359296 | tf_op jit(solution)/shard_map/pallas_call | solution.py:199
  (4 shorter events, 0.0 us)
Async XLA Ops:
  0.6 1.3 %copy-start = (f32[3,4,12,8,256]{4,3,2,1,0:T(8,128)S(1)}, f32[3,4,12,8,256]{4,3,2,1,0:T(8,128)}, u32[]{:S(2)}) copy-start(f32[3,4,12,8,256]{4,3,2,1,0:T(8,128)} %boxes_ref.3) | copy-start | bytes 3538948
  1.9 1.0 %copy-start.2 = (f32[8,12,1000]{2,0,1:T(8,128)S(1)}, f32[8,12,1000]{2,0,1:T(8,128)}, u32[]{:S(2)}) copy-start(f32[8,12,1000]{2,0,1:T(8,128)} %param.14) | copy-start | bytes 1152004
  2.9 0.7 copy-start.3
  3.6 0.7 copy-start.4
  4.3 0.7 copy-start.6
  4.9 42.9 %copy-start.9 = (f32[24,24]{1,0:T(8,128)S(1)}, f32[24,24]{1,0:T(8,128)}, u32[]{:S(2)}) copy-start(f32[24,24]{1,0:T(8,128)} %param.15) | copy-start | bytes 6916
  4.9 42.9 %copy-start.10 = (f32[24,24]{1,0:T(8,128)S(1)}, f32[24,24]{1,0:T(8,128)}, u32[]{:S(2)}) copy-start(f32[24,24]{1,0:T(8,128)} %param.16) | copy-start | bytes 6916
  4.9 42.9 %copy-start.11 = (f32[24,24]{1,0:T(8,128)S(1)}, f32[24,24]{1,0:T(8,128)}, u32[]{:S(2)}) copy-start(f32[24,24]{1,0:T(8,128)} %param.17) | copy-start | bytes 6916
  4.9 53.7 %copy-start.5 = (s32[16]{0:T(128)S(1)}, s32[16]{0:T(128)}, u32[]{:S(2)}) copy-start(s32[16]{0:T(128)} %dest_ref.5) | copy-start | bytes 196
  4.9 53.7 %copy-start.7 = (s32[16]{0:T(128)S(1)}, s32[16]{0:T(128)}, u32[]{:S(2)}) copy-start(s32[16]{0:T(128)} %parent_ref.3) | copy-start | bytes 196
  7.8 7.2 %collective-permute-start.3 = (f32[2,14,8,256]{3,2,1,0:T(8,128)}, f32[2,14,8,256]{3,2,1,0:T(8,128)S(1)}, u32[]{:S(2)}, u32[]{:S(2)}) collective-permute-start(f32[2,14,8,256]{3,2,1,0:T(8,128)} %get-tuple-element.17), channel_id=1, source_target_pairs={{0,4},{4,8},{8,12},{12,0},{1,5},{5,9},{9,13},{13,1},{2,6},{6,10},{... | collective-permute-start | bytes 688136 | tf_op jit(solution)/shard_map/ppermute | solution.py:449
  9.1 15.8 %collective-permute-start.4 = (f32[2,14,8,256]{3,2,1,0:T(8,128)}, f32[2,14,8,256]{3,2,1,0:T(8,128)S(1)}, u32[]{:S(2)}, u32[]{:S(2)}) collective-permute-start(f32[2,14,8,256]{3,2,1,0:T(8,128)} %get-tuple-element.18), channel_id=1, source_target_pairs={{0,8},{4,12},{8,0},{12,4},{1,9},{5,13},{9,1},{13,5},{2,10},{6,14},... | collective-permute-start | bytes 688136 | tf_op jit(solution)/shard_map/ppermute | solution.py:449
  9.2 36.9 %collective-permute-start.5 = (f32[2,14,8,256]{3,2,1,0:T(8,128)S(1)}, f32[2,14,8,256]{3,2,1,0:T(8,128)S(1)}, u32[]{:S(2)}, u32[]{:S(2)}) collective-permute-start(f32[2,14,8,256]{3,2,1,0:T(8,128)S(1)} %get-tuple-element.19), channel_id=1, source_target_pairs={{0,12},{4,0},{8,4},{12,8},{1,13},{5,1},{9,5},{13,9},{2,14},{6,2},{... | collective-permute-start | bytes 688136 | tf_op jit(solution)/shard_map/ppermute | solution.py:449
  12.4 56.8 %collective-permute-start = (f32[2,2,12,8,256]{4,3,2,1,0:T(8,128)S(1)}, f32[2,2,12,8,256]{4,3,2,1,0:T(8,128)S(1)}, u32[]{:S(2)}, u32[]{:S(2)}) collective-permute-start(f32[2,2,12,8,256]{4,3,2,1,0:T(8,128)S(1)} %get-tuple-element.13), channel_id=1, source_target_pairs={{0,4},{4,8},{8,12},{12,0},{1,5},{5,9},{9,13},{13,1},{2,6},{6,10},{... | collective-permute-start | bytes 1179656 | tf_op jit(solution)/shard_map/ppermute | solution.py:449
  12.7 56.4 %collective-permute-start.1 = (f32[2,2,12,8,256]{4,3,2,1,0:T(8,128)S(1)}, f32[2,2,12,8,256]{4,3,2,1,0:T(8,128)S(1)}, u32[]{:S(2)}, u32[]{:S(2)}) collective-permute-start(f32[2,2,12,8,256]{4,3,2,1,0:T(8,128)S(1)} %get-tuple-element.14), channel_id=1, source_target_pairs={{0,8},{4,12},{8,0},{12,4},{1,9},{5,13},{9,1},{13,5},{2,10},{6,14},... | collective-permute-start | bytes 1179656 | tf_op jit(solution)/shard_map/ppermute | solution.py:449
  15.0 43.7 %copy-start.8 = (bf16[256,2304]{1,0:T(8,128)(2,1)S(1)}, bf16[256,2304]{1,0:T(8,128)(2,1)}, u32[]{:S(2)}) copy-start(bf16[256,2304]{1,0:T(8,128)(2,1)} %constant.29.spread_ref) | copy-start | bytes 3538948
  15.0 54.1 %collective-permute-start.2 = (f32[2,2,12,8,256]{4,3,2,1,0:T(8,128)S(1)}, f32[2,2,12,8,256]{4,3,2,1,0:T(8,128)S(1)}, u32[]{:S(2)}, u32[]{:S(2)}) collective-permute-start(f32[2,2,12,8,256]{4,3,2,1,0:T(8,128)S(1)} %get-tuple-element.15), channel_id=1, source_target_pairs={{0,12},{4,0},{8,4},{12,8},{1,13},{5,1},{9,5},{13,9},{2,14},{6,2},{... | collective-permute-start | bytes 1179656 | tf_op jit(solution)/shard_map/ppermute | solution.py:449
  47.1 11.5 %collective-permute-start.6 = (f32[8,14,8,256]{3,2,1,0:T(8,128)S(1)}, f32[8,14,8,256]{3,2,1,0:T(8,128)S(1)}, u32[]{:S(2)}, u32[]{:S(2)}) collective-permute-start(f32[8,14,8,256]{3,2,1,0:T(8,128)S(1)} %get-tuple-element.22.own_ref), channel_id=1, source_target_pairs={{0,1},{1,0},{2,3},{3,2},{4,5},{5,4},{6,7},{7,6},{8,9},{9,8},{10,11... | collective-permute-start | bytes 2752520 | tf_op jit(solution)/shard_map/ppermute | solution.py:459
  47.9 5.5 %collective-permute-start.8 = (f32[8,12,256]{2,1,0:T(8,128)S(1)}, f32[8,12,256]{2,1,0:T(8,128)S(1)}, u32[]{:S(2)}, u32[]{:S(2)}) collective-permute-start(f32[8,12,256]{2,1,0:T(8,128)S(1)} %get-tuple-element.23), channel_id=1, source_target_pairs={{0,3},{3,0},{1,2},{2,1},{4,7},{7,4},{5,6},{6,5},{8,11},{11,8},{9,1... | collective-permute-start | bytes 294920 | tf_op jit(solution)/shard_map/ppermute | solution.py:468
  53.4 5.3 %collective-permute-start.7 = (f32[8,12,256]{2,1,0:T(8,128)S(1)}, f32[8,12,256]{2,1,0:T(8,128)S(1)}, u32[]{:S(2)}, u32[]{:S(2)}) collective-permute-start(f32[8,12,256]{2,1,0:T(8,128)S(1)} %get-tuple-element.23), channel_id=1, source_target_pairs={{0,2},{2,0},{1,3},{3,1},{4,6},{6,4},{5,7},{7,5},{8,10},{10,8},{9,1... | collective-permute-start | bytes 294920 | tf_op jit(solution)/shard_map/ppermute | solution.py:468
  69.1 1.1 %copy-start.1 = (f32[8,12,8,256]{3,2,1,0:T(8,128)S(1)}, f32[8,12,8,256]{3,2,1,0:T(8,128)}, u32[]{:S(2)}) copy-start(f32[8,12,8,256]{3,2,1,0:T(8,128)} %shard_map.125.refs_4_) | copy-start | bytes 2359300

commit v4 on v3

--- a/solution.py
+++ b/solution.py
@@ -44,11 +44,23 @@
             yield shift, k, 2 * lax.rem(own + shift, box_count) + k
 
 
-def first_kernel(per_device, box_count, total, dest_ref, parent_ref, boxes_ref, coarse_ref, table_ref, *refs):
-    outs, (chosen, box_table, face_table, sems) = refs[:box_count], refs[box_count:]
+def first_kernel(per_device, box_count, edge, dest_ref, parent_ref, boxes_ref, coarse_ref, *refs):
+    outs, (shells, chosen, dest, parent, box_table, face_table, sems, in_sems) = refs[:box_count], refs[box_count:]
     fields, coarse_count, cells = coarse_ref.shape
+    planes, cross = outs[0].shape[2:]
     own, slab = lax.axis_index("box"), lax.axis_index("slab")
-    place_boxes(per_device, box_count, dest_ref, box_table)
+    fetches = [
+        pltpu.make_async_copy(coarse_ref, shells, in_sems.at[0]),
+        pltpu.make_async_copy(dest_ref, dest, in_sems.at[1]),
+        pltpu.make_async_copy(parent_ref, parent, in_sems.at[2]),
+    ]
+    for fetch in fetches:
+        fetch.start()
+    index = face_cells(lax.broadcasted_iota(jnp.int32, (1, cross), 1), edge, planes // 2, slab)
+    cell = lax.broadcasted_iota(jnp.int32, (cells, cross), 0)
+    one_hot = (cell == index).astype(jnp.float32).astype(jnp.bfloat16)
+    fetches[1].wait()
+    place_boxes(per_device, box_count, dest, box_table)
 
     def copy(shift, k, b):
         return pltpu.make_async_copy(
@@ -64,14 +76,15 @@
 
         @pl.when(b < 0)
         def _():
-            outs[shift][k, :fields] = jnp.zeros((fields,) + outs[shift].shape[2:], jnp.float32)
+            outs[shift][k, :fields] = jnp.zeros((fields, planes, cross), jnp.float32)
 
     for slot in range(2 * box_count):
         face_table[slot] = -1
+    fetches[2].wait()
 
     def place(b, carry):
-        slot = 2 * dest_ref[b]
-        local = parent_ref[b] - own * coarse_count
+        slot = 2 * dest[b]
+        local = parent[b] - own * coarse_count
 
         @pl.when(jnp.logical_and(local >= 0, local < coarse_count))
         def _():
@@ -79,16 +92,13 @@
 
         return carry
 
-    lax.fori_loop(0, total, place, 0)
-    index = table_ref[0:1] + slab * table_ref[1:2] + jnp.where(slab > 0, table_ref[2:3], 0)
-    cell = lax.broadcasted_iota(jnp.int32, (cells, index.shape[1]), 0)
-    one_hot = (cell == index).astype(jnp.float32).astype(jnp.bfloat16)
+    lax.fori_loop(0, dest.shape[0], place, 0)
+    fetches[0].wait()
     high, middle, low = (
         jnp.dot(part, one_hot, preferred_element_type=jnp.float32)
-        for part in split_three(coarse_ref[...].reshape(fields * coarse_count, cells))
+        for part in split_three(shells[...].reshape(fields * coarse_count, cells))
     )
     chosen[...] = (high + (middle + low)).reshape(chosen.shape)
-    planes = outs[0].shape[2]
     for shift, k, slot in each_slot(box_count):
         local = face_table[slot]
         for row in range(ROWS):
@@ -97,7 +107,7 @@
                 values = chosen[row, pl.ds(jnp.maximum(local, 0), 1)]
                 values = jnp.where(local >= 0, values, 0.0)
             else:
-                values = jnp.zeros((1, chosen.shape[2]), jnp.float32)
+                values = jnp.zeros((1, cross), jnp.float32)
             outs[shift][k, to, row % planes : row % planes + 1] = values
     for shift, k, slot in each_slot(box_count):
         b = box_table[slot]
@@ -107,27 +117,31 @@
             copy(shift, k, b).wait()
 
 
-def pack_first(boxes, coarse, move_dest, parent, table, box_count):
+def pack_first(boxes, coarse, move_dest, parent, edge, box_count):
     per_device, fields, planes, cross = boxes.shape[1:]
     coarse = jnp.transpose(coarse, (1, 0, 2))
-    smem, vmem = pl.BlockSpec(memory_space=pltpu.SMEM), pl.BlockSpec(memory_space=pltpu.VMEM)
+    hbm, vmem = pl.BlockSpec(memory_space=pltpu.HBM), pl.BlockSpec(memory_space=pltpu.VMEM)
     item = (2, fields + ROWS // planes, planes, cross)
     return pl.pallas_call(
-        functools.partial(first_kernel, per_device, box_count, move_dest.shape[0]),
+        functools.partial(first_kernel, per_device, box_count, edge),
         out_shape=[jax.ShapeDtypeStruct(item, jnp.float32)] * box_count,
-        in_specs=[smem, smem, pl.BlockSpec(memory_space=pl.ANY), vmem, vmem],
+        in_specs=[hbm] * 4,
         out_specs=[vmem] * box_count,
         scratch_shapes=[
+            pltpu.VMEM(coarse.shape, jnp.float32),
             pltpu.VMEM(coarse.shape[:2] + (cross,), jnp.float32),
+            pltpu.SMEM(move_dest.shape, jnp.int32),
+            pltpu.SMEM(parent.shape, jnp.int32),
             pltpu.SMEM((2 * box_count,), jnp.int32),
             pltpu.SMEM((2 * box_count,), jnp.int32),
             pltpu.SemaphoreType.DMA((box_count, 2)),
+            pltpu.SemaphoreType.DMA((3,)),
         ],
         compiler_params=pltpu.CompilerParams(vmem_limit_bytes=48 * 2 ** 20),
         cost_estimate=pl.CostEstimate(
             flops=6 * coarse.size * cross, bytes_accessed=4 * (coarse.size + 2 * boxes.size), transcendentals=0
         ),
-    )(move_dest, parent, boxes, coarse, table)
+    )(move_dest, parent, boxes, coarse)
 
 
 def later_kernel(per_device, box_count, levels, dest_ref, boxes_ref, *refs):
@@ -164,7 +178,7 @@
     return pl.pallas_call(
         functools.partial(later_kernel, per_device, box_count, levels),
         out_shape=[jax.ShapeDtypeStruct((levels, 2) + boxes.shape[2:], jnp.float32)] * box_count,
-        in_specs=[pl.BlockSpec(memory_space=pltpu.SMEM), pl.BlockSpec(memory_space=pl.ANY)],
+        in_specs=[pl.BlockSpec(memory_space=pltpu.SMEM), pl.BlockSpec(memory_space=pltpu.HBM)],
         out_specs=[pl.BlockSpec(memory_space=pltpu.VMEM)] * box_count,
         scratch_shapes=[
             pltpu.SMEM((2 * box_count,), jnp.int32),
@@ -199,7 +213,7 @@
     return pl.pallas_call(
         functools.partial(settle_kernel, levels, box_count),
         out_shape=jax.ShapeDtypeStruct(moved.shape, jnp.float32),
-        in_specs=[vmem] * (box_count - 1) + [anywhere] * 2,
+        in_specs=[vmem] * (box_count - 1) + [anywhere, vmem],
         out_specs=anywhere,
         scratch_shapes=[pltpu.SemaphoreType.DMA((box_count,))],
         input_output_aliases={box_count - 1: 0},
@@ -257,24 +271,15 @@
     )(*pieces, own_later)
 
 
-def face_tables(coarse_side, coarse_planes, lanes):
-    half = coarse_side - 2
-    square = coarse_side * coarse_side
-    inner = np.arange(half) + 1
-    sides = []
-    for c in range(coarse_planes):
-        base = (c + 1) * square
-        sides += [base + inner, base + (coarse_side - 1) * coarse_side + inner]
-        sides += [base + inner * coarse_side, base + inner * coarse_side + coarse_side - 1]
-    yz = np.concatenate(sides)
-    x = (inner[:, None] * coarse_side + inner[None, :]).reshape(-1)
-    table = np.zeros((8, lanes), np.int32)
-    table[0] = -(10 ** 6)
-    table[0, : yz.size] = yz
-    table[1, : yz.size] = coarse_planes * square
-    table[0, yz.size : yz.size + x.size] = x
-    table[2, yz.size : yz.size + x.size] = (coarse_side - 1) * square
-    return table
+def face_cells(lane, edge, coarse_planes, slab):
+    half, side = edge // 2, edge // 2 + 2
+    plane, m = lane // (4 * half), lane % half + 1
+    which = (lane // half) % 4
+    rim = jnp.where(which == 0, m, jnp.where(which == 1, (side - 1) * side + m, m * side))
+    rim = jnp.where(which == 3, rim + side - 1, rim) + (slab * coarse_planes + plane + 1) * side * side
+    t = lane - 4 * half * coarse_planes
+    x_rim = jnp.where(slab > 0, (side - 1) * side * side, 0) + (t // half + 1) * side + m
+    return jnp.where(t < 0, rim, jnp.where(t < half * half, x_rim, -1))
 
 
 def expand_table(coarse_planes, edge, lanes):
@@ -335,7 +340,7 @@
 def slope_kernel(
     edge, planes, fields, coarse_planes, per_device, total, coarse_count, slots, slabs,
     dest_ref, parent_ref, own_ref, other_ref, own_low, other_low, own_high, other_high,
-    spread_ref, weight_ref, out_ref, stack, ghosts, table, count,
+    spread_ref, weight_ref, out_ref, token_ref, stack, ghosts, table, count,
 ):
     step = pl.program_id(0)
     cross = edge * edge
@@ -344,6 +349,7 @@
 
     @pl.when(step == 0)
     def _():
+        token_ref[...] = jnp.zeros_like(token_ref)
         stack[...] = jnp.zeros_like(stack)
         for slot in range(slots):
             table[slot] = -1
@@ -438,21 +444,22 @@
     group = lax.axis_index("fld")
     levels, per_device, fields, planes, cross = boxes.shape
     edge = planes * slabs
-    coarse_side = edge // 2 + 2
     coarse_planes = planes // 2
     slots = 2 * box_count
     total = move_dest.shape[0]
     coarse_count = coarse.shape[0]
 
-    def exchange(pieces):
-        around = [[(s, (s + shift) % box_count) for s in range(box_count)] for shift in range(box_count)]
-        return [lax.ppermute(pieces[n], "box", around[n]) for n in range(1, box_count)]
-
-    table = jnp.asarray(face_tables(coarse_side, coarse_planes, cross))
-    first = pack_first(boxes, coarse, move_dest, parent, table, box_count)
+    def send(piece, shift):
+        return lax.ppermute(piece, "box", [(s, (s + shift) % box_count) for s in range(box_count)])
+
+    first = pack_first(boxes, coarse, move_dest, parent, edge, box_count)
     later = pack_later(boxes, move_dest, box_count)
-    arrived = [first[0]] + exchange(first)
-    later_arrived = exchange(later)
+    arrived, later_arrived = [first[0]], []
+    for shift in range(1, box_count):
+        arrived.append(send(first[shift], shift))
+    for shift in range(1, box_count):
+        held, arrived[shift] = lax.optimization_barrier((later[shift], arrived[shift]))
+        later_arrived.append(send(held, shift))
     now, moved, *facing = arrive(arrived, later[0], slabs)
 
     swap = [(0, 1), (1, 0)]
@@ -472,14 +479,17 @@
     weight = mixing_weights((lap_mix, grad_mix, damp_mix), group, fields, planes, coarse_planes)
     spread = jnp.asarray(expand_table(coarse_planes, edge, cross)).astype(jnp.bfloat16)
     smem, vmem = pl.BlockSpec(memory_space=pltpu.SMEM), pl.BlockSpec(memory_space=pltpu.VMEM)
-    slope = pl.pallas_call(
+    slope, token = pl.pallas_call(
         functools.partial(
             slope_kernel, edge, planes, fields, coarse_planes, per_device, total, coarse_count, slots, slabs
         ),
         grid=(slots,),
-        out_shape=jax.ShapeDtypeStruct((slots, fields, planes, cross), jnp.float32),
+        out_shape=[
+            jax.ShapeDtypeStruct((slots, fields, planes, cross), jnp.float32),
+            jax.ShapeDtypeStruct((8, 128), jnp.float32),
+        ],
         in_specs=[smem, smem] + [vmem] * 8,
-        out_specs=pl.BlockSpec((1, fields, planes, cross), lambda n: (n, 0, 0, 0)),
+        out_specs=[pl.BlockSpec((1, fields, planes, cross), lambda n: (n, 0, 0, 0)), vmem],
         scratch_shapes=[
             pltpu.VMEM((weight.shape[1], cross), jnp.float32),
             pltpu.VMEM((2 * ROWS * slots, spread.shape[1]), jnp.float32),
@@ -491,7 +501,7 @@
             flops=12 * slots * weight.size * cross, bytes_accessed=12 * now.size, transcendentals=0
         ),
     )(move_dest, parent, now, now_other, low[0], low[1], high[0], high[1], spread, weight)
-    return settle(later_arrived, moved, slope), slope
+    return settle(later_arrived, moved, token), slope
 
 
 def solution(mesh):

time: 70.6 us -> 71.4 us (1.011)
  the two profiles are of different devices: /device:TPU:21 before, /device:TPU:0 now
where the time goes in v4:
time: 71.4 us; the launch traced here: 71.1 us
  waiting for transfers between devices  36.6 us (51%)
  starting transfers between devices  16.6 us (23%)
  Pallas kernels  13 us (18%)
  local copies, waits for them, and re-layouts  3.68 us (5%)
  between operations  0.79 us (1%)
    ppermute x6, waiting for transfers between devices, send(): lax.ppermute(piece, 'box', [(s, (s + shift) % box_count) for s in range(b...  28.2 us
    ppermute x6, starting transfers between devices, send(): lax.ppermute(piece, 'box', [(s, (s + shift) % box_count) for s in range(b...  14.1 us
    pallas_call x1, Pallas kernels, body(): pl.pallas_call(functools.partial(slope_kernel, edge, planes, fields, coar...  6.68 us
    ppermute x1, waiting for transfers between devices, body(): lax.ppermute(facing[0], ('slab', 'fld'), crossed)  4.34 us
    ppermute x1, waiting for transfers between devices, body(): lax.ppermute(facing[0], 'slab', swap)  4.03 us
    unnamed x24, local copies, waits for them, and re-layouts  3.61 us
    pallas_call x1, Pallas kernels, pack_first(): pl.pallas_call(functools.partial(first_kernel, per_device, box_count, edg...  2.27 us
    pallas_call x1, Pallas kernels, pack_later(): pl.pallas_call(functools.partial(later_kernel, per_device, box_count, lev...  1.96 us
  transfers between devices with their start and end apart: 9, of which 5 were waited for; matrix products, arithmetic and copies ran while one was open for 1% of the time, Pallas kernels for 12%

profile of v4, /device:TPU:0, one launch (start us, length us, event | category | flops | bytes accessed | tf_op | source)
XLA Modules:
  0.0 71.1 jit_solution(10054343297748473984)
XLA Ops:
  0.6 0.0 copy-start
  0.6 1.3 %copy-done = f32[3,4,12,8,256]{4,3,2,1,0:T(8,128)S(1)} copy-done((f32[3,4,12,8,256]{4,3,2,1,0:T(8,128)S(1)}, f32[3,4,12,8,256]{4,3,2,1,0:T(8,128)}, u32[]{:S(2)}) %copy-start) | copy-done | bytes 1179672
  1.9 0.0 copy-start.1
  1.9 1.0 %copy-done.1 = f32[8,12,1000]{2,0,1:T(8,128)S(1)} copy-done((f32[8,12,1000]{2,0,1:T(8,128)S(1)}, f32[8,12,1000]{2,0,1:T(8,128)}, u32[]{:S(2)}) %copy-start.1) | copy-done | bytes 384024
  2.9 0.7 copy-done.2
  3.6 0.0 copy-start.4
  3.6 0.7 copy-done.4
  4.2 0.0 copy-start.9
  4.2 0.0 copy-start.10
  4.2 0.0 copy-start.11
  4.2 0.0 copy-start.7
  4.2 0.0 copy-start.3
  4.2 0.0 copy-start.5
  4.3 2.3 %shard_map.114 = (f32[2,14,8,256]{3,2,1,0:T(8,128)S(1)}, f32[2,14,8,256]{3,2,1,0:T(8,128)S(1)}, f32[2,14,8,256]{3,2,1,0:T(8,128)S(1)}, f32[2,14,8,256]{3,2,1,0:T(8,128)S(1)}) custom-call(s32[16]{0:T(128)S(1)} %copy-done.2, s32[16]{0:T(128)S(1)} %copy-done.4, f32[3,4,12,8,256]{4,3,2,1,0:T(8,128)S(1)} %copy-done, f32[12,8,1000]{2,1,0:T(8,128)S(1)} %bitcast.10), custom_call_target="tpu_custom_call" | custom-call | flops 147456000 | bytes 2743296 | tf_op jit(solution)/shard_map/pallas_call | solution.py:125
  6.5 3.1 %collective-permute-start = (f32[2,14,8,256]{3,2,1,0:T(8,128)S(1)}, f32[2,14,8,256]{3,2,1,0:T(8,128)S(1)}, u32[]{:S(2)}, u32[]{:S(2)}) collective-permute-start(f32[2,14,8,256]{3,2,1,0:T(8,128)S(1)} %get-tuple-element.22), channel_id=1, source_target_pairs={{0,4},{4,8},{8,12},{12,0},{1,5},{5,9},{9,13},{13,1},{2,6},{6,10},{... | collective-permute-start | bytes 688136 | tf_op jit(solution)/shard_map/ppermute | solution.py:453
  9.6 2.6 %collective-permute-start.2 = (f32[2,14,8,256]{3,2,1,0:T(8,128)S(1)}, f32[2,14,8,256]{3,2,1,0:T(8,128)S(1)}, u32[]{:S(2)}, u32[]{:S(2)}) collective-permute-start(f32[2,14,8,256]{3,2,1,0:T(8,128)S(1)} %get-tuple-element.25), channel_id=1, source_target_pairs={{0,8},{4,12},{8,0},{12,4},{1,9},{5,13},{9,1},{13,5},{2,10},{6,14},... | collective-permute-start | bytes 688136 | tf_op jit(solution)/shard_map/ppermute | solution.py:453
  12.2 1.3 %collective-permute-start.4 = (f32[2,14,8,256]{3,2,1,0:T(8,128)S(1)}, f32[2,14,8,256]{3,2,1,0:T(8,128)S(1)}, u32[]{:S(2)}, u32[]{:S(2)}) collective-permute-start(f32[2,14,8,256]{3,2,1,0:T(8,128)S(1)} %get-tuple-element.28), channel_id=1, source_target_pairs={{0,12},{4,0},{8,4},{12,8},{1,13},{5,1},{9,5},{13,9},{2,14},{6,2},{... | collective-permute-start | bytes 688136 | tf_op jit(solution)/shard_map/ppermute | solution.py:453
  13.6 2.0 %shard_map.113 = (f32[2,2,12,8,256]{4,3,2,1,0:T(8,128)S(1)}, f32[2,2,12,8,256]{4,3,2,1,0:T(8,128)S(1)}, f32[2,2,12,8,256]{4,3,2,1,0:T(8,128)S(1)}, f32[2,2,12,8,256]{4,3,2,1,0:T(8,128)S(1)}) custom-call(s32[16]{0:T(128)S(1)} %copy-done.2, f32[3,4,12,8,256]{4,3,2,1,0:T(8,128)S(1)} %copy-done), custom_call_target="tpu_custom_call" | custom-call | bytes 3538944 | tf_op jit(solution)/shard_map/pallas_call | solution.py:178
  15.5 0.0 copy-start.6
  15.5 2.7 %collective-permute-done.refs_1_ = f32[2,14,8,256]{3,2,1,0:T(8,128)S(1)} collective-permute-done((f32[2,14,8,256]{3,2,1,0:T(8,128)S(1)}, f32[2,14,8,256]{3,2,1,0:T(8,128)S(1)}, u32[]{:S(2)}, u32[]{:S(2)}) %collective-permute-start) | collective-permute-done | bytes 229408 | tf_op jit(solution)/shard_map/ppermute | solution.py:453
  18.2 9.0 %collective-permute-done.2.refs_2_ = f32[2,14,8,256]{3,2,1,0:T(8,128)S(1)} collective-permute-done((f32[2,14,8,256]{3,2,1,0:T(8,128)S(1)}, f32[2,14,8,256]{3,2,1,0:T(8,128)S(1)}, u32[]{:S(2)}, u32[]{:S(2)}) %collective-permute-start.2) | collective-permute-done | bytes 229408 | tf_op jit(solution)/shard_map/ppermute | solution.py:453
  27.2 0.0 collective-permute-done.4.refs_3_
  27.2 1.1 %shard_map.115 = (f32[8,14,8,256]{3,2,1,0:T(8,128)S(1)}, f32[3,8,12,8,256]{4,3,2,1,0:T(8,128)}, f32[8,12,256]{2,1,0:T(8,128)S(1)}) custom-call(f32[2,14,8,256]{3,2,1,0:T(8,128)S(1)} %get-tuple-element.30.refs_0_, f32[2,14,8,256]{3,2,1,0:T(8,128)S(1)} %collective-permute-done.refs_1_, f32[2,14,8,256]{3,2,1,0:T(8,128)S(1)} %collective-permute-done.2.refs_2_, ...), custom_call_target="tpu_custom_call" | custom-call | bytes 2752512 | tf_op jit(solution)/shard_map/pallas_call | solution.py:261
  28.3 0.1 collective-permute-start.6
  28.4 0.0 copy-done.9
  28.4 0.0 copy-done.10
  28.4 0.0 copy-done.11
  28.4 0.1 fusion.7
  28.5 6.4 %collective-permute-start.5 = (f32[2,2,12,8,256]{4,3,2,1,0:T(8,128)S(1)}, f32[2,2,12,8,256]{4,3,2,1,0:T(8,128)S(1)}, u32[]{:S(2)}, u32[]{:S(2)}) collective-permute-start(f32[2,2,12,8,256]{4,3,2,1,0:T(8,128)S(1)} %get-tuple-element.29), channel_id=1, source_target_pairs={{0,12},{4,0},{8,4},{12,8},{1,13},{5,1},{9,5},{13,9},{2,14},{6,2},{... | collective-permute-start | bytes 1179656 | tf_op jit(solution)/shard_map/ppermute | solution.py:453
  34.9 0.4 collective-permute-start.3
  35.4 0.2 collective-permute-start.1
  35.5 1.0 %collective-permute-start.8 = (f32[8,12,256]{2,1,0:T(8,128)S(1)}, f32[8,12,256]{2,1,0:T(8,128)S(1)}, u32[]{:S(2)}, u32[]{:S(2)}) collective-permute-start(f32[8,12,256]{2,1,0:T(8,128)S(1)} %get-tuple-element.37), channel_id=1, source_target_pairs={{0,3},{3,0},{1,2},{2,1},{4,7},{7,4},{5,6},{6,5},{8,11},{11,8},{9,1... | collective-permute-start | bytes 294920 | tf_op jit(solution)/shard_map/ppermute | solution.py:475
  36.6 0.0 copy-done.8
  36.6 0.4 fusion.2
  36.9 4.3 %collective-permute-done.8.other_low.other_high = f32[8,12,256]{2,1,0:T(8,128)S(1)} collective-permute-done((f32[8,12,256]{2,1,0:T(8,128)S(1)}, f32[8,12,256]{2,1,0:T(8,128)S(1)}, u32[]{:S(2)}, u32[]{:S(2)}) %collective-permute-start.8) | collective-permute-done | bytes 98336 | tf_op jit(solution)/shard_map/ppermute | solution.py:475
  41.3 1.5 %collective-permute-start.7 = (f32[8,12,256]{2,1,0:T(8,128)S(1)}, f32[8,12,256]{2,1,0:T(8,128)S(1)}, u32[]{:S(2)}, u32[]{:S(2)}) collective-permute-start(f32[8,12,256]{2,1,0:T(8,128)S(1)} %get-tuple-element.37), channel_id=1, source_target_pairs={{0,2},{2,0},{1,3},{3,1},{4,6},{6,4},{5,7},{7,5},{8,10},{10,8},{9,1... | collective-permute-start | bytes 294920 | tf_op jit(solution)/shard_map/ppermute | solution.py:475
  42.7 0.0 copy-done.7
  42.7 0.1 multiply_reduce_fusion
  42.8 4.0 %collective-permute-done.7.own_low.own_high = f32[8,12,256]{2,1,0:T(8,128)S(1)} collective-permute-done((f32[8,12,256]{2,1,0:T(8,128)S(1)}, f32[8,12,256]{2,1,0:T(8,128)S(1)}, u32[]{:S(2)}, u32[]{:S(2)}) %collective-permute-start.7) | collective-permute-done | bytes 98336 | tf_op jit(solution)/shard_map/ppermute | solution.py:475
  46.9 0.0 collective-permute-done.6.other_ref
  46.9 0.0 copy-done.3
  46.9 0.0 copy-done.5
  46.9 0.0 copy-done.6
  46.9 6.7 %shard_map.116 = (f32[8,12,8,256]{3,2,1,0:T(8,128)}, f32[8,128]{1,0:T(8,128)S(1)}) custom-call(s32[16]{0:T(128)S(1)} %copy-done.3, s32[16]{0:T(128)S(1)} %copy-done.5, f32[8,14,8,256]{3,2,1,0:T(8,128)S(1)} %get-tuple-element.36.own_ref, f32[8,14,8,256]{3,2,1,0:T(8,128)S(1)} %collective-permute-done.6.other_ref, ...), custom_call_target="tpu_custom_call" | custom-call | flops 2113929216 | bytes 2752512 | tf_op jit(solution)/shard_map/pallas_call | solution.py:482
  53.6 0.0 collective-permute-done.5.refs_2_
  53.6 16.5 %collective-permute-done.3.refs_1_ = f32[2,2,12,8,256]{4,3,2,1,0:T(8,128)S(1)} collective-permute-done((f32[2,2,12,8,256]{4,3,2,1,0:T(8,128)S(1)}, f32[2,2,12,8,256]{4,3,2,1,0:T(8,128)S(1)}, u32[]{:S(2)}, u32[]{:S(2)}) %collective-permute-start.3) | collective-permute-done | bytes 393248 | tf_op jit(solution)/shard_map/ppermute | solution.py:453
  70.1 0.0 collective-permute-done.1.refs_0_
  70.1 1.0 %shard_map.117 = f32[3,8,12,8,256]{4,3,2,1,0:T(8,128)} custom-call(f32[2,2,12,8,256]{4,3,2,1,0:T(8,128)S(1)} %collective-permute-done.1.refs_0_, f32[2,2,12,8,256]{4,3,2,1,0:T(8,128)S(1)} %collective-permute-done.3.refs_1_, f32[2,2,12,8,256]{4,3,2,1,0:T(8,128)S(1)} %collective-permute-done.5.refs_2_, ...), custom_call_target="tpu_custom_call", output_to_operand_aliasing={{}: (3, {})} | custom-call | bytes 2359296 | tf_op jit(solution)/shard_map/pallas_call | solution.py:213
  (4 shorter events, 0.0 us)
Async XLA Ops:
  0.6 1.3 %copy-start = (f32[3,4,12,8,256]{4,3,2,1,0:T(8,128)S(1)}, f32[3,4,12,8,256]{4,3,2,1,0:T(8,128)}, u32[]{:S(2)}) copy-start(f32[3,4,12,8,256]{4,3,2,1,0:T(8,128)} %boxes_ref.3) | copy-start | bytes 3538948
  1.9 1.0 %copy-start.1 = (f32[8,12,1000]{2,0,1:T(8,128)S(1)}, f32[8,12,1000]{2,0,1:T(8,128)}, u32[]{:S(2)}) copy-start(f32[8,12,1000]{2,0,1:T(8,128)} %param.13) | copy-start | bytes 1152004
  2.9 0.7 copy-start.2
  3.6 0.7 copy-start.4
  4.2 24.1 %copy-start.9 = (f32[24,24]{1,0:T(8,128)S(1)}, f32[24,24]{1,0:T(8,128)}, u32[]{:S(2)}) copy-start(f32[24,24]{1,0:T(8,128)} %param.14) | copy-start | bytes 6916
  4.2 24.2 %copy-start.10 = (f32[24,24]{1,0:T(8,128)S(1)}, f32[24,24]{1,0:T(8,128)}, u32[]{:S(2)}) copy-start(f32[24,24]{1,0:T(8,128)} %param.15) | copy-start | bytes 6916
  4.2 24.2 %copy-start.11 = (f32[24,24]{1,0:T(8,128)S(1)}, f32[24,24]{1,0:T(8,128)}, u32[]{:S(2)}) copy-start(f32[24,24]{1,0:T(8,128)} %param.16) | copy-start | bytes 6916
  4.2 32.3 %copy-start.8 = (f32[24,896,1]{1,0,2:T(8,128)S(1)}, f32[24,896,1]{1,0,2:T(8,128)}, u32[]{:S(2)}) copy-start(f32[24,896,1]{1,0,2:T(8,128)} %constant.27) | copy-start | bytes 258052
  4.2 38.5 %copy-start.7 = (f32[3,8,896]{2,1,0:T(8,128)S(1)}, f32[3,8,896]{2,1,0:T(8,128)}, u32[]{:S(2)}) copy-start(f32[3,8,896]{2,1,0:T(8,128)} %constant.23.clone) | copy-start | bytes 258052
  4.2 42.6 %copy-start.3 = (s32[16]{0:T(128)S(1)}, s32[16]{0:T(128)}, u32[]{:S(2)}) copy-start(s32[16]{0:T(128)} %dest_ref.5) | copy-start | bytes 196
  4.2 42.6 %copy-start.5 = (s32[16]{0:T(128)S(1)}, s32[16]{0:T(128)}, u32[]{:S(2)}) copy-start(s32[16]{0:T(128)} %parent_ref.3) | copy-start | bytes 196
  6.5 11.7 %collective-permute-start = (f32[2,14,8,256]{3,2,1,0:T(8,128)S(1)}, f32[2,14,8,256]{3,2,1,0:T(8,128)S(1)}, u32[]{:S(2)}, u32[]{:S(2)}) collective-permute-start(f32[2,14,8,256]{3,2,1,0:T(8,128)S(1)} %get-tuple-element.22), channel_id=1, source_target_pairs={{0,4},{4,8},{8,12},{12,0},{1,5},{5,9},{9,13},{13,1},{2,6},{6,10},{... | collective-permute-start | bytes 688136 | tf_op jit(solution)/shard_map/ppermute | solution.py:453
  9.6 17.6 %collective-permute-start.2 = (f32[2,14,8,256]{3,2,1,0:T(8,128)S(1)}, f32[2,14,8,256]{3,2,1,0:T(8,128)S(1)}, u32[]{:S(2)}, u32[]{:S(2)}) collective-permute-start(f32[2,14,8,256]{3,2,1,0:T(8,128)S(1)} %get-tuple-element.25), channel_id=1, source_target_pairs={{0,8},{4,12},{8,0},{12,4},{1,9},{5,13},{9,1},{13,5},{2,10},{6,14},... | collective-permute-start | bytes 688136 | tf_op jit(solution)/shard_map/ppermute | solution.py:453
  12.2 15.0 %collective-permute-start.4 = (f32[2,14,8,256]{3,2,1,0:T(8,128)S(1)}, f32[2,14,8,256]{3,2,1,0:T(8,128)S(1)}, u32[]{:S(2)}, u32[]{:S(2)}) collective-permute-start(f32[2,14,8,256]{3,2,1,0:T(8,128)S(1)} %get-tuple-element.28), channel_id=1, source_target_pairs={{0,12},{4,0},{8,4},{12,8},{1,13},{5,1},{9,5},{13,9},{2,14},{6,2},{... | collective-permute-start | bytes 688136 | tf_op jit(solution)/shard_map/ppermute | solution.py:453
  15.5 31.4 %copy-start.6 = (bf16[256,2304]{1,0:T(8,128)(2,1)S(1)}, bf16[256,2304]{1,0:T(8,128)(2,1)}, u32[]{:S(2)}) copy-start(bf16[256,2304]{1,0:T(8,128)(2,1)} %constant.26.spread_ref) | copy-start | bytes 3538948
  28.3 18.6 %collective-permute-start.6 = (f32[8,14,8,256]{3,2,1,0:T(8,128)S(1)}, f32[8,14,8,256]{3,2,1,0:T(8,128)S(1)}, u32[]{:S(2)}, u32[]{:S(2)}) collective-permute-start(f32[8,14,8,256]{3,2,1,0:T(8,128)S(1)} %get-tuple-element.36.own_ref), channel_id=1, source_target_pairs={{0,1},{1,0},{2,3},{3,2},{4,5},{5,4},{6,7},{7,6},{8,9},{9,8},{10,11... | collective-permute-start | bytes 2752520 | tf_op jit(solution)/shard_map/ppermute | solution.py:466
  28.5 25.1 %collective-permute-start.5 = (f32[2,2,12,8,256]{4,3,2,1,0:T(8,128)S(1)}, f32[2,2,12,8,256]{4,3,2,1,0:T(8,128)S(1)}, u32[]{:S(2)}, u32[]{:S(2)}) collective-permute-start(f32[2,2,12,8,256]{4,3,2,1,0:T(8,128)S(1)} %get-tuple-element.29), channel_id=1, source_target_pairs={{0,12},{4,0},{8,4},{12,8},{1,13},{5,1},{9,5},{13,9},{2,14},{6,2},{... | collective-permute-start | bytes 1179656 | tf_op jit(solution)/shard_map/ppermute | solution.py:453
  34.9 35.2 %collective-permute-start.3 = (f32[2,2,12,8,256]{4,3,2,1,0:T(8,128)S(1)}, f32[2,2,12,8,256]{4,3,2,1,0:T(8,128)S(1)}, u32[]{:S(2)}, u32[]{:S(2)}) collective-permute-start(f32[2,2,12,8,256]{4,3,2,1,0:T(8,128)S(1)} %get-tuple-element.26), channel_id=1, source_target_pairs={{0,8},{4,12},{8,0},{12,4},{1,9},{5,13},{9,1},{13,5},{2,10},{6,14},... | collective-permute-start | bytes 1179656 | tf_op jit(solution)/shard_map/ppermute | solution.py:453
  35.4 34.7 %collective-permute-start.1 = (f32[2,2,12,8,256]{4,3,2,1,0:T(8,128)S(1)}, f32[2,2,12,8,256]{4,3,2,1,0:T(8,128)S(1)}, u32[]{:S(2)}, u32[]{:S(2)}) collective-permute-start(f32[2,2,12,8,256]{4,3,2,1,0:T(8,128)S(1)} %get-tuple-element.23), channel_id=1, source_target_pairs={{0,4},{4,8},{8,12},{12,0},{1,5},{5,9},{9,13},{13,1},{2,6},{6,10},{... | collective-permute-start | bytes 1179656 | tf_op jit(solution)/shard_map/ppermute | solution.py:453
  35.5 5.7 %collective-permute-start.8 = (f32[8,12,256]{2,1,0:T(8,128)S(1)}, f32[8,12,256]{2,1,0:T(8,128)S(1)}, u32[]{:S(2)}, u32[]{:S(2)}) collective-permute-start(f32[8,12,256]{2,1,0:T(8,128)S(1)} %get-tuple-element.37), channel_id=1, source_target_pairs={{0,3},{3,0},{1,2},{2,1},{4,7},{7,4},{5,6},{6,5},{8,11},{11,8},{9,1... | collective-permute-start | bytes 294920 | tf_op jit(solution)/shard_map/ppermute | solution.py:475
  41.3 5.6 %collective-permute-start.7 = (f32[8,12,256]{2,1,0:T(8,128)S(1)}, f32[8,12,256]{2,1,0:T(8,128)S(1)}, u32[]{:S(2)}, u32[]{:S(2)}) collective-permute-start(f32[8,12,256]{2,1,0:T(8,128)S(1)} %get-tuple-element.37), channel_id=1, source_target_pairs={{0,2},{2,0},{1,3},{3,1},{4,6},{6,4},{5,7},{7,5},{8,10},{10,8},{9,1... | collective-permute-start | bytes 294920 | tf_op jit(solution)/shard_map/ppermute | solution.py:475

commit v5 on v4

--- a/solution.py
+++ b/solution.py
@@ -137,7 +137,6 @@
             pltpu.SemaphoreType.DMA((box_count, 2)),
             pltpu.SemaphoreType.DMA((3,)),
         ],
-        compiler_params=pltpu.CompilerParams(vmem_limit_bytes=48 * 2 ** 20),
         cost_estimate=pl.CostEstimate(
             flops=6 * coarse.size * cross, bytes_accessed=4 * (coarse.size + 2 * boxes.size), transcendentals=0
         ),
@@ -145,8 +144,11 @@
 
 
 def later_kernel(per_device, box_count, levels, dest_ref, boxes_ref, *refs):
-    outs, (table, sems) = refs[:box_count], refs[box_count:]
-    place_boxes(per_device, box_count, dest_ref, table)
+    outs, (dest, table, sems, in_sem) = refs[:box_count], refs[box_count:]
+    fetch = pltpu.make_async_copy(dest_ref, dest, in_sem)
+    fetch.start()
+    fetch.wait()
+    place_boxes(per_device, box_count, dest, table)
 
     def copy(shift, k, b, n):
         return pltpu.make_async_copy(boxes_ref.at[n + 1, b], outs[shift].at[n, k], sems.at[n, shift, k])
@@ -178,13 +180,14 @@
     return pl.pallas_call(
         functools.partial(later_kernel, per_device, box_count, levels),
         out_shape=[jax.ShapeDtypeStruct((levels, 2) + boxes.shape[2:], jnp.float32)] * box_count,
-        in_specs=[pl.BlockSpec(memory_space=pltpu.SMEM), pl.BlockSpec(memory_space=pltpu.HBM)],
+        in_specs=[pl.BlockSpec(memory_space=pltpu.HBM)] * 2,
         out_specs=[pl.BlockSpec(memory_space=pltpu.VMEM)] * box_count,
         scratch_shapes=[
+            pltpu.SMEM(move_dest.shape, jnp.int32),
             pltpu.SMEM((2 * box_count,), jnp.int32),
             pltpu.SemaphoreType.DMA((levels, box_count, 2)),
+            pltpu.SemaphoreType.DMA,
         ],
-        compiler_params=pltpu.CompilerParams(vmem_limit_bytes=48 * 2 ** 20),
         cost_estimate=pl.CostEstimate(flops=0, bytes_accessed=12 * boxes.size, transcendentals=0),
     )(move_dest, boxes)
 
@@ -453,12 +456,11 @@
         return lax.ppermute(piece, "box", [(s, (s + shift) % box_count) for s in range(box_count)])
 
     first = pack_first(boxes, coarse, move_dest, parent, edge, box_count)
+    arrived = [first[0]] + [send(first[shift], shift) for shift in range(1, box_count)]
     later = pack_later(boxes, move_dest, box_count)
-    arrived, later_arrived = [first[0]], []
-    for shift in range(1, box_count):
-        arrived.append(send(first[shift], shift))
-    for shift in range(1, box_count):
-        held, arrived[shift] = lax.optimization_barrier((later[shift], arrived[shift]))
+    later_arrived = [send(later[1], 1)]
+    for shift in range(2, box_count):
+        held, arrived[shift - 1] = lax.optimization_barrier((later[shift], arrived[shift - 1]))
         later_arrived.append(send(held, shift))
     now, moved, *facing = arrive(arrived, later[0], slabs)
 

time: 71.4 us -> 70.9 us (level)
  waiting for transfers between devices: 36.6 us -> 27.6 us
  starting transfers between devices: 16.6 us -> 24.7 us
  Pallas kernels: 13 us -> 15.1 us
  local copies, waits for them, and re-layouts: 3.68 us -> 2.05 us
    ppermute x6, waiting for transfers between devices: 28.2 us -> 19.2 us  [send(): lax.ppermute(piece, 'box', [(s, (s + shift) % box_count) for s in range(b...]
    ppermute x6, starting transfers between devices: 14.1 us -> 22.1 us  [send(): lax.ppermute(piece, 'box', [(s, (s + shift) % box_count) for s in range(b...]
    unnamed x24 -> x20, local copies, waits for them, and re-layouts: 3.61 us -> 1.98 us
    pallas_call x1, Pallas kernels: 1.96 us -> 3.31 us  [pack_later(): pl.pallas_call(functools.partial(later_kernel, per_device, box_count, lev...]
  transfers between devices with their start and end apart: 9 -> 9, of which waited for: 5 -> 5; matrix products, arithmetic and copies ran while one was open for 1% -> 1% of each run, Pallas kernels for 12% -> 16%
where the time goes in v5:
time: 70.9 us; the launch traced here: 70.6 us
  waiting for transfers between devices  27.6 us (39%)
  starting transfers between devices  24.7 us (35%)
  Pallas kernels  15.1 us (21%)
  local copies, waits for them, and re-layouts  2.05 us (3%)
  between operations  0.8 us (1%)
    ppermute x6, starting transfers between devices, send(): lax.ppermute(piece, 'box', [(s, (s + shift) % box_count) for s in range(b...  22.1 us
    ppermute x6, waiting for transfers between devices, send(): lax.ppermute(piece, 'box', [(s, (s + shift) % box_count) for s in range(b...  19.2 us
    pallas_call x1, Pallas kernels, body(): pl.pallas_call(functools.partial(slope_kernel, edge, planes, fields, coar...  6.68 us
    ppermute x1, waiting for transfers between devices, body(): lax.ppermute(facing[0], ('slab', 'fld'), crossed)  4.34 us
    ppermute x1, waiting for transfers between devices, body(): lax.ppermute(facing[0], 'slab', swap)  4.03 us
    pallas_call x1, Pallas kernels, pack_later(): pl.pallas_call(functools.partial(later_kernel, per_device, box_count, lev...  3.31 us
    pallas_call x1, Pallas kernels, pack_first(): pl.pallas_call(functools.partial(first_kernel, per_device, box_count, edg...  2.98 us
    unnamed x20, local copies, waits for them, and re-layouts  1.98 us
  transfers between devices with their start and end apart: 9, of which 5 were waited for; matrix products, arithmetic and copies ran while one was open for 1% of the time, Pallas kernels for 16%

profile of v5, /device:TPU:0, one launch (start us, length us, event | category | flops | bytes accessed | tf_op | source)
XLA Modules:
  0.0 70.6 jit_solution(11024590507992513300)
XLA Ops:
  0.6 0.0 copy-start.6
  0.6 0.0 copy-start.5
  0.7 0.0 copy-start.9
  0.7 0.0 copy-start.8
  0.7 0.0 copy-start.7
  0.7 0.0 copy-start.2
  0.7 0.0 copy-start.3
  0.7 0.0 copy-start.4
  0.7 3.0 %shard_map.114 = (f32[2,14,8,256]{3,2,1,0:T(8,128)}, f32[2,14,8,256]{3,2,1,0:T(8,128)}, f32[2,14,8,256]{3,2,1,0:T(8,128)}, f32[2,14,8,256]{3,2,1,0:T(8,128)}) custom-call(s32[16]{0:T(128)} %dest_ref.5, s32[16]{0:T(128)} %parent_ref.3, f32[3,4,12,8,256]{4,3,2,1,0:T(8,128)} %boxes_ref.3, f32[12,8,1000]{2,1,0:T(8,128)} %bitcast.11), custom_call_target="tpu_custom_call" | custom-call | flops 147456000 | bytes 2743296 | tf_op jit(solution)/shard_map/pallas_call | solution.py:125
  3.7 3.1 %collective-permute-start.1 = (f32[2,14,8,256]{3,2,1,0:T(8,128)}, f32[2,14,8,256]{3,2,1,0:T(8,128)S(1)}, u32[]{:S(2)}, u32[]{:S(2)}) collective-permute-start(f32[2,14,8,256]{3,2,1,0:T(8,128)} %get-tuple-element.21), channel_id=1, source_target_pairs={{0,4},{4,8},{8,12},{12,0},{1,5},{5,9},{9,13},{13,1},{2,6},{6,10},{... | collective-permute-start | bytes 688136 | tf_op jit(solution)/shard_map/ppermute | solution.py:456
  6.8 2.6 %collective-permute-start.3 = (f32[2,14,8,256]{3,2,1,0:T(8,128)}, f32[2,14,8,256]{3,2,1,0:T(8,128)S(1)}, u32[]{:S(2)}, u32[]{:S(2)}) collective-permute-start(f32[2,14,8,256]{3,2,1,0:T(8,128)} %get-tuple-element.24), channel_id=1, source_target_pairs={{0,8},{4,12},{8,0},{12,4},{1,9},{5,13},{9,1},{13,5},{2,10},{6,14},... | collective-permute-start | bytes 688136 | tf_op jit(solution)/shard_map/ppermute | solution.py:456
  9.3 1.4 %collective-permute-start.5 = (f32[2,14,8,256]{3,2,1,0:T(8,128)}, f32[2,14,8,256]{3,2,1,0:T(8,128)S(1)}, u32[]{:S(2)}, u32[]{:S(2)}) collective-permute-start(f32[2,14,8,256]{3,2,1,0:T(8,128)} %get-tuple-element.29), channel_id=1, source_target_pairs={{0,12},{4,0},{8,4},{12,8},{1,13},{5,1},{9,5},{13,9},{2,14},{6,2},{... | collective-permute-start | bytes 688136 | tf_op jit(solution)/shard_map/ppermute | solution.py:456
  10.7 3.3 %shard_map.113 = (f32[2,2,12,8,256]{4,3,2,1,0:T(8,128)}, f32[2,2,12,8,256]{4,3,2,1,0:T(8,128)}, f32[2,2,12,8,256]{4,3,2,1,0:T(8,128)}, f32[2,2,12,8,256]{4,3,2,1,0:T(8,128)}) custom-call(s32[16]{0:T(128)} %dest_ref.5, f32[3,4,12,8,256]{4,3,2,1,0:T(8,128)} %boxes_ref.3), custom_call_target="tpu_custom_call" | custom-call | bytes 3538944 | tf_op jit(solution)/shard_map/pallas_call | solution.py:180
  14.0 0.7 collective-permute-start
  14.7 0.9 %collective-permute-done.1.refs_1_ = f32[2,14,8,256]{3,2,1,0:T(8,128)S(1)} collective-permute-done((f32[2,14,8,256]{3,2,1,0:T(8,128)}, f32[2,14,8,256]{3,2,1,0:T(8,128)S(1)}, u32[]{:S(2)}, u32[]{:S(2)}) %collective-permute-start.1) | collective-permute-done | bytes 229408 | tf_op jit(solution)/shard_map/ppermute | solution.py:456
  15.6 9.8 %collective-permute-done.3.refs_2_ = f32[2,14,8,256]{3,2,1,0:T(8,128)S(1)} collective-permute-done((f32[2,14,8,256]{3,2,1,0:T(8,128)}, f32[2,14,8,256]{3,2,1,0:T(8,128)S(1)}, u32[]{:S(2)}, u32[]{:S(2)}) %collective-permute-start.3) | collective-permute-done | bytes 229408 | tf_op jit(solution)/shard_map/ppermute | solution.py:456
  25.4 0.0 collective-permute-done.5.refs_3_
  25.4 0.0 copy-start
  25.4 1.0 %copy-done = f32[2,2,12,8,256]{4,3,2,1,0:T(8,128)S(1)} copy-done((f32[2,2,12,8,256]{4,3,2,1,0:T(8,128)S(1)}, f32[2,2,12,8,256]{4,3,2,1,0:T(8,128)}, u32[]{:S(2)}) %copy-start) | copy-done | bytes 393240
  26.4 0.0 copy-start.1
  26.4 0.9 %copy-done.1 = f32[2,14,8,256]{3,2,1,0:T(8,128)S(1)} copy-done((f32[2,14,8,256]{3,2,1,0:T(8,128)S(1)}, f32[2,14,8,256]{3,2,1,0:T(8,128)}, u32[]{:S(2)}) %copy-start.1) | copy-done | bytes 229400
  27.3 1.1 %shard_map.115 = (f32[8,14,8,256]{3,2,1,0:T(8,128)S(1)}, f32[3,8,12,8,256]{4,3,2,1,0:T(8,128)}, f32[8,12,256]{2,1,0:T(8,128)S(1)}) custom-call(f32[2,14,8,256]{3,2,1,0:T(8,128)S(1)} %copy-done.1, f32[2,14,8,256]{3,2,1,0:T(8,128)S(1)} %collective-permute-done.1.refs_1_, f32[2,14,8,256]{3,2,1,0:T(8,128)S(1)} %collective-permute-done.3.refs_2_, ...), custom_call_target="tpu_custom_call" | custom-call | bytes 2752512 | tf_op jit(solution)/shard_map/pallas_call | solution.py:264
  28.4 0.1 collective-permute-start.6
  28.5 0.0 copy-done.9
  28.5 0.0 copy-done.8
  28.5 0.0 copy-done.7
  28.6 0.1 fusion.7
  28.6 6.8 %collective-permute-start.4 = (f32[2,2,12,8,256]{4,3,2,1,0:T(8,128)}, f32[2,2,12,8,256]{4,3,2,1,0:T(8,128)S(1)}, u32[]{:S(2)}, u32[]{:S(2)}) collective-permute-start(f32[2,2,12,8,256]{4,3,2,1,0:T(8,128)} %get-tuple-element.25), channel_id=1, source_target_pairs={{0,12},{4,0},{8,4},{12,8},{1,13},{5,1},{9,5},{13,9},{2,14},{6,2},{... | collective-permute-start | bytes 1179656 | tf_op jit(solution)/shard_map/ppermute | solution.py:456
  35.4 7.7 %collective-permute-start.2 = (f32[2,2,12,8,256]{4,3,2,1,0:T(8,128)}, f32[2,2,12,8,256]{4,3,2,1,0:T(8,128)S(1)}, u32[]{:S(2)}, u32[]{:S(2)}) collective-permute-start(f32[2,2,12,8,256]{4,3,2,1,0:T(8,128)} %get-tuple-element.22), channel_id=1, source_target_pairs={{0,8},{4,12},{8,0},{12,4},{1,9},{5,13},{9,1},{13,5},{2,10},{6,14},... | collective-permute-start | bytes 1179656 | tf_op jit(solution)/shard_map/ppermute | solution.py:456
  43.1 1.0 %collective-permute-start.8 = (f32[8,12,256]{2,1,0:T(8,128)S(1)}, f32[8,12,256]{2,1,0:T(8,128)S(1)}, u32[]{:S(2)}, u32[]{:S(2)}) collective-permute-start(f32[8,12,256]{2,1,0:T(8,128)S(1)} %get-tuple-element.33), channel_id=1, source_target_pairs={{0,3},{3,0},{1,2},{2,1},{4,7},{7,4},{5,6},{6,5},{8,11},{11,8},{9,1... | collective-permute-start | bytes 294920 | tf_op jit(solution)/shard_map/ppermute | solution.py:477
  44.1 0.0 copy-done.6
  44.1 0.3 fusion.2
  44.4 4.3 %collective-permute-done.8.other_low.other_high = f32[8,12,256]{2,1,0:T(8,128)S(1)} collective-permute-done((f32[8,12,256]{2,1,0:T(8,128)S(1)}, f32[8,12,256]{2,1,0:T(8,128)S(1)}, u32[]{:S(2)}, u32[]{:S(2)}) %collective-permute-start.8) | collective-permute-done | bytes 98336 | tf_op jit(solution)/shard_map/ppermute | solution.py:477
  48.8 1.5 %collective-permute-start.7 = (f32[8,12,256]{2,1,0:T(8,128)S(1)}, f32[8,12,256]{2,1,0:T(8,128)S(1)}, u32[]{:S(2)}, u32[]{:S(2)}) collective-permute-start(f32[8,12,256]{2,1,0:T(8,128)S(1)} %get-tuple-element.33), channel_id=1, source_target_pairs={{0,2},{2,0},{1,3},{3,1},{4,6},{6,4},{5,7},{7,5},{8,10},{10,8},{9,1... | collective-permute-start | bytes 294920 | tf_op jit(solution)/shard_map/ppermute | solution.py:477
  50.3 0.0 copy-done.5
  50.3 0.1 multiply_reduce_fusion
  50.4 4.0 %collective-permute-done.7.own_low.own_high = f32[8,12,256]{2,1,0:T(8,128)S(1)} collective-permute-done((f32[8,12,256]{2,1,0:T(8,128)S(1)}, f32[8,12,256]{2,1,0:T(8,128)S(1)}, u32[]{:S(2)}, u32[]{:S(2)}) %collective-permute-start.7) | collective-permute-done | bytes 98336 | tf_op jit(solution)/shard_map/ppermute | solution.py:477
  54.4 0.0 collective-permute-done.6.other_ref
  54.4 0.0 copy-done.2
  54.4 0.0 copy-done.3
  54.4 0.0 copy-done.4
  54.4 6.7 %shard_map.116 = (f32[8,12,8,256]{3,2,1,0:T(8,128)}, f32[8,128]{1,0:T(8,128)S(1)}) custom-call(s32[16]{0:T(128)S(1)} %copy-done.2, s32[16]{0:T(128)S(1)} %copy-done.3, f32[8,14,8,256]{3,2,1,0:T(8,128)S(1)} %get-tuple-element.32.own_ref, f32[8,14,8,256]{3,2,1,0:T(8,128)S(1)} %collective-permute-done.6.other_ref, ...), custom_call_target="tpu_custom_call" | custom-call | flops 2113929216 | bytes 2752512 | tf_op jit(solution)/shard_map/pallas_call | solution.py:484
  61.1 0.0 collective-permute-done.refs_0_
  61.1 0.0 collective-permute-done.4.refs_2_
  61.1 8.5 %collective-permute-done.2.refs_1_ = f32[2,2,12,8,256]{4,3,2,1,0:T(8,128)S(1)} collective-permute-done((f32[2,2,12,8,256]{4,3,2,1,0:T(8,128)}, f32[2,2,12,8,256]{4,3,2,1,0:T(8,128)S(1)}, u32[]{:S(2)}, u32[]{:S(2)}) %collective-permute-start.2) | collective-permute-done | bytes 393248 | tf_op jit(solution)/shard_map/ppermute | solution.py:456
  69.6 1.0 %shard_map.117 = f32[3,8,12,8,256]{4,3,2,1,0:T(8,128)} custom-call(f32[2,2,12,8,256]{4,3,2,1,0:T(8,128)S(1)} %collective-permute-done.refs_0_, f32[2,2,12,8,256]{4,3,2,1,0:T(8,128)S(1)} %collective-permute-done.2.refs_1_, f32[2,2,12,8,256]{4,3,2,1,0:T(8,128)S(1)} %collective-permute-done.4.refs_2_, ...), custom_call_target="tpu_custom_call", output_to_operand_aliasing={{}: (3, {})} | custom-call | bytes 2359296 | tf_op jit(solution)/shard_map/pallas_call | solution.py:216
  (2 shorter events, 0.0 us)
Async XLA Ops:
  0.6 43.4 %copy-start.6 = (f32[24,896,1]{1,0,2:T(8,128)S(1)}, f32[24,896,1]{1,0,2:T(8,128)}, u32[]{:S(2)}) copy-start(f32[24,896,1]{1,0,2:T(8,128)} %constant.27) | copy-start | bytes 258052
  0.6 49.6 %copy-start.5 = (f32[3,8,896]{2,1,0:T(8,128)S(1)}, f32[3,8,896]{2,1,0:T(8,128)}, u32[]{:S(2)}) copy-start(f32[3,8,896]{2,1,0:T(8,128)} %constant.23.clone) | copy-start | bytes 258052
  0.7 27.8 %copy-start.9 = (f32[24,24]{1,0:T(8,128)S(1)}, f32[24,24]{1,0:T(8,128)}, u32[]{:S(2)}) copy-start(f32[24,24]{1,0:T(8,128)} %param.16) | copy-start | bytes 6916
  0.7 27.8 %copy-start.8 = (f32[24,24]{1,0:T(8,128)S(1)}, f32[24,24]{1,0:T(8,128)}, u32[]{:S(2)}) copy-start(f32[24,24]{1,0:T(8,128)} %param.15) | copy-start | bytes 6916
  0.7 27.8 %copy-start.7 = (f32[24,24]{1,0:T(8,128)S(1)}, f32[24,24]{1,0:T(8,128)}, u32[]{:S(2)}) copy-start(f32[24,24]{1,0:T(8,128)} %param.14) | copy-start | bytes 6916
  0.7 53.7 %copy-start.2 = (s32[16]{0:T(128)S(1)}, s32[16]{0:T(128)}, u32[]{:S(2)}) copy-start(s32[16]{0:T(128)} %dest_ref.5) | copy-start | bytes 196
  0.7 53.7 %copy-start.3 = (s32[16]{0:T(128)S(1)}, s32[16]{0:T(128)}, u32[]{:S(2)}) copy-start(s32[16]{0:T(128)} %parent_ref.3) | copy-start | bytes 196
  0.7 53.7 %copy-start.4 = (bf16[256,2304]{1,0:T(8,128)(2,1)S(1)}, bf16[256,2304]{1,0:T(8,128)(2,1)}, u32[]{:S(2)}) copy-start(bf16[256,2304]{1,0:T(8,128)(2,1)} %constant.26.spread_ref) | copy-start | bytes 3538948
  3.7 11.9 %collective-permute-start.1 = (f32[2,14,8,256]{3,2,1,0:T(8,128)}, f32[2,14,8,256]{3,2,1,0:T(8,128)S(1)}, u32[]{:S(2)}, u32[]{:S(2)}) collective-permute-start(f32[2,14,8,256]{3,2,1,0:T(8,128)} %get-tuple-element.21), channel_id=1, source_target_pairs={{0,4},{4,8},{8,12},{12,0},{1,5},{5,9},{9,13},{13,1},{2,6},{6,10},{... | collective-permute-start | bytes 688136 | tf_op jit(solution)/shard_map/ppermute | solution.py:456
  6.8 18.6 %collective-permute-start.3 = (f32[2,14,8,256]{3,2,1,0:T(8,128)}, f32[2,14,8,256]{3,2,1,0:T(8,128)S(1)}, u32[]{:S(2)}, u32[]{:S(2)}) collective-permute-start(f32[2,14,8,256]{3,2,1,0:T(8,128)} %get-tuple-element.24), channel_id=1, source_target_pairs={{0,8},{4,12},{8,0},{12,4},{1,9},{5,13},{9,1},{13,5},{2,10},{6,14},... | collective-permute-start | bytes 688136 | tf_op jit(solution)/shard_map/ppermute | solution.py:456
  9.3 16.1 %collective-permute-start.5 = (f32[2,14,8,256]{3,2,1,0:T(8,128)}, f32[2,14,8,256]{3,2,1,0:T(8,128)S(1)}, u32[]{:S(2)}, u32[]{:S(2)}) collective-permute-start(f32[2,14,8,256]{3,2,1,0:T(8,128)} %get-tuple-element.29), channel_id=1, source_target_pairs={{0,12},{4,0},{8,4},{12,8},{1,13},{5,1},{9,5},{13,9},{2,14},{6,2},{... | collective-permute-start | bytes 688136 | tf_op jit(solution)/shard_map/ppermute | solution.py:456
  14.0 47.1 %collective-permute-start = (f32[2,2,12,8,256]{4,3,2,1,0:T(8,128)}, f32[2,2,12,8,256]{4,3,2,1,0:T(8,128)S(1)}, u32[]{:S(2)}, u32[]{:S(2)}) collective-permute-start(f32[2,2,12,8,256]{4,3,2,1,0:T(8,128)} %get-tuple-element.19), channel_id=1, source_target_pairs={{0,4},{4,8},{8,12},{12,0},{1,5},{5,9},{9,13},{13,1},{2,6},{6,10},{... | collective-permute-start | bytes 1179656 | tf_op jit(solution)/shard_map/ppermute | solution.py:456
  25.4 1.0 %copy-start = (f32[2,2,12,8,256]{4,3,2,1,0:T(8,128)S(1)}, f32[2,2,12,8,256]{4,3,2,1,0:T(8,128)}, u32[]{:S(2)}) copy-start(f32[2,2,12,8,256]{4,3,2,1,0:T(8,128)} %get-tuple-element.30.refs_4_) | copy-start | bytes 1179652
  26.4 0.9 %copy-start.1 = (f32[2,14,8,256]{3,2,1,0:T(8,128)S(1)}, f32[2,14,8,256]{3,2,1,0:T(8,128)}, u32[]{:S(2)}) copy-start(f32[2,14,8,256]{3,2,1,0:T(8,128)} %get-tuple-element.26.refs_0_) | copy-start | bytes 688132
  28.4 26.0 %collective-permute-start.6 = (f32[8,14,8,256]{3,2,1,0:T(8,128)S(1)}, f32[8,14,8,256]{3,2,1,0:T(8,128)S(1)}, u32[]{:S(2)}, u32[]{:S(2)}) collective-permute-start(f32[8,14,8,256]{3,2,1,0:T(8,128)S(1)} %get-tuple-element.32.own_ref), channel_id=1, source_target_pairs={{0,1},{1,0},{2,3},{3,2},{4,5},{5,4},{6,7},{7,6},{8,9},{9,8},{10,11... | collective-permute-start | bytes 2752520 | tf_op jit(solution)/shard_map/ppermute | solution.py:468
  28.6 32.5 %collective-permute-start.4 = (f32[2,2,12,8,256]{4,3,2,1,0:T(8,128)}, f32[2,2,12,8,256]{4,3,2,1,0:T(8,128)S(1)}, u32[]{:S(2)}, u32[]{:S(2)}) collective-permute-start(f32[2,2,12,8,256]{4,3,2,1,0:T(8,128)} %get-tuple-element.25), channel_id=1, source_target_pairs={{0,12},{4,0},{8,4},{12,8},{1,13},{5,1},{9,5},{13,9},{2,14},{6,2},{... | collective-permute-start | bytes 1179656 | tf_op jit(solution)/shard_map/ppermute | solution.py:456
  35.4 34.2 %collective-permute-start.2 = (f32[2,2,12,8,256]{4,3,2,1,0:T(8,128)}, f32[2,2,12,8,256]{4,3,2,1,0:T(8,128)S(1)}, u32[]{:S(2)}, u32[]{:S(2)}) collective-permute-start(f32[2,2,12,8,256]{4,3,2,1,0:T(8,128)} %get-tuple-element.22), channel_id=1, source_target_pairs={{0,8},{4,12},{8,0},{12,4},{1,9},{5,13},{9,1},{13,5},{2,10},{6,14},... | collective-permute-start | bytes 1179656 | tf_op jit(solution)/shard_map/ppermute | solution.py:456
  43.1 5.7 %collective-permute-start.8 = (f32[8,12,256]{2,1,0:T(8,128)S(1)}, f32[8,12,256]{2,1,0:T(8,128)S(1)}, u32[]{:S(2)}, u32[]{:S(2)}) collective-permute-start(f32[8,12,256]{2,1,0:T(8,128)S(1)} %get-tuple-element.33), channel_id=1, source_target_pairs={{0,3},{3,0},{1,2},{2,1},{4,7},{7,4},{5,6},{6,5},{8,11},{11,8},{9,1... | collective-permute-start | bytes 294920 | tf_op jit(solution)/shard_map/ppermute | solution.py:477
  48.8 5.6 %collective-permute-start.7 = (f32[8,12,256]{2,1,0:T(8,128)S(1)}, f32[8,12,256]{2,1,0:T(8,128)S(1)}, u32[]{:S(2)}, u32[]{:S(2)}) collective-permute-start(f32[8,12,256]{2,1,0:T(8,128)S(1)} %get-tuple-element.33), channel_id=1, source_target_pairs={{0,2},{2,0},{1,3},{3,1},{4,6},{6,4},{5,7},{7,5},{8,10},{10,8},{9,1... | collective-permute-start | bytes 294920 | tf_op jit(solution)/shard_map/ppermute | solution.py:477

commit v6 on v5

--- a/solution.py
+++ b/solution.py
@@ -37,11 +37,15 @@
     lax.fori_loop(0, per_device, place, 0)
 
 
+def partner(own, turn, box_count):
+    return own ^ turn
+
+
 def each_slot(box_count):
     own = lax.axis_index("box")
-    for shift in range(box_count):
+    for turn in range(box_count):
         for k in range(2):
-            yield shift, k, 2 * lax.rem(own + shift, box_count) + k
+            yield turn, k, 2 * partner(own, turn, box_count) + k
 
 
 def first_kernel(per_device, box_count, edge, dest_ref, parent_ref, boxes_ref, coarse_ref, *refs):
@@ -143,135 +147,157 @@
     )(move_dest, parent, boxes, coarse)
 
 
-def later_kernel(per_device, box_count, levels, dest_ref, boxes_ref, *refs):
-    outs, (dest, table, sems, in_sem) = refs[:box_count], refs[box_count:]
+def later_kernel(per_device, box_count, levels, dest_ref, boxes_ref, after_ref, *refs):
+    outs, moved_ref = refs[: box_count - 1], refs[box_count - 1]
+    stay, dest, table, sems, in_sem, out_sem = refs[box_count:]
+    own = lax.axis_index("box")
     fetch = pltpu.make_async_copy(dest_ref, dest, in_sem)
     fetch.start()
     fetch.wait()
     place_boxes(per_device, box_count, dest, table)
 
-    def copy(shift, k, b, n):
-        return pltpu.make_async_copy(boxes_ref.at[n + 1, b], outs[shift].at[n, k], sems.at[n, shift, k])
-
-    for shift, k, slot in each_slot(box_count):
+    def copies(turn, k, b):
+        for n in range(0 if turn == 0 else 1, levels):
+            to = stay.at[n, k] if turn == 0 else outs[turn - 1].at[n - 1, k]
+            yield pltpu.make_async_copy(boxes_ref.at[n, b], to, sems.at[n, turn, k])
+
+    for turn, k, slot in each_slot(box_count):
         b = table[slot]
 
         @pl.when(b >= 0)
         def _():
-            for n in range(levels):
-                copy(shift, k, b, n).start()
+            for copy in copies(turn, k, b):
+                copy.start()
 
         @pl.when(b < 0)
         def _():
-            for n in range(levels):
-                outs[shift][n, k] = jnp.zeros(outs[shift].shape[2:], jnp.float32)
-
-    for shift, k, slot in each_slot(box_count):
+            to = stay if turn == 0 else outs[turn - 1]
+            for n in range(to.shape[0]):
+                to[n, k] = jnp.zeros(to.shape[2:], jnp.float32)
+
+    for turn, k, slot in each_slot(box_count):
         b = table[slot]
 
         @pl.when(b >= 0)
         def _():
-            for n in range(levels):
-                copy(shift, k, b, n).wait()
-
-
-def pack_later(boxes, move_dest, box_count):
-    levels, per_device = boxes.shape[0] - 1, boxes.shape[1]
+            for copy in copies(turn, k, b):
+                copy.wait()
+
+        if (turn, k) == (0, 1):
+            settled = pltpu.make_async_copy(stay, moved_ref.at[:, pl.ds(2 * own, 2)], out_sem)
+            settled.start()
+    settled.wait()
+
+
+def pack_later(boxes, move_dest, after, box_count):
+    levels, per_device = boxes.shape[:2]
+    item = boxes.shape[2:]
+    hbm, vmem = pl.BlockSpec(memory_space=pltpu.HBM), pl.BlockSpec(memory_space=pltpu.VMEM)
     return pl.pallas_call(
         functools.partial(later_kernel, per_device, box_count, levels),
-        out_shape=[jax.ShapeDtypeStruct((levels, 2) + boxes.shape[2:], jnp.float32)] * box_count,
-        in_specs=[pl.BlockSpec(memory_space=pltpu.HBM)] * 2,
-        out_specs=[pl.BlockSpec(memory_space=pltpu.VMEM)] * box_count,
+        out_shape=[jax.ShapeDtypeStruct((levels - 1, 2) + item, jnp.float32)] * (box_count - 1)
+        + [jax.ShapeDtypeStruct((levels, 2 * box_count) + item, jnp.float32)],
+        in_specs=[hbm] * 3,
+        out_specs=[vmem] * (box_count - 1) + [hbm],
         scratch_shapes=[
+            pltpu.VMEM((levels, 2) + item, jnp.float32),
             pltpu.SMEM(move_dest.shape, jnp.int32),
             pltpu.SMEM((2 * box_count,), jnp.int32),
             pltpu.SemaphoreType.DMA((levels, box_count, 2)),
             pltpu.SemaphoreType.DMA,
+            pltpu.SemaphoreType.DMA,
         ],
         cost_estimate=pl.CostEstimate(flops=0, bytes_accessed=12 * boxes.size, transcendentals=0),
-    )(move_dest, boxes)
-
-
-def source_of(shift, box_count):
-    return lax.rem(lax.axis_index("box") - shift + box_count, box_count)
-
-
-def settle_kernel(levels, box_count, *refs):
-    pieces, out_ref, sems = refs[: box_count - 1], refs[-2], refs[-1]
-
-    def copy(shift):
-        to = out_ref.at[pl.ds(1, levels), pl.ds(2 * source_of(shift, box_count), 2)]
-        return pltpu.make_async_copy(pieces[shift - 1], to, sems.at[shift])
-
-    for shift in range(1, box_count):
-        copy(shift).start()
-    for shift in range(1, box_count):
-        copy(shift).wait()
-
-
-def settle(pieces, moved, after):
-    box_count = len(pieces) + 1
-    levels = moved.shape[0] - 1
-    vmem, anywhere = pl.BlockSpec(memory_space=pltpu.VMEM), pl.BlockSpec(memory_space=pl.ANY)
+    )(move_dest, boxes, after)
+
+
+def settle_later(piece, turn, moved_ref, sem):
+    source = partner(lax.axis_index("box"), turn, moved_ref.shape[1] // 2)
+    to = moved_ref.at[pl.ds(1, moved_ref.shape[0] - 1), pl.ds(2 * source, 2)]
+    return pltpu.make_async_copy(piece, to, sem)
+
+
+def settle_kernel(turns, *refs):
+    out_ref, sems = refs[-2:]
+    copies = [settle_later(refs[n], turn, out_ref, sems.at[n]) for n, turn in enumerate(turns)]
+    for copy in copies:
+        copy.start()
+    for copy in copies:
+        copy.wait()
+
+
+def settle(turns, pieces, moved, after):
+    count = len(pieces)
+    vmem, hbm = pl.BlockSpec(memory_space=pltpu.VMEM), pl.BlockSpec(memory_space=pltpu.HBM)
     return pl.pallas_call(
-        functools.partial(settle_kernel, levels, box_count),
+        functools.partial(settle_kernel, turns),
         out_shape=jax.ShapeDtypeStruct(moved.shape, jnp.float32),
-        in_specs=[vmem] * (box_count - 1) + [anywhere, vmem],
-        out_specs=anywhere,
-        scratch_shapes=[pltpu.SemaphoreType.DMA((box_count,))],
-        input_output_aliases={box_count - 1: 0},
+        in_specs=[vmem] * count + [hbm, vmem],
+        out_specs=hbm,
+        scratch_shapes=[pltpu.SemaphoreType.DMA((count,))],
+        input_output_aliases={count: 0},
         compiler_params=pltpu.CompilerParams(vmem_limit_bytes=48 * 2 ** 20),
         cost_estimate=pl.CostEstimate(
-            flops=0, bytes_accessed=8 * (box_count - 1) * pieces[0].size, transcendentals=0
+            flops=0, bytes_accessed=8 * count * pieces[0].size, transcendentals=0
         ),
     )(*pieces, moved, after)
 
 
-def arrive_kernel(box_count, slabs, levels, fields, *refs):
-    pieces, own_later, (now_ref, moved_ref) = refs[:box_count], refs[box_count], refs[box_count + 1 : box_count + 3]
-    edges, sems = refs[box_count + 3 : -1], refs[-1]
-    slab = lax.axis_index("slab")
+def arrive_kernel(box_count, slabs, early, fields, *refs):
+    pieces, later = refs[:box_count], refs[box_count : box_count + len(early)]
+    now_ref, moved_ref, *edges, sems = refs[box_count + len(early) + 1 :]
+    own, slab = lax.axis_index("box"), lax.axis_index("slab")
     planes = now_ref.shape[2]
+    mine = pltpu.make_async_copy(pieces[0], now_ref.at[pl.ds(2 * own, 2)], sems.at[0])
+    mine.start()
     copies = []
-    for shift in range(box_count):
-        to = moved_ref.at[0, pl.ds(2 * source_of(shift, box_count), 2)]
-        copies.append(pltpu.make_async_copy(pieces[shift].at[:, pl.ds(0, fields)], to, sems.at[shift]))
-    to = moved_ref.at[pl.ds(1, levels - 1), pl.ds(2 * source_of(0, box_count), 2)]
-    copies.append(pltpu.make_async_copy(own_later, to, sems.at[box_count]))
+    for turn in range(1, box_count):
+        to = moved_ref.at[0, pl.ds(2 * partner(own, turn, box_count), 2)]
+        copies.append(pltpu.make_async_copy(pieces[turn].at[:, pl.ds(0, fields)], to, sems.at[turn]))
+    for n, turn in enumerate(early):
+        copies.append(settle_later(later[n], turn, moved_ref, sems.at[box_count + n]))
     for copy in copies:
         copy.start()
     faced = [jnp.where(slab == 0, planes - 1, 0)] if slabs == 2 else [0, planes - 1]
-    for shift in range(box_count):
-        source = source_of(shift, box_count)
+
+    def cut(source):
         for k in range(2):
-            now_ref[2 * source + k] = pieces[shift][k]
             for edge_ref, plane in zip(edges, faced):
                 for f in range(fields):
-                    edge_ref[2 * source + k, f : f + 1] = pieces[shift][k, f, pl.ds(plane, 1)]
+                    edge_ref[2 * source + k, f : f + 1] = now_ref[2 * source + k, f, pl.ds(plane, 1)]
+
+    for turn in range(1, box_count):
+        source = partner(own, turn, box_count)
+        for k in range(2):
+            now_ref[2 * source + k] = pieces[turn][k]
+        cut(source)
+    mine.wait()
+    cut(own)
     for copy in copies:
         copy.wait()
 
 
-def arrive(pieces, own_later, slabs):
+def arrive(pieces, early, later, moved, slabs):
     box_count = len(pieces)
     _, blocks, planes, cross = pieces[0].shape
-    levels, fields = own_later.shape[0] + 1, own_later.shape[2]
+    fields = moved.shape[2]
     slots = 2 * box_count
     sides = 1 if slabs == 2 else 2
-    vmem, anywhere = pl.BlockSpec(memory_space=pltpu.VMEM), pl.BlockSpec(memory_space=pl.ANY)
-    shapes = [(slots, blocks, planes, cross), (levels, slots, fields, planes, cross)]
-    shapes += [(slots, fields, cross)] * sides
+    vmem, hbm = pl.BlockSpec(memory_space=pltpu.VMEM), pl.BlockSpec(memory_space=pltpu.HBM)
+    shapes = [(slots, blocks, planes, cross), moved.shape] + [(slots, fields, cross)] * sides
+    count = box_count + len(later)
     return pl.pallas_call(
-        functools.partial(arrive_kernel, box_count, slabs, levels, fields),
+        functools.partial(arrive_kernel, box_count, slabs, early, fields),
         out_shape=[jax.ShapeDtypeStruct(shape, jnp.float32) for shape in shapes],
-        in_specs=[vmem] * (box_count + 1),
-        out_specs=[vmem, anywhere] + [vmem] * sides,
-        scratch_shapes=[pltpu.SemaphoreType.DMA((box_count + 1,))],
+        in_specs=[hbm] + [vmem] * (count - 1) + [hbm],
+        out_specs=[vmem, hbm] + [vmem] * sides,
+        scratch_shapes=[pltpu.SemaphoreType.DMA((count,))],
+        input_output_aliases={count: 1},
         compiler_params=pltpu.CompilerParams(vmem_limit_bytes=48 * 2 ** 20),
         cost_estimate=pl.CostEstimate(
             flops=0, bytes_accessed=12 * box_count * pieces[0].size, transcendentals=0
         ),
-    )(*pieces, own_later)
+    )(*pieces, *later, moved)
 
 
 def face_cells(lane, edge, coarse_planes, slab):
@@ -452,17 +478,14 @@
     total = move_dest.shape[0]
     coarse_count = coarse.shape[0]
 
-    def send(piece, shift):
-        return lax.ppermute(piece, "box", [(s, (s + shift) % box_count) for s in range(box_count)])
+    def send(piece, turn):
+        return lax.ppermute(piece, "box", [(s, partner(s, turn, box_count)) for s in range(box_count)])
 
     first = pack_first(boxes, coarse, move_dest, parent, edge, box_count)
-    arrived = [first[0]] + [send(first[shift], shift) for shift in range(1, box_count)]
-    later = pack_later(boxes, move_dest, box_count)
-    later_arrived = [send(later[1], 1)]
-    for shift in range(2, box_count):
-        held, arrived[shift - 1] = lax.optimization_barrier((later[shift], arrived[shift - 1]))
-        later_arrived.append(send(held, shift))
-    now, moved, *facing = arrive(arrived, later[0], slabs)
+    arrived = [first[0]] + [send(first[turn], turn) for turn in range(1, box_count)]
+    *later, moved = pack_later(boxes, move_dest, first[0], box_count)
+    later = [send(piece, n + 1) for n, piece in enumerate(later)]
+    now, moved, *facing = arrive(arrived, (1,), later[:1], moved, slabs)
 
     swap = [(0, 1), (1, 0)]
     now_other = lax.ppermute(now, "fld", swap)
@@ -503,7 +526,7 @@
             flops=12 * slots * weight.size * cross, bytes_accessed=12 * now.size, transcendentals=0
         ),
     )(move_dest, parent, now, now_other, low[0], low[1], high[0], high[1], spread, weight)
-    return settle(later_arrived, moved, token), slope
+    return settle(tuple(range(2, box_count)), later[1:], moved, token), slope
 
 
 def solution(mesh):

time: 70.9 us -> 72.9 us (1.028)
  the two profiles are of different devices: /device:TPU:0 before, /device:TPU:17 now
where the time goes in v6:
time: 72.9 us; the launch traced here: 74.1 us
  starting transfers between devices  29.3 us (40%)
  waiting for transfers between devices  22.8 us (31%)
  Pallas kernels  19.7 us (27%)
  local copies, waits for them, and re-layouts  1.05 us (1%)
  between operations  0.75 us (1%)
    ppermute x1, starting transfers between devices, body(): now_other = lax.ppermute(now, 'fld', swap)  21.2 us
    ppermute x6, waiting for transfers between devices, send(): lax.ppermute(piece, 'box', [(s, partner(s, turn, box_count)) for s in ran...  16.2 us
    pallas_call x1, Pallas kernels, body(): pl.pallas_call(functools.partial(slope_kernel, edge, planes, fields, coar...  10.5 us
    ppermute x6, starting transfers between devices, send(): lax.ppermute(piece, 'box', [(s, partner(s, turn, box_count)) for s in ran...  6.37 us
    pallas_call x1, Pallas kernels, pack_later(): pl.pallas_call(functools.partial(later_kernel, per_device, box_count, lev...  4.04 us
    ppermute x1, waiting for transfers between devices, body(): lax.ppermute(facing[0], 'slab', swap)  3.34 us
    ppermute x1, waiting for transfers between devices, body(): lax.ppermute(facing[0], ('slab', 'fld'), crossed)  3.24 us
    pallas_call x1, Pallas kernels, pack_first(): pl.pallas_call(functools.partial(first_kernel, per_device, box_count, edg...  2.99 us
  transfers between devices with their start and end apart: 9, of which 3 were waited for; matrix products, arithmetic and copies ran while one was open for 1% of the time, Pallas kernels for 16%

profile of v6, /device:TPU:17, one launch (start us, length us, event | category | flops | bytes accessed | tf_op | source)
XLA Modules:
  0.0 74.1 jit_solution(12439358807474474406)
XLA Ops:
  0.6 3.0 %shard_map.113 = (f32[2,14,8,256]{3,2,1,0:T(8,128)}, f32[2,14,8,256]{3,2,1,0:T(8,128)}, f32[2,14,8,256]{3,2,1,0:T(8,128)}, f32[2,14,8,256]{3,2,1,0:T(8,128)}) custom-call(s32[16]{0:T(128)} %dest_ref.5, s32[16]{0:T(128)} %parent_ref.3, f32[3,4,12,8,256]{4,3,2,1,0:T(8,128)} %boxes_ref.3, f32[12,8,1000]{2,1,0:T(8,128)} %bitcast.11), custom_call_target="tpu_custom_call" | custom-call | flops 147456000 | bytes 2743296 | tf_op jit(solution)/shard_map/pallas_call | solution.py:129
  3.6 0.0 copy-start.6
  3.6 0.0 copy-start.7
  3.7 0.0 copy-start.8
  3.7 0.0 copy-start.5
  3.7 0.0 copy-start.4
  3.7 4.0 %shard_map.114 = (f32[2,2,12,8,256]{4,3,2,1,0:T(8,128)}, f32[2,2,12,8,256]{4,3,2,1,0:T(8,128)}, f32[2,2,12,8,256]{4,3,2,1,0:T(8,128)}, f32[3,8,12,8,256]{4,3,2,1,0:T(8,128)}) custom-call(s32[16]{0:T(128)} %dest_ref.5, f32[3,4,12,8,256]{4,3,2,1,0:T(8,128)} %boxes_ref.3, f32[2,14,8,256]{3,2,1,0:T(8,128)} %get-tuple-element.15.after_ref.refs_0_), custom_call_target="tpu_custom_call" | custom-call | bytes 3538944 | tf_op jit(solution)/shard_map/pallas_call | solution.py:196
  7.7 0.9 %collective-permute-start.5 = (f32[2,2,12,8,256]{4,3,2,1,0:T(8,128)}, f32[2,2,12,8,256]{4,3,2,1,0:T(8,128)S(1)}, u32[]{:S(2)}, u32[]{:S(2)}) collective-permute-start(f32[2,2,12,8,256]{4,3,2,1,0:T(8,128)} %get-tuple-element.21), channel_id=1, source_target_pairs={{0,4},{4,0},{8,12},{12,8},{1,5},{5,1},{9,13},{13,9},{2,6},{6,2},{1... | collective-permute-start | bytes 1179656 | tf_op jit(solution)/shard_map/ppermute | solution.py:482
  8.7 0.6 collective-permute-start.2
  9.3 0.0 collective-permute-start.3
  9.3 2.0 %collective-permute-start.4 = (f32[2,14,8,256]{3,2,1,0:T(8,128)}, f32[2,14,8,256]{3,2,1,0:T(8,128)S(1)}, u32[]{:S(2)}, u32[]{:S(2)}) collective-permute-start(f32[2,14,8,256]{3,2,1,0:T(8,128)} %get-tuple-element.20), channel_id=1, source_target_pairs={{0,12},{4,8},{8,4},{12,0},{1,13},{5,9},{9,5},{13,1},{2,14},{6,10},... | collective-permute-start | bytes 688136 | tf_op jit(solution)/shard_map/ppermute | solution.py:482
  11.3 1.4 %collective-permute-start = (f32[2,2,12,8,256]{4,3,2,1,0:T(8,128)}, f32[2,2,12,8,256]{4,3,2,1,0:T(8,128)S(1)}, u32[]{:S(2)}, u32[]{:S(2)}) collective-permute-start(f32[2,2,12,8,256]{4,3,2,1,0:T(8,128)} %get-tuple-element.16), channel_id=1, source_target_pairs={{0,8},{4,12},{8,0},{12,4},{1,9},{5,13},{9,1},{13,5},{2,10},{6,14},... | collective-permute-start | bytes 1179656 | tf_op jit(solution)/shard_map/ppermute | solution.py:482
  12.7 16.2 %collective-permute-done.2.refs_1_ = f32[2,14,8,256]{3,2,1,0:T(8,128)S(1)} collective-permute-done((f32[2,14,8,256]{3,2,1,0:T(8,128)}, f32[2,14,8,256]{3,2,1,0:T(8,128)S(1)}, u32[]{:S(2)}, u32[]{:S(2)}) %collective-permute-start.2) | collective-permute-done | bytes 229408 | tf_op jit(solution)/shard_map/ppermute | solution.py:482
  28.9 1.4 %collective-permute-start.1 = (f32[2,2,12,8,256]{4,3,2,1,0:T(8,128)}, f32[2,2,12,8,256]{4,3,2,1,0:T(8,128)S(1)}, u32[]{:S(2)}, u32[]{:S(2)}) collective-permute-start(f32[2,2,12,8,256]{4,3,2,1,0:T(8,128)} %get-tuple-element.17), channel_id=1, source_target_pairs={{0,12},{4,8},{8,4},{12,0},{1,13},{5,9},{9,5},{13,1},{2,14},{6,10},... | collective-permute-start | bytes 1179656 | tf_op jit(solution)/shard_map/ppermute | solution.py:482
  30.3 0.0 collective-permute-done.3.refs_2_
  30.3 0.0 collective-permute-done.4.refs_3_
  30.3 0.0 collective-permute-done.5.refs_4_
  30.3 0.0 copy-start
  30.3 0.9 %copy-done = f32[2,14,8,256]{3,2,1,0:T(8,128)S(1)} copy-done((f32[2,14,8,256]{3,2,1,0:T(8,128)S(1)}, f32[2,14,8,256]{3,2,1,0:T(8,128)}, u32[]{:S(2)}) %copy-start) | copy-done | bytes 229400
  31.3 0.0 copy-start.1
  31.3 0.0 copy-start.2
  31.3 0.0 copy-start.3
  31.3 1.3 %shard_map.115 = (f32[8,14,8,256]{3,2,1,0:T(8,128)S(1)}, f32[3,8,12,8,256]{4,3,2,1,0:T(8,128)}, f32[8,12,256]{2,1,0:T(8,128)S(1)}) custom-call(f32[2,14,8,256]{3,2,1,0:T(8,128)S(1)} %copy-done, f32[2,14,8,256]{3,2,1,0:T(8,128)S(1)} %collective-permute-done.2.refs_1_, ...), custom_call_target="tpu_custom_call", output_to_operand_aliasing={{1}: (5, {})} | custom-call | bytes 2752512 | tf_op jit(solution)/shard_map/pallas_call | solution.py:289
  32.5 21.2 %collective-permute-start.6 = (f32[8,14,8,256]{3,2,1,0:T(8,128)S(1)}, f32[8,14,8,256]{3,2,1,0:T(8,128)S(1)}, u32[]{:S(2)}, u32[]{:S(2)}) collective-permute-start(f32[8,14,8,256]{3,2,1,0:T(8,128)S(1)} %get-tuple-element.24.own_ref), channel_id=1, source_target_pairs={{0,1},{1,0},{2,3},{3,2},{4,5},{5,4},{6,7},{7,6},{8,9},{9,8},{10,11... | collective-permute-start | bytes 2752520 | tf_op jit(solution)/shard_map/ppermute | solution.py:491
  53.8 0.0 copy-done.6
  53.8 0.0 copy-done.7
  53.8 0.0 copy-done.8
  53.8 0.1 fusion.7
  53.9 0.0 copy-done.5
  53.9 0.4 fusion.2
  54.3 1.3 %collective-permute-start.7 = (f32[8,12,256]{2,1,0:T(8,128)S(1)}, f32[8,12,256]{2,1,0:T(8,128)S(1)}, u32[]{:S(2)}, u32[]{:S(2)}) collective-permute-start(f32[8,12,256]{2,1,0:T(8,128)S(1)} %get-tuple-element.25), channel_id=1, source_target_pairs={{0,2},{2,0},{1,3},{3,1},{4,6},{6,4},{5,7},{7,5},{8,10},{10,8},{9,1... | collective-permute-start | bytes 294920 | tf_op jit(solution)/shard_map/ppermute | solution.py:500
  55.5 0.5 collective-permute-start.8
  56.0 0.0 copy-done.4
  56.0 0.1 multiply_reduce_fusion
  56.1 3.3 %collective-permute-done.7.own_low.own_high = f32[8,12,256]{2,1,0:T(8,128)S(1)} collective-permute-done((f32[8,12,256]{2,1,0:T(8,128)S(1)}, f32[8,12,256]{2,1,0:T(8,128)S(1)}, u32[]{:S(2)}, u32[]{:S(2)}) %collective-permute-start.7) | collective-permute-done | bytes 98336 | tf_op jit(solution)/shard_map/ppermute | solution.py:500
  59.4 3.2 %collective-permute-done.8.other_low.other_high = f32[8,12,256]{2,1,0:T(8,128)S(1)} collective-permute-done((f32[8,12,256]{2,1,0:T(8,128)S(1)}, f32[8,12,256]{2,1,0:T(8,128)S(1)}, u32[]{:S(2)}, u32[]{:S(2)}) %collective-permute-start.8) | collective-permute-done | bytes 98336 | tf_op jit(solution)/shard_map/ppermute | solution.py:500
  62.7 0.0 collective-permute-done.6.other_ref
  62.7 0.0 copy-done.1
  62.7 0.0 copy-done.2
  62.7 0.0 copy-done.3
  62.7 10.5 %shard_map.116 = (f32[8,12,8,256]{3,2,1,0:T(8,128)}, f32[8,128]{1,0:T(8,128)S(1)}) custom-call(s32[16]{0:T(128)S(1)} %copy-done.1, s32[16]{0:T(128)S(1)} %copy-done.2, f32[8,14,8,256]{3,2,1,0:T(8,128)S(1)} %get-tuple-element.24.own_ref, f32[8,14,8,256]{3,2,1,0:T(8,128)S(1)} %collective-permute-done.6.other_ref, ...), custom_call_target="tpu_custom_call" | custom-call | flops 2113929216 | bytes 2752512 | tf_op jit(solution)/shard_map/pallas_call | solution.py:507
  73.1 0.0 collective-permute-done.refs_0_
  73.1 0.0 collective-permute-done.1.refs_1_
  73.2 0.9 %shard_map.117 = f32[3,8,12,8,256]{4,3,2,1,0:T(8,128)} custom-call(f32[2,2,12,8,256]{4,3,2,1,0:T(8,128)S(1)} %collective-permute-done.refs_0_, f32[2,2,12,8,256]{4,3,2,1,0:T(8,128)S(1)} %collective-permute-done.1.refs_1_, f32[3,8,12,8,256]{4,3,2,1,0:T(8,128)} %get-tuple-element.23.refs_2_, ...), custom_call_target="tpu_custom_call", output_to_operand_aliasing={{}: (2, {})} | custom-call | bytes 1572864 | tf_op jit(solution)/shard_map/pallas_call | solution.py:232
  (2 shorter events, 0.0 us)
Async XLA Ops:
  3.6 50.1 %copy-start.6 = (f32[24,24]{1,0:T(8,128)S(1)}, f32[24,24]{1,0:T(8,128)}, u32[]{:S(2)}) copy-start(f32[24,24]{1,0:T(8,128)} %param.14) | copy-start | bytes 6916
  3.6 50.1 %copy-start.7 = (f32[24,24]{1,0:T(8,128)S(1)}, f32[24,24]{1,0:T(8,128)}, u32[]{:S(2)}) copy-start(f32[24,24]{1,0:T(8,128)} %param.15) | copy-start | bytes 6916
  3.7 50.1 %copy-start.8 = (f32[24,24]{1,0:T(8,128)S(1)}, f32[24,24]{1,0:T(8,128)}, u32[]{:S(2)}) copy-start(f32[24,24]{1,0:T(8,128)} %param.16) | copy-start | bytes 6916
  3.7 50.2 %copy-start.5 = (f32[24,896,1]{1,0,2:T(8,128)S(1)}, f32[24,896,1]{1,0,2:T(8,128)}, u32[]{:S(2)}) copy-start(f32[24,896,1]{1,0,2:T(8,128)} %constant.27) | copy-start | bytes 258052
  3.7 52.3 %copy-start.4 = (f32[3,8,896]{2,1,0:T(8,128)S(1)}, f32[3,8,896]{2,1,0:T(8,128)}, u32[]{:S(2)}) copy-start(f32[3,8,896]{2,1,0:T(8,128)} %constant.23.clone) | copy-start | bytes 258052
  7.7 22.6 %collective-permute-start.5 = (f32[2,2,12,8,256]{4,3,2,1,0:T(8,128)}, f32[2,2,12,8,256]{4,3,2,1,0:T(8,128)S(1)}, u32[]{:S(2)}, u32[]{:S(2)}) collective-permute-start(f32[2,2,12,8,256]{4,3,2,1,0:T(8,128)} %get-tuple-element.21), channel_id=1, source_target_pairs={{0,4},{4,0},{8,12},{12,8},{1,5},{5,1},{9,13},{13,9},{2,6},{6,2},{1... | collective-permute-start | bytes 1179656 | tf_op jit(solution)/shard_map/ppermute | solution.py:482
  8.7 20.2 %collective-permute-start.2 = (f32[2,14,8,256]{3,2,1,0:T(8,128)}, f32[2,14,8,256]{3,2,1,0:T(8,128)S(1)}, u32[]{:S(2)}, u32[]{:S(2)}) collective-permute-start(f32[2,14,8,256]{3,2,1,0:T(8,128)} %get-tuple-element.18), channel_id=1, source_target_pairs={{0,4},{4,0},{8,12},{12,8},{1,5},{5,1},{9,13},{13,9},{2,6},{6,2},{1... | collective-permute-start | bytes 688136 | tf_op jit(solution)/shard_map/ppermute | solution.py:482
  9.3 21.0 %collective-permute-start.3 = (f32[2,14,8,256]{3,2,1,0:T(8,128)}, f32[2,14,8,256]{3,2,1,0:T(8,128)S(1)}, u32[]{:S(2)}, u32[]{:S(2)}) collective-permute-start(f32[2,14,8,256]{3,2,1,0:T(8,128)} %get-tuple-element.19), channel_id=1, source_target_pairs={{0,8},{4,12},{8,0},{12,4},{1,9},{5,13},{9,1},{13,5},{2,10},{6,14},... | collective-permute-start | bytes 688136 | tf_op jit(solution)/shard_map/ppermute | solution.py:482
  9.3 21.0 %collective-permute-start.4 = (f32[2,14,8,256]{3,2,1,0:T(8,128)}, f32[2,14,8,256]{3,2,1,0:T(8,128)S(1)}, u32[]{:S(2)}, u32[]{:S(2)}) collective-permute-start(f32[2,14,8,256]{3,2,1,0:T(8,128)} %get-tuple-element.20), channel_id=1, source_target_pairs={{0,12},{4,8},{8,4},{12,0},{1,13},{5,9},{9,5},{13,1},{2,14},{6,10},... | collective-permute-start | bytes 688136 | tf_op jit(solution)/shard_map/ppermute | solution.py:482
  11.3 61.8 %collective-permute-start = (f32[2,2,12,8,256]{4,3,2,1,0:T(8,128)}, f32[2,2,12,8,256]{4,3,2,1,0:T(8,128)S(1)}, u32[]{:S(2)}, u32[]{:S(2)}) collective-permute-start(f32[2,2,12,8,256]{4,3,2,1,0:T(8,128)} %get-tuple-element.16), channel_id=1, source_target_pairs={{0,8},{4,12},{8,0},{12,4},{1,9},{5,13},{9,1},{13,5},{2,10},{6,14},... | collective-permute-start | bytes 1179656 | tf_op jit(solution)/shard_map/ppermute | solution.py:482
  28.9 44.2 %collective-permute-start.1 = (f32[2,2,12,8,256]{4,3,2,1,0:T(8,128)}, f32[2,2,12,8,256]{4,3,2,1,0:T(8,128)S(1)}, u32[]{:S(2)}, u32[]{:S(2)}) collective-permute-start(f32[2,2,12,8,256]{4,3,2,1,0:T(8,128)} %get-tuple-element.17), channel_id=1, source_target_pairs={{0,12},{4,8},{8,4},{12,0},{1,13},{5,9},{9,5},{13,1},{2,14},{6,10},... | collective-permute-start | bytes 1179656 | tf_op jit(solution)/shard_map/ppermute | solution.py:482
  30.3 0.9 %copy-start = (f32[2,14,8,256]{3,2,1,0:T(8,128)S(1)}, f32[2,14,8,256]{3,2,1,0:T(8,128)}, u32[]{:S(2)}) copy-start(f32[2,14,8,256]{3,2,1,0:T(8,128)} %get-tuple-element.15.after_ref.refs_0_) | copy-start | bytes 688132
  31.3 31.4 %copy-start.1 = (s32[16]{0:T(128)S(1)}, s32[16]{0:T(128)}, u32[]{:S(2)}) copy-start(s32[16]{0:T(128)} %dest_ref.5) | copy-start | bytes 196
  31.3 31.4 %copy-start.2 = (s32[16]{0:T(128)S(1)}, s32[16]{0:T(128)}, u32[]{:S(2)}) copy-start(s32[16]{0:T(128)} %parent_ref.3) | copy-start | bytes 196
  31.3 31.4 %copy-start.3 = (bf16[256,2304]{1,0:T(8,128)(2,1)S(1)}, bf16[256,2304]{1,0:T(8,128)(2,1)}, u32[]{:S(2)}) copy-start(bf16[256,2304]{1,0:T(8,128)(2,1)} %constant.26.spread_ref) | copy-start | bytes 3538948
  32.5 30.1 %collective-permute-start.6 = (f32[8,14,8,256]{3,2,1,0:T(8,128)S(1)}, f32[8,14,8,256]{3,2,1,0:T(8,128)S(1)}, u32[]{:S(2)}, u32[]{:S(2)}) collective-permute-start(f32[8,14,8,256]{3,2,1,0:T(8,128)S(1)} %get-tuple-element.24.own_ref), channel_id=1, source_target_pairs={{0,1},{1,0},{2,3},{3,2},{4,5},{5,4},{6,7},{7,6},{8,9},{9,8},{10,11... | collective-permute-start | bytes 2752520 | tf_op jit(solution)/shard_map/ppermute | solution.py:491
  54.3 5.2 %collective-permute-start.7 = (f32[8,12,256]{2,1,0:T(8,128)S(1)}, f32[8,12,256]{2,1,0:T(8,128)S(1)}, u32[]{:S(2)}, u32[]{:S(2)}) collective-permute-start(f32[8,12,256]{2,1,0:T(8,128)S(1)} %get-tuple-element.25), channel_id=1, source_target_pairs={{0,2},{2,0},{1,3},{3,1},{4,6},{6,4},{5,7},{7,5},{8,10},{10,8},{9,1... | collective-permute-start | bytes 294920 | tf_op jit(solution)/shard_map/ppermute | solution.py:500
  55.5 7.1 %collective-permute-start.8 = (f32[8,12,256]{2,1,0:T(8,128)S(1)}, f32[8,12,256]{2,1,0:T(8,128)S(1)}, u32[]{:S(2)}, u32[]{:S(2)}) collective-permute-start(f32[8,12,256]{2,1,0:T(8,128)S(1)} %get-tuple-element.25), channel_id=1, source_target_pairs={{0,3},{3,0},{1,2},{2,1},{4,7},{7,4},{5,6},{6,5},{8,11},{11,8},{9,1... | collective-permute-start | bytes 294920 | tf_op jit(solution)/shard_map/ppermute | solution.py:500

commit v7 on v6

--- a/solution.py
+++ b/solution.py
@@ -147,90 +147,95 @@
     )(move_dest, parent, boxes, coarse)
 
 
-def later_kernel(per_device, box_count, levels, dest_ref, boxes_ref, after_ref, *refs):
-    outs, moved_ref = refs[: box_count - 1], refs[box_count - 1]
-    stay, dest, table, sems, in_sem, out_sem = refs[box_count:]
+def later_kernel(turns, per_device, box_count, levels, dest_ref, boxes_ref, *refs):
+    outs, (dest, table, sems, in_sem) = refs[: len(turns)], refs[len(turns) :]
     own = lax.axis_index("box")
     fetch = pltpu.make_async_copy(dest_ref, dest, in_sem)
     fetch.start()
     fetch.wait()
     place_boxes(per_device, box_count, dest, table)
-
-    def copies(turn, k, b):
-        for n in range(0 if turn == 0 else 1, levels):
-            to = stay.at[n, k] if turn == 0 else outs[turn - 1].at[n - 1, k]
-            yield pltpu.make_async_copy(boxes_ref.at[n, b], to, sems.at[n, turn, k])
-
-    for turn, k, slot in each_slot(box_count):
+    places = [(n, turn, k, 2 * partner(own, turn, box_count) + k) for n, turn in enumerate(turns) for k in range(2)]
+
+    def copies(n, turn, k, b):
+        skip = min(turn, 1)
+        for level in range(skip, levels):
+            yield pltpu.make_async_copy(boxes_ref.at[level, b], outs[n].at[level - skip, k], sems.at[n, level, k])
+
+    for n, turn, k, slot in places:
         b = table[slot]
 
         @pl.when(b >= 0)
         def _():
-            for copy in copies(turn, k, b):
+            for copy in copies(n, turn, k, b):
                 copy.start()
 
         @pl.when(b < 0)
         def _():
-            to = stay if turn == 0 else outs[turn - 1]
-            for n in range(to.shape[0]):
-                to[n, k] = jnp.zeros(to.shape[2:], jnp.float32)
-
-    for turn, k, slot in each_slot(box_count):
+            for level in range(outs[n].shape[0]):
+                outs[n][level, k] = jnp.zeros(outs[n].shape[2:], jnp.float32)
+
+    for n, turn, k, slot in places:
         b = table[slot]
 
         @pl.when(b >= 0)
         def _():
-            for copy in copies(turn, k, b):
+            for copy in copies(n, turn, k, b):
                 copy.wait()
 
-        if (turn, k) == (0, 1):
-            settled = pltpu.make_async_copy(stay, moved_ref.at[:, pl.ds(2 * own, 2)], out_sem)
-            settled.start()
-    settled.wait()
-
-
-def pack_later(boxes, move_dest, after, box_count):
+
+def pack_later(turns, boxes, move_dest, box_count):
     levels, per_device = boxes.shape[:2]
     item = boxes.shape[2:]
     hbm, vmem = pl.BlockSpec(memory_space=pltpu.HBM), pl.BlockSpec(memory_space=pltpu.VMEM)
+    size = int(np.prod(item)) * 4
     return pl.pallas_call(
-        functools.partial(later_kernel, per_device, box_count, levels),
-        out_shape=[jax.ShapeDtypeStruct((levels - 1, 2) + item, jnp.float32)] * (box_count - 1)
-        + [jax.ShapeDtypeStruct((levels, 2 * box_count) + item, jnp.float32)],
-        in_specs=[hbm] * 3,
-        out_specs=[vmem] * (box_count - 1) + [hbm],
+        functools.partial(later_kernel, turns, per_device, box_count, levels),
+        out_shape=[jax.ShapeDtypeStruct((levels - min(turn, 1), 2) + item, jnp.float32) for turn in turns],
+        in_specs=[hbm] * 2,
+        out_specs=[vmem] * len(turns),
         scratch_shapes=[
-            pltpu.VMEM((levels, 2) + item, jnp.float32),
             pltpu.SMEM(move_dest.shape, jnp.int32),
             pltpu.SMEM((2 * box_count,), jnp.int32),
-            pltpu.SemaphoreType.DMA((levels, box_count, 2)),
-            pltpu.SemaphoreType.DMA,
+            pltpu.SemaphoreType.DMA((len(turns), levels, 2)),
             pltpu.SemaphoreType.DMA,
         ],
-        cost_estimate=pl.CostEstimate(flops=0, bytes_accessed=12 * boxes.size, transcendentals=0),
-    )(move_dest, boxes, after)
-
-
-def settle_later(piece, turn, moved_ref, sem):
-    source = partner(lax.axis_index("box"), turn, moved_ref.shape[1] // 2)
-    to = moved_ref.at[pl.ds(1, moved_ref.shape[0] - 1), pl.ds(2 * source, 2)]
-    return pltpu.make_async_copy(piece, to, sem)
-
-
-def settle_kernel(turns, *refs):
+        cost_estimate=pl.CostEstimate(
+            flops=0, bytes_accessed=4 * len(turns) * levels * size, transcendentals=0
+        ),
+    )(move_dest, boxes)
+
+
+def settle_kernel(box_count, *refs):
     out_ref, sems = refs[-2:]
-    copies = [settle_later(refs[n], turn, out_ref, sems.at[n]) for n, turn in enumerate(turns)]
-    for copy in copies:
-        copy.start()
-    for copy in copies:
-        copy.wait()
-
-
-def settle(turns, pieces, moved, after):
+    own = lax.axis_index("box")
+    levels = out_ref.shape[0]
+    middle = jnp.logical_or(own == box_count // 2, own == box_count // 2 - 1)
+
+    def copy(turn, piece):
+        to = out_ref.at[pl.ds(1, levels - 1), pl.ds(2 * partner(own, turn, box_count), 2)]
+        return pltpu.make_async_copy(piece, to, sems.at[turn])
+
+    last = box_count - 1
+
+    @pl.when(middle)
+    def _():
+        copy(last, refs[last]).start()
+
+    @pl.when(jnp.logical_not(middle))
+    def _():
+        copy(last, refs[last - 1]).start()
+
+    for turn in range(1, last):
+        copy(turn, refs[turn - 1]).start()
+    for turn in range(1, box_count):
+        copy(turn, refs[turn - 1]).wait()
+
+
+def settle(pieces, moved, after):
     count = len(pieces)
     vmem, hbm = pl.BlockSpec(memory_space=pltpu.VMEM), pl.BlockSpec(memory_space=pltpu.HBM)
     return pl.pallas_call(
-        functools.partial(settle_kernel, turns),
+        functools.partial(settle_kernel, count),
         out_shape=jax.ShapeDtypeStruct(moved.shape, jnp.float32),
         in_specs=[vmem] * count + [hbm, vmem],
         out_specs=hbm,
@@ -243,19 +248,17 @@
     )(*pieces, moved, after)
 
 
-def arrive_kernel(box_count, slabs, early, fields, *refs):
-    pieces, later = refs[:box_count], refs[box_count : box_count + len(early)]
-    now_ref, moved_ref, *edges, sems = refs[box_count + len(early) + 1 :]
+def arrive_kernel(box_count, slabs, fields, *refs):
+    pieces, stay = refs[:box_count], refs[box_count]
+    now_ref, moved_ref, *edges, sems = refs[box_count + 1 :]
     own, slab = lax.axis_index("box"), lax.axis_index("slab")
     planes = now_ref.shape[2]
     mine = pltpu.make_async_copy(pieces[0], now_ref.at[pl.ds(2 * own, 2)], sems.at[0])
     mine.start()
-    copies = []
+    copies = [pltpu.make_async_copy(stay, moved_ref.at[:, pl.ds(2 * own, 2)], sems.at[box_count])]
     for turn in range(1, box_count):
         to = moved_ref.at[0, pl.ds(2 * partner(own, turn, box_count), 2)]
         copies.append(pltpu.make_async_copy(pieces[turn].at[:, pl.ds(0, fields)], to, sems.at[turn]))
-    for n, turn in enumerate(early):
-        copies.append(settle_later(later[n], turn, moved_ref, sems.at[box_count + n]))
     for copy in copies:
         copy.start()
     faced = [jnp.where(slab == 0, planes - 1, 0)] if slabs == 2 else [0, planes - 1]
@@ -277,27 +280,25 @@
         copy.wait()
 
 
-def arrive(pieces, early, later, moved, slabs):
+def arrive(pieces, stay, slabs):
     box_count = len(pieces)
     _, blocks, planes, cross = pieces[0].shape
-    fields = moved.shape[2]
+    levels, _, fields = stay.shape[:3]
     slots = 2 * box_count
     sides = 1 if slabs == 2 else 2
     vmem, hbm = pl.BlockSpec(memory_space=pltpu.VMEM), pl.BlockSpec(memory_space=pltpu.HBM)
-    shapes = [(slots, blocks, planes, cross), moved.shape] + [(slots, fields, cross)] * sides
-    count = box_count + len(later)
+    shapes = [(slots, blocks, planes, cross), (levels, slots, fields, planes, cross)] + [(slots, fields, cross)] * sides
     return pl.pallas_call(
-        functools.partial(arrive_kernel, box_count, slabs, early, fields),
+        functools.partial(arrive_kernel, box_count, slabs, fields),
         out_shape=[jax.ShapeDtypeStruct(shape, jnp.float32) for shape in shapes],
-        in_specs=[hbm] + [vmem] * (count - 1) + [hbm],
+        in_specs=[hbm] + [vmem] * box_count,
         out_specs=[vmem, hbm] + [vmem] * sides,
-        scratch_shapes=[pltpu.SemaphoreType.DMA((count,))],
-        input_output_aliases={count: 1},
+        scratch_shapes=[pltpu.SemaphoreType.DMA((box_count + 1,))],
         compiler_params=pltpu.CompilerParams(vmem_limit_bytes=48 * 2 ** 20),
         cost_estimate=pl.CostEstimate(
             flops=0, bytes_accessed=12 * box_count * pieces[0].size, transcendentals=0
         ),
-    )(*pieces, *later, moved)
+    )(*pieces, stay)
 
 
 def face_cells(lane, edge, coarse_planes, slab):
@@ -478,14 +479,22 @@
     total = move_dest.shape[0]
     coarse_count = coarse.shape[0]
 
-    def send(piece, turn):
-        return lax.ppermute(piece, "box", [(s, partner(s, turn, box_count)) for s in range(box_count)])
-
+    def send(piece, turn, members=range(box_count)):
+        return lax.ppermute(piece, "box", [(s, partner(s, turn, box_count)) for s in members])
+
+    last = box_count - 1
+    middle = (box_count // 2 - 1, box_count // 2)
+    outer = [s for s in range(box_count) if s not in middle]
+    fill = pack_later((1, last), boxes, move_dest, box_count)
+    fillers = [send(fill[0], 1), send(fill[1], last, middle)]
     first = pack_first(boxes, coarse, move_dest, parent, edge, box_count)
     arrived = [first[0]] + [send(first[turn], turn) for turn in range(1, box_count)]
-    *later, moved = pack_later(boxes, move_dest, first[0], box_count)
-    later = [send(piece, n + 1) for n, piece in enumerate(later)]
-    now, moved, *facing = arrive(arrived, (1,), later[:1], moved, slabs)
+    stay, *rest = pack_later((0,) + tuple(range(2, last)), boxes, move_dest, box_count)
+    held, arrived[last] = lax.optimization_barrier((tuple(rest), arrived[last]))
+    rest = list(held)
+    rest = [send(piece, n + 2) for n, piece in enumerate(rest)] + [send(fill[1], last, outer)]
+    now, moved, *facing = arrive(arrived, stay, slabs)
+    now, *fillers = lax.optimization_barrier((now, *fillers))
 
     swap = [(0, 1), (1, 0)]
     now_other = lax.ppermute(now, "fld", swap)
@@ -526,7 +535,7 @@
             flops=12 * slots * weight.size * cross, bytes_accessed=12 * now.size, transcendentals=0
         ),
     )(move_dest, parent, now, now_other, low[0], low[1], high[0], high[1], spread, weight)
-    return settle(tuple(range(2, box_count)), later[1:], moved, token), slope
+    return settle([fillers[0]] + rest + [fillers[1]], moved, token), slope
 
 
 def solution(mesh):

time: 72.9 us -> 74.2 us (1.018)
  the two profiles are of different devices: /device:TPU:17 before, /device:TPU:0 now
where the time goes in v7:
time: 74.2 us; the launch traced here: 73.8 us
  waiting for transfers between devices  37.2 us (50%)
  Pallas kernels  18.9 us (25%)
  starting transfers between devices  14.2 us (19%)
  local copies, waits for them, and re-layouts  2.13 us (3%)
  between operations  0.88 us (1%)
    ppermute x7, waiting for transfers between devices, send(): lax.ppermute(piece, 'box', [(s, partner(s, turn, box_count)) for s in mem...  30.8 us
    ppermute x7, starting transfers between devices, send(): lax.ppermute(piece, 'box', [(s, partner(s, turn, box_count)) for s in mem...  12 us
    pallas_call x1, Pallas kernels, body(): pl.pallas_call(functools.partial(slope_kernel, edge, planes, fields, coar...  7.89 us
    pallas_call x2, Pallas kernels, pack_later(): pl.pallas_call(functools.partial(later_kernel, turns, per_device, box_cou...  5.73 us
    ppermute x1, waiting for transfers between devices, body(): lax.ppermute(facing[0], 'slab', swap)  3.22 us
    ppermute x1, waiting for transfers between devices, body(): lax.ppermute(facing[0], ('slab', 'fld'), crossed)  3.2 us
    pallas_call x1, Pallas kernels, pack_first(): pl.pallas_call(functools.partial(first_kernel, per_device, box_count, edg...  2.96 us
    unnamed x22, local copies, waits for them, and re-layouts  2.06 us
  transfers between devices with their start and end apart: 10, of which 5 were waited for; matrix products, arithmetic and copies ran while one was open for 1% of the time, Pallas kernels for 20%

profile of v7, /device:TPU:0, one launch (start us, length us, event | category | flops | bytes accessed | tf_op | source)
XLA Modules:
  0.0 73.8 jit_solution(2504645263318112433)
XLA Ops:
  0.6 2.8 %shard_map.116 = (f32[2,2,12,8,256]{4,3,2,1,0:T(8,128)}, f32[2,2,12,8,256]{4,3,2,1,0:T(8,128)}) custom-call(s32[16]{0:T(128)} %dest_ref.7, f32[3,4,12,8,256]{4,3,2,1,0:T(8,128)} %boxes_ref.5), custom_call_target="tpu_custom_call" | custom-call | bytes 2359296 | tf_op jit(solution)/shard_map/pallas_call | solution.py:191
  3.4 0.0 copy-start.10
  3.4 0.0 copy-start.7
  3.5 0.0 copy-start.8
  3.5 0.0 copy-start.9
  3.5 0.0 copy-start.6
  3.5 2.1 %collective-permute-start.3 = (f32[2,2,12,8,256]{4,3,2,1,0:T(8,128)}, f32[2,2,12,8,256]{4,3,2,1,0:T(8,128)S(1)}, u32[]{:S(2)}, u32[]{:S(2)}) collective-permute-start(f32[2,2,12,8,256]{4,3,2,1,0:T(8,128)} %get-tuple-element.28), channel_id=1, source_target_pairs={{0,4},{4,0},{8,12},{12,8},{1,5},{5,1},{9,13},{13,9},{2,6},{6,2},{1... | collective-permute-start | bytes 1179656 | tf_op jit(solution)/shard_map/ppermute | solution.py:483
  5.6 0.7 collective-permute-start.4
  6.3 0.0 copy-start.5
  6.3 0.0 copy-start.2
  6.3 0.0 copy-start.3
  6.3 0.0 copy-start.4
  6.3 3.0 %shard_map.113 = (f32[2,14,8,256]{3,2,1,0:T(8,128)}, f32[2,14,8,256]{3,2,1,0:T(8,128)}, f32[2,14,8,256]{3,2,1,0:T(8,128)}, f32[2,14,8,256]{3,2,1,0:T(8,128)}) custom-call(s32[16]{0:T(128)} %dest_ref.7, s32[16]{0:T(128)} %parent_ref.3, f32[3,4,12,8,256]{4,3,2,1,0:T(8,128)} %boxes_ref.5, f32[12,8,1000]{2,1,0:T(8,128)} %bitcast.11), custom_call_target="tpu_custom_call" | custom-call | flops 147456000 | bytes 2743296 | tf_op jit(solution)/shard_map/pallas_call | solution.py:129
  9.3 3.5 %collective-permute-start.2 = (f32[2,14,8,256]{3,2,1,0:T(8,128)}, f32[2,14,8,256]{3,2,1,0:T(8,128)S(1)}, u32[]{:S(2)}, u32[]{:S(2)}) collective-permute-start(f32[2,14,8,256]{3,2,1,0:T(8,128)} %get-tuple-element.24), channel_id=1, source_target_pairs={{0,12},{4,8},{8,4},{12,0},{1,13},{5,9},{9,5},{13,1},{2,14},{6,10},... | collective-permute-start | bytes 688136 | tf_op jit(solution)/shard_map/ppermute | solution.py:483
  12.8 2.0 %collective-permute-start = (f32[2,14,8,256]{3,2,1,0:T(8,128)}, f32[2,14,8,256]{3,2,1,0:T(8,128)S(1)}, u32[]{:S(2)}, u32[]{:S(2)}) collective-permute-start(f32[2,14,8,256]{3,2,1,0:T(8,128)} %get-tuple-element.21), channel_id=1, source_target_pairs={{0,4},{4,0},{8,12},{12,8},{1,5},{5,1},{9,13},{13,9},{2,6},{6,2},{1... | collective-permute-start | bytes 688136 | tf_op jit(solution)/shard_map/ppermute | solution.py:483
  14.8 1.4 %collective-permute-start.1 = (f32[2,14,8,256]{3,2,1,0:T(8,128)}, f32[2,14,8,256]{3,2,1,0:T(8,128)S(1)}, u32[]{:S(2)}, u32[]{:S(2)}) collective-permute-start(f32[2,14,8,256]{3,2,1,0:T(8,128)} %get-tuple-element.22), channel_id=1, source_target_pairs={{0,8},{4,12},{8,0},{12,4},{1,9},{5,13},{9,1},{13,5},{2,10},{6,14},... | collective-permute-start | bytes 688136 | tf_op jit(solution)/shard_map/ppermute | solution.py:483
  16.2 2.9 %shard_map.114 = (f32[3,2,12,8,256]{4,3,2,1,0:T(8,128)}, f32[2,2,12,8,256]{4,3,2,1,0:T(8,128)}) custom-call(s32[16]{0:T(128)} %dest_ref.7, f32[3,4,12,8,256]{4,3,2,1,0:T(8,128)} %boxes_ref.5), custom_call_target="tpu_custom_call" | custom-call | bytes 2359296 | tf_op jit(solution)/shard_map/pallas_call | solution.py:191
  19.1 5.0 %collective-permute-done.2.refs_3_ = f32[2,14,8,256]{3,2,1,0:T(8,128)S(1)} collective-permute-done((f32[2,14,8,256]{3,2,1,0:T(8,128)}, f32[2,14,8,256]{3,2,1,0:T(8,128)S(1)}, u32[]{:S(2)}, u32[]{:S(2)}) %collective-permute-start.2) | collective-permute-done | bytes 229408 | tf_op jit(solution)/shard_map/ppermute | solution.py:483
  24.2 0.0 copy-done.10
  24.2 2.3 %collective-permute-start.6 = (f32[2,2,12,8,256]{4,3,2,1,0:T(8,128)S(1)}, f32[2,2,12,8,256]{4,3,2,1,0:T(8,128)S(1)}, u32[]{:S(2)}, u32[]{:S(2)}) collective-permute-start(f32[2,2,12,8,256]{4,3,2,1,0:T(8,128)S(1)} %copy-done.10), channel_id=1, source_target_pairs={{0,12},{12,0},{1,13},{13,1},{2,14},{14,2},{3,15},{15,3},{16,28},{2... | collective-permute-start | bytes 1179656 | tf_op jit(solution)/shard_map/ppermute | solution.py:483
  26.5 0.0 collective-permute-done.refs_1_
  26.5 21.7 %collective-permute-done.1.refs_2_ = f32[2,14,8,256]{3,2,1,0:T(8,128)S(1)} collective-permute-done((f32[2,14,8,256]{3,2,1,0:T(8,128)}, f32[2,14,8,256]{3,2,1,0:T(8,128)S(1)}, u32[]{:S(2)}, u32[]{:S(2)}) %collective-permute-start.1) | collective-permute-done | bytes 229408 | tf_op jit(solution)/shard_map/ppermute | solution.py:483
  48.2 1.1 %copy-done = f32[3,2,12,8,256]{4,3,2,1,0:T(8,128)S(1)} copy-done((f32[3,2,12,8,256]{4,3,2,1,0:T(8,128)S(1)}, f32[3,2,12,8,256]{4,3,2,1,0:T(8,128)}, u32[]{:S(2)}) %copy-start) | copy-done | bytes 589848
  49.3 0.9 %copy-done.1 = f32[2,14,8,256]{3,2,1,0:T(8,128)S(1)} copy-done((f32[2,14,8,256]{3,2,1,0:T(8,128)S(1)}, f32[2,14,8,256]{3,2,1,0:T(8,128)}, u32[]{:S(2)}) %copy-start.1) | copy-done | bytes 229400
  50.2 1.3 %shard_map.115 = (f32[8,14,8,256]{3,2,1,0:T(8,128)S(1)}, f32[3,8,12,8,256]{4,3,2,1,0:T(8,128)}, f32[8,12,256]{2,1,0:T(8,128)S(1)}) custom-call(f32[2,14,8,256]{3,2,1,0:T(8,128)S(1)} %copy-done.1, f32[2,14,8,256]{3,2,1,0:T(8,128)S(1)} %collective-permute-done.refs_1_, f32[2,14,8,256]{3,2,1,0:T(8,128)S(1)} %collective-permute-done.1.refs_2_, ...), custom_call_target="tpu_custom_call" | custom-call | bytes 2752512 | tf_op jit(solution)/shard_map/pallas_call | solution.py:291
  51.5 0.0 collective-permute-done.3.refs_0_
  51.5 0.0 collective-permute-done.4.refs_3_
  51.5 0.1 collective-permute-start.7
  51.6 0.0 copy-done.7
  51.6 0.0 copy-done.8
  51.6 0.0 copy-done.9
  51.7 0.1 fusion.7
  51.8 0.0 collective-permute-start.5
  51.8 0.0 copy-done.6
  51.8 0.4 fusion.2
  52.2 1.6 %collective-permute-start.9 = (f32[8,12,256]{2,1,0:T(8,128)S(1)}, f32[8,12,256]{2,1,0:T(8,128)S(1)}, u32[]{:S(2)}, u32[]{:S(2)}) collective-permute-start(f32[8,12,256]{2,1,0:T(8,128)S(1)} %get-tuple-element.35), channel_id=1, source_target_pairs={{0,3},{3,0},{1,2},{2,1},{4,7},{7,4},{5,6},{6,5},{8,11},{11,8},{9,1... | collective-permute-start | bytes 294920 | tf_op jit(solution)/shard_map/ppermute | solution.py:509
  53.8 0.5 collective-permute-start.8
  54.3 0.0 copy-done.5
  54.3 0.1 multiply_reduce_fusion
  54.4 3.2 %collective-permute-done.9.other_low.other_high = f32[8,12,256]{2,1,0:T(8,128)S(1)} collective-permute-done((f32[8,12,256]{2,1,0:T(8,128)S(1)}, f32[8,12,256]{2,1,0:T(8,128)S(1)}, u32[]{:S(2)}, u32[]{:S(2)}) %collective-permute-start.9) | collective-permute-done | bytes 98336 | tf_op jit(solution)/shard_map/ppermute | solution.py:509
  57.6 3.2 %collective-permute-done.8.own_low.own_high = f32[8,12,256]{2,1,0:T(8,128)S(1)} collective-permute-done((f32[8,12,256]{2,1,0:T(8,128)S(1)}, f32[8,12,256]{2,1,0:T(8,128)S(1)}, u32[]{:S(2)}, u32[]{:S(2)}) %collective-permute-start.8) | collective-permute-done | bytes 98336 | tf_op jit(solution)/shard_map/ppermute | solution.py:509
  60.8 0.0 collective-permute-done.7.other_ref
  60.8 0.0 copy-done.2
  60.8 0.0 copy-done.3
  60.8 7.9 %shard_map.117 = (f32[8,12,8,256]{3,2,1,0:T(8,128)}, f32[8,128]{1,0:T(8,128)S(1)}) custom-call(s32[16]{0:T(128)S(1)} %copy-done.2, s32[16]{0:T(128)S(1)} %copy-done.3, f32[8,14,8,256]{3,2,1,0:T(8,128)S(1)} %get-tuple-element.34.own_ref, f32[8,14,8,256]{3,2,1,0:T(8,128)S(1)} %collective-permute-done.7.other_ref, ...), custom_call_target="tpu_custom_call" | custom-call | flops 2113929216 | bytes 2752512 | tf_op jit(solution)/shard_map/pallas_call | solution.py:516
  68.7 0.0 collective-permute-done.6.refs_2_
  68.7 4.0 %collective-permute-done.5.refs_1_ = f32[2,2,12,8,256]{4,3,2,1,0:T(8,128)S(1)} collective-permute-done((f32[2,2,12,8,256]{4,3,2,1,0:T(8,128)}, f32[2,2,12,8,256]{4,3,2,1,0:T(8,128)S(1)}, u32[]{:S(2)}, u32[]{:S(2)}) %collective-permute-start.5) | collective-permute-done | bytes 393248 | tf_op jit(solution)/shard_map/ppermute | solution.py:483
  72.8 1.0 %shard_map.118 = f32[3,8,12,8,256]{4,3,2,1,0:T(8,128)} custom-call(f32[2,2,12,8,256]{4,3,2,1,0:T(8,128)S(1)} %collective-permute-done.3.refs_0_, f32[2,2,12,8,256]{4,3,2,1,0:T(8,128)S(1)} %collective-permute-done.5.refs_1_, f32[2,2,12,8,256]{4,3,2,1,0:T(8,128)S(1)} %collective-permute-done.6.refs_2_, ...), custom_call_target="tpu_custom_call", output_to_operand_aliasing={{}: (4, {})} | custom-call | bytes 3145728 | tf_op jit(solution)/shard_map/pallas_call | solution.py:237
  (5 shorter events, 0.0 us)
Async XLA Ops:
  3.4 20.7 %copy-start.10 = (f32[2,2,12,8,256]{4,3,2,1,0:T(8,128)S(1)}, f32[2,2,12,8,256]{4,3,2,1,0:T(8,128)}, u32[]{:S(2)}) copy-start(f32[2,2,12,8,256]{4,3,2,1,0:T(8,128)} %get-tuple-element.29) | copy-start | bytes 1179652
  3.4 48.2 %copy-start.7 = (f32[24,24]{1,0:T(8,128)S(1)}, f32[24,24]{1,0:T(8,128)}, u32[]{:S(2)}) copy-start(f32[24,24]{1,0:T(8,128)} %param.14) | copy-start | bytes 6916
  3.5 48.2 %copy-start.8 = (f32[24,24]{1,0:T(8,128)S(1)}, f32[24,24]{1,0:T(8,128)}, u32[]{:S(2)}) copy-start(f32[24,24]{1,0:T(8,128)} %param.15) | copy-start | bytes 6916
  3.5 48.2 %copy-start.9 = (f32[24,24]{1,0:T(8,128)S(1)}, f32[24,24]{1,0:T(8,128)}, u32[]{:S(2)}) copy-start(f32[24,24]{1,0:T(8,128)} %param.16) | copy-start | bytes 6916
  3.5 48.3 %copy-start.6 = (f32[24,896,1]{1,0,2:T(8,128)S(1)}, f32[24,896,1]{1,0,2:T(8,128)}, u32[]{:S(2)}) copy-start(f32[24,896,1]{1,0,2:T(8,128)} %constant.27) | copy-start | bytes 258052
  3.5 48.0 %collective-permute-start.3 = (f32[2,2,12,8,256]{4,3,2,1,0:T(8,128)}, f32[2,2,12,8,256]{4,3,2,1,0:T(8,128)S(1)}, u32[]{:S(2)}, u32[]{:S(2)}) collective-permute-start(f32[2,2,12,8,256]{4,3,2,1,0:T(8,128)} %get-tuple-element.28), channel_id=1, source_target_pairs={{0,4},{4,0},{8,12},{12,8},{1,5},{5,1},{9,13},{13,9},{2,6},{6,2},{1... | collective-permute-start | bytes 1179656 | tf_op jit(solution)/shard_map/ppermute | solution.py:483
  5.6 45.9 %collective-permute-start.4 = (f32[2,2,12,8,256]{4,3,2,1,0:T(8,128)}, f32[2,2,12,8,256]{4,3,2,1,0:T(8,128)S(1)}, u32[]{:S(2)}, u32[]{:S(2)}) collective-permute-start(f32[2,2,12,8,256]{4,3,2,1,0:T(8,128)} %get-tuple-element.29), channel_id=1, source_target_pairs={{4,8},{8,4},{5,9},{9,5},{6,10},{10,6},{7,11},{11,7},{20,24},{24,20... | collective-permute-start | bytes 1179656 | tf_op jit(solution)/shard_map/ppermute | solution.py:483
  6.3 48.0 %copy-start.5 = (f32[3,8,896]{2,1,0:T(8,128)S(1)}, f32[3,8,896]{2,1,0:T(8,128)}, u32[]{:S(2)}) copy-start(f32[3,8,896]{2,1,0:T(8,128)} %constant.23.clone) | copy-start | bytes 258052
  6.3 54.5 %copy-start.2 = (s32[16]{0:T(128)S(1)}, s32[16]{0:T(128)}, u32[]{:S(2)}) copy-start(s32[16]{0:T(128)} %dest_ref.7) | copy-start | bytes 196
  6.3 54.5 %copy-start.3 = (s32[16]{0:T(128)S(1)}, s32[16]{0:T(128)}, u32[]{:S(2)}) copy-start(s32[16]{0:T(128)} %parent_ref.3) | copy-start | bytes 196
  6.3 54.5 %copy-start.4 = (bf16[256,2304]{1,0:T(8,128)(2,1)S(1)}, bf16[256,2304]{1,0:T(8,128)(2,1)}, u32[]{:S(2)}) copy-start(bf16[256,2304]{1,0:T(8,128)(2,1)} %constant.26.spread_ref) | copy-start | bytes 3538948
  9.3 14.9 %collective-permute-start.2 = (f32[2,14,8,256]{3,2,1,0:T(8,128)}, f32[2,14,8,256]{3,2,1,0:T(8,128)S(1)}, u32[]{:S(2)}, u32[]{:S(2)}) collective-permute-start(f32[2,14,8,256]{3,2,1,0:T(8,128)} %get-tuple-element.24), channel_id=1, source_target_pairs={{0,12},{4,8},{8,4},{12,0},{1,13},{5,9},{9,5},{13,1},{2,14},{6,10},... | collective-permute-start | bytes 688136 | tf_op jit(solution)/shard_map/ppermute | solution.py:483
  12.8 13.7 %collective-permute-start = (f32[2,14,8,256]{3,2,1,0:T(8,128)}, f32[2,14,8,256]{3,2,1,0:T(8,128)S(1)}, u32[]{:S(2)}, u32[]{:S(2)}) collective-permute-start(f32[2,14,8,256]{3,2,1,0:T(8,128)} %get-tuple-element.21), channel_id=1, source_target_pairs={{0,4},{4,0},{8,12},{12,8},{1,5},{5,1},{9,13},{13,9},{2,6},{6,2},{1... | collective-permute-start | bytes 688136 | tf_op jit(solution)/shard_map/ppermute | solution.py:483
  14.8 33.4 %collective-permute-start.1 = (f32[2,14,8,256]{3,2,1,0:T(8,128)}, f32[2,14,8,256]{3,2,1,0:T(8,128)S(1)}, u32[]{:S(2)}, u32[]{:S(2)}) collective-permute-start(f32[2,14,8,256]{3,2,1,0:T(8,128)} %get-tuple-element.22), channel_id=1, source_target_pairs={{0,8},{4,12},{8,0},{12,4},{1,9},{5,13},{9,1},{13,5},{2,10},{6,14},... | collective-permute-start | bytes 688136 | tf_op jit(solution)/shard_map/ppermute | solution.py:483
  24.2 44.6 %collective-permute-start.6 = (f32[2,2,12,8,256]{4,3,2,1,0:T(8,128)S(1)}, f32[2,2,12,8,256]{4,3,2,1,0:T(8,128)S(1)}, u32[]{:S(2)}, u32[]{:S(2)}) collective-permute-start(f32[2,2,12,8,256]{4,3,2,1,0:T(8,128)S(1)} %copy-done.10), channel_id=1, source_target_pairs={{0,12},{12,0},{1,13},{13,1},{2,14},{14,2},{3,15},{15,3},{16,28},{2... | collective-permute-start | bytes 1179656 | tf_op jit(solution)/shard_map/ppermute | solution.py:483
  48.2 1.1 %copy-start = (f32[3,2,12,8,256]{4,3,2,1,0:T(8,128)S(1)}, f32[3,2,12,8,256]{4,3,2,1,0:T(8,128)}, u32[]{:S(2)}) copy-start(f32[3,2,12,8,256]{4,3,2,1,0:T(8,128)} %get-tuple-element.26.refs_4_) | copy-start | bytes 1769476
  49.3 0.9 %copy-start.1 = (f32[2,14,8,256]{3,2,1,0:T(8,128)S(1)}, f32[2,14,8,256]{3,2,1,0:T(8,128)}, u32[]{:S(2)}) copy-start(f32[2,14,8,256]{3,2,1,0:T(8,128)} %get-tuple-element.20.refs_0_) | copy-start | bytes 688132
  51.5 9.3 %collective-permute-start.7 = (f32[8,14,8,256]{3,2,1,0:T(8,128)S(1)}, f32[8,14,8,256]{3,2,1,0:T(8,128)S(1)}, u32[]{:S(2)}, u32[]{:S(2)}) collective-permute-start(f32[8,14,8,256]{3,2,1,0:T(8,128)S(1)} %get-tuple-element.34.own_ref), channel_id=1, source_target_pairs={{0,1},{1,0},{2,3},{3,2},{4,5},{5,4},{6,7},{7,6},{8,9},{9,8},{10,11... | collective-permute-start | bytes 2752520 | tf_op jit(solution)/shard_map/ppermute | solution.py:500
  51.8 21.0 %collective-permute-start.5 = (f32[2,2,12,8,256]{4,3,2,1,0:T(8,128)}, f32[2,2,12,8,256]{4,3,2,1,0:T(8,128)S(1)}, u32[]{:S(2)}, u32[]{:S(2)}) collective-permute-start(f32[2,2,12,8,256]{4,3,2,1,0:T(8,128)} %get-tuple-element.31), channel_id=1, source_target_pairs={{0,8},{4,12},{8,0},{12,4},{1,9},{5,13},{9,1},{13,5},{2,10},{6,14},... | collective-permute-start | bytes 1179656 | tf_op jit(solution)/shard_map/ppermute | solution.py:483
  52.2 5.5 %collective-permute-start.9 = (f32[8,12,256]{2,1,0:T(8,128)S(1)}, f32[8,12,256]{2,1,0:T(8,128)S(1)}, u32[]{:S(2)}, u32[]{:S(2)}) collective-permute-start(f32[8,12,256]{2,1,0:T(8,128)S(1)} %get-tuple-element.35), channel_id=1, source_target_pairs={{0,3},{3,0},{1,2},{2,1},{4,7},{7,4},{5,6},{6,5},{8,11},{11,8},{9,1... | collective-permute-start | bytes 294920 | tf_op jit(solution)/shard_map/ppermute | solution.py:509
  53.8 7.0 %collective-permute-start.8 = (f32[8,12,256]{2,1,0:T(8,128)S(1)}, f32[8,12,256]{2,1,0:T(8,128)S(1)}, u32[]{:S(2)}, u32[]{:S(2)}) collective-permute-start(f32[8,12,256]{2,1,0:T(8,128)S(1)} %get-tuple-element.35), channel_id=1, source_target_pairs={{0,2},{2,0},{1,3},{3,1},{4,6},{6,4},{5,7},{7,5},{8,10},{10,8},{9,1... | collective-permute-start | bytes 294920 | tf_op jit(solution)/shard_map/ppermute | solution.py:509

commit v8 on v7

--- a/solution.py
+++ b/solution.py
@@ -490,9 +490,8 @@
     first = pack_first(boxes, coarse, move_dest, parent, edge, box_count)
     arrived = [first[0]] + [send(first[turn], turn) for turn in range(1, box_count)]
     stay, *rest = pack_later((0,) + tuple(range(2, last)), boxes, move_dest, box_count)
-    held, arrived[last] = lax.optimization_barrier((tuple(rest), arrived[last]))
-    rest = list(held)
-    rest = [send(piece, n + 2) for n, piece in enumerate(rest)] + [send(fill[1], last, outer)]
+    held, *arrived[last - 1 :] = lax.optimization_barrier((rest + [fill[1]], *arrived[last - 1 :]))
+    rest = [send(piece, n + 2) for n, piece in enumerate(held[:-1])] + [send(held[-1], last, outer)]
     now, moved, *facing = arrive(arrived, stay, slabs)
     now, *fillers = lax.optimization_barrier((now, *fillers))
 

time: 74.2 us -> 73.3 us (0.988)
  waiting for transfers between devices: 37.2 us -> 29.7 us
  starting transfers between devices: 14.2 us -> 20.9 us
    ppermute x7, waiting for transfers between devices: 30.8 us -> 22.7 us  [send(): lax.ppermute(piece, 'box', [(s, partner(s, turn, box_count)) for s in mem...]
    ppermute x7, starting transfers between devices: 12 us -> 19.2 us  [send(): lax.ppermute(piece, 'box', [(s, partner(s, turn, box_count)) for s in mem...]
    ppermute x1, waiting for transfers between devices: 3.2 us -> 4.06 us  [body(): lax.ppermute(facing[0], ('slab', 'fld'), crossed)]
  transfers between devices with their start and end apart: 10 -> 10, of which waited for: 5 -> 4; matrix products, arithmetic and copies ran while one was open for 1% -> 1% of each run, Pallas kernels for 20% -> 21%
where the time goes in v8:
time: 73.3 us; the launch traced here: 72.9 us
  waiting for transfers between devices  29.7 us (41%)
  starting transfers between devices  20.9 us (29%)
  Pallas kernels  18.9 us (26%)
  local copies, waits for them, and re-layouts  2.13 us (3%)
  between operations  0.86 us (1%)
    ppermute x7, waiting for transfers between devices, send(): lax.ppermute(piece, 'box', [(s, partner(s, turn, box_count)) for s in mem...  22.7 us
    ppermute x7, starting transfers between devices, send(): lax.ppermute(piece, 'box', [(s, partner(s, turn, box_count)) for s in mem...  19.2 us
    pallas_call x1, Pallas kernels, body(): pl.pallas_call(functools.partial(slope_kernel, edge, planes, fields, coar...  7.89 us
    pallas_call x2, Pallas kernels, pack_later(): pl.pallas_call(functools.partial(later_kernel, turns, per_device, box_cou...  5.69 us
    ppermute x1, waiting for transfers between devices, body(): lax.ppermute(facing[0], ('slab', 'fld'), crossed)  4.06 us
    pallas_call x1, Pallas kernels, pack_first(): pl.pallas_call(functools.partial(first_kernel, per_device, box_count, edg...  2.94 us
    ppermute x1, waiting for transfers between devices, body(): lax.ppermute(facing[0], 'slab', swap)  2.9 us
    unnamed x22, local copies, waits for them, and re-layouts  2.06 us
  transfers between devices with their start and end apart: 10, of which 4 were waited for; matrix products, arithmetic and copies ran while one was open for 1% of the time, Pallas kernels for 21%

profile of v8, /device:TPU:0, one launch (start us, length us, event | category | flops | bytes accessed | tf_op | source)
XLA Modules:
  0.0 72.9 jit_solution(13887753998688088978)
XLA Ops:
  0.6 2.8 %shard_map.115 = (f32[2,2,12,8,256]{4,3,2,1,0:T(8,128)}, f32[2,2,12,8,256]{4,3,2,1,0:T(8,128)}) custom-call(s32[16]{0:T(128)} %dest_ref.7, f32[3,4,12,8,256]{4,3,2,1,0:T(8,128)} %boxes_ref.5), custom_call_target="tpu_custom_call" | custom-call | bytes 2359296 | tf_op jit(solution)/shard_map/pallas_call | solution.py:191
  3.4 0.0 copy-start.7
  3.4 0.0 copy-start.8
  3.4 0.0 copy-start.9
  3.4 0.0 copy-start.10
  3.4 0.0 copy-start.6
  3.5 3.1 %collective-permute-start.3 = (f32[2,2,12,8,256]{4,3,2,1,0:T(8,128)}, f32[2,2,12,8,256]{4,3,2,1,0:T(8,128)S(1)}, u32[]{:S(2)}, u32[]{:S(2)}) collective-permute-start(f32[2,2,12,8,256]{4,3,2,1,0:T(8,128)} %get-tuple-element.32), channel_id=1, source_target_pairs={{0,4},{4,0},{8,12},{12,8},{1,5},{5,1},{9,13},{13,9},{2,6},{6,2},{1... | collective-permute-start | bytes 1179656 | tf_op jit(solution)/shard_map/ppermute | solution.py:483
  6.6 0.7 collective-permute-start.4
  7.3 0.0 copy-start.5
  7.3 0.0 copy-start.2
  7.3 0.0 copy-start.3
  7.3 0.0 copy-start.4
  7.3 2.9 %shard_map.113 = (f32[2,14,8,256]{3,2,1,0:T(8,128)}, f32[2,14,8,256]{3,2,1,0:T(8,128)}, f32[2,14,8,256]{3,2,1,0:T(8,128)}, f32[2,14,8,256]{3,2,1,0:T(8,128)}) custom-call(s32[16]{0:T(128)} %dest_ref.7, s32[16]{0:T(128)} %parent_ref.3, f32[3,4,12,8,256]{4,3,2,1,0:T(8,128)} %boxes_ref.5, f32[12,8,1000]{2,1,0:T(8,128)} %bitcast.11), custom_call_target="tpu_custom_call" | custom-call | flops 147456000 | bytes 2743296 | tf_op jit(solution)/shard_map/pallas_call | solution.py:129
  10.3 3.9 %collective-permute-start.1 = (f32[2,14,8,256]{3,2,1,0:T(8,128)}, f32[2,14,8,256]{3,2,1,0:T(8,128)S(1)}, u32[]{:S(2)}, u32[]{:S(2)}) collective-permute-start(f32[2,14,8,256]{3,2,1,0:T(8,128)} %get-tuple-element.26), channel_id=1, source_target_pairs={{0,8},{4,12},{8,0},{12,4},{1,9},{5,13},{9,1},{13,5},{2,10},{6,14},... | collective-permute-start | bytes 688136 | tf_op jit(solution)/shard_map/ppermute | solution.py:483
  14.2 2.9 %collective-permute-start.2 = (f32[2,14,8,256]{3,2,1,0:T(8,128)}, f32[2,14,8,256]{3,2,1,0:T(8,128)S(1)}, u32[]{:S(2)}, u32[]{:S(2)}) collective-permute-start(f32[2,14,8,256]{3,2,1,0:T(8,128)} %get-tuple-element.27), channel_id=1, source_target_pairs={{0,12},{4,8},{8,4},{12,0},{1,13},{5,9},{9,5},{13,1},{2,14},{6,10},... | collective-permute-start | bytes 688136 | tf_op jit(solution)/shard_map/ppermute | solution.py:483
  17.1 0.0 collective-permute-start
  17.1 2.9 %shard_map.114 = (f32[3,2,12,8,256]{4,3,2,1,0:T(8,128)}, f32[2,2,12,8,256]{4,3,2,1,0:T(8,128)}) custom-call(s32[16]{0:T(128)} %dest_ref.7, f32[3,4,12,8,256]{4,3,2,1,0:T(8,128)} %boxes_ref.5), custom_call_target="tpu_custom_call" | custom-call | bytes 2359296 | tf_op jit(solution)/shard_map/pallas_call | solution.py:191
  20.0 16.0 %collective-permute-done.1.refs_2_ = f32[2,14,8,256]{3,2,1,0:T(8,128)S(1)} collective-permute-done((f32[2,14,8,256]{3,2,1,0:T(8,128)}, f32[2,14,8,256]{3,2,1,0:T(8,128)S(1)}, u32[]{:S(2)}, u32[]{:S(2)}) %collective-permute-start.1) | collective-permute-done | bytes 229408 | tf_op jit(solution)/shard_map/ppermute | solution.py:483
  36.0 0.0 collective-permute-done.2.refs_3_
  36.0 0.0 collective-permute-done.refs_1_
  36.0 1.1 %copy-done = f32[3,2,12,8,256]{4,3,2,1,0:T(8,128)S(1)} copy-done((f32[3,2,12,8,256]{4,3,2,1,0:T(8,128)S(1)}, f32[3,2,12,8,256]{4,3,2,1,0:T(8,128)}, u32[]{:S(2)}) %copy-start) | copy-done | bytes 589848
  37.1 0.9 %copy-done.1 = f32[2,14,8,256]{3,2,1,0:T(8,128)S(1)} copy-done((f32[2,14,8,256]{3,2,1,0:T(8,128)S(1)}, f32[2,14,8,256]{3,2,1,0:T(8,128)}, u32[]{:S(2)}) %copy-start.1) | copy-done | bytes 229400
  38.0 1.3 %shard_map.116 = (f32[8,14,8,256]{3,2,1,0:T(8,128)S(1)}, f32[3,8,12,8,256]{4,3,2,1,0:T(8,128)}, f32[8,12,256]{2,1,0:T(8,128)S(1)}) custom-call(f32[2,14,8,256]{3,2,1,0:T(8,128)S(1)} %copy-done.1, f32[2,14,8,256]{3,2,1,0:T(8,128)S(1)} %collective-permute-done.refs_1_, f32[2,14,8,256]{3,2,1,0:T(8,128)S(1)} %collective-permute-done.1.refs_2_, ...), custom_call_target="tpu_custom_call" | custom-call | bytes 2752512 | tf_op jit(solution)/shard_map/pallas_call | solution.py:291
  39.3 0.0 collective-permute-done.3.refs_0_
  39.3 0.0 collective-permute-done.4.refs_3_
  39.3 0.1 collective-permute-start.7
  39.4 0.0 copy-done.7
  39.4 0.0 copy-done.8
  39.4 0.0 copy-done.9
  39.5 0.1 fusion.7
  39.6 5.5 %collective-permute-start.5 = (f32[2,2,12,8,256]{4,3,2,1,0:T(8,128)}, f32[2,2,12,8,256]{4,3,2,1,0:T(8,128)S(1)}, u32[]{:S(2)}, u32[]{:S(2)}) collective-permute-start(f32[2,2,12,8,256]{4,3,2,1,0:T(8,128)} %get-tuple-element.34), channel_id=1, source_target_pairs={{0,8},{4,12},{8,0},{12,4},{1,9},{5,13},{9,1},{13,5},{2,10},{6,14},... | collective-permute-start | bytes 1179656 | tf_op jit(solution)/shard_map/ppermute | solution.py:483
  45.1 0.0 copy-done.10
  45.1 3.1 %collective-permute-start.6 = (f32[2,2,12,8,256]{4,3,2,1,0:T(8,128)S(1)}, f32[2,2,12,8,256]{4,3,2,1,0:T(8,128)S(1)}, u32[]{:S(2)}, u32[]{:S(2)}) collective-permute-start(f32[2,2,12,8,256]{4,3,2,1,0:T(8,128)S(1)} %copy-done.10), channel_id=1, source_target_pairs={{0,12},{12,0},{1,13},{13,1},{2,14},{14,2},{3,15},{15,3},{16,28},{2... | collective-permute-start | bytes 1179656 | tf_op jit(solution)/shard_map/ppermute | solution.py:483
  48.2 0.0 copy-done.6
  48.2 0.4 fusion.2
  48.5 1.1 %collective-permute-start.9 = (f32[8,12,256]{2,1,0:T(8,128)S(1)}, f32[8,12,256]{2,1,0:T(8,128)S(1)}, u32[]{:S(2)}, u32[]{:S(2)}) collective-permute-start(f32[8,12,256]{2,1,0:T(8,128)S(1)} %get-tuple-element.39), channel_id=1, source_target_pairs={{0,3},{3,0},{1,2},{2,1},{4,7},{7,4},{5,6},{6,5},{8,11},{11,8},{9,1... | collective-permute-start | bytes 294920 | tf_op jit(solution)/shard_map/ppermute | solution.py:508
  49.6 0.6 collective-permute-start.8
  50.2 0.0 copy-done.5
  50.2 0.1 multiply_reduce_fusion
  50.3 4.1 %collective-permute-done.9.other_low.other_high = f32[8,12,256]{2,1,0:T(8,128)S(1)} collective-permute-done((f32[8,12,256]{2,1,0:T(8,128)S(1)}, f32[8,12,256]{2,1,0:T(8,128)S(1)}, u32[]{:S(2)}, u32[]{:S(2)}) %collective-permute-start.9) | collective-permute-done | bytes 98336 | tf_op jit(solution)/shard_map/ppermute | solution.py:508
  54.3 2.9 %collective-permute-done.8.own_low.own_high = f32[8,12,256]{2,1,0:T(8,128)S(1)} collective-permute-done((f32[8,12,256]{2,1,0:T(8,128)S(1)}, f32[8,12,256]{2,1,0:T(8,128)S(1)}, u32[]{:S(2)}, u32[]{:S(2)}) %collective-permute-start.8) | collective-permute-done | bytes 98336 | tf_op jit(solution)/shard_map/ppermute | solution.py:508
  57.2 0.0 collective-permute-done.7.other_ref
  57.2 0.0 copy-done.2
  57.2 0.0 copy-done.3
  57.2 7.9 %shard_map.117 = (f32[8,12,8,256]{3,2,1,0:T(8,128)}, f32[8,128]{1,0:T(8,128)S(1)}) custom-call(s32[16]{0:T(128)S(1)} %copy-done.2, s32[16]{0:T(128)S(1)} %copy-done.3, f32[8,14,8,256]{3,2,1,0:T(8,128)S(1)} %get-tuple-element.38.own_ref, f32[8,14,8,256]{3,2,1,0:T(8,128)S(1)} %collective-permute-done.7.other_ref, ...), custom_call_target="tpu_custom_call" | custom-call | flops 2113929216 | bytes 2752512 | tf_op jit(solution)/shard_map/pallas_call | solution.py:515
  65.1 6.8 %collective-permute-done.5.refs_1_ = f32[2,2,12,8,256]{4,3,2,1,0:T(8,128)S(1)} collective-permute-done((f32[2,2,12,8,256]{4,3,2,1,0:T(8,128)}, f32[2,2,12,8,256]{4,3,2,1,0:T(8,128)S(1)}, u32[]{:S(2)}, u32[]{:S(2)}) %collective-permute-start.5) | collective-permute-done | bytes 393248 | tf_op jit(solution)/shard_map/ppermute | solution.py:483
  71.9 0.0 collective-permute-done.6.refs_2_
  71.9 1.0 %shard_map.118 = f32[3,8,12,8,256]{4,3,2,1,0:T(8,128)} custom-call(f32[2,2,12,8,256]{4,3,2,1,0:T(8,128)S(1)} %collective-permute-done.3.refs_0_, f32[2,2,12,8,256]{4,3,2,1,0:T(8,128)S(1)} %collective-permute-done.5.refs_1_, f32[2,2,12,8,256]{4,3,2,1,0:T(8,128)S(1)} %collective-permute-done.6.refs_2_, ...), custom_call_target="tpu_custom_call", output_to_operand_aliasing={{}: (4, {})} | custom-call | bytes 3145728 | tf_op jit(solution)/shard_map/pallas_call | solution.py:237
  (5 shorter events, 0.0 us)
Async XLA Ops:
  3.4 36.0 %copy-start.7 = (f32[24,24]{1,0:T(8,128)S(1)}, f32[24,24]{1,0:T(8,128)}, u32[]{:S(2)}) copy-start(f32[24,24]{1,0:T(8,128)} %param.14) | copy-start | bytes 6916
  3.4 36.0 %copy-start.8 = (f32[24,24]{1,0:T(8,128)S(1)}, f32[24,24]{1,0:T(8,128)}, u32[]{:S(2)}) copy-start(f32[24,24]{1,0:T(8,128)} %param.15) | copy-start | bytes 6916
  3.4 36.0 %copy-start.9 = (f32[24,24]{1,0:T(8,128)S(1)}, f32[24,24]{1,0:T(8,128)}, u32[]{:S(2)}) copy-start(f32[24,24]{1,0:T(8,128)} %param.16) | copy-start | bytes 6916
  3.4 41.6 %copy-start.10 = (f32[2,2,12,8,256]{4,3,2,1,0:T(8,128)S(1)}, f32[2,2,12,8,256]{4,3,2,1,0:T(8,128)}, u32[]{:S(2)}) copy-start(f32[2,2,12,8,256]{4,3,2,1,0:T(8,128)} %get-tuple-element.35) | copy-start | bytes 1179652
  3.4 44.7 %copy-start.6 = (f32[24,896,1]{1,0,2:T(8,128)S(1)}, f32[24,896,1]{1,0,2:T(8,128)}, u32[]{:S(2)}) copy-start(f32[24,896,1]{1,0,2:T(8,128)} %constant.27) | copy-start | bytes 258052
  3.5 35.9 %collective-permute-start.3 = (f32[2,2,12,8,256]{4,3,2,1,0:T(8,128)}, f32[2,2,12,8,256]{4,3,2,1,0:T(8,128)S(1)}, u32[]{:S(2)}, u32[]{:S(2)}) collective-permute-start(f32[2,2,12,8,256]{4,3,2,1,0:T(8,128)} %get-tuple-element.32), channel_id=1, source_target_pairs={{0,4},{4,0},{8,12},{12,8},{1,5},{5,1},{9,13},{13,9},{2,6},{6,2},{1... | collective-permute-start | bytes 1179656 | tf_op jit(solution)/shard_map/ppermute | solution.py:483
  6.6 32.8 %collective-permute-start.4 = (f32[2,2,12,8,256]{4,3,2,1,0:T(8,128)}, f32[2,2,12,8,256]{4,3,2,1,0:T(8,128)S(1)}, u32[]{:S(2)}, u32[]{:S(2)}) collective-permute-start(f32[2,2,12,8,256]{4,3,2,1,0:T(8,128)} %get-tuple-element.35), channel_id=1, source_target_pairs={{4,8},{8,4},{5,9},{9,5},{6,10},{10,6},{7,11},{11,7},{20,24},{24,20... | collective-permute-start | bytes 1179656 | tf_op jit(solution)/shard_map/ppermute | solution.py:483
  7.3 42.9 %copy-start.5 = (f32[3,8,896]{2,1,0:T(8,128)S(1)}, f32[3,8,896]{2,1,0:T(8,128)}, u32[]{:S(2)}) copy-start(f32[3,8,896]{2,1,0:T(8,128)} %constant.23.clone) | copy-start | bytes 258052
  7.3 49.9 %copy-start.2 = (s32[16]{0:T(128)S(1)}, s32[16]{0:T(128)}, u32[]{:S(2)}) copy-start(s32[16]{0:T(128)} %dest_ref.7) | copy-start | bytes 196
  7.3 49.9 %copy-start.3 = (s32[16]{0:T(128)S(1)}, s32[16]{0:T(128)}, u32[]{:S(2)}) copy-start(s32[16]{0:T(128)} %parent_ref.3) | copy-start | bytes 196
  7.3 49.9 %copy-start.4 = (bf16[256,2304]{1,0:T(8,128)(2,1)S(1)}, bf16[256,2304]{1,0:T(8,128)(2,1)}, u32[]{:S(2)}) copy-start(bf16[256,2304]{1,0:T(8,128)(2,1)} %constant.26.spread_ref) | copy-start | bytes 3538948
  10.3 25.7 %collective-permute-start.1 = (f32[2,14,8,256]{3,2,1,0:T(8,128)}, f32[2,14,8,256]{3,2,1,0:T(8,128)S(1)}, u32[]{:S(2)}, u32[]{:S(2)}) collective-permute-start(f32[2,14,8,256]{3,2,1,0:T(8,128)} %get-tuple-element.26), channel_id=1, source_target_pairs={{0,8},{4,12},{8,0},{12,4},{1,9},{5,13},{9,1},{13,5},{2,10},{6,14},... | collective-permute-start | bytes 688136 | tf_op jit(solution)/shard_map/ppermute | solution.py:483
  14.2 21.8 %collective-permute-start.2 = (f32[2,14,8,256]{3,2,1,0:T(8,128)}, f32[2,14,8,256]{3,2,1,0:T(8,128)S(1)}, u32[]{:S(2)}, u32[]{:S(2)}) collective-permute-start(f32[2,14,8,256]{3,2,1,0:T(8,128)} %get-tuple-element.27), channel_id=1, source_target_pairs={{0,12},{4,8},{8,4},{12,0},{1,13},{5,9},{9,5},{13,1},{2,14},{6,10},... | collective-permute-start | bytes 688136 | tf_op jit(solution)/shard_map/ppermute | solution.py:483
  17.1 18.9 %collective-permute-start = (f32[2,14,8,256]{3,2,1,0:T(8,128)}, f32[2,14,8,256]{3,2,1,0:T(8,128)S(1)}, u32[]{:S(2)}, u32[]{:S(2)}) collective-permute-start(f32[2,14,8,256]{3,2,1,0:T(8,128)} %get-tuple-element.23), channel_id=1, source_target_pairs={{0,4},{4,0},{8,12},{12,8},{1,5},{5,1},{9,13},{13,9},{2,6},{6,2},{1... | collective-permute-start | bytes 688136 | tf_op jit(solution)/shard_map/ppermute | solution.py:483
  36.0 1.1 %copy-start = (f32[3,2,12,8,256]{4,3,2,1,0:T(8,128)S(1)}, f32[3,2,12,8,256]{4,3,2,1,0:T(8,128)}, u32[]{:S(2)}) copy-start(f32[3,2,12,8,256]{4,3,2,1,0:T(8,128)} %get-tuple-element.30.refs_4_) | copy-start | bytes 1769476
  37.1 0.9 %copy-start.1 = (f32[2,14,8,256]{3,2,1,0:T(8,128)S(1)}, f32[2,14,8,256]{3,2,1,0:T(8,128)}, u32[]{:S(2)}) copy-start(f32[2,14,8,256]{3,2,1,0:T(8,128)} %get-tuple-element.22.refs_0_) | copy-start | bytes 688132
  39.3 17.9 %collective-permute-start.7 = (f32[8,14,8,256]{3,2,1,0:T(8,128)S(1)}, f32[8,14,8,256]{3,2,1,0:T(8,128)S(1)}, u32[]{:S(2)}, u32[]{:S(2)}) collective-permute-start(f32[8,14,8,256]{3,2,1,0:T(8,128)S(1)} %get-tuple-element.38.own_ref), channel_id=1, source_target_pairs={{0,1},{1,0},{2,3},{3,2},{4,5},{5,4},{6,7},{7,6},{8,9},{9,8},{10,11... | collective-permute-start | bytes 2752520 | tf_op jit(solution)/shard_map/ppermute | solution.py:499
  39.6 32.3 %collective-permute-start.5 = (f32[2,2,12,8,256]{4,3,2,1,0:T(8,128)}, f32[2,2,12,8,256]{4,3,2,1,0:T(8,128)S(1)}, u32[]{:S(2)}, u32[]{:S(2)}) collective-permute-start(f32[2,2,12,8,256]{4,3,2,1,0:T(8,128)} %get-tuple-element.34), channel_id=1, source_target_pairs={{0,8},{4,12},{8,0},{12,4},{1,9},{5,13},{9,1},{13,5},{2,10},{6,14},... | collective-permute-start | bytes 1179656 | tf_op jit(solution)/shard_map/ppermute | solution.py:483
  45.1 26.8 %collective-permute-start.6 = (f32[2,2,12,8,256]{4,3,2,1,0:T(8,128)S(1)}, f32[2,2,12,8,256]{4,3,2,1,0:T(8,128)S(1)}, u32[]{:S(2)}, u32[]{:S(2)}) collective-permute-start(f32[2,2,12,8,256]{4,3,2,1,0:T(8,128)S(1)} %copy-done.10), channel_id=1, source_target_pairs={{0,12},{12,0},{1,13},{13,1},{2,14},{14,2},{3,15},{15,3},{16,28},{2... | collective-permute-start | bytes 1179656 | tf_op jit(solution)/shard_map/ppermute | solution.py:483
  48.5 5.8 %collective-permute-start.9 = (f32[8,12,256]{2,1,0:T(8,128)S(1)}, f32[8,12,256]{2,1,0:T(8,128)S(1)}, u32[]{:S(2)}, u32[]{:S(2)}) collective-permute-start(f32[8,12,256]{2,1,0:T(8,128)S(1)} %get-tuple-element.39), channel_id=1, source_target_pairs={{0,3},{3,0},{1,2},{2,1},{4,7},{7,4},{5,6},{6,5},{8,11},{11,8},{9,1... | collective-permute-start | bytes 294920 | tf_op jit(solution)/shard_map/ppermute | solution.py:508
  49.6 7.6 %collective-permute-start.8 = (f32[8,12,256]{2,1,0:T(8,128)S(1)}, f32[8,12,256]{2,1,0:T(8,128)S(1)}, u32[]{:S(2)}, u32[]{:S(2)}) collective-permute-start(f32[8,12,256]{2,1,0:T(8,128)S(1)} %get-tuple-element.39), channel_id=1, source_target_pairs={{0,2},{2,0},{1,3},{3,1},{4,6},{6,4},{5,7},{7,5},{8,10},{10,8},{9,1... | collective-permute-start | bytes 294920 | tf_op jit(solution)/shard_map/ppermute | solution.py:508

commit v9 on v6

--- a/solution.py
+++ b/solution.py
@@ -37,15 +37,19 @@
     lax.fori_loop(0, per_device, place, 0)
 
 
-def partner(own, turn, box_count):
-    return own ^ turn
+def target_of(own, turn, box_count):
+    return lax.rem(own + turn, box_count)
+
+
+def source_of(own, turn, box_count):
+    return lax.rem(own - turn + box_count, box_count)
 
 
 def each_slot(box_count):
     own = lax.axis_index("box")
     for turn in range(box_count):
         for k in range(2):
-            yield turn, k, 2 * partner(own, turn, box_count) + k
+            yield turn, k, 2 * target_of(own, turn, box_count) + k
 
 
 def first_kernel(per_device, box_count, edge, dest_ref, parent_ref, boxes_ref, coarse_ref, *refs):
@@ -147,72 +151,75 @@
     )(move_dest, parent, boxes, coarse)
 
 
-def later_kernel(per_device, box_count, levels, dest_ref, boxes_ref, after_ref, *refs):
-    outs, moved_ref = refs[: box_count - 1], refs[box_count - 1]
-    stay, dest, table, sems, in_sem, out_sem = refs[box_count:]
+def later_kernel(turns, per_device, box_count, levels, dest_ref, boxes_ref, *refs):
+    outs, (dest, table, sems, in_sem, *stay) = refs[: len(turns)], refs[len(turns) :]
     own = lax.axis_index("box")
     fetch = pltpu.make_async_copy(dest_ref, dest, in_sem)
     fetch.start()
     fetch.wait()
     place_boxes(per_device, box_count, dest, table)
-
-    def copies(turn, k, b):
-        for n in range(0 if turn == 0 else 1, levels):
-            to = stay.at[n, k] if turn == 0 else outs[turn - 1].at[n - 1, k]
-            yield pltpu.make_async_copy(boxes_ref.at[n, b], to, sems.at[n, turn, k])
-
-    for turn, k, slot in each_slot(box_count):
+    places = [(n, k, 2 * target_of(own, turn, box_count) + k) for n, turn in enumerate(turns) for k in range(2)]
+    held = [stay[0] if turn == 0 else out for turn, out in zip(turns, outs)]
+
+    def copies(n, k, b):
+        skip = levels - held[n].shape[0]
+        for level in range(skip, levels):
+            yield pltpu.make_async_copy(boxes_ref.at[level, b], held[n].at[level - skip, k], sems.at[n, level, k])
+
+    for n, k, slot in places:
         b = table[slot]
 
         @pl.when(b >= 0)
         def _():
-            for copy in copies(turn, k, b):
+            for copy in copies(n, k, b):
                 copy.start()
 
         @pl.when(b < 0)
         def _():
-            to = stay if turn == 0 else outs[turn - 1]
-            for n in range(to.shape[0]):
-                to[n, k] = jnp.zeros(to.shape[2:], jnp.float32)
-
-    for turn, k, slot in each_slot(box_count):
+            for level in range(held[n].shape[0]):
+                held[n][level, k] = jnp.zeros(held[n].shape[2:], jnp.float32)
+
+    for n, k, slot in places:
         b = table[slot]
 
         @pl.when(b >= 0)
         def _():
-            for copy in copies(turn, k, b):
+            for copy in copies(n, k, b):
                 copy.wait()
 
-        if (turn, k) == (0, 1):
-            settled = pltpu.make_async_copy(stay, moved_ref.at[:, pl.ds(2 * own, 2)], out_sem)
+    for n, turn in enumerate(turns):
+        if turn == 0:
+            settled = pltpu.make_async_copy(held[n], outs[n].at[:, pl.ds(2 * own, 2)], in_sem)
             settled.start()
-    settled.wait()
-
-
-def pack_later(boxes, move_dest, after, box_count):
+            settled.wait()
+
+
+def pack_later(turns, boxes, move_dest, box_count):
     levels, per_device = boxes.shape[:2]
     item = boxes.shape[2:]
     hbm, vmem = pl.BlockSpec(memory_space=pltpu.HBM), pl.BlockSpec(memory_space=pltpu.VMEM)
+    size = int(np.prod(item)) * 4
+    shapes = [(levels - 1, 2) + item if turn else (levels, 2 * box_count) + item for turn in turns]
     return pl.pallas_call(
-        functools.partial(later_kernel, per_device, box_count, levels),
-        out_shape=[jax.ShapeDtypeStruct((levels - 1, 2) + item, jnp.float32)] * (box_count - 1)
-        + [jax.ShapeDtypeStruct((levels, 2 * box_count) + item, jnp.float32)],
-        in_specs=[hbm] * 3,
-        out_specs=[vmem] * (box_count - 1) + [hbm],
+        functools.partial(later_kernel, turns, per_device, box_count, levels),
+        out_shape=[jax.ShapeDtypeStruct(shape, jnp.float32) for shape in shapes],
+        in_specs=[hbm] * 2,
+        out_specs=[vmem if turn else hbm for turn in turns],
         scratch_shapes=[
-            pltpu.VMEM((levels, 2) + item, jnp.float32),
             pltpu.SMEM(move_dest.shape, jnp.int32),
             pltpu.SMEM((2 * box_count,), jnp.int32),
-            pltpu.SemaphoreType.DMA((levels, box_count, 2)),
+            pltpu.SemaphoreType.DMA((len(turns), levels, 2)),
             pltpu.SemaphoreType.DMA,
-            pltpu.SemaphoreType.DMA,
-        ],
-        cost_estimate=pl.CostEstimate(flops=0, bytes_accessed=12 * boxes.size, transcendentals=0),
-    )(move_dest, boxes, after)
+        ]
+        + [pltpu.VMEM((levels, 2) + item, jnp.float32) for turn in turns if turn == 0],
+        cost_estimate=pl.CostEstimate(
+            flops=0, bytes_accessed=4 * len(turns) * levels * size, transcendentals=0
+        ),
+    )(move_dest, boxes)
 
 
 def settle_later(piece, turn, moved_ref, sem):
-    source = partner(lax.axis_index("box"), turn, moved_ref.shape[1] // 2)
+    source = source_of(lax.axis_index("box"), turn, moved_ref.shape[1] // 2)
     to = moved_ref.at[pl.ds(1, moved_ref.shape[0] - 1), pl.ds(2 * source, 2)]
     return pltpu.make_async_copy(piece, to, sem)
 
@@ -252,7 +259,7 @@
     mine.start()
     copies = []
     for turn in range(1, box_count):
-        to = moved_ref.at[0, pl.ds(2 * partner(own, turn, box_count), 2)]
+        to = moved_ref.at[0, pl.ds(2 * source_of(own, turn, box_count), 2)]
         copies.append(pltpu.make_async_copy(pieces[turn].at[:, pl.ds(0, fields)], to, sems.at[turn]))
     for n, turn in enumerate(early):
         copies.append(settle_later(later[n], turn, moved_ref, sems.at[box_count + n]))
@@ -267,7 +274,7 @@
                     edge_ref[2 * source + k, f : f + 1] = now_ref[2 * source + k, f, pl.ds(plane, 1)]
 
     for turn in range(1, box_count):
-        source = partner(own, turn, box_count)
+        source = source_of(own, turn, box_count)
         for k in range(2):
             now_ref[2 * source + k] = pieces[turn][k]
         cut(source)
@@ -369,7 +376,7 @@
 def slope_kernel(
     edge, planes, fields, coarse_planes, per_device, total, coarse_count, slots, slabs,
     dest_ref, parent_ref, own_ref, other_ref, own_low, other_low, own_high, other_high,
-    spread_ref, weight_ref, out_ref, token_ref, stack, ghosts, table, count,
+    spread_ref, weight_ref, out_ref, token_ref, stack, parts, ghosts, table, count,
 ):
     step = pl.program_id(0)
     cross = edge * edge
@@ -380,6 +387,10 @@
     def _():
         token_ref[...] = jnp.zeros_like(token_ref)
         stack[...] = jnp.zeros_like(stack)
+        half = weight_ref.shape[0]
+        weights = weight_ref[...]
+        parts[:half] = weights.astype(jnp.bfloat16)
+        parts[half:] = (weights - weights.astype(jnp.bfloat16).astype(jnp.float32)).astype(jnp.bfloat16)
         for slot in range(slots):
             table[slot] = -1
             count[slot] = 0
@@ -449,12 +460,18 @@
         base += 4 * ROWS
         for n in range(2 * coarse_planes):
             stack[base + 2 * ROWS * n : base + 2 * ROWS * (n + 1)] = rim[:, n * cross : (n + 1) * cross]
-        mixed = jnp.dot(weight_ref[...], stack[...], precision=HIGHEST, preferred_element_type=jnp.float32)
+        values = stack[...]
+        high = values.astype(jnp.bfloat16)
+        low = (values - high.astype(jnp.float32)).astype(jnp.bfloat16)
+        half = weight_ref.shape[0]
+        both = jnp.dot(parts[...], high, preferred_element_type=jnp.float32)
+        mixed = jnp.dot(parts[:half], low, preferred_element_type=jnp.float32)
+        mixed = both[:half] + (both[half:] + mixed)
         if planes % 8:
             for f in range(fields):
                 out_ref[0, f] = mixed[f * planes : (f + 1) * planes]
         else:
-            out_ref[0] = mixed.reshape(fields, planes, cross)
+            out_ref[0] = mixed[:rows].reshape(fields, planes, cross)
 
 
 def mixing_weights(mixes, group, fields, planes, coarse_planes):
@@ -464,7 +481,8 @@
     terms = lax.dynamic_slice_in_dim(terms, group * fields, fields, 1)
     terms = jnp.where(group == 0, terms, jnp.roll(terms, fields, axis=2))
     terms = jnp.einsum("tfg,gk->tfk", terms, jnp.asarray(select), precision=HIGHEST)
-    return jnp.sum(terms[:, :, None, :] * jnp.asarray(masks)[:, None], axis=0).reshape(fields * planes, -1)
+    weight = jnp.sum(terms[:, :, None, :] * jnp.asarray(masks)[:, None], axis=0).reshape(fields * planes, -1)
+    return jnp.pad(weight, ((0, round_up(fields * planes, 16) - fields * planes), (0, 0)))
 
 
 def body(boxes, move_dest, parent, coarse, lap_mix, grad_mix, damp_mix):
@@ -479,27 +497,28 @@
     coarse_count = coarse.shape[0]
 
     def send(piece, turn):
-        return lax.ppermute(piece, "box", [(s, partner(s, turn, box_count)) for s in range(box_count)])
-
+        return lax.ppermute(piece, "box", [(s, (s + turn) % box_count) for s in range(box_count)])
+
+    near = pack_later((1, box_count - 1), boxes, move_dest, box_count)
+    near = [send(near[0], 1), send(near[1], box_count - 1)]
     first = pack_first(boxes, coarse, move_dest, parent, edge, box_count)
     arrived = [first[0]] + [send(first[turn], turn) for turn in range(1, box_count)]
-    *later, moved = pack_later(boxes, move_dest, first[0], box_count)
-    later = [send(piece, n + 1) for n, piece in enumerate(later)]
-    now, moved, *facing = arrive(arrived, (1,), later[:1], moved, slabs)
+    moved, *middle = pack_later((0,) + tuple(range(2, box_count - 1)), boxes, move_dest, box_count)
+    middle, arrived[1:] = lax.optimization_barrier((middle, arrived[1:]))
+    middle = [send(piece, n + 2) for n, piece in enumerate(middle)]
+    later_arrived = [near[0]] + middle + [near[1]]
+    now, moved, *facing = arrive(arrived, (), [], moved, slabs)
 
     swap = [(0, 1), (1, 0)]
     now_other = lax.ppermute(now, "fld", swap)
 
     def shifted(values, up):
         pairs = [(s, s + 1) if up else (s + 1, s) for s in range(slabs - 1)]
-        crossed = [(2 * a + f, 2 * b + 1 - f) for a, b in pairs for f in range(2)]
-        return lax.ppermute(values, "slab", pairs), lax.ppermute(values, ("slab", "fld"), crossed)
-
-    if slabs == 2:
-        crossed = [(0, 3), (3, 0), (1, 2), (2, 1)]
-        low = high = (lax.ppermute(facing[0], "slab", swap), lax.ppermute(facing[0], ("slab", "fld"), crossed))
-    else:
-        low, high = shifted(facing[1], True), shifted(facing[0], False)
+        own_group = lax.ppermute(values, "slab", swap if slabs == 2 else pairs)
+        return own_group, lax.ppermute(own_group, "fld", swap)
+
+    low = shifted(facing[-1], True)
+    high = low if slabs == 2 else shifted(facing[0], False)
 
     weight = mixing_weights((lap_mix, grad_mix, damp_mix), group, fields, planes, coarse_planes)
     spread = jnp.asarray(expand_table(coarse_planes, edge, cross)).astype(jnp.bfloat16)
@@ -517,16 +536,17 @@
         out_specs=[pl.BlockSpec((1, fields, planes, cross), lambda n: (n, 0, 0, 0)), vmem],
         scratch_shapes=[
             pltpu.VMEM((weight.shape[1], cross), jnp.float32),
+            pltpu.VMEM((2 * weight.shape[0], weight.shape[1]), jnp.bfloat16),
             pltpu.VMEM((2 * ROWS * slots, spread.shape[1]), jnp.float32),
             pltpu.SMEM((slots,), jnp.int32),
             pltpu.SMEM((slots,), jnp.int32),
         ],
         compiler_params=pltpu.CompilerParams(vmem_limit_bytes=48 * 2 ** 20),
         cost_estimate=pl.CostEstimate(
-            flops=12 * slots * weight.size * cross, bytes_accessed=12 * now.size, transcendentals=0
+            flops=3 * slots * weight.size * cross, bytes_accessed=12 * now.size, transcendentals=0
         ),
     )(move_dest, parent, now, now_other, low[0], low[1], high[0], high[1], spread, weight)
-    return settle(tuple(range(2, box_count)), later[1:], moved, token), slope
+    return settle(tuple(range(1, box_count)), later_arrived, moved, token), slope
 
 
 def solution(mesh):

time: 72.9 us -> 64.4 us (0.88)
  the two profiles are of different devices: /device:TPU:17 before, /device:TPU:0 now
where the time goes in v9:
time: 64.4 us; the launch traced here: 64.1 us
  starting transfers between devices  24.7 us (38%)
  Pallas kernels  19.7 us (31%)
  waiting for transfers between devices  18.3 us (28%)
  between operations  0.85 us (1%)
    ppermute x6, starting transfers between devices, send(): lax.ppermute(piece, 'box', [(s, (s + turn) % box_count) for s in range(bo...  22.8 us
    ppermute x6, waiting for transfers between devices, send(): lax.ppermute(piece, 'box', [(s, (s + turn) % box_count) for s in range(bo...  17.1 us
    pallas_call x1, Pallas kernels, body(): pl.pallas_call(functools.partial(slope_kernel, edge, planes, fields, coar...  8.1 us
    pallas_call x2, Pallas kernels, pack_later(): pl.pallas_call(functools.partial(later_kernel, turns, per_device, box_cou...  6.44 us
    pallas_call x1, Pallas kernels, pack_first(): pl.pallas_call(functools.partial(first_kernel, per_device, box_count, edg...  2.99 us
    ppermute x1, starting transfers between devices, shifted(): own_group = lax.ppermute(values, 'slab', swap if slabs == 2 else pairs)  1.72 us
  transfers between devices with their start and end apart: 9, of which 3 were waited for; matrix products, arithmetic and copies ran while one was open for 1% of the time, Pallas kernels for 24%

profile of v9, /device:TPU:0, one launch (start us, length us, event | category | flops | bytes accessed | tf_op | source)
XLA Modules:
  0.0 64.1 jit_solution(12837849791127561152)
XLA Ops:
  0.6 3.0 %shard_map.115 = (f32[2,14,8,256]{3,2,1,0:T(8,128)}, f32[2,14,8,256]{3,2,1,0:T(8,128)}, f32[2,14,8,256]{3,2,1,0:T(8,128)}, f32[2,14,8,256]{3,2,1,0:T(8,128)}) custom-call(s32[16]{0:T(128)} %dest_ref.7, s32[16]{0:T(128)} %parent_ref.3, f32[3,4,12,8,256]{4,3,2,1,0:T(8,128)} %boxes_ref.5, f32[12,8,1000]{2,1,0:T(8,128)} %bitcast.11), custom_call_target="tpu_custom_call" | custom-call | flops 147456000 | bytes 2743296 | tf_op jit(solution)/shard_map/pallas_call | solution.py:133
  3.6 0.0 copy-start.1
  3.6 3.1 %collective-permute-start.1 = (f32[2,14,8,256]{3,2,1,0:T(8,128)}, f32[2,14,8,256]{3,2,1,0:T(8,128)S(1)}, u32[]{:S(2)}, u32[]{:S(2)}) collective-permute-start(f32[2,14,8,256]{3,2,1,0:T(8,128)} %get-tuple-element.21), channel_id=1, source_target_pairs={{0,4},{4,8},{8,12},{12,0},{1,5},{5,9},{9,13},{13,1},{2,6},{6,10},{... | collective-permute-start | bytes 688136 | tf_op jit(solution)/shard_map/ppermute | solution.py:500
  6.7 2.6 %collective-permute-start.2 = (f32[2,14,8,256]{3,2,1,0:T(8,128)}, f32[2,14,8,256]{3,2,1,0:T(8,128)S(1)}, u32[]{:S(2)}, u32[]{:S(2)}) collective-permute-start(f32[2,14,8,256]{3,2,1,0:T(8,128)} %get-tuple-element.22), channel_id=1, source_target_pairs={{0,8},{4,12},{8,0},{12,4},{1,9},{5,13},{9,1},{13,5},{2,10},{6,14},... | collective-permute-start | bytes 688136 | tf_op jit(solution)/shard_map/ppermute | solution.py:500
  9.3 1.3 %collective-permute-start.3 = (f32[2,14,8,256]{3,2,1,0:T(8,128)}, f32[2,14,8,256]{3,2,1,0:T(8,128)S(1)}, u32[]{:S(2)}, u32[]{:S(2)}) collective-permute-start(f32[2,14,8,256]{3,2,1,0:T(8,128)} %get-tuple-element.23), channel_id=1, source_target_pairs={{0,12},{4,0},{8,4},{12,8},{1,13},{5,1},{9,5},{13,9},{2,14},{6,2},{... | collective-permute-start | bytes 688136 | tf_op jit(solution)/shard_map/ppermute | solution.py:500
  10.7 2.8 %shard_map.113 = (f32[2,2,12,8,256]{4,3,2,1,0:T(8,128)}, f32[2,2,12,8,256]{4,3,2,1,0:T(8,128)}) custom-call(s32[16]{0:T(128)} %dest_ref.7, f32[3,4,12,8,256]{4,3,2,1,0:T(8,128)} %boxes_ref.5), custom_call_target="tpu_custom_call" | custom-call | bytes 2359296 | tf_op jit(solution)/shard_map/pallas_call | solution.py:203
  13.5 0.0 copy-start.6
  13.5 0.0 copy-start.7
  13.5 0.0 copy-start.8
  13.5 0.9 %collective-permute-start = (f32[2,2,12,8,256]{4,3,2,1,0:T(8,128)}, f32[2,2,12,8,256]{4,3,2,1,0:T(8,128)S(1)}, u32[]{:S(2)}, u32[]{:S(2)}) collective-permute-start(f32[2,2,12,8,256]{4,3,2,1,0:T(8,128)} %get-tuple-element.19), channel_id=1, source_target_pairs={{0,4},{4,8},{8,12},{12,0},{1,5},{5,9},{9,13},{13,1},{2,6},{6,10},{... | collective-permute-start | bytes 1179656 | tf_op jit(solution)/shard_map/ppermute | solution.py:500
  14.4 3.0 %collective-permute-start.5 = (f32[2,2,12,8,256]{4,3,2,1,0:T(8,128)}, f32[2,2,12,8,256]{4,3,2,1,0:T(8,128)S(1)}, u32[]{:S(2)}, u32[]{:S(2)}) collective-permute-start(f32[2,2,12,8,256]{4,3,2,1,0:T(8,128)} %get-tuple-element.25), channel_id=1, source_target_pairs={{0,12},{4,0},{8,4},{12,8},{1,13},{5,1},{9,5},{13,9},{2,14},{6,2},{... | collective-permute-start | bytes 1179656 | tf_op jit(solution)/shard_map/ppermute | solution.py:500
  17.4 0.0 copy-start.5
  17.4 0.0 copy-start.4
  17.4 3.7 %shard_map.114 = (f32[3,8,12,8,256]{4,3,2,1,0:T(8,128)}, f32[2,2,12,8,256]{4,3,2,1,0:T(8,128)}) custom-call(s32[16]{0:T(128)} %dest_ref.7, f32[3,4,12,8,256]{4,3,2,1,0:T(8,128)} %boxes_ref.5), custom_call_target="tpu_custom_call" | custom-call | bytes 2359296 | tf_op jit(solution)/shard_map/pallas_call | solution.py:203
  21.0 0.0 copy-start.9
  21.1 0.0 copy-start
  21.1 0.0 copy-start.2
  21.1 0.0 copy-start.3
  21.1 0.0 collective-permute-done.1.refs_1_
  21.1 4.3 %collective-permute-done.2.refs_2_ = f32[2,14,8,256]{3,2,1,0:T(8,128)S(1)} collective-permute-done((f32[2,14,8,256]{3,2,1,0:T(8,128)}, f32[2,14,8,256]{3,2,1,0:T(8,128)S(1)}, u32[]{:S(2)}, u32[]{:S(2)}) %collective-permute-start.2) | collective-permute-done | bytes 229408 | tf_op jit(solution)/shard_map/ppermute | solution.py:500
  25.4 0.0 collective-permute-done.3.refs_3_
  25.4 0.0 copy-done.1
  25.4 1.1 %shard_map.116 = (f32[8,14,8,256]{3,2,1,0:T(8,128)S(1)}, f32[3,8,12,8,256]{4,3,2,1,0:T(8,128)}, f32[8,12,256]{2,1,0:T(8,128)S(1)}) custom-call(f32[2,14,8,256]{3,2,1,0:T(8,128)S(1)} %copy-done.1, f32[2,14,8,256]{3,2,1,0:T(8,128)S(1)} %collective-permute-done.1.refs_1_, ...), custom_call_target="tpu_custom_call", output_to_operand_aliasing={{1}: (4, {})} | custom-call | bytes 2752512 | tf_op jit(solution)/shard_map/pallas_call | solution.py:296
  26.6 0.1 collective-permute-start.6
  26.7 0.0 copy-done.6
  26.7 0.0 copy-done.7
  26.7 0.0 copy-done.8
  26.7 0.1 fusion.7
  26.8 1.7 %collective-permute-start.7 = (f32[8,12,256]{2,1,0:T(8,128)S(1)}, f32[8,12,256]{2,1,0:T(8,128)S(1)}, u32[]{:S(2)}, u32[]{:S(2)}) collective-permute-start(f32[8,12,256]{2,1,0:T(8,128)S(1)} %get-tuple-element.33), channel_id=1, source_target_pairs={{0,2},{2,0},{1,3},{3,1},{4,6},{6,4},{5,7},{7,5},{8,10},{10,8},{9,1... | collective-permute-start | bytes 294920 | tf_op jit(solution)/shard_map/ppermute | solution.py:517
  28.5 0.0 copy-done.9
  28.5 11.9 %collective-permute-start.4 = (f32[2,2,12,8,256]{4,3,2,1,0:T(8,128)S(1)}, f32[2,2,12,8,256]{4,3,2,1,0:T(8,128)S(1)}, u32[]{:S(2)}, u32[]{:S(2)}) collective-permute-start(f32[2,2,12,8,256]{4,3,2,1,0:T(8,128)S(1)} %copy-done.9), channel_id=1, source_target_pairs={{0,8},{4,12},{8,0},{12,4},{1,9},{5,13},{9,1},{13,5},{2,10},{6,14},... | collective-permute-start | bytes 1179656 | tf_op jit(solution)/shard_map/ppermute | solution.py:500
  40.4 0.0 copy-done.5
  40.4 0.4 fusion.2
  40.8 0.0 collective-permute-done.7.own_low.own_high
  40.8 0.1 collective-permute-start.8
  40.9 0.0 copy-done.4
  40.9 0.1 multiply_reduce_fusion
  41.0 1.2 %collective-permute-done.8.other_low.other_high = f32[8,12,256]{2,1,0:T(8,128)S(1)} collective-permute-done((f32[8,12,256]{2,1,0:T(8,128)S(1)}, f32[8,12,256]{2,1,0:T(8,128)S(1)}, u32[]{:S(2)}, u32[]{:S(2)}) %collective-permute-start.8) | collective-permute-done | bytes 98336 | tf_op jit(solution)/shard_map/ppermute | solution.py:518
  42.2 0.0 collective-permute-done.6.other_ref
  42.2 0.0 copy-done
  42.2 0.0 copy-done.2
  42.2 0.0 copy-done.3
  42.2 8.1 %shard_map.117 = (f32[8,12,8,256]{3,2,1,0:T(8,128)}, f32[8,128]{1,0:T(8,128)S(1)}) custom-call(s32[16]{0:T(128)S(1)} %copy-done.2, s32[16]{0:T(128)S(1)} %copy-done.3, f32[8,14,8,256]{3,2,1,0:T(8,128)S(1)} %get-tuple-element.32.own_ref, f32[8,14,8,256]{3,2,1,0:T(8,128)S(1)} %collective-permute-done.6.other_ref, ...), custom_call_target="tpu_custom_call" | custom-call | flops 528482304 | bytes 2752512 | tf_op jit(solution)/shard_map/pallas_call | solution.py:526
  50.3 0.0 collective-permute-done.refs_0_
  50.3 0.0 collective-permute-done.5.refs_2_
  50.4 12.8 %collective-permute-done.4.refs_1_ = f32[2,2,12,8,256]{4,3,2,1,0:T(8,128)S(1)} collective-permute-done((f32[2,2,12,8,256]{4,3,2,1,0:T(8,128)S(1)}, f32[2,2,12,8,256]{4,3,2,1,0:T(8,128)S(1)}, u32[]{:S(2)}, u32[]{:S(2)}) %collective-permute-start.4) | collective-permute-done | bytes 393248 | tf_op jit(solution)/shard_map/ppermute | solution.py:500
  63.1 1.0 %shard_map.118 = f32[3,8,12,8,256]{4,3,2,1,0:T(8,128)} custom-call(f32[2,2,12,8,256]{4,3,2,1,0:T(8,128)S(1)} %collective-permute-done.refs_0_, f32[2,2,12,8,256]{4,3,2,1,0:T(8,128)S(1)} %collective-permute-done.4.refs_1_, f32[2,2,12,8,256]{4,3,2,1,0:T(8,128)S(1)} %collective-permute-done.5.refs_2_, ...), custom_call_target="tpu_custom_call", output_to_operand_aliasing={{}: (3, {})} | custom-call | bytes 2359296 | tf_op jit(solution)/shard_map/pallas_call | solution.py:239
  (2 shorter events, 0.0 us)
Async XLA Ops:
  3.6 21.8 %copy-start.1 = (f32[2,14,8,256]{3,2,1,0:T(8,128)S(1)}, f32[2,14,8,256]{3,2,1,0:T(8,128)}, u32[]{:S(2)}) copy-start(f32[2,14,8,256]{3,2,1,0:T(8,128)} %get-tuple-element.26.refs_0_) | copy-start | bytes 688132
  3.6 17.5 %collective-permute-start.1 = (f32[2,14,8,256]{3,2,1,0:T(8,128)}, f32[2,14,8,256]{3,2,1,0:T(8,128)S(1)}, u32[]{:S(2)}, u32[]{:S(2)}) collective-permute-start(f32[2,14,8,256]{3,2,1,0:T(8,128)} %get-tuple-element.21), channel_id=1, source_target_pairs={{0,4},{4,8},{8,12},{12,0},{1,5},{5,9},{9,13},{13,1},{2,6},{6,10},{... | collective-permute-start | bytes 688136 | tf_op jit(solution)/shard_map/ppermute | solution.py:500
  6.7 18.7 %collective-permute-start.2 = (f32[2,14,8,256]{3,2,1,0:T(8,128)}, f32[2,14,8,256]{3,2,1,0:T(8,128)S(1)}, u32[]{:S(2)}, u32[]{:S(2)}) collective-permute-start(f32[2,14,8,256]{3,2,1,0:T(8,128)} %get-tuple-element.22), channel_id=1, source_target_pairs={{0,8},{4,12},{8,0},{12,4},{1,9},{5,13},{9,1},{13,5},{2,10},{6,14},... | collective-permute-start | bytes 688136 | tf_op jit(solution)/shard_map/ppermute | solution.py:500
  9.3 16.1 %collective-permute-start.3 = (f32[2,14,8,256]{3,2,1,0:T(8,128)}, f32[2,14,8,256]{3,2,1,0:T(8,128)S(1)}, u32[]{:S(2)}, u32[]{:S(2)}) collective-permute-start(f32[2,14,8,256]{3,2,1,0:T(8,128)} %get-tuple-element.23), channel_id=1, source_target_pairs={{0,12},{4,0},{8,4},{12,8},{1,13},{5,1},{9,5},{13,9},{2,14},{6,2},{... | collective-permute-start | bytes 688136 | tf_op jit(solution)/shard_map/ppermute | solution.py:500
  13.5 13.2 %copy-start.6 = (f32[24,24]{1,0:T(8,128)S(1)}, f32[24,24]{1,0:T(8,128)}, u32[]{:S(2)}) copy-start(f32[24,24]{1,0:T(8,128)} %param.14) | copy-start | bytes 6916
  13.5 13.2 %copy-start.7 = (f32[24,24]{1,0:T(8,128)S(1)}, f32[24,24]{1,0:T(8,128)}, u32[]{:S(2)}) copy-start(f32[24,24]{1,0:T(8,128)} %param.15) | copy-start | bytes 6916
  13.5 13.2 %copy-start.8 = (f32[24,24]{1,0:T(8,128)S(1)}, f32[24,24]{1,0:T(8,128)}, u32[]{:S(2)}) copy-start(f32[24,24]{1,0:T(8,128)} %param.16) | copy-start | bytes 6916
  13.5 36.9 %collective-permute-start = (f32[2,2,12,8,256]{4,3,2,1,0:T(8,128)}, f32[2,2,12,8,256]{4,3,2,1,0:T(8,128)S(1)}, u32[]{:S(2)}, u32[]{:S(2)}) collective-permute-start(f32[2,2,12,8,256]{4,3,2,1,0:T(8,128)} %get-tuple-element.19), channel_id=1, source_target_pairs={{0,4},{4,8},{8,12},{12,0},{1,5},{5,9},{9,13},{13,1},{2,6},{6,10},{... | collective-permute-start | bytes 1179656 | tf_op jit(solution)/shard_map/ppermute | solution.py:500
  14.4 35.9 %collective-permute-start.5 = (f32[2,2,12,8,256]{4,3,2,1,0:T(8,128)}, f32[2,2,12,8,256]{4,3,2,1,0:T(8,128)S(1)}, u32[]{:S(2)}, u32[]{:S(2)}) collective-permute-start(f32[2,2,12,8,256]{4,3,2,1,0:T(8,128)} %get-tuple-element.25), channel_id=1, source_target_pairs={{0,12},{4,0},{8,4},{12,8},{1,13},{5,1},{9,5},{13,9},{2,14},{6,2},{... | collective-permute-start | bytes 1179656 | tf_op jit(solution)/shard_map/ppermute | solution.py:500
  17.4 23.1 %copy-start.5 = (f32[24,896,1]{1,0,2:T(8,128)S(1)}, f32[24,896,1]{1,0,2:T(8,128)}, u32[]{:S(2)}) copy-start(f32[24,896,1]{1,0,2:T(8,128)} %constant.27) | copy-start | bytes 258052
  17.4 23.5 %copy-start.4 = (f32[3,8,896]{2,1,0:T(8,128)S(1)}, f32[3,8,896]{2,1,0:T(8,128)}, u32[]{:S(2)}) copy-start(f32[3,8,896]{2,1,0:T(8,128)} %constant.23.clone) | copy-start | bytes 258052
  21.0 7.5 %copy-start.9 = (f32[2,2,12,8,256]{4,3,2,1,0:T(8,128)S(1)}, f32[2,2,12,8,256]{4,3,2,1,0:T(8,128)}, u32[]{:S(2)}) copy-start(f32[2,2,12,8,256]{4,3,2,1,0:T(8,128)} %get-tuple-element.24) | copy-start | bytes 1179652
  21.1 21.2 %copy-start = (bf16[256,2304]{1,0:T(8,128)(2,1)S(1)}, bf16[256,2304]{1,0:T(8,128)(2,1)}, u32[]{:S(2)}) copy-start(bf16[256,2304]{1,0:T(8,128)(2,1)} %constant.26.spread_ref) | copy-start | bytes 3538948
  21.1 21.2 %copy-start.2 = (s32[16]{0:T(128)S(1)}, s32[16]{0:T(128)}, u32[]{:S(2)}) copy-start(s32[16]{0:T(128)} %dest_ref.7) | copy-start | bytes 196
  21.1 21.1 %copy-start.3 = (s32[16]{0:T(128)S(1)}, s32[16]{0:T(128)}, u32[]{:S(2)}) copy-start(s32[16]{0:T(128)} %parent_ref.3) | copy-start | bytes 196
  26.6 15.6 %collective-permute-start.6 = (f32[8,14,8,256]{3,2,1,0:T(8,128)S(1)}, f32[8,14,8,256]{3,2,1,0:T(8,128)S(1)}, u32[]{:S(2)}, u32[]{:S(2)}) collective-permute-start(f32[8,14,8,256]{3,2,1,0:T(8,128)S(1)} %get-tuple-element.32.own_ref), channel_id=1, source_target_pairs={{0,1},{1,0},{2,3},{3,2},{4,5},{5,4},{6,7},{7,6},{8,9},{9,8},{10,11... | collective-permute-start | bytes 2752520 | tf_op jit(solution)/shard_map/ppermute | solution.py:513
  26.8 14.0 %collective-permute-start.7 = (f32[8,12,256]{2,1,0:T(8,128)S(1)}, f32[8,12,256]{2,1,0:T(8,128)S(1)}, u32[]{:S(2)}, u32[]{:S(2)}) collective-permute-start(f32[8,12,256]{2,1,0:T(8,128)S(1)} %get-tuple-element.33), channel_id=1, source_target_pairs={{0,2},{2,0},{1,3},{3,1},{4,6},{6,4},{5,7},{7,5},{8,10},{10,8},{9,1... | collective-permute-start | bytes 294920 | tf_op jit(solution)/shard_map/ppermute | solution.py:517
  28.5 34.6 %collective-permute-start.4 = (f32[2,2,12,8,256]{4,3,2,1,0:T(8,128)S(1)}, f32[2,2,12,8,256]{4,3,2,1,0:T(8,128)S(1)}, u32[]{:S(2)}, u32[]{:S(2)}) collective-permute-start(f32[2,2,12,8,256]{4,3,2,1,0:T(8,128)S(1)} %copy-done.9), channel_id=1, source_target_pairs={{0,8},{4,12},{8,0},{12,4},{1,9},{5,13},{9,1},{13,5},{2,10},{6,14},... | collective-permute-start | bytes 1179656 | tf_op jit(solution)/shard_map/ppermute | solution.py:500
  40.8 1.4 %collective-permute-start.8 = (f32[8,12,256]{2,1,0:T(8,128)S(1)}, f32[8,12,256]{2,1,0:T(8,128)S(1)}, u32[]{:S(2)}, u32[]{:S(2)}) collective-permute-start(f32[8,12,256]{2,1,0:T(8,128)S(1)} %collective-permute-done.7.own_low.own_high), channel_id=1, source_target_pairs={{0,1},{1,0},{2,3},{3,2},{4,5},{5,4},{6,7},{7,6},{8,9},{9,8},{10,11... | collective-permute-start | bytes 294920 | tf_op jit(solution)/shard_map/ppermute | solution.py:518

commit v10 on v9

--- a/solution.py
+++ b/solution.py
@@ -504,7 +504,6 @@
     first = pack_first(boxes, coarse, move_dest, parent, edge, box_count)
     arrived = [first[0]] + [send(first[turn], turn) for turn in range(1, box_count)]
     moved, *middle = pack_later((0,) + tuple(range(2, box_count - 1)), boxes, move_dest, box_count)
-    middle, arrived[1:] = lax.optimization_barrier((middle, arrived[1:]))
     middle = [send(piece, n + 2) for n, piece in enumerate(middle)]
     later_arrived = [near[0]] + middle + [near[1]]
     now, moved, *facing = arrive(arrived, (), [], moved, slabs)

time: 64.4 us -> 62.1 us (0.964)
  the two profiles are of different devices: /device:TPU:0 before, /device:TPU:9 now
where the time goes in v10:
time: 62.1 us; the launch traced here: 61.9 us
  waiting for transfers between devices  31.9 us (51%)
  Pallas kernels  19.5 us (31%)
  starting transfers between devices  9.09 us (15%)
  between operations  0.78 us (1%)
    ppermute x6, waiting for transfers between devices, send(): lax.ppermute(piece, 'box', [(s, (s + turn) % box_count) for s in range(bo...  27.5 us
    pallas_call x1, Pallas kernels, body(): pl.pallas_call(functools.partial(slope_kernel, edge, planes, fields, coar...  8.1 us
    ppermute x6, starting transfers between devices, send(): lax.ppermute(piece, 'box', [(s, (s + turn) % box_count) for s in range(bo...  6.39 us
    pallas_call x2, Pallas kernels, pack_later(): pl.pallas_call(functools.partial(later_kernel, turns, per_device, box_cou...  6.33 us
    ppermute x1, waiting for transfers between devices, shifted(): own_group = lax.ppermute(values, 'slab', swap if slabs == 2 else pairs)  3.51 us
    pallas_call x1, Pallas kernels, pack_first(): pl.pallas_call(functools.partial(first_kernel, per_device, box_count, edg...  2.94 us
  transfers between devices with their start and end apart: 9, of which 4 were waited for; matrix products, arithmetic and copies ran while one was open for 1% of the time, Pallas kernels for 25%

profile of v10, /device:TPU:9, one launch (start us, length us, event | category | flops | bytes accessed | tf_op | source)
XLA Modules:
  0.0 61.9 jit_solution(5622865041211774455)
XLA Ops:
  0.6 2.9 %shard_map.115 = (f32[2,14,8,256]{3,2,1,0:T(8,128)}, f32[2,14,8,256]{3,2,1,0:T(8,128)}, f32[2,14,8,256]{3,2,1,0:T(8,128)}, f32[2,14,8,256]{3,2,1,0:T(8,128)}) custom-call(s32[16]{0:T(128)} %dest_ref.7, s32[16]{0:T(128)} %parent_ref.3, f32[3,4,12,8,256]{4,3,2,1,0:T(8,128)} %boxes_ref.5, f32[12,8,1000]{2,1,0:T(8,128)} %bitcast.11), custom_call_target="tpu_custom_call" | custom-call | flops 147456000 | bytes 2743296 | tf_op jit(solution)/shard_map/pallas_call | solution.py:133
  3.6 0.0 copy-start.1
  3.6 1.4 %collective-permute-start.3 = (f32[2,14,8,256]{3,2,1,0:T(8,128)}, f32[2,14,8,256]{3,2,1,0:T(8,128)S(1)}, u32[]{:S(2)}, u32[]{:S(2)}) collective-permute-start(f32[2,14,8,256]{3,2,1,0:T(8,128)} %get-tuple-element.19), channel_id=1, source_target_pairs={{0,4},{4,8},{8,12},{12,0},{1,5},{5,9},{9,13},{13,1},{2,6},{6,10},{... | collective-permute-start | bytes 688136 | tf_op jit(solution)/shard_map/ppermute | solution.py:500
  5.0 1.1 %collective-permute-start.4 = (f32[2,14,8,256]{3,2,1,0:T(8,128)}, f32[2,14,8,256]{3,2,1,0:T(8,128)S(1)}, u32[]{:S(2)}, u32[]{:S(2)}) collective-permute-start(f32[2,14,8,256]{3,2,1,0:T(8,128)} %get-tuple-element.20), channel_id=1, source_target_pairs={{0,8},{4,12},{8,0},{12,4},{1,9},{5,13},{9,1},{13,5},{2,10},{6,14},... | collective-permute-start | bytes 688136 | tf_op jit(solution)/shard_map/ppermute | solution.py:500
  6.1 1.4 %collective-permute-start.5 = (f32[2,14,8,256]{3,2,1,0:T(8,128)}, f32[2,14,8,256]{3,2,1,0:T(8,128)S(1)}, u32[]{:S(2)}, u32[]{:S(2)}) collective-permute-start(f32[2,14,8,256]{3,2,1,0:T(8,128)} %get-tuple-element.21), channel_id=1, source_target_pairs={{0,12},{4,0},{8,4},{12,8},{1,13},{5,1},{9,5},{13,9},{2,14},{6,2},{... | collective-permute-start | bytes 688136 | tf_op jit(solution)/shard_map/ppermute | solution.py:500
  7.4 3.6 %shard_map.114 = (f32[3,8,12,8,256]{4,3,2,1,0:T(8,128)}, f32[2,2,12,8,256]{4,3,2,1,0:T(8,128)}) custom-call(s32[16]{0:T(128)} %dest_ref.7, f32[3,4,12,8,256]{4,3,2,1,0:T(8,128)} %boxes_ref.5), custom_call_target="tpu_custom_call" | custom-call | bytes 2359296 | tf_op jit(solution)/shard_map/pallas_call | solution.py:203
  11.0 0.0 copy-start.6
  11.0 0.0 copy-start.7
  11.0 0.0 copy-start.8
  11.0 0.0 copy-start.5
  11.0 0.0 copy-start.4
  11.1 0.1 collective-permute-start.1
  11.1 2.8 %shard_map.113 = (f32[2,2,12,8,256]{4,3,2,1,0:T(8,128)}, f32[2,2,12,8,256]{4,3,2,1,0:T(8,128)}) custom-call(s32[16]{0:T(128)} %dest_ref.7, f32[3,4,12,8,256]{4,3,2,1,0:T(8,128)} %boxes_ref.5), custom_call_target="tpu_custom_call" | custom-call | bytes 2359296 | tf_op jit(solution)/shard_map/pallas_call | solution.py:203
  13.9 0.0 copy-start
  13.9 0.0 copy-start.2
  14.0 0.0 copy-start.3
  14.0 2.5 %collective-permute-start = (f32[2,2,12,8,256]{4,3,2,1,0:T(8,128)}, f32[2,2,12,8,256]{4,3,2,1,0:T(8,128)S(1)}, u32[]{:S(2)}, u32[]{:S(2)}) collective-permute-start(f32[2,2,12,8,256]{4,3,2,1,0:T(8,128)} %get-tuple-element.15), channel_id=1, source_target_pairs={{0,4},{4,8},{8,12},{12,0},{1,5},{5,9},{9,13},{13,1},{2,6},{6,10},{... | collective-permute-start | bytes 1179656 | tf_op jit(solution)/shard_map/ppermute | solution.py:500
  16.4 0.0 collective-permute-done.3.refs_1_
  16.4 0.0 collective-permute-start.2
  16.4 16.3 %collective-permute-done.4.refs_2_ = f32[2,14,8,256]{3,2,1,0:T(8,128)S(1)} collective-permute-done((f32[2,14,8,256]{3,2,1,0:T(8,128)}, f32[2,14,8,256]{3,2,1,0:T(8,128)S(1)}, u32[]{:S(2)}, u32[]{:S(2)}) %collective-permute-start.4) | collective-permute-done | bytes 229408 | tf_op jit(solution)/shard_map/ppermute | solution.py:500
  32.8 11.2 %collective-permute-done.5.refs_3_ = f32[2,14,8,256]{3,2,1,0:T(8,128)S(1)} collective-permute-done((f32[2,14,8,256]{3,2,1,0:T(8,128)}, f32[2,14,8,256]{3,2,1,0:T(8,128)S(1)}, u32[]{:S(2)}, u32[]{:S(2)}) %collective-permute-start.5) | collective-permute-done | bytes 229408 | tf_op jit(solution)/shard_map/ppermute | solution.py:500
  43.9 0.0 copy-done.1
  43.9 1.1 %shard_map.116 = (f32[8,14,8,256]{3,2,1,0:T(8,128)S(1)}, f32[3,8,12,8,256]{4,3,2,1,0:T(8,128)}, f32[8,12,256]{2,1,0:T(8,128)S(1)}) custom-call(f32[2,14,8,256]{3,2,1,0:T(8,128)S(1)} %copy-done.1, f32[2,14,8,256]{3,2,1,0:T(8,128)S(1)} %collective-permute-done.3.refs_1_, ...), custom_call_target="tpu_custom_call", output_to_operand_aliasing={{1}: (4, {})} | custom-call | bytes 2752512 | tf_op jit(solution)/shard_map/pallas_call | solution.py:296
  45.1 0.7 %collective-permute-start.6 = (f32[8,14,8,256]{3,2,1,0:T(8,128)S(1)}, f32[8,14,8,256]{3,2,1,0:T(8,128)S(1)}, u32[]{:S(2)}, u32[]{:S(2)}) collective-permute-start(f32[8,14,8,256]{3,2,1,0:T(8,128)S(1)} %get-tuple-element.24.own_ref), channel_id=1, source_target_pairs={{0,1},{1,0},{2,3},{3,2},{4,5},{5,4},{6,7},{7,6},{8,9},{9,8},{10,11... | collective-permute-start | bytes 2752520 | tf_op jit(solution)/shard_map/ppermute | solution.py:512
  45.7 0.0 copy-done.6
  45.7 0.0 copy-done.7
  45.7 0.0 copy-done.8
  45.8 0.1 fusion.7
  45.8 1.2 %collective-permute-start.7 = (f32[8,12,256]{2,1,0:T(8,128)S(1)}, f32[8,12,256]{2,1,0:T(8,128)S(1)}, u32[]{:S(2)}, u32[]{:S(2)}) collective-permute-start(f32[8,12,256]{2,1,0:T(8,128)S(1)} %get-tuple-element.25), channel_id=1, source_target_pairs={{0,2},{2,0},{1,3},{3,1},{4,6},{6,4},{5,7},{7,5},{8,10},{10,8},{9,1... | collective-permute-start | bytes 294920 | tf_op jit(solution)/shard_map/ppermute | solution.py:516
  47.1 0.0 copy-done.5
  47.1 0.4 fusion.2
  47.4 3.5 %collective-permute-done.7.own_low.own_high = f32[8,12,256]{2,1,0:T(8,128)S(1)} collective-permute-done((f32[8,12,256]{2,1,0:T(8,128)S(1)}, f32[8,12,256]{2,1,0:T(8,128)S(1)}, u32[]{:S(2)}, u32[]{:S(2)}) %collective-permute-start.7) | collective-permute-done | bytes 98336 | tf_op jit(solution)/shard_map/ppermute | solution.py:516
  50.9 0.8 %collective-permute-start.8 = (f32[8,12,256]{2,1,0:T(8,128)S(1)}, f32[8,12,256]{2,1,0:T(8,128)S(1)}, u32[]{:S(2)}, u32[]{:S(2)}) collective-permute-start(f32[8,12,256]{2,1,0:T(8,128)S(1)} %collective-permute-done.7.own_low.own_high), channel_id=1, source_target_pairs={{0,1},{1,0},{2,3},{3,2},{4,5},{5,4},{6,7},{7,6},{8,9},{9,8},{10,11... | collective-permute-start | bytes 294920 | tf_op jit(solution)/shard_map/ppermute | solution.py:517
  51.8 0.0 copy-done.4
  51.8 0.1 multiply_reduce_fusion
  51.8 0.9 %collective-permute-done.8.other_low.other_high = f32[8,12,256]{2,1,0:T(8,128)S(1)} collective-permute-done((f32[8,12,256]{2,1,0:T(8,128)S(1)}, f32[8,12,256]{2,1,0:T(8,128)S(1)}, u32[]{:S(2)}, u32[]{:S(2)}) %collective-permute-start.8) | collective-permute-done | bytes 98336 | tf_op jit(solution)/shard_map/ppermute | solution.py:517
  52.7 0.0 collective-permute-done.6.other_ref
  52.7 0.0 copy-done
  52.7 0.0 copy-done.2
  52.8 0.0 copy-done.3
  52.8 8.1 %shard_map.117 = (f32[8,12,8,256]{3,2,1,0:T(8,128)}, f32[8,128]{1,0:T(8,128)S(1)}) custom-call(s32[16]{0:T(128)S(1)} %copy-done.2, s32[16]{0:T(128)S(1)} %copy-done.3, f32[8,14,8,256]{3,2,1,0:T(8,128)S(1)} %get-tuple-element.24.own_ref, f32[8,14,8,256]{3,2,1,0:T(8,128)S(1)} %collective-permute-done.6.other_ref, ...), custom_call_target="tpu_custom_call" | custom-call | flops 528482304 | bytes 2752512 | tf_op jit(solution)/shard_map/pallas_call | solution.py:525
  60.9 0.0 collective-permute-done.1.refs_1_
  60.9 0.0 collective-permute-done.refs_0_
  60.9 0.0 collective-permute-done.2.refs_2_
  60.9 1.0 %shard_map.118 = f32[3,8,12,8,256]{4,3,2,1,0:T(8,128)} custom-call(f32[2,2,12,8,256]{4,3,2,1,0:T(8,128)S(1)} %collective-permute-done.refs_0_, f32[2,2,12,8,256]{4,3,2,1,0:T(8,128)S(1)} %collective-permute-done.1.refs_1_, f32[2,2,12,8,256]{4,3,2,1,0:T(8,128)S(1)} %collective-permute-done.2.refs_2_, ...), custom_call_target="tpu_custom_call", output_to_operand_aliasing={{}: (3, {})} | custom-call | bytes 2359296 | tf_op jit(solution)/shard_map/pallas_call | solution.py:239
  (2 shorter events, 0.0 us)
Async XLA Ops:
  3.6 40.4 %copy-start.1 = (f32[2,14,8,256]{3,2,1,0:T(8,128)S(1)}, f32[2,14,8,256]{3,2,1,0:T(8,128)}, u32[]{:S(2)}) copy-start(f32[2,14,8,256]{3,2,1,0:T(8,128)} %get-tuple-element.18.refs_0_) | copy-start | bytes 688132
  3.6 12.8 %collective-permute-start.3 = (f32[2,14,8,256]{3,2,1,0:T(8,128)}, f32[2,14,8,256]{3,2,1,0:T(8,128)S(1)}, u32[]{:S(2)}, u32[]{:S(2)}) collective-permute-start(f32[2,14,8,256]{3,2,1,0:T(8,128)} %get-tuple-element.19), channel_id=1, source_target_pairs={{0,4},{4,8},{8,12},{12,0},{1,5},{5,9},{9,13},{13,1},{2,6},{6,10},{... | collective-permute-start | bytes 688136 | tf_op jit(solution)/shard_map/ppermute | solution.py:500
  5.0 27.8 %collective-permute-start.4 = (f32[2,14,8,256]{3,2,1,0:T(8,128)}, f32[2,14,8,256]{3,2,1,0:T(8,128)S(1)}, u32[]{:S(2)}, u32[]{:S(2)}) collective-permute-start(f32[2,14,8,256]{3,2,1,0:T(8,128)} %get-tuple-element.20), channel_id=1, source_target_pairs={{0,8},{4,12},{8,0},{12,4},{1,9},{5,13},{9,1},{13,5},{2,10},{6,14},... | collective-permute-start | bytes 688136 | tf_op jit(solution)/shard_map/ppermute | solution.py:500
  6.1 37.9 %collective-permute-start.5 = (f32[2,14,8,256]{3,2,1,0:T(8,128)}, f32[2,14,8,256]{3,2,1,0:T(8,128)S(1)}, u32[]{:S(2)}, u32[]{:S(2)}) collective-permute-start(f32[2,14,8,256]{3,2,1,0:T(8,128)} %get-tuple-element.21), channel_id=1, source_target_pairs={{0,12},{4,0},{8,4},{12,8},{1,13},{5,1},{9,5},{13,9},{2,14},{6,2},{... | collective-permute-start | bytes 688136 | tf_op jit(solution)/shard_map/ppermute | solution.py:500
  11.0 34.7 %copy-start.6 = (f32[24,24]{1,0:T(8,128)S(1)}, f32[24,24]{1,0:T(8,128)}, u32[]{:S(2)}) copy-start(f32[24,24]{1,0:T(8,128)} %param.14) | copy-start | bytes 6916
  11.0 34.7 %copy-start.7 = (f32[24,24]{1,0:T(8,128)S(1)}, f32[24,24]{1,0:T(8,128)}, u32[]{:S(2)}) copy-start(f32[24,24]{1,0:T(8,128)} %param.15) | copy-start | bytes 6916
  11.0 34.7 %copy-start.8 = (f32[24,24]{1,0:T(8,128)S(1)}, f32[24,24]{1,0:T(8,128)}, u32[]{:S(2)}) copy-start(f32[24,24]{1,0:T(8,128)} %param.16) | copy-start | bytes 6916
  11.0 36.0 %copy-start.5 = (f32[24,896,1]{1,0,2:T(8,128)S(1)}, f32[24,896,1]{1,0,2:T(8,128)}, u32[]{:S(2)}) copy-start(f32[24,896,1]{1,0,2:T(8,128)} %constant.27) | copy-start | bytes 258052
  11.0 40.7 %copy-start.4 = (f32[3,8,896]{2,1,0:T(8,128)S(1)}, f32[3,8,896]{2,1,0:T(8,128)}, u32[]{:S(2)}) copy-start(f32[3,8,896]{2,1,0:T(8,128)} %constant.23.clone) | copy-start | bytes 258052
  11.1 49.8 %collective-permute-start.1 = (f32[2,2,12,8,256]{4,3,2,1,0:T(8,128)}, f32[2,2,12,8,256]{4,3,2,1,0:T(8,128)S(1)}, u32[]{:S(2)}, u32[]{:S(2)}) collective-permute-start(f32[2,2,12,8,256]{4,3,2,1,0:T(8,128)} %get-tuple-element.16), channel_id=1, source_target_pairs={{0,8},{4,12},{8,0},{12,4},{1,9},{5,13},{9,1},{13,5},{2,10},{6,14},... | collective-permute-start | bytes 1179656 | tf_op jit(solution)/shard_map/ppermute | solution.py:500
  13.9 38.8 %copy-start = (bf16[256,2304]{1,0:T(8,128)(2,1)S(1)}, bf16[256,2304]{1,0:T(8,128)(2,1)}, u32[]{:S(2)}) copy-start(bf16[256,2304]{1,0:T(8,128)(2,1)} %constant.26.spread_ref) | copy-start | bytes 3538948
  13.9 38.8 %copy-start.2 = (s32[16]{0:T(128)S(1)}, s32[16]{0:T(128)}, u32[]{:S(2)}) copy-start(s32[16]{0:T(128)} %dest_ref.7) | copy-start | bytes 196
  14.0 38.8 %copy-start.3 = (s32[16]{0:T(128)S(1)}, s32[16]{0:T(128)}, u32[]{:S(2)}) copy-start(s32[16]{0:T(128)} %parent_ref.3) | copy-start | bytes 196
  14.0 46.9 %collective-permute-start = (f32[2,2,12,8,256]{4,3,2,1,0:T(8,128)}, f32[2,2,12,8,256]{4,3,2,1,0:T(8,128)S(1)}, u32[]{:S(2)}, u32[]{:S(2)}) collective-permute-start(f32[2,2,12,8,256]{4,3,2,1,0:T(8,128)} %get-tuple-element.15), channel_id=1, source_target_pairs={{0,4},{4,8},{8,12},{12,0},{1,5},{5,9},{9,13},{13,1},{2,6},{6,10},{... | collective-permute-start | bytes 1179656 | tf_op jit(solution)/shard_map/ppermute | solution.py:500
  16.4 44.4 %collective-permute-start.2 = (f32[2,2,12,8,256]{4,3,2,1,0:T(8,128)}, f32[2,2,12,8,256]{4,3,2,1,0:T(8,128)S(1)}, u32[]{:S(2)}, u32[]{:S(2)}) collective-permute-start(f32[2,2,12,8,256]{4,3,2,1,0:T(8,128)} %get-tuple-element.17), channel_id=1, source_target_pairs={{0,12},{4,0},{8,4},{12,8},{1,13},{5,1},{9,5},{13,9},{2,14},{6,2},{... | collective-permute-start | bytes 1179656 | tf_op jit(solution)/shard_map/ppermute | solution.py:500
  45.1 7.7 %collective-permute-start.6 = (f32[8,14,8,256]{3,2,1,0:T(8,128)S(1)}, f32[8,14,8,256]{3,2,1,0:T(8,128)S(1)}, u32[]{:S(2)}, u32[]{:S(2)}) collective-permute-start(f32[8,14,8,256]{3,2,1,0:T(8,128)S(1)} %get-tuple-element.24.own_ref), channel_id=1, source_target_pairs={{0,1},{1,0},{2,3},{3,2},{4,5},{5,4},{6,7},{7,6},{8,9},{9,8},{10,11... | collective-permute-start | bytes 2752520 | tf_op jit(solution)/shard_map/ppermute | solution.py:512
  45.8 5.1 %collective-permute-start.7 = (f32[8,12,256]{2,1,0:T(8,128)S(1)}, f32[8,12,256]{2,1,0:T(8,128)S(1)}, u32[]{:S(2)}, u32[]{:S(2)}) collective-permute-start(f32[8,12,256]{2,1,0:T(8,128)S(1)} %get-tuple-element.25), channel_id=1, source_target_pairs={{0,2},{2,0},{1,3},{3,1},{4,6},{6,4},{5,7},{7,5},{8,10},{10,8},{9,1... | collective-permute-start | bytes 294920 | tf_op jit(solution)/shard_map/ppermute | solution.py:516
  50.9 1.8 %collective-permute-start.8 = (f32[8,12,256]{2,1,0:T(8,128)S(1)}, f32[8,12,256]{2,1,0:T(8,128)S(1)}, u32[]{:S(2)}, u32[]{:S(2)}) collective-permute-start(f32[8,12,256]{2,1,0:T(8,128)S(1)} %collective-permute-done.7.own_low.own_high), channel_id=1, source_target_pairs={{0,1},{1,0},{2,3},{3,2},{4,5},{5,4},{6,7},{7,6},{8,9},{9,8},{10,11... | collective-permute-start | bytes 294920 | tf_op jit(solution)/shard_map/ppermute | solution.py:517

commit v11 on v10

--- a/solution.py
+++ b/solution.py
@@ -373,10 +373,42 @@
     return select, masks
 
 
+def expand_faces(slots_ref, fields, spread_ref, out_ref):
+    slots, _, planes, cross = slots_ref.shape
+    for slot in range(slots):
+        for block in range(ROWS // planes):
+            at = slot * ROWS + block * planes
+            out_ref[at : at + planes, :cross] = slots_ref[slot, fields + block]
+    cells = out_ref[:, :cross]
+    high = cells.astype(jnp.bfloat16)
+    low = (cells - high.astype(jnp.float32)).astype(jnp.bfloat16)
+    both = jnp.dot(jnp.concatenate([high, low], axis=0), spread_ref[...], preferred_element_type=jnp.float32)
+    out_ref[...] = both[: slots * ROWS] + both[slots * ROWS :]
+
+
+def own_ghosts(now, fields, spread):
+    vmem = pl.BlockSpec(memory_space=pltpu.VMEM)
+    shape = (now.shape[0] * ROWS, spread.shape[1])
+
+    def kernel(now_ref, spread_ref, out_ref):
+        expand_faces(now_ref, fields, spread_ref, out_ref)
+
+    return pl.pallas_call(
+        kernel,
+        out_shape=jax.ShapeDtypeStruct(shape, jnp.float32),
+        in_specs=[vmem] * 2,
+        out_specs=vmem,
+        compiler_params=pltpu.CompilerParams(vmem_limit_bytes=48 * 2 ** 20),
+        cost_estimate=pl.CostEstimate(
+            flops=4 * shape[0] * spread.size, bytes_accessed=4 * shape[0] * shape[1], transcendentals=0
+        ),
+    )(now, spread)
+
+
 def slope_kernel(
     edge, planes, fields, coarse_planes, per_device, total, coarse_count, slots, slabs,
     dest_ref, parent_ref, own_ref, other_ref, own_low, other_low, own_high, other_high,
-    spread_ref, weight_ref, out_ref, token_ref, stack, parts, ghosts, table, count,
+    own_rim, spread_ref, weight_ref, out_ref, token_ref, stack, parts, other_rim, table, count,
 ):
     step = pl.program_id(0)
     cross = edge * edge
@@ -406,16 +438,7 @@
             return carry
 
         lax.fori_loop(0, total, place, 0)
-        for slot in range(slots):
-            for n, ref in enumerate((own_ref, other_ref)):
-                at = (2 * slot + n) * ROWS
-                for block in range(ROWS // planes):
-                    ghosts[at + block * planes : at + (block + 1) * planes, :cross] = ref[slot, fields + block]
-        high, middle, low = (
-            jnp.dot(part, spread_ref[...], preferred_element_type=jnp.float32)
-            for part in split_three(ghosts[:, :cross])
-        )
-        ghosts[...] = high + (middle + low)
+        expand_faces(other_ref, fields, spread_ref, other_rim)
 
     face = table[step]
 
@@ -441,7 +464,8 @@
         stack[2 * rows : 4 * rows] = jnp.where(y > 0, pltpu.roll(cells, edge, 1), 0.0) + jnp.where(
             z > 0, pltpu.roll(cells, 1, 1), 0.0
         )
-        rim = ghosts[pl.ds(pl.multiple_of(2 * ROWS * face, 2 * ROWS), 2 * ROWS)]
+        here = pl.ds(pl.multiple_of(ROWS * face, ROWS), ROWS)
+        rim = jnp.concatenate([own_rim[here], other_rim[here]], axis=0)
         base = 6 * rows
         x_face = rim[:, 2 * coarse_planes * cross :]
         stack[base : base + 2 * ROWS] = x_face
@@ -505,22 +529,27 @@
     arrived = [first[0]] + [send(first[turn], turn) for turn in range(1, box_count)]
     moved, *middle = pack_later((0,) + tuple(range(2, box_count - 1)), boxes, move_dest, box_count)
     middle = [send(piece, n + 2) for n, piece in enumerate(middle)]
-    later_arrived = [near[0]] + middle + [near[1]]
     now, moved, *facing = arrive(arrived, (), [], moved, slabs)
 
     swap = [(0, 1), (1, 0)]
     now_other = lax.ppermute(now, "fld", swap)
 
+    spread = jnp.asarray(expand_table(coarse_planes, edge, cross)).astype(jnp.bfloat16)
+    rim = own_ghosts(now, fields, spread)
+
     def shifted(values, up):
         pairs = [(s, s + 1) if up else (s + 1, s) for s in range(slabs - 1)]
-        own_group = lax.ppermute(values, "slab", swap if slabs == 2 else pairs)
-        return own_group, lax.ppermute(own_group, "fld", swap)
+        return lax.ppermute(values, "slab", swap if slabs == 2 else pairs)
 
     low = shifted(facing[-1], True)
-    high = low if slabs == 2 else shifted(facing[0], False)
+    low, rim = lax.optimization_barrier((low, rim))
+    low = low, lax.ppermute(low, "fld", swap)
+    high = low
+    if slabs != 2:
+        high = shifted(facing[0], False)
+        high = high, lax.ppermute(high, "fld", swap)
 
     weight = mixing_weights((lap_mix, grad_mix, damp_mix), group, fields, planes, coarse_planes)
-    spread = jnp.asarray(expand_table(coarse_planes, edge, cross)).astype(jnp.bfloat16)
     smem, vmem = pl.BlockSpec(memory_space=pltpu.SMEM), pl.BlockSpec(memory_space=pltpu.VMEM)
     slope, token = pl.pallas_call(
         functools.partial(
@@ -531,12 +560,12 @@
             jax.ShapeDtypeStruct((slots, fields, planes, cross), jnp.float32),
             jax.ShapeDtypeStruct((8, 128), jnp.float32),
         ],
-        in_specs=[smem, smem] + [vmem] * 8,
+        in_specs=[smem, smem] + [vmem] * 9,
         out_specs=[pl.BlockSpec((1, fields, planes, cross), lambda n: (n, 0, 0, 0)), vmem],
         scratch_shapes=[
             pltpu.VMEM((weight.shape[1], cross), jnp.float32),
             pltpu.VMEM((2 * weight.shape[0], weight.shape[1]), jnp.bfloat16),
-            pltpu.VMEM((2 * ROWS * slots, spread.shape[1]), jnp.float32),
+            pltpu.VMEM((ROWS * slots, spread.shape[1]), jnp.float32),
             pltpu.SMEM((slots,), jnp.int32),
             pltpu.SMEM((slots,), jnp.int32),
         ],
@@ -544,8 +573,9 @@
         cost_estimate=pl.CostEstimate(
             flops=3 * slots * weight.size * cross, bytes_accessed=12 * now.size, transcendentals=0
         ),
-    )(move_dest, parent, now, now_other, low[0], low[1], high[0], high[1], spread, weight)
-    return settle(tuple(range(1, box_count)), later_arrived, moved, token), slope
+    )(move_dest, parent, now, now_other, low[0], low[1], high[0], high[1], rim, spread, weight)
+    moved = settle(tuple(range(2, box_count - 1)), middle, moved, token)
+    return settle((1, box_count - 1), near, moved, token), slope
 
 
 def solution(mesh):

time: 62.1 us -> 61.9 us (level)
  waiting for transfers between devices: 31.9 us -> 33.2 us
  Pallas kernels: 19.5 us -> 18.2 us
    pallas_call x1, Pallas kernels: 8.1 us -> 5.5 us  [body(): pl.pallas_call(functools.partial(slope_kernel, edge, planes, fields, coar...]
    ppermute x6, waiting for transfers between devices: 27.5 us -> 29.3 us  [send(): lax.ppermute(piece, 'box', [(s, (s + turn) % box_count) for s in range(bo...]
    pallas_call x1 -> x2, Pallas kernels: 1.05 us -> 1.64 us  [settle(): pl.pallas_call(functools.partial(settle_kernel, turns), out_shape=jax.Sha...]
  transfers between devices with their start and end apart: 9 -> 9, of which waited for: 4 -> 5; matrix products, arithmetic and copies ran while one was open for 1% -> 1% of each run, Pallas kernels for 25% -> 23%
where the time goes in v11:
time: 61.9 us; the launch traced here: 61.7 us
  waiting for transfers between devices  33.2 us (54%)
  Pallas kernels  18.2 us (29%)
  starting transfers between devices  8.89 us (14%)
  between operations  0.8 us (1%)
    ppermute x6, waiting for transfers between devices, send(): lax.ppermute(piece, 'box', [(s, (s + turn) % box_count) for s in range(bo...  29.3 us
    pallas_call x2, Pallas kernels, pack_later(): pl.pallas_call(functools.partial(later_kernel, turns, per_device, box_cou...  6.46 us
    ppermute x6, starting transfers between devices, send(): lax.ppermute(piece, 'box', [(s, (s + turn) % box_count) for s in range(bo...  6.19 us
    pallas_call x1, Pallas kernels, body(): pl.pallas_call(functools.partial(slope_kernel, edge, planes, fields, coar...  5.5 us
    ppermute x1, waiting for transfers between devices, shifted(): return lax.ppermute(values, 'slab', swap if slabs == 2 else pairs)  3.01 us
    pallas_call x1, Pallas kernels, pack_first(): pl.pallas_call(functools.partial(first_kernel, per_device, box_count, edg...  2.98 us
    pallas_call x2, Pallas kernels, settle(): pl.pallas_call(functools.partial(settle_kernel, turns), out_shape=jax.Sha...  1.64 us
  transfers between devices with their start and end apart: 9, of which 5 were waited for; matrix products, arithmetic and copies ran while one was open for 1% of the time, Pallas kernels for 23%

profile of v11, /device:TPU:9, one launch (start us, length us, event | category | flops | bytes accessed | tf_op | source)
XLA Modules:
  0.0 61.7 jit_solution(14405366557607473122)
XLA Ops:
  0.6 3.0 %shard_map.115 = (f32[2,14,8,256]{3,2,1,0:T(8,128)}, f32[2,14,8,256]{3,2,1,0:T(8,128)}, f32[2,14,8,256]{3,2,1,0:T(8,128)}, f32[2,14,8,256]{3,2,1,0:T(8,128)}) custom-call(s32[16]{0:T(128)} %dest_ref.7, s32[16]{0:T(128)} %parent_ref.3, f32[3,4,12,8,256]{4,3,2,1,0:T(8,128)} %boxes_ref.5, f32[12,8,1000]{2,1,0:T(8,128)} %bitcast.11), custom_call_target="tpu_custom_call" | custom-call | flops 147456000 | bytes 2743296 | tf_op jit(solution)/shard_map/pallas_call | solution.py:133
  3.6 0.0 copy-start.1
  3.6 1.3 %collective-permute-start.3 = (f32[2,14,8,256]{3,2,1,0:T(8,128)}, f32[2,14,8,256]{3,2,1,0:T(8,128)S(1)}, u32[]{:S(2)}, u32[]{:S(2)}) collective-permute-start(f32[2,14,8,256]{3,2,1,0:T(8,128)} %get-tuple-element.21), channel_id=1, source_target_pairs={{0,4},{4,8},{8,12},{12,0},{1,5},{5,9},{9,13},{13,1},{2,6},{6,10},{... | collective-permute-start | bytes 688136 | tf_op jit(solution)/shard_map/ppermute | solution.py:524
  5.0 1.1 %collective-permute-start.4 = (f32[2,14,8,256]{3,2,1,0:T(8,128)}, f32[2,14,8,256]{3,2,1,0:T(8,128)S(1)}, u32[]{:S(2)}, u32[]{:S(2)}) collective-permute-start(f32[2,14,8,256]{3,2,1,0:T(8,128)} %get-tuple-element.22), channel_id=1, source_target_pairs={{0,8},{4,12},{8,0},{12,4},{1,9},{5,13},{9,1},{13,5},{2,10},{6,14},... | collective-permute-start | bytes 688136 | tf_op jit(solution)/shard_map/ppermute | solution.py:524
  6.0 1.4 %collective-permute-start.5 = (f32[2,14,8,256]{3,2,1,0:T(8,128)}, f32[2,14,8,256]{3,2,1,0:T(8,128)S(1)}, u32[]{:S(2)}, u32[]{:S(2)}) collective-permute-start(f32[2,14,8,256]{3,2,1,0:T(8,128)} %get-tuple-element.23), channel_id=1, source_target_pairs={{0,12},{4,0},{8,4},{12,8},{1,13},{5,1},{9,5},{13,9},{2,14},{6,2},{... | collective-permute-start | bytes 688136 | tf_op jit(solution)/shard_map/ppermute | solution.py:524
  7.4 3.5 %shard_map.114 = (f32[3,8,12,8,256]{4,3,2,1,0:T(8,128)}, f32[2,2,12,8,256]{4,3,2,1,0:T(8,128)}) custom-call(s32[16]{0:T(128)} %dest_ref.7, f32[3,4,12,8,256]{4,3,2,1,0:T(8,128)} %boxes_ref.5), custom_call_target="tpu_custom_call" | custom-call | bytes 2359296 | tf_op jit(solution)/shard_map/pallas_call | solution.py:203
  10.9 0.0 copy-start.6
  10.9 0.0 copy-start.7
  11.0 0.0 copy-start.8
  11.0 0.0 copy-start.5
  11.0 0.0 copy-start
  11.0 0.2 collective-permute-start.2
  11.2 2.9 %shard_map.113 = (f32[2,2,12,8,256]{4,3,2,1,0:T(8,128)}, f32[2,2,12,8,256]{4,3,2,1,0:T(8,128)}) custom-call(s32[16]{0:T(128)} %dest_ref.7, f32[3,4,12,8,256]{4,3,2,1,0:T(8,128)} %boxes_ref.5), custom_call_target="tpu_custom_call" | custom-call | bytes 2359296 | tf_op jit(solution)/shard_map/pallas_call | solution.py:203
  14.2 2.2 %collective-permute-start = (f32[2,2,12,8,256]{4,3,2,1,0:T(8,128)}, f32[2,2,12,8,256]{4,3,2,1,0:T(8,128)S(1)}, u32[]{:S(2)}, u32[]{:S(2)}) collective-permute-start(f32[2,2,12,8,256]{4,3,2,1,0:T(8,128)} %get-tuple-element.17), channel_id=1, source_target_pairs={{0,4},{4,8},{8,12},{12,0},{1,5},{5,9},{9,13},{13,1},{2,6},{6,10},{... | collective-permute-start | bytes 1179656 | tf_op jit(solution)/shard_map/ppermute | solution.py:524
  16.4 0.0 collective-permute-done.3.refs_1_
  16.4 0.0 collective-permute-start.1
  16.4 16.4 %collective-permute-done.4.refs_2_ = f32[2,14,8,256]{3,2,1,0:T(8,128)S(1)} collective-permute-done((f32[2,14,8,256]{3,2,1,0:T(8,128)}, f32[2,14,8,256]{3,2,1,0:T(8,128)S(1)}, u32[]{:S(2)}, u32[]{:S(2)}) %collective-permute-start.4) | collective-permute-done | bytes 229408 | tf_op jit(solution)/shard_map/ppermute | solution.py:524
  32.8 11.2 %collective-permute-done.5.refs_3_ = f32[2,14,8,256]{3,2,1,0:T(8,128)S(1)} collective-permute-done((f32[2,14,8,256]{3,2,1,0:T(8,128)}, f32[2,14,8,256]{3,2,1,0:T(8,128)S(1)}, u32[]{:S(2)}, u32[]{:S(2)}) %collective-permute-start.5) | collective-permute-done | bytes 229408 | tf_op jit(solution)/shard_map/ppermute | solution.py:524
  43.9 0.0 copy-done.1
  43.9 1.1 %shard_map.116 = (f32[8,14,8,256]{3,2,1,0:T(8,128)S(1)}, f32[3,8,12,8,256]{4,3,2,1,0:T(8,128)}, f32[8,12,256]{2,1,0:T(8,128)S(1)}) custom-call(f32[2,14,8,256]{3,2,1,0:T(8,128)S(1)} %copy-done.1, f32[2,14,8,256]{3,2,1,0:T(8,128)S(1)} %collective-permute-done.3.refs_1_, ...), custom_call_target="tpu_custom_call", output_to_operand_aliasing={{1}: (4, {})} | custom-call | bytes 2752512 | tf_op jit(solution)/shard_map/pallas_call | solution.py:296
  45.0 0.0 copy-start.4
  45.1 0.0 copy-start.2
  45.1 0.0 copy-start.3
  45.1 0.7 %collective-permute-start.6 = (f32[8,14,8,256]{3,2,1,0:T(8,128)S(1)}, f32[8,14,8,256]{3,2,1,0:T(8,128)S(1)}, u32[]{:S(2)}, u32[]{:S(2)}) collective-permute-start(f32[8,14,8,256]{3,2,1,0:T(8,128)S(1)} %get-tuple-element.26.now_ref.own_ref), channel_id=1, source_target_pairs={{0,1},{1,0},{2,3},{3,2},{4,5},{5,4},{6,7},{7,6},{8,9},{9,8},{10,11... | collective-permute-start | bytes 2752520 | tf_op jit(solution)/shard_map/ppermute | solution.py:535
  45.7 0.0 copy-done.6
  45.7 0.0 copy-done.7
  45.7 0.0 copy-done.8
  45.8 0.1 fusion.7
  45.8 1.2 %collective-permute-start.7 = (f32[8,12,256]{2,1,0:T(8,128)S(1)}, f32[8,12,256]{2,1,0:T(8,128)S(1)}, u32[]{:S(2)}, u32[]{:S(2)}) collective-permute-start(f32[8,12,256]{2,1,0:T(8,128)S(1)} %get-tuple-element.27), channel_id=1, source_target_pairs={{0,2},{2,0},{1,3},{3,1},{4,6},{6,4},{5,7},{7,5},{8,10},{10,8},{9,1... | collective-permute-start | bytes 294920 | tf_op jit(solution)/shard_map/ppermute | solution.py:542
  47.1 0.0 copy-done.5
  47.1 0.4 fusion.2
  47.4 0.0 copy-done
  47.4 0.5 shard_map.117.own_rim
  47.9 3.0 %collective-permute-done.7.own_low.own_high = f32[8,12,256]{2,1,0:T(8,128)S(1)} collective-permute-done((f32[8,12,256]{2,1,0:T(8,128)S(1)}, f32[8,12,256]{2,1,0:T(8,128)S(1)}, u32[]{:S(2)}, u32[]{:S(2)}) %collective-permute-start.7) | collective-permute-done | bytes 98336 | tf_op jit(solution)/shard_map/ppermute | solution.py:542
  50.9 0.8 %collective-permute-start.8 = (f32[8,12,256]{2,1,0:T(8,128)S(1)}, f32[8,12,256]{2,1,0:T(8,128)S(1)}, u32[]{:S(2)}, u32[]{:S(2)}) collective-permute-start(f32[8,12,256]{2,1,0:T(8,128)S(1)} %collective-permute-done.7.own_low.own_high), channel_id=1, source_target_pairs={{0,1},{1,0},{2,3},{3,2},{4,5},{5,4},{6,7},{7,6},{8,9},{9,8},{10,11... | collective-permute-start | bytes 294920 | tf_op jit(solution)/shard_map/ppermute | solution.py:546
  51.8 0.0 copy-done.4
  51.8 0.1 multiply_reduce_fusion
  51.9 0.9 %collective-permute-done.8.other_low.other_high = f32[8,12,256]{2,1,0:T(8,128)S(1)} collective-permute-done((f32[8,12,256]{2,1,0:T(8,128)S(1)}, f32[8,12,256]{2,1,0:T(8,128)S(1)}, u32[]{:S(2)}, u32[]{:S(2)}) %collective-permute-start.8) | collective-permute-done | bytes 98336 | tf_op jit(solution)/shard_map/ppermute | solution.py:546
  52.8 0.0 collective-permute-done.6.other_ref
  52.8 0.0 copy-done.2
  52.8 0.0 copy-done.3
  52.8 5.5 %shard_map.118 = (f32[8,12,8,256]{3,2,1,0:T(8,128)}, f32[8,128]{1,0:T(8,128)S(1)}) custom-call(s32[16]{0:T(128)S(1)} %copy-done.2, s32[16]{0:T(128)S(1)} %copy-done.3, f32[8,14,8,256]{3,2,1,0:T(8,128)S(1)} %get-tuple-element.26.now_ref.own_ref, f32[8,14,8,256]{3,2,1,0:T(8,128)S(1)} %collective-permute-done.6.other_ref, ...), custom_call_target="tpu_custom_call" | custom-call | flops 528482304 | bytes 2752512 | tf_op jit(solution)/shard_map/pallas_call | solution.py:554
  58.3 0.0 collective-permute-done.2.refs_0_
  58.3 0.8 %shard_map.119.refs_2_ = f32[3,8,12,8,256]{4,3,2,1,0:T(8,128)} custom-call(f32[2,2,12,8,256]{4,3,2,1,0:T(8,128)S(1)} %collective-permute-done.2.refs_0_, f32[3,8,12,8,256]{4,3,2,1,0:T(8,128)} %get-tuple-element.25.refs_1_, f32[8,128]{1,0:T(8,128)S(1)} %get-tuple-element.30.refs_2_.refs_3_), custom_call_target="tpu_custom_call", output_to_operand_aliasing={{}: (1, {})} | custom-call | bytes 786432 | tf_op jit(solution)/shard_map/pallas_call | solution.py:239
  59.0 0.0 collective-permute-done.refs_0_
  59.0 1.7 %collective-permute-done.1.refs_1_ = f32[2,2,12,8,256]{4,3,2,1,0:T(8,128)S(1)} collective-permute-done((f32[2,2,12,8,256]{4,3,2,1,0:T(8,128)}, f32[2,2,12,8,256]{4,3,2,1,0:T(8,128)S(1)}, u32[]{:S(2)}, u32[]{:S(2)}) %collective-permute-start.1) | collective-permute-done | bytes 393248 | tf_op jit(solution)/shard_map/ppermute | solution.py:524
  60.8 0.9 %shard_map.120 = f32[3,8,12,8,256]{4,3,2,1,0:T(8,128)} custom-call(f32[2,2,12,8,256]{4,3,2,1,0:T(8,128)S(1)} %collective-permute-done.refs_0_, f32[2,2,12,8,256]{4,3,2,1,0:T(8,128)S(1)} %collective-permute-done.1.refs_1_, f32[3,8,12,8,256]{4,3,2,1,0:T(8,128)} %shard_map.119.refs_2_, ...), custom_call_target="tpu_custom_call", output_to_operand_aliasing={{}: (2, {})} | custom-call | bytes 1572864 | tf_op jit(solution)/shard_map/pallas_call | solution.py:239
  (2 shorter events, 0.0 us)
Async XLA Ops:
  3.6 40.3 %copy-start.1 = (f32[2,14,8,256]{3,2,1,0:T(8,128)S(1)}, f32[2,14,8,256]{3,2,1,0:T(8,128)}, u32[]{:S(2)}) copy-start(f32[2,14,8,256]{3,2,1,0:T(8,128)} %get-tuple-element.20.refs_0_) | copy-start | bytes 688132
  3.6 12.7 %collective-permute-start.3 = (f32[2,14,8,256]{3,2,1,0:T(8,128)}, f32[2,14,8,256]{3,2,1,0:T(8,128)S(1)}, u32[]{:S(2)}, u32[]{:S(2)}) collective-permute-start(f32[2,14,8,256]{3,2,1,0:T(8,128)} %get-tuple-element.21), channel_id=1, source_target_pairs={{0,4},{4,8},{8,12},{12,0},{1,5},{5,9},{9,13},{13,1},{2,6},{6,10},{... | collective-permute-start | bytes 688136 | tf_op jit(solution)/shard_map/ppermute | solution.py:524
  5.0 27.8 %collective-permute-start.4 = (f32[2,14,8,256]{3,2,1,0:T(8,128)}, f32[2,14,8,256]{3,2,1,0:T(8,128)S(1)}, u32[]{:S(2)}, u32[]{:S(2)}) collective-permute-start(f32[2,14,8,256]{3,2,1,0:T(8,128)} %get-tuple-element.22), channel_id=1, source_target_pairs={{0,8},{4,12},{8,0},{12,4},{1,9},{5,13},{9,1},{13,5},{2,10},{6,14},... | collective-permute-start | bytes 688136 | tf_op jit(solution)/shard_map/ppermute | solution.py:524
  6.0 37.9 %collective-permute-start.5 = (f32[2,14,8,256]{3,2,1,0:T(8,128)}, f32[2,14,8,256]{3,2,1,0:T(8,128)S(1)}, u32[]{:S(2)}, u32[]{:S(2)}) collective-permute-start(f32[2,14,8,256]{3,2,1,0:T(8,128)} %get-tuple-element.23), channel_id=1, source_target_pairs={{0,12},{4,0},{8,4},{12,8},{1,13},{5,1},{9,5},{13,9},{2,14},{6,2},{... | collective-permute-start | bytes 688136 | tf_op jit(solution)/shard_map/ppermute | solution.py:524
  10.9 34.8 %copy-start.6 = (f32[24,24]{1,0:T(8,128)S(1)}, f32[24,24]{1,0:T(8,128)}, u32[]{:S(2)}) copy-start(f32[24,24]{1,0:T(8,128)} %param.14) | copy-start | bytes 6916
  10.9 34.8 %copy-start.7 = (f32[24,24]{1,0:T(8,128)S(1)}, f32[24,24]{1,0:T(8,128)}, u32[]{:S(2)}) copy-start(f32[24,24]{1,0:T(8,128)} %param.15) | copy-start | bytes 6916
  11.0 34.8 %copy-start.8 = (f32[24,24]{1,0:T(8,128)S(1)}, f32[24,24]{1,0:T(8,128)}, u32[]{:S(2)}) copy-start(f32[24,24]{1,0:T(8,128)} %param.16) | copy-start | bytes 6916
  11.0 36.1 %copy-start.5 = (f32[24,896,1]{1,0,2:T(8,128)S(1)}, f32[24,896,1]{1,0,2:T(8,128)}, u32[]{:S(2)}) copy-start(f32[24,896,1]{1,0,2:T(8,128)} %constant.27) | copy-start | bytes 258052
  11.0 36.4 %copy-start = (bf16[256,2304]{1,0:T(8,128)(2,1)S(1)}, bf16[256,2304]{1,0:T(8,128)(2,1)}, u32[]{:S(2)}) copy-start(bf16[256,2304]{1,0:T(8,128)(2,1)} %constant.26.spread_ref) | copy-start | bytes 3538948
  11.0 47.3 %collective-permute-start.2 = (f32[2,2,12,8,256]{4,3,2,1,0:T(8,128)}, f32[2,2,12,8,256]{4,3,2,1,0:T(8,128)S(1)}, u32[]{:S(2)}, u32[]{:S(2)}) collective-permute-start(f32[2,2,12,8,256]{4,3,2,1,0:T(8,128)} %get-tuple-element.19), channel_id=1, source_target_pairs={{0,8},{4,12},{8,0},{12,4},{1,9},{5,13},{9,1},{13,5},{2,10},{6,14},... | collective-permute-start | bytes 1179656 | tf_op jit(solution)/shard_map/ppermute | solution.py:524
  14.2 44.9 %collective-permute-start = (f32[2,2,12,8,256]{4,3,2,1,0:T(8,128)}, f32[2,2,12,8,256]{4,3,2,1,0:T(8,128)S(1)}, u32[]{:S(2)}, u32[]{:S(2)}) collective-permute-start(f32[2,2,12,8,256]{4,3,2,1,0:T(8,128)} %get-tuple-element.17), channel_id=1, source_target_pairs={{0,4},{4,8},{8,12},{12,0},{1,5},{5,9},{9,13},{13,1},{2,6},{6,10},{... | collective-permute-start | bytes 1179656 | tf_op jit(solution)/shard_map/ppermute | solution.py:524
  16.4 44.4 %collective-permute-start.1 = (f32[2,2,12,8,256]{4,3,2,1,0:T(8,128)}, f32[2,2,12,8,256]{4,3,2,1,0:T(8,128)S(1)}, u32[]{:S(2)}, u32[]{:S(2)}) collective-permute-start(f32[2,2,12,8,256]{4,3,2,1,0:T(8,128)} %get-tuple-element.18), channel_id=1, source_target_pairs={{0,12},{4,0},{8,4},{12,8},{1,13},{5,1},{9,5},{13,9},{2,14},{6,2},{... | collective-permute-start | bytes 1179656 | tf_op jit(solution)/shard_map/ppermute | solution.py:524
  45.0 6.7 %copy-start.4 = (f32[3,8,896]{2,1,0:T(8,128)S(1)}, f32[3,8,896]{2,1,0:T(8,128)}, u32[]{:S(2)}) copy-start(f32[3,8,896]{2,1,0:T(8,128)} %constant.24.clone) | copy-start | bytes 258052
  45.1 7.7 %copy-start.2 = (s32[16]{0:T(128)S(1)}, s32[16]{0:T(128)}, u32[]{:S(2)}) copy-start(s32[16]{0:T(128)} %dest_ref.7) | copy-start | bytes 196
  45.1 7.7 %copy-start.3 = (s32[16]{0:T(128)S(1)}, s32[16]{0:T(128)}, u32[]{:S(2)}) copy-start(s32[16]{0:T(128)} %parent_ref.3) | copy-start | bytes 196
  45.1 7.7 %collective-permute-start.6 = (f32[8,14,8,256]{3,2,1,0:T(8,128)S(1)}, f32[8,14,8,256]{3,2,1,0:T(8,128)S(1)}, u32[]{:S(2)}, u32[]{:S(2)}) collective-permute-start(f32[8,14,8,256]{3,2,1,0:T(8,128)S(1)} %get-tuple-element.26.now_ref.own_ref), channel_id=1, source_target_pairs={{0,1},{1,0},{2,3},{3,2},{4,5},{5,4},{6,7},{7,6},{8,9},{9,8},{10,11... | collective-permute-start | bytes 2752520 | tf_op jit(solution)/shard_map/ppermute | solution.py:535
  45.8 5.1 %collective-permute-start.7 = (f32[8,12,256]{2,1,0:T(8,128)S(1)}, f32[8,12,256]{2,1,0:T(8,128)S(1)}, u32[]{:S(2)}, u32[]{:S(2)}) collective-permute-start(f32[8,12,256]{2,1,0:T(8,128)S(1)} %get-tuple-element.27), channel_id=1, source_target_pairs={{0,2},{2,0},{1,3},{3,1},{4,6},{6,4},{5,7},{7,5},{8,10},{10,8},{9,1... | collective-permute-start | bytes 294920 | tf_op jit(solution)/shard_map/ppermute | solution.py:542
  50.9 1.8 %collective-permute-start.8 = (f32[8,12,256]{2,1,0:T(8,128)S(1)}, f32[8,12,256]{2,1,0:T(8,128)S(1)}, u32[]{:S(2)}, u32[]{:S(2)}) collective-permute-start(f32[8,12,256]{2,1,0:T(8,128)S(1)} %collective-permute-done.7.own_low.own_high), channel_id=1, source_target_pairs={{0,1},{1,0},{2,3},{3,2},{4,5},{5,4},{6,7},{7,6},{8,9},{9,8},{10,11... | collective-permute-start | bytes 294920 | tf_op jit(solution)/shard_map/ppermute | solution.py:546

commit v12 on v11

--- a/solution.py
+++ b/solution.py
@@ -55,7 +55,7 @@
 def first_kernel(per_device, box_count, edge, dest_ref, parent_ref, boxes_ref, coarse_ref, *refs):
     outs, (shells, chosen, dest, parent, box_table, face_table, sems, in_sems) = refs[:box_count], refs[box_count:]
     fields, coarse_count, cells = coarse_ref.shape
-    planes, cross = outs[0].shape[2:]
+    planes, cross = outs[0].shape[1:]
     own, slab = lax.axis_index("box"), lax.axis_index("slab")
     fetches = [
         pltpu.make_async_copy(coarse_ref, shells, in_sems.at[0]),
@@ -72,7 +72,7 @@
 
     def copy(shift, k, b):
         return pltpu.make_async_copy(
-            boxes_ref.at[0, b], outs[shift].at[k, pl.ds(0, fields)], sems.at[shift, k]
+            boxes_ref.at[0, b], outs[shift].at[pl.ds(k * fields, fields)], sems.at[shift, k]
         )
 
     for shift, k, slot in each_slot(box_count):
@@ -84,7 +84,7 @@
 
         @pl.when(b < 0)
         def _():
-            outs[shift][k, :fields] = jnp.zeros((fields, planes, cross), jnp.float32)
+            outs[shift][k * fields : (k + 1) * fields] = jnp.zeros((fields, planes, cross), jnp.float32)
 
     for slot in range(2 * box_count):
         face_table[slot] = -1
@@ -109,14 +109,10 @@
     chosen[...] = (high + (middle + low)).reshape(chosen.shape)
     for shift, k, slot in each_slot(box_count):
         local = face_table[slot]
-        for row in range(ROWS):
-            to = fields + row // planes
-            if row < fields:
-                values = chosen[row, pl.ds(jnp.maximum(local, 0), 1)]
-                values = jnp.where(local >= 0, values, 0.0)
-            else:
-                values = jnp.zeros((1, cross), jnp.float32)
-            outs[shift][k, to, row % planes : row % planes + 1] = values
+        for f in range(fields):
+            values = chosen[f, pl.ds(jnp.maximum(local, 0), 1)]
+            block, row = divmod(k * fields + f, planes)
+            outs[shift][2 * fields + block, row : row + 1] = jnp.where(local >= 0, values, 0.0)
     for shift, k, slot in each_slot(box_count):
         b = box_table[slot]
 
@@ -129,7 +125,7 @@
     per_device, fields, planes, cross = boxes.shape[1:]
     coarse = jnp.transpose(coarse, (1, 0, 2))
     hbm, vmem = pl.BlockSpec(memory_space=pltpu.HBM), pl.BlockSpec(memory_space=pltpu.VMEM)
-    item = (2, fields + ROWS // planes, planes, cross)
+    item = (2 * fields + 2 * fields // planes, planes, cross)
     return pl.pallas_call(
         functools.partial(first_kernel, per_device, box_count, edge),
         out_shape=[jax.ShapeDtypeStruct(item, jnp.float32)] * box_count,
@@ -250,25 +246,34 @@
     )(*pieces, moved, after)
 
 
-def arrive_kernel(box_count, slabs, early, fields, *refs):
-    pieces, later = refs[:box_count], refs[box_count : box_count + len(early)]
-    now_ref, moved_ref, *edges, sems = refs[box_count + len(early) + 1 :]
+def arrive_kernel(box_count, slabs, fields, *refs):
+    pieces = refs[:box_count]
+    now_ref, moved_ref, *edges, own_rows, sems, own_sem = refs[box_count + 1 :]
     own, slab = lax.axis_index("box"), lax.axis_index("slab")
-    planes = now_ref.shape[2]
-    mine = pltpu.make_async_copy(pieces[0], now_ref.at[pl.ds(2 * own, 2)], sems.at[0])
-    mine.start()
+    planes, cross = now_ref.shape[2:]
+    faces = pl.ds(2 * fields, own_rows.shape[0])
+    mine = [pltpu.make_async_copy(pieces[0].at[faces], own_rows, own_sem)]
     copies = []
-    for turn in range(1, box_count):
-        to = moved_ref.at[0, pl.ds(2 * source_of(own, turn, box_count), 2)]
-        copies.append(pltpu.make_async_copy(pieces[turn].at[:, pl.ds(0, fields)], to, sems.at[turn]))
-    for n, turn in enumerate(early):
-        copies.append(settle_later(later[n], turn, moved_ref, sems.at[box_count + n]))
-    for copy in copies:
+    for turn in range(box_count):
+        source = source_of(own, turn, box_count)
+        for k in range(2):
+            box = pieces[turn].at[pl.ds(k * fields, fields)]
+            if turn:
+                copies.append(pltpu.make_async_copy(box, moved_ref.at[0, 2 * source + k], sems.at[turn, k]))
+            else:
+                mine.append(pltpu.make_async_copy(box, now_ref.at[2 * own + k, pl.ds(0, fields)], sems.at[0, k]))
+    for copy in mine + copies:
         copy.start()
     faced = [jnp.where(slab == 0, planes - 1, 0)] if slabs == 2 else [0, planes - 1]
 
-    def cut(source):
+    def place_rows(rows_ref, first_block, source):
         for k in range(2):
+            for f in range(ROWS):
+                values = jnp.zeros((1, cross), jnp.float32)
+                if f < fields:
+                    block, row = divmod(k * fields + f, planes)
+                    values = rows_ref[first_block + block, row : row + 1]
+                now_ref[2 * source + k, fields + f // planes, f % planes : f % planes + 1] = values
             for edge_ref, plane in zip(edges, faced):
                 for f in range(fields):
                     edge_ref[2 * source + k, f : f + 1] = now_ref[2 * source + k, f, pl.ds(plane, 1)]
@@ -276,35 +281,39 @@
     for turn in range(1, box_count):
         source = source_of(own, turn, box_count)
         for k in range(2):
-            now_ref[2 * source + k] = pieces[turn][k]
-        cut(source)
-    mine.wait()
-    cut(own)
+            now_ref[2 * source + k, :fields] = pieces[turn][k * fields : (k + 1) * fields]
+        place_rows(pieces[turn], 2 * fields, source)
+    for copy in mine:
+        copy.wait()
+    place_rows(own_rows, 0, own)
     for copy in copies:
         copy.wait()
 
 
-def arrive(pieces, early, later, moved, slabs):
+def arrive(pieces, moved, slabs):
     box_count = len(pieces)
-    _, blocks, planes, cross = pieces[0].shape
+    _, planes, cross = pieces[0].shape
     fields = moved.shape[2]
     slots = 2 * box_count
     sides = 1 if slabs == 2 else 2
     vmem, hbm = pl.BlockSpec(memory_space=pltpu.VMEM), pl.BlockSpec(memory_space=pltpu.HBM)
-    shapes = [(slots, blocks, planes, cross), moved.shape] + [(slots, fields, cross)] * sides
-    count = box_count + len(later)
+    shapes = [(slots, fields + ROWS // planes, planes, cross), moved.shape] + [(slots, fields, cross)] * sides
     return pl.pallas_call(
-        functools.partial(arrive_kernel, box_count, slabs, early, fields),
+        functools.partial(arrive_kernel, box_count, slabs, fields),
         out_shape=[jax.ShapeDtypeStruct(shape, jnp.float32) for shape in shapes],
-        in_specs=[hbm] + [vmem] * (count - 1) + [hbm],
+        in_specs=[hbm] + [vmem] * (box_count - 1) + [hbm],
         out_specs=[vmem, hbm] + [vmem] * sides,
-        scratch_shapes=[pltpu.SemaphoreType.DMA((count,))],
-        input_output_aliases={count: 1},
+        scratch_shapes=[
+            pltpu.VMEM((2 * fields // planes, planes, cross), jnp.float32),
+            pltpu.SemaphoreType.DMA((box_count, 2)),
+            pltpu.SemaphoreType.DMA,
+        ],
+        input_output_aliases={box_count: 1},
         compiler_params=pltpu.CompilerParams(vmem_limit_bytes=48 * 2 ** 20),
         cost_estimate=pl.CostEstimate(
             flops=0, bytes_accessed=12 * box_count * pieces[0].size, transcendentals=0
         ),
-    )(*pieces, *later, moved)
+    )(*pieces, moved)
 
 
 def face_cells(lane, edge, coarse_planes, slab):
@@ -529,7 +538,7 @@
     arrived = [first[0]] + [send(first[turn], turn) for turn in range(1, box_count)]
     moved, *middle = pack_later((0,) + tuple(range(2, box_count - 1)), boxes, move_dest, box_count)
     middle = [send(piece, n + 2) for n, piece in enumerate(middle)]
-    now, moved, *facing = arrive(arrived, (), [], moved, slabs)
+    now, moved, *facing = arrive(arrived, moved, slabs)
 
     swap = [(0, 1), (1, 0)]
     now_other = lax.ppermute(now, "fld", swap)

time: 61.9 us -> 61.4 us (level)
  starting transfers between devices: 8.89 us -> 8.17 us
    ppermute x6, starting transfers between devices: 6.19 us -> 5.47 us  [send(): lax.ppermute(piece, 'box', [(s, (s + turn) % box_count) for s in range(bo...]
    pallas_call x1, Pallas kernels: 5.5 us -> 6.16 us  [body(): pl.pallas_call(functools.partial(slope_kernel, edge, planes, fields, coar...]
  transfers between devices with their start and end apart: 9 -> 9, of which waited for: 5 -> 5; matrix products, arithmetic and copies ran while one was open for 1% -> 1% of each run, Pallas kernels for 23% -> 25%
where the time goes in v12:
time: 61.4 us; the launch traced here: 61 us
  waiting for transfers between devices  32.6 us (53%)
  Pallas kernels  18.8 us (31%)
  starting transfers between devices  8.17 us (13%)
  between operations  0.8 us (1%)
    ppermute x6, waiting for transfers between devices, send(): lax.ppermute(piece, 'box', [(s, (s + turn) % box_count) for s in range(bo...  28.7 us
    pallas_call x2, Pallas kernels, pack_later(): pl.pallas_call(functools.partial(later_kernel, turns, per_device, box_cou...  6.42 us
    pallas_call x1, Pallas kernels, body(): pl.pallas_call(functools.partial(slope_kernel, edge, planes, fields, coar...  6.16 us
    ppermute x6, starting transfers between devices, send(): lax.ppermute(piece, 'box', [(s, (s + turn) % box_count) for s in range(bo...  5.47 us
    ppermute x1, waiting for transfers between devices, shifted(): return lax.ppermute(values, 'slab', swap if slabs == 2 else pairs)  3.01 us
    pallas_call x1, Pallas kernels, pack_first(): pl.pallas_call(functools.partial(first_kernel, per_device, box_count, edg...  2.95 us
    pallas_call x2, Pallas kernels, settle(): pl.pallas_call(functools.partial(settle_kernel, turns), out_shape=jax.Sha...  1.64 us
  transfers between devices with their start and end apart: 9, of which 5 were waited for; matrix products, arithmetic and copies ran while one was open for 1% of the time, Pallas kernels for 25%

profile of v12, /device:TPU:9, one launch (start us, length us, event | category | flops | bytes accessed | tf_op | source)
XLA Modules:
  0.0 61.0 jit_solution(12654220631972799607)
XLA Ops:
  0.6 3.0 %shard_map.115 = (f32[27,8,256]{2,1,0:T(8,128)}, f32[27,8,256]{2,1,0:T(8,128)}, f32[27,8,256]{2,1,0:T(8,128)}, f32[27,8,256]{2,1,0:T(8,128)}) custom-call(s32[16]{0:T(128)} %dest_ref.7, s32[16]{0:T(128)} %parent_ref.3, f32[3,4,12,8,256]{4,3,2,1,0:T(8,128)} %boxes_ref.5, f32[12,8,1000]{2,1,0:T(8,128)} %bitcast.11), custom_call_target="tpu_custom_call" | custom-call | flops 147456000 | bytes 2743296 | tf_op jit(solution)/shard_map/pallas_call | solution.py:129
  3.6 0.0 copy-start.1
  3.6 1.3 %collective-permute-start.3 = (f32[27,8,256]{2,1,0:T(8,128)}, f32[27,8,256]{2,1,0:T(8,128)S(1)}, u32[]{:S(2)}, u32[]{:S(2)}) collective-permute-start(f32[27,8,256]{2,1,0:T(8,128)} %get-tuple-element.21), channel_id=1, source_target_pairs={{0,4},{4,8},{8,12},{12,0},{1,5},{5,9},{9,13},{13,1},{2,6},{6,10},{... | collective-permute-start | bytes 663560 | tf_op jit(solution)/shard_map/ppermute | solution.py:533
  4.9 1.1 %collective-permute-start.4 = (f32[27,8,256]{2,1,0:T(8,128)}, f32[27,8,256]{2,1,0:T(8,128)S(1)}, u32[]{:S(2)}, u32[]{:S(2)}) collective-permute-start(f32[27,8,256]{2,1,0:T(8,128)} %get-tuple-element.22), channel_id=1, source_target_pairs={{0,8},{4,12},{8,0},{12,4},{1,9},{5,13},{9,1},{13,5},{2,10},{6,14},... | collective-permute-start | bytes 663560 | tf_op jit(solution)/shard_map/ppermute | solution.py:533
  6.1 1.4 %collective-permute-start.5 = (f32[27,8,256]{2,1,0:T(8,128)}, f32[27,8,256]{2,1,0:T(8,128)S(1)}, u32[]{:S(2)}, u32[]{:S(2)}) collective-permute-start(f32[27,8,256]{2,1,0:T(8,128)} %get-tuple-element.23), channel_id=1, source_target_pairs={{0,12},{4,0},{8,4},{12,8},{1,13},{5,1},{9,5},{13,9},{2,14},{6,2},{... | collective-permute-start | bytes 663560 | tf_op jit(solution)/shard_map/ppermute | solution.py:533
  7.5 3.5 %shard_map.114 = (f32[3,8,12,8,256]{4,3,2,1,0:T(8,128)}, f32[2,2,12,8,256]{4,3,2,1,0:T(8,128)}) custom-call(s32[16]{0:T(128)} %dest_ref.7, f32[3,4,12,8,256]{4,3,2,1,0:T(8,128)} %boxes_ref.5), custom_call_target="tpu_custom_call" | custom-call | bytes 2359296 | tf_op jit(solution)/shard_map/pallas_call | solution.py:199
  11.0 0.0 copy-start.6
  11.0 0.0 copy-start.7
  11.0 0.0 copy-start.8
  11.0 0.0 copy-start.5
  11.0 0.0 copy-start
  11.0 0.1 collective-permute-start.2
  11.1 2.9 %shard_map.113 = (f32[2,2,12,8,256]{4,3,2,1,0:T(8,128)}, f32[2,2,12,8,256]{4,3,2,1,0:T(8,128)}) custom-call(s32[16]{0:T(128)} %dest_ref.7, f32[3,4,12,8,256]{4,3,2,1,0:T(8,128)} %boxes_ref.5), custom_call_target="tpu_custom_call" | custom-call | bytes 2359296 | tf_op jit(solution)/shard_map/pallas_call | solution.py:199
  14.0 1.2 %collective-permute-start = (f32[2,2,12,8,256]{4,3,2,1,0:T(8,128)}, f32[2,2,12,8,256]{4,3,2,1,0:T(8,128)S(1)}, u32[]{:S(2)}, u32[]{:S(2)}) collective-permute-start(f32[2,2,12,8,256]{4,3,2,1,0:T(8,128)} %get-tuple-element.17), channel_id=1, source_target_pairs={{0,4},{4,8},{8,12},{12,0},{1,5},{5,9},{9,13},{13,1},{2,6},{6,10},{... | collective-permute-start | bytes 1179656 | tf_op jit(solution)/shard_map/ppermute | solution.py:533
  15.2 0.0 collective-permute-done.3.refs_1_
  15.2 0.4 collective-permute-start.1
  15.6 16.5 %collective-permute-done.4.refs_2_ = f32[27,8,256]{2,1,0:T(8,128)S(1)} collective-permute-done((f32[27,8,256]{2,1,0:T(8,128)}, f32[27,8,256]{2,1,0:T(8,128)S(1)}, u32[]{:S(2)}, u32[]{:S(2)}) %collective-permute-start.4) | collective-permute-done | bytes 221216 | tf_op jit(solution)/shard_map/ppermute | solution.py:533
  32.0 11.2 %collective-permute-done.5.refs_3_ = f32[27,8,256]{2,1,0:T(8,128)S(1)} collective-permute-done((f32[27,8,256]{2,1,0:T(8,128)}, f32[27,8,256]{2,1,0:T(8,128)S(1)}, u32[]{:S(2)}, u32[]{:S(2)}) %collective-permute-start.5) | collective-permute-done | bytes 221216 | tf_op jit(solution)/shard_map/ppermute | solution.py:533
  43.2 0.0 copy-done.1
  43.2 1.1 %shard_map.116 = (f32[8,14,8,256]{3,2,1,0:T(8,128)S(1)}, f32[3,8,12,8,256]{4,3,2,1,0:T(8,128)}, f32[8,12,256]{2,1,0:T(8,128)S(1)}) custom-call(f32[27,8,256]{2,1,0:T(8,128)S(1)} %copy-done.1, f32[27,8,256]{2,1,0:T(8,128)S(1)} %collective-permute-done.3.refs_1_, f32[27,8,256]{2,1,0:T(8,128)S(1)} %collective-permute-done.4.refs_2_, ...), custom_call_target="tpu_custom_call", output_to_operand_aliasing={{1}: (4, {})} | custom-call | bytes 2654208 | tf_op jit(solution)/shard_map/pallas_call | solution.py:301
  44.4 0.0 copy-start.4
  44.4 0.0 copy-start.2
  44.4 0.0 copy-start.3
  44.4 0.7 %collective-permute-start.6 = (f32[8,14,8,256]{3,2,1,0:T(8,128)S(1)}, f32[8,14,8,256]{3,2,1,0:T(8,128)S(1)}, u32[]{:S(2)}, u32[]{:S(2)}) collective-permute-start(f32[8,14,8,256]{3,2,1,0:T(8,128)S(1)} %get-tuple-element.26.now_ref.own_ref), channel_id=1, source_target_pairs={{0,1},{1,0},{2,3},{3,2},{4,5},{5,4},{6,7},{7,6},{8,9},{9,8},{10,11... | collective-permute-start | bytes 2752520 | tf_op jit(solution)/shard_map/ppermute | solution.py:544
  45.1 0.0 copy-done.6
  45.1 0.0 copy-done.7
  45.1 0.0 copy-done.8
  45.1 0.1 fusion.7
  45.2 1.2 %collective-permute-start.7 = (f32[8,12,256]{2,1,0:T(8,128)S(1)}, f32[8,12,256]{2,1,0:T(8,128)S(1)}, u32[]{:S(2)}, u32[]{:S(2)}) collective-permute-start(f32[8,12,256]{2,1,0:T(8,128)S(1)} %get-tuple-element.27), channel_id=1, source_target_pairs={{0,2},{2,0},{1,3},{3,1},{4,6},{6,4},{5,7},{7,5},{8,10},{10,8},{9,1... | collective-permute-start | bytes 294920 | tf_op jit(solution)/shard_map/ppermute | solution.py:551
  46.4 0.0 copy-done.5
  46.4 0.4 fusion.2
  46.8 0.0 copy-done
  46.8 0.5 shard_map.117.own_rim
  47.3 3.0 %collective-permute-done.7.own_low.own_high = f32[8,12,256]{2,1,0:T(8,128)S(1)} collective-permute-done((f32[8,12,256]{2,1,0:T(8,128)S(1)}, f32[8,12,256]{2,1,0:T(8,128)S(1)}, u32[]{:S(2)}, u32[]{:S(2)}) %collective-permute-start.7) | collective-permute-done | bytes 98336 | tf_op jit(solution)/shard_map/ppermute | solution.py:551
  50.3 0.8 %collective-permute-start.8 = (f32[8,12,256]{2,1,0:T(8,128)S(1)}, f32[8,12,256]{2,1,0:T(8,128)S(1)}, u32[]{:S(2)}, u32[]{:S(2)}) collective-permute-start(f32[8,12,256]{2,1,0:T(8,128)S(1)} %collective-permute-done.7.own_low.own_high), channel_id=1, source_target_pairs={{0,1},{1,0},{2,3},{3,2},{4,5},{5,4},{6,7},{7,6},{8,9},{9,8},{10,11... | collective-permute-start | bytes 294920 | tf_op jit(solution)/shard_map/ppermute | solution.py:555
  51.1 0.0 copy-done.4
  51.1 0.1 multiply_reduce_fusion
  51.2 0.9 %collective-permute-done.8.other_low.other_high = f32[8,12,256]{2,1,0:T(8,128)S(1)} collective-permute-done((f32[8,12,256]{2,1,0:T(8,128)S(1)}, f32[8,12,256]{2,1,0:T(8,128)S(1)}, u32[]{:S(2)}, u32[]{:S(2)}) %collective-permute-start.8) | collective-permute-done | bytes 98336 | tf_op jit(solution)/shard_map/ppermute | solution.py:555
  52.1 0.0 collective-permute-done.6.other_ref
  52.1 0.0 copy-done.2
  52.1 0.0 copy-done.3
  52.1 6.2 %shard_map.118 = (f32[8,12,8,256]{3,2,1,0:T(8,128)}, f32[8,128]{1,0:T(8,128)S(1)}) custom-call(s32[16]{0:T(128)S(1)} %copy-done.2, s32[16]{0:T(128)S(1)} %copy-done.3, f32[8,14,8,256]{3,2,1,0:T(8,128)S(1)} %get-tuple-element.26.now_ref.own_ref, f32[8,14,8,256]{3,2,1,0:T(8,128)S(1)} %collective-permute-done.6.other_ref, ...), custom_call_target="tpu_custom_call" | custom-call | flops 528482304 | bytes 2752512 | tf_op jit(solution)/shard_map/pallas_call | solution.py:563
  58.3 0.0 collective-permute-done.2.refs_0_
  58.3 0.8 %shard_map.119.refs_2_ = f32[3,8,12,8,256]{4,3,2,1,0:T(8,128)} custom-call(f32[2,2,12,8,256]{4,3,2,1,0:T(8,128)S(1)} %collective-permute-done.2.refs_0_, f32[3,8,12,8,256]{4,3,2,1,0:T(8,128)} %get-tuple-element.25.refs_1_, f32[8,128]{1,0:T(8,128)S(1)} %get-tuple-element.30.refs_2_.refs_3_), custom_call_target="tpu_custom_call", output_to_operand_aliasing={{}: (1, {})} | custom-call | bytes 786432 | tf_op jit(solution)/shard_map/pallas_call | solution.py:235
  59.0 0.0 collective-permute-done.refs_0_
  59.1 1.0 %collective-permute-done.1.refs_1_ = f32[2,2,12,8,256]{4,3,2,1,0:T(8,128)S(1)} collective-permute-done((f32[2,2,12,8,256]{4,3,2,1,0:T(8,128)}, f32[2,2,12,8,256]{4,3,2,1,0:T(8,128)S(1)}, u32[]{:S(2)}, u32[]{:S(2)}) %collective-permute-start.1) | collective-permute-done | bytes 393248 | tf_op jit(solution)/shard_map/ppermute | solution.py:533
  60.1 0.9 %shard_map.120 = f32[3,8,12,8,256]{4,3,2,1,0:T(8,128)} custom-call(f32[2,2,12,8,256]{4,3,2,1,0:T(8,128)S(1)} %collective-permute-done.refs_0_, f32[2,2,12,8,256]{4,3,2,1,0:T(8,128)S(1)} %collective-permute-done.1.refs_1_, f32[3,8,12,8,256]{4,3,2,1,0:T(8,128)} %shard_map.119.refs_2_, ...), custom_call_target="tpu_custom_call", output_to_operand_aliasing={{}: (2, {})} | custom-call | bytes 1572864 | tf_op jit(solution)/shard_map/pallas_call | solution.py:235
  (2 shorter events, 0.0 us)
Async XLA Ops:
  3.6 39.7 %copy-start.1 = (f32[27,8,256]{2,1,0:T(8,128)S(1)}, f32[27,8,256]{2,1,0:T(8,128)}, u32[]{:S(2)}) copy-start(f32[27,8,256]{2,1,0:T(8,128)} %get-tuple-element.20.refs_0_) | copy-start | bytes 663556
  3.6 11.6 %collective-permute-start.3 = (f32[27,8,256]{2,1,0:T(8,128)}, f32[27,8,256]{2,1,0:T(8,128)S(1)}, u32[]{:S(2)}, u32[]{:S(2)}) collective-permute-start(f32[27,8,256]{2,1,0:T(8,128)} %get-tuple-element.21), channel_id=1, source_target_pairs={{0,4},{4,8},{8,12},{12,0},{1,5},{5,9},{9,13},{13,1},{2,6},{6,10},{... | collective-permute-start | bytes 663560 | tf_op jit(solution)/shard_map/ppermute | solution.py:533
  4.9 27.1 %collective-permute-start.4 = (f32[27,8,256]{2,1,0:T(8,128)}, f32[27,8,256]{2,1,0:T(8,128)S(1)}, u32[]{:S(2)}, u32[]{:S(2)}) collective-permute-start(f32[27,8,256]{2,1,0:T(8,128)} %get-tuple-element.22), channel_id=1, source_target_pairs={{0,8},{4,12},{8,0},{12,4},{1,9},{5,13},{9,1},{13,5},{2,10},{6,14},... | collective-permute-start | bytes 663560 | tf_op jit(solution)/shard_map/ppermute | solution.py:533
  6.1 37.2 %collective-permute-start.5 = (f32[27,8,256]{2,1,0:T(8,128)}, f32[27,8,256]{2,1,0:T(8,128)S(1)}, u32[]{:S(2)}, u32[]{:S(2)}) collective-permute-start(f32[27,8,256]{2,1,0:T(8,128)} %get-tuple-element.23), channel_id=1, source_target_pairs={{0,12},{4,0},{8,4},{12,8},{1,13},{5,1},{9,5},{13,9},{2,14},{6,2},{... | collective-permute-start | bytes 663560 | tf_op jit(solution)/shard_map/ppermute | solution.py:533
  11.0 34.1 %copy-start.6 = (f32[24,24]{1,0:T(8,128)S(1)}, f32[24,24]{1,0:T(8,128)}, u32[]{:S(2)}) copy-start(f32[24,24]{1,0:T(8,128)} %param.14) | copy-start | bytes 6916
  11.0 34.1 %copy-start.7 = (f32[24,24]{1,0:T(8,128)S(1)}, f32[24,24]{1,0:T(8,128)}, u32[]{:S(2)}) copy-start(f32[24,24]{1,0:T(8,128)} %param.15) | copy-start | bytes 6916
  11.0 34.1 %copy-start.8 = (f32[24,24]{1,0:T(8,128)S(1)}, f32[24,24]{1,0:T(8,128)}, u32[]{:S(2)}) copy-start(f32[24,24]{1,0:T(8,128)} %param.16) | copy-start | bytes 6916
  11.0 35.4 %copy-start.5 = (f32[24,896,1]{1,0,2:T(8,128)S(1)}, f32[24,896,1]{1,0,2:T(8,128)}, u32[]{:S(2)}) copy-start(f32[24,896,1]{1,0,2:T(8,128)} %constant.27) | copy-start | bytes 258052
  11.0 35.8 %copy-start = (bf16[256,2304]{1,0:T(8,128)(2,1)S(1)}, bf16[256,2304]{1,0:T(8,128)(2,1)}, u32[]{:S(2)}) copy-start(bf16[256,2304]{1,0:T(8,128)(2,1)} %constant.26.spread_ref) | copy-start | bytes 3538948
  11.0 47.3 %collective-permute-start.2 = (f32[2,2,12,8,256]{4,3,2,1,0:T(8,128)}, f32[2,2,12,8,256]{4,3,2,1,0:T(8,128)S(1)}, u32[]{:S(2)}, u32[]{:S(2)}) collective-permute-start(f32[2,2,12,8,256]{4,3,2,1,0:T(8,128)} %get-tuple-element.19), channel_id=1, source_target_pairs={{0,8},{4,12},{8,0},{12,4},{1,9},{5,13},{9,1},{13,5},{2,10},{6,14},... | collective-permute-start | bytes 1179656 | tf_op jit(solution)/shard_map/ppermute | solution.py:533
  14.0 45.0 %collective-permute-start = (f32[2,2,12,8,256]{4,3,2,1,0:T(8,128)}, f32[2,2,12,8,256]{4,3,2,1,0:T(8,128)S(1)}, u32[]{:S(2)}, u32[]{:S(2)}) collective-permute-start(f32[2,2,12,8,256]{4,3,2,1,0:T(8,128)} %get-tuple-element.17), channel_id=1, source_target_pairs={{0,4},{4,8},{8,12},{12,0},{1,5},{5,9},{9,13},{13,1},{2,6},{6,10},{... | collective-permute-start | bytes 1179656 | tf_op jit(solution)/shard_map/ppermute | solution.py:533
  15.2 44.9 %collective-permute-start.1 = (f32[2,2,12,8,256]{4,3,2,1,0:T(8,128)}, f32[2,2,12,8,256]{4,3,2,1,0:T(8,128)S(1)}, u32[]{:S(2)}, u32[]{:S(2)}) collective-permute-start(f32[2,2,12,8,256]{4,3,2,1,0:T(8,128)} %get-tuple-element.18), channel_id=1, source_target_pairs={{0,12},{4,0},{8,4},{12,8},{1,13},{5,1},{9,5},{13,9},{2,14},{6,2},{... | collective-permute-start | bytes 1179656 | tf_op jit(solution)/shard_map/ppermute | solution.py:533
  44.4 6.7 %copy-start.4 = (f32[3,8,896]{2,1,0:T(8,128)S(1)}, f32[3,8,896]{2,1,0:T(8,128)}, u32[]{:S(2)}) copy-start(f32[3,8,896]{2,1,0:T(8,128)} %constant.24.clone) | copy-start | bytes 258052
  44.4 7.7 %copy-start.2 = (s32[16]{0:T(128)S(1)}, s32[16]{0:T(128)}, u32[]{:S(2)}) copy-start(s32[16]{0:T(128)} %dest_ref.7) | copy-start | bytes 196
  44.4 7.7 %copy-start.3 = (s32[16]{0:T(128)S(1)}, s32[16]{0:T(128)}, u32[]{:S(2)}) copy-start(s32[16]{0:T(128)} %parent_ref.3) | copy-start | bytes 196
  44.4 7.7 %collective-permute-start.6 = (f32[8,14,8,256]{3,2,1,0:T(8,128)S(1)}, f32[8,14,8,256]{3,2,1,0:T(8,128)S(1)}, u32[]{:S(2)}, u32[]{:S(2)}) collective-permute-start(f32[8,14,8,256]{3,2,1,0:T(8,128)S(1)} %get-tuple-element.26.now_ref.own_ref), channel_id=1, source_target_pairs={{0,1},{1,0},{2,3},{3,2},{4,5},{5,4},{6,7},{7,6},{8,9},{9,8},{10,11... | collective-permute-start | bytes 2752520 | tf_op jit(solution)/shard_map/ppermute | solution.py:544
  45.2 5.1 %collective-permute-start.7 = (f32[8,12,256]{2,1,0:T(8,128)S(1)}, f32[8,12,256]{2,1,0:T(8,128)S(1)}, u32[]{:S(2)}, u32[]{:S(2)}) collective-permute-start(f32[8,12,256]{2,1,0:T(8,128)S(1)} %get-tuple-element.27), channel_id=1, source_target_pairs={{0,2},{2,0},{1,3},{3,1},{4,6},{6,4},{5,7},{7,5},{8,10},{10,8},{9,1... | collective-permute-start | bytes 294920 | tf_op jit(solution)/shard_map/ppermute | solution.py:551
  50.3 1.8 %collective-permute-start.8 = (f32[8,12,256]{2,1,0:T(8,128)S(1)}, f32[8,12,256]{2,1,0:T(8,128)S(1)}, u32[]{:S(2)}, u32[]{:S(2)}) collective-permute-start(f32[8,12,256]{2,1,0:T(8,128)S(1)} %collective-permute-done.7.own_low.own_high), channel_id=1, source_target_pairs={{0,1},{1,0},{2,3},{3,2},{4,5},{5,4},{6,7},{7,6},{8,9},{9,8},{10,11... | collective-permute-start | bytes 294920 | tf_op jit(solution)/shard_map/ppermute | solution.py:555

commit v13 on v12

--- a/solution.py
+++ b/solution.py
@@ -16,12 +16,10 @@
     return -(-value // unit) * unit
 
 
-def split_three(values):
+def split_two(values):
     high = values.astype(jnp.bfloat16)
-    rest = values - high.astype(jnp.float32)
-    middle = rest.astype(jnp.bfloat16)
-    low = (rest - middle.astype(jnp.float32)).astype(jnp.bfloat16)
-    return high, middle, low
+    low = (values - high.astype(jnp.float32)).astype(jnp.bfloat16)
+    return jnp.concatenate([high, low], axis=0)
 
 
 def place_boxes(per_device, box_count, dest_ref, table):
@@ -102,11 +100,9 @@
 
     lax.fori_loop(0, dest.shape[0], place, 0)
     fetches[0].wait()
-    high, middle, low = (
-        jnp.dot(part, one_hot, preferred_element_type=jnp.float32)
-        for part in split_three(shells[...].reshape(fields * coarse_count, cells))
-    )
-    chosen[...] = (high + (middle + low)).reshape(chosen.shape)
+    count = fields * coarse_count
+    both = jnp.dot(split_two(shells[...].reshape(count, cells)), one_hot, preferred_element_type=jnp.float32)
+    chosen[...] = (both[:count] + both[count:]).reshape(chosen.shape)
     for shift, k, slot in each_slot(box_count):
         local = face_table[slot]
         for f in range(fields):
@@ -388,10 +384,7 @@
         for block in range(ROWS // planes):
             at = slot * ROWS + block * planes
             out_ref[at : at + planes, :cross] = slots_ref[slot, fields + block]
-    cells = out_ref[:, :cross]
-    high = cells.astype(jnp.bfloat16)
-    low = (cells - high.astype(jnp.float32)).astype(jnp.bfloat16)
-    both = jnp.dot(jnp.concatenate([high, low], axis=0), spread_ref[...], preferred_element_type=jnp.float32)
+    both = jnp.dot(split_two(out_ref[:, :cross]), spread_ref[...], preferred_element_type=jnp.float32)
     out_ref[...] = both[: slots * ROWS] + both[slots * ROWS :]
 
 

time: 61.4 us -> 61.4 us (level)
  starting transfers between devices: 8.17 us -> 8.9 us
    ppermute x6, starting transfers between devices: 5.47 us -> 6.2 us  [send(): lax.ppermute(piece, 'box', [(s, (s + turn) % box_count) for s in range(bo...]
    pallas_call x1, Pallas kernels: 6.16 us -> 5.5 us  [body(): pl.pallas_call(functools.partial(slope_kernel, edge, planes, fields, coar...]
  transfers between devices with their start and end apart: 9 -> 9, of which waited for: 5 -> 5; matrix products, arithmetic and copies ran while one was open for 1% -> 1% of each run, Pallas kernels for 25% -> 24%
where the time goes in v13:
time: 61.4 us; the launch traced here: 61 us
  waiting for transfers between devices  32.5 us (53%)
  Pallas kernels  18.2 us (30%)
  starting transfers between devices  8.9 us (14%)
  between operations  0.81 us (1%)
    ppermute x6, waiting for transfers between devices, send(): lax.ppermute(piece, 'box', [(s, (s + turn) % box_count) for s in range(bo...  28.6 us
    pallas_call x2, Pallas kernels, pack_later(): pl.pallas_call(functools.partial(later_kernel, turns, per_device, box_cou...  6.46 us
    ppermute x6, starting transfers between devices, send(): lax.ppermute(piece, 'box', [(s, (s + turn) % box_count) for s in range(bo...  6.2 us
    pallas_call x1, Pallas kernels, body(): pl.pallas_call(functools.partial(slope_kernel, edge, planes, fields, coar...  5.5 us
    ppermute x1, waiting for transfers between devices, shifted(): return lax.ppermute(values, 'slab', swap if slabs == 2 else pairs)  3.02 us
    pallas_call x1, Pallas kernels, pack_first(): pl.pallas_call(functools.partial(first_kernel, per_device, box_count, edg...  2.93 us
    pallas_call x2, Pallas kernels, settle(): pl.pallas_call(functools.partial(settle_kernel, turns), out_shape=jax.Sha...  1.64 us
  transfers between devices with their start and end apart: 9, of which 5 were waited for; matrix products, arithmetic and copies ran while one was open for 1% of the time, Pallas kernels for 24%

profile of v13, /device:TPU:9, one launch (start us, length us, event | category | flops | bytes accessed | tf_op | source)
XLA Modules:
  0.0 61.0 jit_solution(6666389103950948759)
XLA Ops:
  0.6 2.9 %shard_map.115 = (f32[27,8,256]{2,1,0:T(8,128)}, f32[27,8,256]{2,1,0:T(8,128)}, f32[27,8,256]{2,1,0:T(8,128)}, f32[27,8,256]{2,1,0:T(8,128)}) custom-call(s32[16]{0:T(128)} %dest_ref.7, s32[16]{0:T(128)} %parent_ref.3, f32[3,4,12,8,256]{4,3,2,1,0:T(8,128)} %boxes_ref.5, f32[12,8,1000]{2,1,0:T(8,128)} %bitcast.11), custom_call_target="tpu_custom_call" | custom-call | flops 147456000 | bytes 2743296 | tf_op jit(solution)/shard_map/pallas_call | solution.py:125
  3.6 0.0 copy-start.1
  3.6 1.3 %collective-permute-start.3 = (f32[27,8,256]{2,1,0:T(8,128)}, f32[27,8,256]{2,1,0:T(8,128)S(1)}, u32[]{:S(2)}, u32[]{:S(2)}) collective-permute-start(f32[27,8,256]{2,1,0:T(8,128)} %get-tuple-element.21), channel_id=1, source_target_pairs={{0,4},{4,8},{8,12},{12,0},{1,5},{5,9},{9,13},{13,1},{2,6},{6,10},{... | collective-permute-start | bytes 663560 | tf_op jit(solution)/shard_map/ppermute | solution.py:526
  4.9 1.1 %collective-permute-start.4 = (f32[27,8,256]{2,1,0:T(8,128)}, f32[27,8,256]{2,1,0:T(8,128)S(1)}, u32[]{:S(2)}, u32[]{:S(2)}) collective-permute-start(f32[27,8,256]{2,1,0:T(8,128)} %get-tuple-element.22), channel_id=1, source_target_pairs={{0,8},{4,12},{8,0},{12,4},{1,9},{5,13},{9,1},{13,5},{2,10},{6,14},... | collective-permute-start | bytes 663560 | tf_op jit(solution)/shard_map/ppermute | solution.py:526
  6.0 1.4 %collective-permute-start.5 = (f32[27,8,256]{2,1,0:T(8,128)}, f32[27,8,256]{2,1,0:T(8,128)S(1)}, u32[]{:S(2)}, u32[]{:S(2)}) collective-permute-start(f32[27,8,256]{2,1,0:T(8,128)} %get-tuple-element.23), channel_id=1, source_target_pairs={{0,12},{4,0},{8,4},{12,8},{1,13},{5,1},{9,5},{13,9},{2,14},{6,2},{... | collective-permute-start | bytes 663560 | tf_op jit(solution)/shard_map/ppermute | solution.py:526
  7.4 3.6 %shard_map.114 = (f32[3,8,12,8,256]{4,3,2,1,0:T(8,128)}, f32[2,2,12,8,256]{4,3,2,1,0:T(8,128)}) custom-call(s32[16]{0:T(128)} %dest_ref.7, f32[3,4,12,8,256]{4,3,2,1,0:T(8,128)} %boxes_ref.5), custom_call_target="tpu_custom_call" | custom-call | bytes 2359296 | tf_op jit(solution)/shard_map/pallas_call | solution.py:195
  11.0 0.0 copy-start.6
  11.0 0.0 copy-start.7
  11.0 0.0 copy-start.8
  11.0 0.0 copy-start.5
  11.0 0.0 copy-start
  11.1 0.1 collective-permute-start.2
  11.1 2.9 %shard_map.113 = (f32[2,2,12,8,256]{4,3,2,1,0:T(8,128)}, f32[2,2,12,8,256]{4,3,2,1,0:T(8,128)}) custom-call(s32[16]{0:T(128)} %dest_ref.7, f32[3,4,12,8,256]{4,3,2,1,0:T(8,128)} %boxes_ref.5), custom_call_target="tpu_custom_call" | custom-call | bytes 2359296 | tf_op jit(solution)/shard_map/pallas_call | solution.py:195
  14.1 2.3 %collective-permute-start = (f32[2,2,12,8,256]{4,3,2,1,0:T(8,128)}, f32[2,2,12,8,256]{4,3,2,1,0:T(8,128)S(1)}, u32[]{:S(2)}, u32[]{:S(2)}) collective-permute-start(f32[2,2,12,8,256]{4,3,2,1,0:T(8,128)} %get-tuple-element.17), channel_id=1, source_target_pairs={{0,4},{4,8},{8,12},{12,0},{1,5},{5,9},{9,13},{13,1},{2,6},{6,10},{... | collective-permute-start | bytes 1179656 | tf_op jit(solution)/shard_map/ppermute | solution.py:526
  16.3 0.0 collective-permute-done.3.refs_1_
  16.3 0.0 collective-permute-start.1
  16.3 15.7 %collective-permute-done.4.refs_2_ = f32[27,8,256]{2,1,0:T(8,128)S(1)} collective-permute-done((f32[27,8,256]{2,1,0:T(8,128)}, f32[27,8,256]{2,1,0:T(8,128)S(1)}, u32[]{:S(2)}, u32[]{:S(2)}) %collective-permute-start.4) | collective-permute-done | bytes 221216 | tf_op jit(solution)/shard_map/ppermute | solution.py:526
  32.0 11.2 %collective-permute-done.5.refs_3_ = f32[27,8,256]{2,1,0:T(8,128)S(1)} collective-permute-done((f32[27,8,256]{2,1,0:T(8,128)}, f32[27,8,256]{2,1,0:T(8,128)S(1)}, u32[]{:S(2)}, u32[]{:S(2)}) %collective-permute-start.5) | collective-permute-done | bytes 221216 | tf_op jit(solution)/shard_map/ppermute | solution.py:526
  43.2 0.0 copy-done.1
  43.2 1.1 %shard_map.116 = (f32[8,14,8,256]{3,2,1,0:T(8,128)S(1)}, f32[3,8,12,8,256]{4,3,2,1,0:T(8,128)}, f32[8,12,256]{2,1,0:T(8,128)S(1)}) custom-call(f32[27,8,256]{2,1,0:T(8,128)S(1)} %copy-done.1, f32[27,8,256]{2,1,0:T(8,128)S(1)} %collective-permute-done.3.refs_1_, f32[27,8,256]{2,1,0:T(8,128)S(1)} %collective-permute-done.4.refs_2_, ...), custom_call_target="tpu_custom_call", output_to_operand_aliasing={{1}: (4, {})} | custom-call | bytes 2654208 | tf_op jit(solution)/shard_map/pallas_call | solution.py:297
  44.4 0.0 copy-start.4
  44.4 0.0 copy-start.2
  44.4 0.0 copy-start.3
  44.4 0.7 %collective-permute-start.6 = (f32[8,14,8,256]{3,2,1,0:T(8,128)S(1)}, f32[8,14,8,256]{3,2,1,0:T(8,128)S(1)}, u32[]{:S(2)}, u32[]{:S(2)}) collective-permute-start(f32[8,14,8,256]{3,2,1,0:T(8,128)S(1)} %get-tuple-element.26.now_ref.own_ref), channel_id=1, source_target_pairs={{0,1},{1,0},{2,3},{3,2},{4,5},{5,4},{6,7},{7,6},{8,9},{9,8},{10,11... | collective-permute-start | bytes 2752520 | tf_op jit(solution)/shard_map/ppermute | solution.py:537
  45.1 0.0 copy-done.6
  45.1 0.0 copy-done.7
  45.1 0.0 copy-done.8
  45.1 0.1 fusion.7
  45.2 1.2 %collective-permute-start.7 = (f32[8,12,256]{2,1,0:T(8,128)S(1)}, f32[8,12,256]{2,1,0:T(8,128)S(1)}, u32[]{:S(2)}, u32[]{:S(2)}) collective-permute-start(f32[8,12,256]{2,1,0:T(8,128)S(1)} %get-tuple-element.27), channel_id=1, source_target_pairs={{0,2},{2,0},{1,3},{3,1},{4,6},{6,4},{5,7},{7,5},{8,10},{10,8},{9,1... | collective-permute-start | bytes 294920 | tf_op jit(solution)/shard_map/ppermute | solution.py:544
  46.4 0.0 copy-done.5
  46.4 0.3 fusion.2
  46.8 0.0 copy-done
  46.8 0.5 shard_map.117.own_rim
  47.3 3.0 %collective-permute-done.7.own_low.own_high = f32[8,12,256]{2,1,0:T(8,128)S(1)} collective-permute-done((f32[8,12,256]{2,1,0:T(8,128)S(1)}, f32[8,12,256]{2,1,0:T(8,128)S(1)}, u32[]{:S(2)}, u32[]{:S(2)}) %collective-permute-start.7) | collective-permute-done | bytes 98336 | tf_op jit(solution)/shard_map/ppermute | solution.py:544
  50.3 0.8 %collective-permute-start.8 = (f32[8,12,256]{2,1,0:T(8,128)S(1)}, f32[8,12,256]{2,1,0:T(8,128)S(1)}, u32[]{:S(2)}, u32[]{:S(2)}) collective-permute-start(f32[8,12,256]{2,1,0:T(8,128)S(1)} %collective-permute-done.7.own_low.own_high), channel_id=1, source_target_pairs={{0,1},{1,0},{2,3},{3,2},{4,5},{5,4},{6,7},{7,6},{8,9},{9,8},{10,11... | collective-permute-start | bytes 294920 | tf_op jit(solution)/shard_map/ppermute | solution.py:548
  51.1 0.0 copy-done.4
  51.1 0.1 multiply_reduce_fusion
  51.2 0.9 %collective-permute-done.8.other_low.other_high = f32[8,12,256]{2,1,0:T(8,128)S(1)} collective-permute-done((f32[8,12,256]{2,1,0:T(8,128)S(1)}, f32[8,12,256]{2,1,0:T(8,128)S(1)}, u32[]{:S(2)}, u32[]{:S(2)}) %collective-permute-start.8) | collective-permute-done | bytes 98336 | tf_op jit(solution)/shard_map/ppermute | solution.py:548
  52.1 0.0 collective-permute-done.6.other_ref
  52.1 0.0 copy-done.2
  52.1 0.0 copy-done.3
  52.1 5.5 %shard_map.118 = (f32[8,12,8,256]{3,2,1,0:T(8,128)}, f32[8,128]{1,0:T(8,128)S(1)}) custom-call(s32[16]{0:T(128)S(1)} %copy-done.2, s32[16]{0:T(128)S(1)} %copy-done.3, f32[8,14,8,256]{3,2,1,0:T(8,128)S(1)} %get-tuple-element.26.now_ref.own_ref, f32[8,14,8,256]{3,2,1,0:T(8,128)S(1)} %collective-permute-done.6.other_ref, ...), custom_call_target="tpu_custom_call" | custom-call | flops 528482304 | bytes 2752512 | tf_op jit(solution)/shard_map/pallas_call | solution.py:556
  57.6 0.0 collective-permute-done.2.refs_0_
  57.6 0.8 %shard_map.119.refs_2_ = f32[3,8,12,8,256]{4,3,2,1,0:T(8,128)} custom-call(f32[2,2,12,8,256]{4,3,2,1,0:T(8,128)S(1)} %collective-permute-done.2.refs_0_, f32[3,8,12,8,256]{4,3,2,1,0:T(8,128)} %get-tuple-element.25.refs_1_, f32[8,128]{1,0:T(8,128)S(1)} %get-tuple-element.30.refs_2_.refs_3_), custom_call_target="tpu_custom_call", output_to_operand_aliasing={{}: (1, {})} | custom-call | bytes 786432 | tf_op jit(solution)/shard_map/pallas_call | solution.py:231
  58.4 0.0 collective-permute-done.refs_0_
  58.4 1.7 %collective-permute-done.1.refs_1_ = f32[2,2,12,8,256]{4,3,2,1,0:T(8,128)S(1)} collective-permute-done((f32[2,2,12,8,256]{4,3,2,1,0:T(8,128)}, f32[2,2,12,8,256]{4,3,2,1,0:T(8,128)S(1)}, u32[]{:S(2)}, u32[]{:S(2)}) %collective-permute-start.1) | collective-permute-done | bytes 393248 | tf_op jit(solution)/shard_map/ppermute | solution.py:526
  60.1 0.9 %shard_map.120 = f32[3,8,12,8,256]{4,3,2,1,0:T(8,128)} custom-call(f32[2,2,12,8,256]{4,3,2,1,0:T(8,128)S(1)} %collective-permute-done.refs_0_, f32[2,2,12,8,256]{4,3,2,1,0:T(8,128)S(1)} %collective-permute-done.1.refs_1_, f32[3,8,12,8,256]{4,3,2,1,0:T(8,128)} %shard_map.119.refs_2_, ...), custom_call_target="tpu_custom_call", output_to_operand_aliasing={{}: (2, {})} | custom-call | bytes 1572864 | tf_op jit(solution)/shard_map/pallas_call | solution.py:231
  (2 shorter events, 0.0 us)
Async XLA Ops:
  3.6 39.7 %copy-start.1 = (f32[27,8,256]{2,1,0:T(8,128)S(1)}, f32[27,8,256]{2,1,0:T(8,128)}, u32[]{:S(2)}) copy-start(f32[27,8,256]{2,1,0:T(8,128)} %get-tuple-element.20.refs_0_) | copy-start | bytes 663556
  3.6 12.8 %collective-permute-start.3 = (f32[27,8,256]{2,1,0:T(8,128)}, f32[27,8,256]{2,1,0:T(8,128)S(1)}, u32[]{:S(2)}, u32[]{:S(2)}) collective-permute-start(f32[27,8,256]{2,1,0:T(8,128)} %get-tuple-element.21), channel_id=1, source_target_pairs={{0,4},{4,8},{8,12},{12,0},{1,5},{5,9},{9,13},{13,1},{2,6},{6,10},{... | collective-permute-start | bytes 663560 | tf_op jit(solution)/shard_map/ppermute | solution.py:526
  4.9 27.1 %collective-permute-start.4 = (f32[27,8,256]{2,1,0:T(8,128)}, f32[27,8,256]{2,1,0:T(8,128)S(1)}, u32[]{:S(2)}, u32[]{:S(2)}) collective-permute-start(f32[27,8,256]{2,1,0:T(8,128)} %get-tuple-element.22), channel_id=1, source_target_pairs={{0,8},{4,12},{8,0},{12,4},{1,9},{5,13},{9,1},{13,5},{2,10},{6,14},... | collective-permute-start | bytes 663560 | tf_op jit(solution)/shard_map/ppermute | solution.py:526
  6.0 37.2 %collective-permute-start.5 = (f32[27,8,256]{2,1,0:T(8,128)}, f32[27,8,256]{2,1,0:T(8,128)S(1)}, u32[]{:S(2)}, u32[]{:S(2)}) collective-permute-start(f32[27,8,256]{2,1,0:T(8,128)} %get-tuple-element.23), channel_id=1, source_target_pairs={{0,12},{4,0},{8,4},{12,8},{1,13},{5,1},{9,5},{13,9},{2,14},{6,2},{... | collective-permute-start | bytes 663560 | tf_op jit(solution)/shard_map/ppermute | solution.py:526
  11.0 34.1 %copy-start.6 = (f32[24,24]{1,0:T(8,128)S(1)}, f32[24,24]{1,0:T(8,128)}, u32[]{:S(2)}) copy-start(f32[24,24]{1,0:T(8,128)} %param.14) | copy-start | bytes 6916
  11.0 34.1 %copy-start.7 = (f32[24,24]{1,0:T(8,128)S(1)}, f32[24,24]{1,0:T(8,128)}, u32[]{:S(2)}) copy-start(f32[24,24]{1,0:T(8,128)} %param.15) | copy-start | bytes 6916
  11.0 34.1 %copy-start.8 = (f32[24,24]{1,0:T(8,128)S(1)}, f32[24,24]{1,0:T(8,128)}, u32[]{:S(2)}) copy-start(f32[24,24]{1,0:T(8,128)} %param.16) | copy-start | bytes 6916
  11.0 35.4 %copy-start.5 = (f32[24,896,1]{1,0,2:T(8,128)S(1)}, f32[24,896,1]{1,0,2:T(8,128)}, u32[]{:S(2)}) copy-start(f32[24,896,1]{1,0,2:T(8,128)} %constant.27) | copy-start | bytes 258052
  11.0 35.7 %copy-start = (bf16[256,2304]{1,0:T(8,128)(2,1)S(1)}, bf16[256,2304]{1,0:T(8,128)(2,1)}, u32[]{:S(2)}) copy-start(bf16[256,2304]{1,0:T(8,128)(2,1)} %constant.26.spread_ref) | copy-start | bytes 3538948
  11.1 46.6 %collective-permute-start.2 = (f32[2,2,12,8,256]{4,3,2,1,0:T(8,128)}, f32[2,2,12,8,256]{4,3,2,1,0:T(8,128)S(1)}, u32[]{:S(2)}, u32[]{:S(2)}) collective-permute-start(f32[2,2,12,8,256]{4,3,2,1,0:T(8,128)} %get-tuple-element.19), channel_id=1, source_target_pairs={{0,8},{4,12},{8,0},{12,4},{1,9},{5,13},{9,1},{13,5},{2,10},{6,14},... | collective-permute-start | bytes 1179656 | tf_op jit(solution)/shard_map/ppermute | solution.py:526
  14.1 44.3 %collective-permute-start = (f32[2,2,12,8,256]{4,3,2,1,0:T(8,128)}, f32[2,2,12,8,256]{4,3,2,1,0:T(8,128)S(1)}, u32[]{:S(2)}, u32[]{:S(2)}) collective-permute-start(f32[2,2,12,8,256]{4,3,2,1,0:T(8,128)} %get-tuple-element.17), channel_id=1, source_target_pairs={{0,4},{4,8},{8,12},{12,0},{1,5},{5,9},{9,13},{13,1},{2,6},{6,10},{... | collective-permute-start | bytes 1179656 | tf_op jit(solution)/shard_map/ppermute | solution.py:526
  16.3 43.7 %collective-permute-start.1 = (f32[2,2,12,8,256]{4,3,2,1,0:T(8,128)}, f32[2,2,12,8,256]{4,3,2,1,0:T(8,128)S(1)}, u32[]{:S(2)}, u32[]{:S(2)}) collective-permute-start(f32[2,2,12,8,256]{4,3,2,1,0:T(8,128)} %get-tuple-element.18), channel_id=1, source_target_pairs={{0,12},{4,0},{8,4},{12,8},{1,13},{5,1},{9,5},{13,9},{2,14},{6,2},{... | collective-permute-start | bytes 1179656 | tf_op jit(solution)/shard_map/ppermute | solution.py:526
  44.4 6.7 %copy-start.4 = (f32[3,8,896]{2,1,0:T(8,128)S(1)}, f32[3,8,896]{2,1,0:T(8,128)}, u32[]{:S(2)}) copy-start(f32[3,8,896]{2,1,0:T(8,128)} %constant.24.clone) | copy-start | bytes 258052
  44.4 7.7 %copy-start.2 = (s32[16]{0:T(128)S(1)}, s32[16]{0:T(128)}, u32[]{:S(2)}) copy-start(s32[16]{0:T(128)} %dest_ref.7) | copy-start | bytes 196
  44.4 7.7 %copy-start.3 = (s32[16]{0:T(128)S(1)}, s32[16]{0:T(128)}, u32[]{:S(2)}) copy-start(s32[16]{0:T(128)} %parent_ref.3) | copy-start | bytes 196
  44.4 7.7 %collective-permute-start.6 = (f32[8,14,8,256]{3,2,1,0:T(8,128)S(1)}, f32[8,14,8,256]{3,2,1,0:T(8,128)S(1)}, u32[]{:S(2)}, u32[]{:S(2)}) collective-permute-start(f32[8,14,8,256]{3,2,1,0:T(8,128)S(1)} %get-tuple-element.26.now_ref.own_ref), channel_id=1, source_target_pairs={{0,1},{1,0},{2,3},{3,2},{4,5},{5,4},{6,7},{7,6},{8,9},{9,8},{10,11... | collective-permute-start | bytes 2752520 | tf_op jit(solution)/shard_map/ppermute | solution.py:537
  45.2 5.1 %collective-permute-start.7 = (f32[8,12,256]{2,1,0:T(8,128)S(1)}, f32[8,12,256]{2,1,0:T(8,128)S(1)}, u32[]{:S(2)}, u32[]{:S(2)}) collective-permute-start(f32[8,12,256]{2,1,0:T(8,128)S(1)} %get-tuple-element.27), channel_id=1, source_target_pairs={{0,2},{2,0},{1,3},{3,1},{4,6},{6,4},{5,7},{7,5},{8,10},{10,8},{9,1... | collective-permute-start | bytes 294920 | tf_op jit(solution)/shard_map/ppermute | solution.py:544
  50.3 1.8 %collective-permute-start.8 = (f32[8,12,256]{2,1,0:T(8,128)S(1)}, f32[8,12,256]{2,1,0:T(8,128)S(1)}, u32[]{:S(2)}, u32[]{:S(2)}) collective-permute-start(f32[8,12,256]{2,1,0:T(8,128)S(1)} %collective-permute-done.7.own_low.own_high), channel_id=1, source_target_pairs={{0,1},{1,0},{2,3},{3,2},{4,5},{5,4},{6,7},{7,6},{8,9},{9,8},{10,11... | collective-permute-start | bytes 294920 | tf_op jit(solution)/shard_map/ppermute | solution.py:548

commit v14 on v13

--- a/solution.py
+++ b/solution.py
@@ -51,38 +51,41 @@
 
 
 def first_kernel(per_device, box_count, edge, dest_ref, parent_ref, boxes_ref, coarse_ref, *refs):
-    outs, (shells, chosen, dest, parent, box_table, face_table, sems, in_sems) = refs[:box_count], refs[box_count:]
+    outs, (boxes, zeros, shells, chosen, rows, dest, parent, box_table, face_table, sems, row_sems, in_sems) = (
+        refs[:box_count], refs[box_count:]
+    )
     fields, coarse_count, cells = coarse_ref.shape
     planes, cross = outs[0].shape[1:]
     own, slab = lax.axis_index("box"), lax.axis_index("slab")
     fetches = [
-        pltpu.make_async_copy(coarse_ref, shells, in_sems.at[0]),
-        pltpu.make_async_copy(dest_ref, dest, in_sems.at[1]),
+        pltpu.make_async_copy(dest_ref, dest, in_sems.at[0]),
+        pltpu.make_async_copy(boxes_ref.at[0], boxes, in_sems.at[1]),
         pltpu.make_async_copy(parent_ref, parent, in_sems.at[2]),
+        pltpu.make_async_copy(coarse_ref, shells, in_sems.at[3]),
     ]
     for fetch in fetches:
         fetch.start()
+    zeros[...] = jnp.zeros_like(zeros)
     index = face_cells(lax.broadcasted_iota(jnp.int32, (1, cross), 1), edge, planes // 2, slab)
     cell = lax.broadcasted_iota(jnp.int32, (cells, cross), 0)
     one_hot = (cell == index).astype(jnp.float32).astype(jnp.bfloat16)
+    fetches[0].wait()
+    place_boxes(per_device, box_count, dest, box_table)
     fetches[1].wait()
-    place_boxes(per_device, box_count, dest, box_table)
-
-    def copy(shift, k, b):
-        return pltpu.make_async_copy(
-            boxes_ref.at[0, b], outs[shift].at[pl.ds(k * fields, fields)], sems.at[shift, k]
-        )
+
+    def copy(shift, k, values):
+        return pltpu.make_async_copy(values, outs[shift].at[pl.ds(k * fields, fields)], sems.at[shift, k])
 
     for shift, k, slot in each_slot(box_count):
         b = box_table[slot]
 
         @pl.when(b >= 0)
         def _():
-            copy(shift, k, b).start()
+            copy(shift, k, boxes.at[b]).start()
 
         @pl.when(b < 0)
         def _():
-            outs[shift][k * fields : (k + 1) * fields] = jnp.zeros((fields, planes, cross), jnp.float32)
+            copy(shift, k, zeros).start()
 
     for slot in range(2 * box_count):
         face_table[slot] = -1
@@ -99,43 +102,51 @@
         return carry
 
     lax.fori_loop(0, dest.shape[0], place, 0)
-    fetches[0].wait()
+    fetches[3].wait()
     count = fields * coarse_count
     both = jnp.dot(split_two(shells[...].reshape(count, cells)), one_hot, preferred_element_type=jnp.float32)
     chosen[...] = (both[:count] + both[count:]).reshape(chosen.shape)
+    sent = []
     for shift, k, slot in each_slot(box_count):
         local = face_table[slot]
         for f in range(fields):
             values = chosen[f, pl.ds(jnp.maximum(local, 0), 1)]
             block, row = divmod(k * fields + f, planes)
-            outs[shift][2 * fields + block, row : row + 1] = jnp.where(local >= 0, values, 0.0)
+            rows[shift, block, row : row + 1] = jnp.where(local >= 0, values, 0.0)
+        if k == 1:
+            to = outs[shift].at[pl.ds(2 * fields, rows.shape[1])]
+            sent.append(pltpu.make_async_copy(rows.at[shift], to, row_sems.at[shift]))
+            sent[-1].start()
     for shift, k, slot in each_slot(box_count):
-        b = box_table[slot]
-
-        @pl.when(b >= 0)
-        def _():
-            copy(shift, k, b).wait()
+        copy(shift, k, zeros).wait()
+    for rows_copy in sent:
+        rows_copy.wait()
 
 
 def pack_first(boxes, coarse, move_dest, parent, edge, box_count):
     per_device, fields, planes, cross = boxes.shape[1:]
     coarse = jnp.transpose(coarse, (1, 0, 2))
-    hbm, vmem = pl.BlockSpec(memory_space=pltpu.HBM), pl.BlockSpec(memory_space=pltpu.VMEM)
-    item = (2 * fields + 2 * fields // planes, planes, cross)
+    hbm = pl.BlockSpec(memory_space=pltpu.HBM)
+    face_blocks = 2 * fields // planes
+    item = (2 * fields + face_blocks, planes, cross)
     return pl.pallas_call(
         functools.partial(first_kernel, per_device, box_count, edge),
         out_shape=[jax.ShapeDtypeStruct(item, jnp.float32)] * box_count,
         in_specs=[hbm] * 4,
-        out_specs=[vmem] * box_count,
+        out_specs=[hbm] * box_count,
         scratch_shapes=[
+            pltpu.VMEM(boxes.shape[1:], jnp.float32),
+            pltpu.VMEM(boxes.shape[2:], jnp.float32),
             pltpu.VMEM(coarse.shape, jnp.float32),
             pltpu.VMEM(coarse.shape[:2] + (cross,), jnp.float32),
+            pltpu.VMEM((box_count, face_blocks, planes, cross), jnp.float32),
             pltpu.SMEM(move_dest.shape, jnp.int32),
             pltpu.SMEM(parent.shape, jnp.int32),
             pltpu.SMEM((2 * box_count,), jnp.int32),
             pltpu.SMEM((2 * box_count,), jnp.int32),
             pltpu.SemaphoreType.DMA((box_count, 2)),
-            pltpu.SemaphoreType.DMA((3,)),
+            pltpu.SemaphoreType.DMA((box_count,)),
+            pltpu.SemaphoreType.DMA((4,)),
         ],
         cost_estimate=pl.CostEstimate(
             flops=6 * coarse.size * cross, bytes_accessed=4 * (coarse.size + 2 * boxes.size), transcendentals=0
@@ -410,94 +421,102 @@
 def slope_kernel(
     edge, planes, fields, coarse_planes, per_device, total, coarse_count, slots, slabs,
     dest_ref, parent_ref, own_ref, other_ref, own_low, other_low, own_high, other_high,
-    own_rim, spread_ref, weight_ref, out_ref, token_ref, stack, parts, other_rim, table, count,
+    own_rim, spread_ref, weight_ref, out_ref, token_ref, stack, parts, other_rim, staged, table, count, sems,
 ):
-    step = pl.program_id(0)
     cross = edge * edge
     rows = fields * planes
     own, slab = lax.axis_index("box"), lax.axis_index("slab")
 
-    @pl.when(step == 0)
-    def _():
-        token_ref[...] = jnp.zeros_like(token_ref)
-        stack[...] = jnp.zeros_like(stack)
-        half = weight_ref.shape[0]
-        weights = weight_ref[...]
-        parts[:half] = weights.astype(jnp.bfloat16)
-        parts[half:] = (weights - weights.astype(jnp.bfloat16).astype(jnp.float32)).astype(jnp.bfloat16)
-        for slot in range(slots):
-            table[slot] = -1
-            count[slot] = 0
-
-        def place(b, carry):
-            @pl.when(dest_ref[b] == own)
+    token_ref[...] = jnp.zeros_like(token_ref)
+    stack[...] = jnp.zeros_like(stack)
+    half = weight_ref.shape[0]
+    weights = weight_ref[...]
+    parts[:half] = weights.astype(jnp.bfloat16)
+    parts[half:] = (weights - weights.astype(jnp.bfloat16).astype(jnp.float32)).astype(jnp.bfloat16)
+    for slot in range(slots):
+        table[slot] = -1
+        count[slot] = 0
+
+    def place(b, carry):
+        @pl.when(dest_ref[b] == own)
+        def _():
+            slot = 2 * (b // per_device)
+            owner = parent_ref[b] // coarse_count
+            table[jnp.where(table[slot] >= 0, slot + 1, slot)] = 2 * owner + count[owner]
+            count[owner] = count[owner] + 1
+
+        return carry
+
+    lax.fori_loop(0, total, place, 0)
+    expand_faces(other_ref, fields, spread_ref, other_rim)
+
+    def write(step):
+        return pltpu.make_async_copy(staged.at[step], out_ref.at[step], sems.at[step])
+
+    def one_slot(step, carry):
+        face = table[step]
+
+        @pl.when(face < 0)
+        def _():
+            staged[step] = jnp.zeros(staged.shape[1:], jnp.float32)
+
+        @pl.when(face >= 0)
+        def _():
+            lane = lax.broadcasted_iota(jnp.int32, (1, cross), 1)
+            y, z = lane // edge, lane % edge
+            for n, ref in enumerate((own_ref, other_ref)):
+                at = (4 + n) * rows
+                if planes % 8:
+                    for f in range(fields):
+                        stack[at + f * planes : at + (f + 1) * planes] = ref[step, f]
+                else:
+                    stack[at : at + rows] = ref[step, :fields].reshape(rows, cross)
+            cells = stack[4 * rows : 6 * rows]
+            stack[0 : 2 * rows] = jnp.where(y < edge - 1, pltpu.roll(cells, cross - edge, 1), 0.0) + jnp.where(
+                z < edge - 1, pltpu.roll(cells, cross - 1, 1), 0.0
+            )
+            stack[2 * rows : 4 * rows] = jnp.where(y > 0, pltpu.roll(cells, edge, 1), 0.0) + jnp.where(
+                z > 0, pltpu.roll(cells, 1, 1), 0.0
+            )
+            here = pl.ds(pl.multiple_of(ROWS * face, ROWS), ROWS)
+            rim = jnp.concatenate([own_rim[here], other_rim[here]], axis=0)
+            base = 6 * rows
+            x_face = rim[:, 2 * coarse_planes * cross :]
+            stack[base : base + 2 * ROWS] = x_face
+            stack[base + 2 * ROWS : base + 4 * ROWS] = x_face
+
+            @pl.when(slab > 0)
             def _():
-                slot = 2 * (b // per_device)
-                owner = parent_ref[b] // coarse_count
-                table[jnp.where(table[slot] >= 0, slot + 1, slot)] = 2 * owner + count[owner]
-                count[owner] = count[owner] + 1
-
-            return carry
-
-        lax.fori_loop(0, total, place, 0)
-        expand_faces(other_ref, fields, spread_ref, other_rim)
-
-    face = table[step]
-
-    @pl.when(face < 0)
-    def _():
-        out_ref[...] = jnp.zeros_like(out_ref)
-
-    @pl.when(face >= 0)
-    def _():
-        lane = lax.broadcasted_iota(jnp.int32, (1, cross), 1)
-        y, z = lane // edge, lane % edge
-        for n, ref in enumerate((own_ref, other_ref)):
-            at = (4 + n) * rows
+                stack[base : base + fields] = own_low[step]
+                stack[base + ROWS : base + ROWS + fields] = other_low[step]
+
+            @pl.when(slab < slabs - 1)
+            def _():
+                stack[base + 2 * ROWS : base + 2 * ROWS + fields] = own_high[step]
+                stack[base + 3 * ROWS : base + 3 * ROWS + fields] = other_high[step]
+
+            base += 4 * ROWS
+            for n in range(2 * coarse_planes):
+                stack[base + 2 * ROWS * n : base + 2 * ROWS * (n + 1)] = rim[:, n * cross : (n + 1) * cross]
+            values = stack[...]
+            high = values.astype(jnp.bfloat16)
+            low = (values - high.astype(jnp.float32)).astype(jnp.bfloat16)
+            half = weight_ref.shape[0]
+            both = jnp.dot(parts[...], high, preferred_element_type=jnp.float32)
+            mixed = jnp.dot(parts[:half], low, preferred_element_type=jnp.float32)
+            mixed = both[:half] + (both[half:] + mixed)
             if planes % 8:
                 for f in range(fields):
-                    stack[at + f * planes : at + (f + 1) * planes] = ref[step, f]
+                    staged[step, f] = mixed[f * planes : (f + 1) * planes]
             else:
-                stack[at : at + rows] = ref[step, :fields].reshape(rows, cross)
-        cells = stack[4 * rows : 6 * rows]
-        stack[0 : 2 * rows] = jnp.where(y < edge - 1, pltpu.roll(cells, cross - edge, 1), 0.0) + jnp.where(
-            z < edge - 1, pltpu.roll(cells, cross - 1, 1), 0.0
-        )
-        stack[2 * rows : 4 * rows] = jnp.where(y > 0, pltpu.roll(cells, edge, 1), 0.0) + jnp.where(
-            z > 0, pltpu.roll(cells, 1, 1), 0.0
-        )
-        here = pl.ds(pl.multiple_of(ROWS * face, ROWS), ROWS)
-        rim = jnp.concatenate([own_rim[here], other_rim[here]], axis=0)
-        base = 6 * rows
-        x_face = rim[:, 2 * coarse_planes * cross :]
-        stack[base : base + 2 * ROWS] = x_face
-        stack[base + 2 * ROWS : base + 4 * ROWS] = x_face
-
-        @pl.when(slab > 0)
-        def _():
-            stack[base : base + fields] = own_low[step]
-            stack[base + ROWS : base + ROWS + fields] = other_low[step]
-
-        @pl.when(slab < slabs - 1)
-        def _():
-            stack[base + 2 * ROWS : base + 2 * ROWS + fields] = own_high[step]
-            stack[base + 3 * ROWS : base + 3 * ROWS + fields] = other_high[step]
-
-        base += 4 * ROWS
-        for n in range(2 * coarse_planes):
-            stack[base + 2 * ROWS * n : base + 2 * ROWS * (n + 1)] = rim[:, n * cross : (n + 1) * cross]
-        values = stack[...]
-        high = values.astype(jnp.bfloat16)
-        low = (values - high.astype(jnp.float32)).astype(jnp.bfloat16)
-        half = weight_ref.shape[0]
-        both = jnp.dot(parts[...], high, preferred_element_type=jnp.float32)
-        mixed = jnp.dot(parts[:half], low, preferred_element_type=jnp.float32)
-        mixed = both[:half] + (both[half:] + mixed)
-        if planes % 8:
-            for f in range(fields):
-                out_ref[0, f] = mixed[f * planes : (f + 1) * planes]
-        else:
-            out_ref[0] = mixed[:rows].reshape(fields, planes, cross)
+                staged[step] = mixed[:rows].reshape(fields, planes, cross)
+
+        write(step).start()
+        return carry
+
+    lax.fori_loop(0, slots, one_slot, 0)
+    for step in range(slots):
+        write(step).wait()
 
 
 def mixing_weights(mixes, group, fields, planes, coarse_planes):
@@ -557,19 +576,20 @@
         functools.partial(
             slope_kernel, edge, planes, fields, coarse_planes, per_device, total, coarse_count, slots, slabs
         ),
-        grid=(slots,),
         out_shape=[
             jax.ShapeDtypeStruct((slots, fields, planes, cross), jnp.float32),
             jax.ShapeDtypeStruct((8, 128), jnp.float32),
         ],
         in_specs=[smem, smem] + [vmem] * 9,
-        out_specs=[pl.BlockSpec((1, fields, planes, cross), lambda n: (n, 0, 0, 0)), vmem],
+        out_specs=[pl.BlockSpec(memory_space=pltpu.HBM), vmem],
         scratch_shapes=[
             pltpu.VMEM((weight.shape[1], cross), jnp.float32),
             pltpu.VMEM((2 * weight.shape[0], weight.shape[1]), jnp.bfloat16),
             pltpu.VMEM((ROWS * slots, spread.shape[1]), jnp.float32),
+            pltpu.VMEM((slots, fields, planes, cross), jnp.float32),
             pltpu.SMEM((slots,), jnp.int32),
             pltpu.SMEM((slots,), jnp.int32),
+            pltpu.SemaphoreType.DMA((slots,)),
         ],
         compiler_params=pltpu.CompilerParams(vmem_limit_bytes=48 * 2 ** 20),
         cost_estimate=pl.CostEstimate(

time: 61.4 us -> 60.6 us (0.987)
  Pallas kernels: 18.2 us -> 15.9 us
  starting transfers between devices: 8.9 us -> 9.73 us
  waiting for transfers between devices: 32.5 us -> 33.3 us
    pallas_call x2, Pallas kernels: 6.46 us -> 5.49 us  [pack_later(): pl.pallas_call(functools.partial(later_kernel, turns, per_device, box_cou...]
    ppermute x6, starting transfers between devices: 6.2 us -> 7.03 us  [send(): lax.ppermute(piece, 'box', [(s, (s + turn) % box_count) for s in range(bo...]
    ppermute x6, waiting for transfers between devices: 28.6 us -> 29.4 us  [send(): lax.ppermute(piece, 'box', [(s, (s + turn) % box_count) for s in range(bo...]
    pallas_call x1, Pallas kernels: 5.5 us -> 4.77 us  [body(): pl.pallas_call(functools.partial(slope_kernel, edge, planes, fields, coar...]
  transfers between devices with their start and end apart: 9 -> 9, of which waited for: 5 -> 5; matrix products, arithmetic and copies ran while one was open for 1% -> 1% of each run, Pallas kernels for 24% -> 21%
where the time goes in v14:
time: 60.6 us; the launch traced here: 60.3 us
  waiting for transfers between devices  33.3 us (55%)
  Pallas kernels  15.9 us (26%)
  starting transfers between devices  9.73 us (16%)
  between operations  0.82 us (1%)
    ppermute x6, waiting for transfers between devices, send(): lax.ppermute(piece, 'box', [(s, (s + turn) % box_count) for s in range(bo...  29.4 us
    ppermute x6, starting transfers between devices, send(): lax.ppermute(piece, 'box', [(s, (s + turn) % box_count) for s in range(bo...  7.03 us
    pallas_call x2, Pallas kernels, pack_later(): pl.pallas_call(functools.partial(later_kernel, turns, per_device, box_cou...  5.49 us
    pallas_call x1, Pallas kernels, body(): pl.pallas_call(functools.partial(slope_kernel, edge, planes, fields, coar...  4.77 us
    ppermute x1, waiting for transfers between devices, shifted(): return lax.ppermute(values, 'slab', swap if slabs == 2 else pairs)  3.01 us
    pallas_call x1, Pallas kernels, pack_first(): pl.pallas_call(functools.partial(first_kernel, per_device, box_count, edg...  2.33 us
    pallas_call x2, Pallas kernels, settle(): pl.pallas_call(functools.partial(settle_kernel, turns), out_shape=jax.Sha...  1.66 us
    ppermute x1, starting transfers between devices, shifted(): return lax.ppermute(values, 'slab', swap if slabs == 2 else pairs)  1.22 us
  transfers between devices with their start and end apart: 9, of which 5 were waited for; matrix products, arithmetic and copies ran while one was open for 1% of the time, Pallas kernels for 21%

profile of v14, /device:TPU:9, one launch (start us, length us, event | category | flops | bytes accessed | tf_op | source)
XLA Modules:
  0.0 60.3 jit_solution(15057382301715341067)
XLA Ops:
  0.6 2.3 %shard_map.115 = (f32[27,8,256]{2,1,0:T(8,128)}, f32[27,8,256]{2,1,0:T(8,128)}, f32[27,8,256]{2,1,0:T(8,128)}, f32[27,8,256]{2,1,0:T(8,128)}) custom-call(s32[16]{0:T(128)} %dest_ref.7, s32[16]{0:T(128)} %parent_ref.3, f32[3,4,12,8,256]{4,3,2,1,0:T(8,128)} %boxes_ref.5, f32[12,8,1000]{2,1,0:T(8,128)} %bitcast.11), custom_call_target="tpu_custom_call" | custom-call | flops 147456000 | bytes 2743296 | tf_op jit(solution)/shard_map/pallas_call | solution.py:132
  3.0 0.0 copy-start.1
  3.0 1.3 %collective-permute-start.3 = (f32[27,8,256]{2,1,0:T(8,128)}, f32[27,8,256]{2,1,0:T(8,128)S(1)}, u32[]{:S(2)}, u32[]{:S(2)}) collective-permute-start(f32[27,8,256]{2,1,0:T(8,128)} %get-tuple-element.21), channel_id=1, source_target_pairs={{0,4},{4,8},{8,12},{12,0},{1,5},{5,9},{9,13},{13,1},{2,6},{6,10},{... | collective-permute-start | bytes 663560 | tf_op jit(solution)/shard_map/ppermute | solution.py:545
  4.3 1.1 %collective-permute-start.4 = (f32[27,8,256]{2,1,0:T(8,128)}, f32[27,8,256]{2,1,0:T(8,128)S(1)}, u32[]{:S(2)}, u32[]{:S(2)}) collective-permute-start(f32[27,8,256]{2,1,0:T(8,128)} %get-tuple-element.22), channel_id=1, source_target_pairs={{0,8},{4,12},{8,0},{12,4},{1,9},{5,13},{9,1},{13,5},{2,10},{6,14},... | collective-permute-start | bytes 663560 | tf_op jit(solution)/shard_map/ppermute | solution.py:545
  5.4 1.4 %collective-permute-start.5 = (f32[27,8,256]{2,1,0:T(8,128)}, f32[27,8,256]{2,1,0:T(8,128)S(1)}, u32[]{:S(2)}, u32[]{:S(2)}) collective-permute-start(f32[27,8,256]{2,1,0:T(8,128)} %get-tuple-element.23), channel_id=1, source_target_pairs={{0,12},{4,0},{8,4},{12,8},{1,13},{5,1},{9,5},{13,9},{2,14},{6,2},{... | collective-permute-start | bytes 663560 | tf_op jit(solution)/shard_map/ppermute | solution.py:545
  6.8 2.5 %shard_map.114 = (f32[3,8,12,8,256]{4,3,2,1,0:T(8,128)}, f32[2,2,12,8,256]{4,3,2,1,0:T(8,128)}) custom-call(s32[16]{0:T(128)} %dest_ref.7, f32[3,4,12,8,256]{4,3,2,1,0:T(8,128)} %boxes_ref.5), custom_call_target="tpu_custom_call" | custom-call | bytes 2359296 | tf_op jit(solution)/shard_map/pallas_call | solution.py:206
  9.3 0.0 copy-start.6
  9.4 0.0 copy-start.7
  9.4 0.0 copy-start.8
  9.4 0.0 copy-start.5
  9.4 0.0 copy-start
  9.4 1.1 %collective-permute-start.2 = (f32[2,2,12,8,256]{4,3,2,1,0:T(8,128)}, f32[2,2,12,8,256]{4,3,2,1,0:T(8,128)S(1)}, u32[]{:S(2)}, u32[]{:S(2)}) collective-permute-start(f32[2,2,12,8,256]{4,3,2,1,0:T(8,128)} %get-tuple-element.19), channel_id=1, source_target_pairs={{0,8},{4,12},{8,0},{12,4},{1,9},{5,13},{9,1},{13,5},{2,10},{6,14},... | collective-permute-start | bytes 1179656 | tf_op jit(solution)/shard_map/ppermute | solution.py:545
  10.5 3.0 %shard_map.113 = (f32[2,2,12,8,256]{4,3,2,1,0:T(8,128)}, f32[2,2,12,8,256]{4,3,2,1,0:T(8,128)}) custom-call(s32[16]{0:T(128)} %dest_ref.7, f32[3,4,12,8,256]{4,3,2,1,0:T(8,128)} %boxes_ref.5), custom_call_target="tpu_custom_call" | custom-call | bytes 2359296 | tf_op jit(solution)/shard_map/pallas_call | solution.py:206
  13.5 2.1 %collective-permute-start = (f32[2,2,12,8,256]{4,3,2,1,0:T(8,128)}, f32[2,2,12,8,256]{4,3,2,1,0:T(8,128)S(1)}, u32[]{:S(2)}, u32[]{:S(2)}) collective-permute-start(f32[2,2,12,8,256]{4,3,2,1,0:T(8,128)} %get-tuple-element.17), channel_id=1, source_target_pairs={{0,4},{4,8},{8,12},{12,0},{1,5},{5,9},{9,13},{13,1},{2,6},{6,10},{... | collective-permute-start | bytes 1179656 | tf_op jit(solution)/shard_map/ppermute | solution.py:545
  15.6 0.0 collective-permute-done.3.refs_1_
  15.6 0.0 collective-permute-start.1
  15.6 15.8 %collective-permute-done.4.refs_2_ = f32[27,8,256]{2,1,0:T(8,128)S(1)} collective-permute-done((f32[27,8,256]{2,1,0:T(8,128)}, f32[27,8,256]{2,1,0:T(8,128)S(1)}, u32[]{:S(2)}, u32[]{:S(2)}) %collective-permute-start.4) | collective-permute-done | bytes 221216 | tf_op jit(solution)/shard_map/ppermute | solution.py:545
  31.4 11.2 %collective-permute-done.5.refs_3_ = f32[27,8,256]{2,1,0:T(8,128)S(1)} collective-permute-done((f32[27,8,256]{2,1,0:T(8,128)}, f32[27,8,256]{2,1,0:T(8,128)S(1)}, u32[]{:S(2)}, u32[]{:S(2)}) %collective-permute-start.5) | collective-permute-done | bytes 221216 | tf_op jit(solution)/shard_map/ppermute | solution.py:545
  42.6 0.0 copy-done.1
  42.6 1.1 %shard_map.116 = (f32[8,14,8,256]{3,2,1,0:T(8,128)S(1)}, f32[3,8,12,8,256]{4,3,2,1,0:T(8,128)}, f32[8,12,256]{2,1,0:T(8,128)S(1)}) custom-call(f32[27,8,256]{2,1,0:T(8,128)S(1)} %copy-done.1, f32[27,8,256]{2,1,0:T(8,128)S(1)} %collective-permute-done.3.refs_1_, f32[27,8,256]{2,1,0:T(8,128)S(1)} %collective-permute-done.4.refs_2_, ...), custom_call_target="tpu_custom_call", output_to_operand_aliasing={{1}: (4, {})} | custom-call | bytes 2654208 | tf_op jit(solution)/shard_map/pallas_call | solution.py:308
  43.8 0.0 copy-start.4
  43.8 0.0 copy-start.2
  43.8 0.0 copy-start.3
  43.8 0.7 %collective-permute-start.6 = (f32[8,14,8,256]{3,2,1,0:T(8,128)S(1)}, f32[8,14,8,256]{3,2,1,0:T(8,128)S(1)}, u32[]{:S(2)}, u32[]{:S(2)}) collective-permute-start(f32[8,14,8,256]{3,2,1,0:T(8,128)S(1)} %get-tuple-element.26.now_ref.own_ref), channel_id=1, source_target_pairs={{0,1},{1,0},{2,3},{3,2},{4,5},{5,4},{6,7},{7,6},{8,9},{9,8},{10,11... | collective-permute-start | bytes 2752520 | tf_op jit(solution)/shard_map/ppermute | solution.py:556
  44.4 0.0 copy-done.6
  44.4 0.0 copy-done.7
  44.4 0.0 copy-done.8
  44.5 0.1 fusion.7
  44.6 1.2 %collective-permute-start.7 = (f32[8,12,256]{2,1,0:T(8,128)S(1)}, f32[8,12,256]{2,1,0:T(8,128)S(1)}, u32[]{:S(2)}, u32[]{:S(2)}) collective-permute-start(f32[8,12,256]{2,1,0:T(8,128)S(1)} %get-tuple-element.27), channel_id=1, source_target_pairs={{0,2},{2,0},{1,3},{3,1},{4,6},{6,4},{5,7},{7,5},{8,10},{10,8},{9,1... | collective-permute-start | bytes 294920 | tf_op jit(solution)/shard_map/ppermute | solution.py:563
  45.8 0.0 copy-done.5
  45.8 0.4 fusion.2
  46.1 0.0 copy-done
  46.2 0.5 shard_map.117.own_rim
  46.6 3.0 %collective-permute-done.7.own_low.own_high = f32[8,12,256]{2,1,0:T(8,128)S(1)} collective-permute-done((f32[8,12,256]{2,1,0:T(8,128)S(1)}, f32[8,12,256]{2,1,0:T(8,128)S(1)}, u32[]{:S(2)}, u32[]{:S(2)}) %collective-permute-start.7) | collective-permute-done | bytes 98336 | tf_op jit(solution)/shard_map/ppermute | solution.py:563
  49.7 0.8 %collective-permute-start.8 = (f32[8,12,256]{2,1,0:T(8,128)S(1)}, f32[8,12,256]{2,1,0:T(8,128)S(1)}, u32[]{:S(2)}, u32[]{:S(2)}) collective-permute-start(f32[8,12,256]{2,1,0:T(8,128)S(1)} %collective-permute-done.7.own_low.own_high), channel_id=1, source_target_pairs={{0,1},{1,0},{2,3},{3,2},{4,5},{5,4},{6,7},{7,6},{8,9},{9,8},{10,11... | collective-permute-start | bytes 294920 | tf_op jit(solution)/shard_map/ppermute | solution.py:567
  50.5 0.0 copy-done.4
  50.5 0.1 multiply_reduce_fusion
  50.6 0.9 %collective-permute-done.8.other_low.other_high = f32[8,12,256]{2,1,0:T(8,128)S(1)} collective-permute-done((f32[8,12,256]{2,1,0:T(8,128)S(1)}, f32[8,12,256]{2,1,0:T(8,128)S(1)}, u32[]{:S(2)}, u32[]{:S(2)}) %collective-permute-start.8) | collective-permute-done | bytes 98336 | tf_op jit(solution)/shard_map/ppermute | solution.py:567
  51.5 0.0 collective-permute-done.6.other_ref
  51.5 0.0 copy-done.2
  51.5 0.0 copy-done.3
  51.5 4.8 %shard_map.118 = (f32[8,12,8,256]{3,2,1,0:T(8,128)}, f32[8,128]{1,0:T(8,128)S(1)}) custom-call(s32[16]{0:T(128)S(1)} %copy-done.2, s32[16]{0:T(128)S(1)} %copy-done.3, f32[8,14,8,256]{3,2,1,0:T(8,128)S(1)} %get-tuple-element.26.now_ref.own_ref, f32[8,14,8,256]{3,2,1,0:T(8,128)S(1)} %collective-permute-done.6.other_ref, ...), custom_call_target="tpu_custom_call" | custom-call | flops 528482304 | bytes 2752512 | tf_op jit(solution)/shard_map/pallas_call | solution.py:575
  56.3 0.0 collective-permute-done.2.refs_0_
  56.3 0.8 %shard_map.119.refs_2_ = f32[3,8,12,8,256]{4,3,2,1,0:T(8,128)} custom-call(f32[2,2,12,8,256]{4,3,2,1,0:T(8,128)S(1)} %collective-permute-done.2.refs_0_, f32[3,8,12,8,256]{4,3,2,1,0:T(8,128)} %get-tuple-element.25.refs_1_, f32[8,128]{1,0:T(8,128)S(1)} %get-tuple-element.30.refs_2_.refs_3_), custom_call_target="tpu_custom_call", output_to_operand_aliasing={{}: (1, {})} | custom-call | bytes 786432 | tf_op jit(solution)/shard_map/pallas_call | solution.py:242
  57.0 0.0 collective-permute-done.refs_0_
  57.1 2.4 %collective-permute-done.1.refs_1_ = f32[2,2,12,8,256]{4,3,2,1,0:T(8,128)S(1)} collective-permute-done((f32[2,2,12,8,256]{4,3,2,1,0:T(8,128)}, f32[2,2,12,8,256]{4,3,2,1,0:T(8,128)S(1)}, u32[]{:S(2)}, u32[]{:S(2)}) %collective-permute-start.1) | collective-permute-done | bytes 393248 | tf_op jit(solution)/shard_map/ppermute | solution.py:545
  59.5 0.9 %shard_map.120 = f32[3,8,12,8,256]{4,3,2,1,0:T(8,128)} custom-call(f32[2,2,12,8,256]{4,3,2,1,0:T(8,128)S(1)} %collective-permute-done.refs_0_, f32[2,2,12,8,256]{4,3,2,1,0:T(8,128)S(1)} %collective-permute-done.1.refs_1_, f32[3,8,12,8,256]{4,3,2,1,0:T(8,128)} %shard_map.119.refs_2_, ...), custom_call_target="tpu_custom_call", output_to_operand_aliasing={{}: (2, {})} | custom-call | bytes 1572864 | tf_op jit(solution)/shard_map/pallas_call | solution.py:242
  (2 shorter events, 0.0 us)
Async XLA Ops:
  3.0 39.6 %copy-start.1 = (f32[27,8,256]{2,1,0:T(8,128)S(1)}, f32[27,8,256]{2,1,0:T(8,128)}, u32[]{:S(2)}) copy-start(f32[27,8,256]{2,1,0:T(8,128)} %get-tuple-element.20.refs_0_) | copy-start | bytes 663556
  3.0 12.6 %collective-permute-start.3 = (f32[27,8,256]{2,1,0:T(8,128)}, f32[27,8,256]{2,1,0:T(8,128)S(1)}, u32[]{:S(2)}, u32[]{:S(2)}) collective-permute-start(f32[27,8,256]{2,1,0:T(8,128)} %get-tuple-element.21), channel_id=1, source_target_pairs={{0,4},{4,8},{8,12},{12,0},{1,5},{5,9},{9,13},{13,1},{2,6},{6,10},{... | collective-permute-start | bytes 663560 | tf_op jit(solution)/shard_map/ppermute | solution.py:545
  4.3 27.1 %collective-permute-start.4 = (f32[27,8,256]{2,1,0:T(8,128)}, f32[27,8,256]{2,1,0:T(8,128)S(1)}, u32[]{:S(2)}, u32[]{:S(2)}) collective-permute-start(f32[27,8,256]{2,1,0:T(8,128)} %get-tuple-element.22), channel_id=1, source_target_pairs={{0,8},{4,12},{8,0},{12,4},{1,9},{5,13},{9,1},{13,5},{2,10},{6,14},... | collective-permute-start | bytes 663560 | tf_op jit(solution)/shard_map/ppermute | solution.py:545
  5.4 37.2 %collective-permute-start.5 = (f32[27,8,256]{2,1,0:T(8,128)}, f32[27,8,256]{2,1,0:T(8,128)S(1)}, u32[]{:S(2)}, u32[]{:S(2)}) collective-permute-start(f32[27,8,256]{2,1,0:T(8,128)} %get-tuple-element.23), channel_id=1, source_target_pairs={{0,12},{4,0},{8,4},{12,8},{1,13},{5,1},{9,5},{13,9},{2,14},{6,2},{... | collective-permute-start | bytes 663560 | tf_op jit(solution)/shard_map/ppermute | solution.py:545
  9.3 35.1 %copy-start.6 = (f32[24,24]{1,0:T(8,128)S(1)}, f32[24,24]{1,0:T(8,128)}, u32[]{:S(2)}) copy-start(f32[24,24]{1,0:T(8,128)} %param.14) | copy-start | bytes 6916
  9.4 35.1 %copy-start.7 = (f32[24,24]{1,0:T(8,128)S(1)}, f32[24,24]{1,0:T(8,128)}, u32[]{:S(2)}) copy-start(f32[24,24]{1,0:T(8,128)} %param.15) | copy-start | bytes 6916
  9.4 35.1 %copy-start.8 = (f32[24,24]{1,0:T(8,128)S(1)}, f32[24,24]{1,0:T(8,128)}, u32[]{:S(2)}) copy-start(f32[24,24]{1,0:T(8,128)} %param.16) | copy-start | bytes 6916
  9.4 36.4 %copy-start.5 = (f32[24,896,1]{1,0,2:T(8,128)S(1)}, f32[24,896,1]{1,0,2:T(8,128)}, u32[]{:S(2)}) copy-start(f32[24,896,1]{1,0,2:T(8,128)} %constant.27) | copy-start | bytes 258052
  9.4 36.7 %copy-start = (bf16[256,2304]{1,0:T(8,128)(2,1)S(1)}, bf16[256,2304]{1,0:T(8,128)(2,1)}, u32[]{:S(2)}) copy-start(bf16[256,2304]{1,0:T(8,128)(2,1)} %constant.26.spread_ref) | copy-start | bytes 3538948
  9.4 46.9 %collective-permute-start.2 = (f32[2,2,12,8,256]{4,3,2,1,0:T(8,128)}, f32[2,2,12,8,256]{4,3,2,1,0:T(8,128)S(1)}, u32[]{:S(2)}, u32[]{:S(2)}) collective-permute-start(f32[2,2,12,8,256]{4,3,2,1,0:T(8,128)} %get-tuple-element.19), channel_id=1, source_target_pairs={{0,8},{4,12},{8,0},{12,4},{1,9},{5,13},{9,1},{13,5},{2,10},{6,14},... | collective-permute-start | bytes 1179656 | tf_op jit(solution)/shard_map/ppermute | solution.py:545
  13.5 43.6 %collective-permute-start = (f32[2,2,12,8,256]{4,3,2,1,0:T(8,128)}, f32[2,2,12,8,256]{4,3,2,1,0:T(8,128)S(1)}, u32[]{:S(2)}, u32[]{:S(2)}) collective-permute-start(f32[2,2,12,8,256]{4,3,2,1,0:T(8,128)} %get-tuple-element.17), channel_id=1, source_target_pairs={{0,4},{4,8},{8,12},{12,0},{1,5},{5,9},{9,13},{13,1},{2,6},{6,10},{... | collective-permute-start | bytes 1179656 | tf_op jit(solution)/shard_map/ppermute | solution.py:545
  15.6 43.9 %collective-permute-start.1 = (f32[2,2,12,8,256]{4,3,2,1,0:T(8,128)}, f32[2,2,12,8,256]{4,3,2,1,0:T(8,128)S(1)}, u32[]{:S(2)}, u32[]{:S(2)}) collective-permute-start(f32[2,2,12,8,256]{4,3,2,1,0:T(8,128)} %get-tuple-element.18), channel_id=1, source_target_pairs={{0,12},{4,0},{8,4},{12,8},{1,13},{5,1},{9,5},{13,9},{2,14},{6,2},{... | collective-permute-start | bytes 1179656 | tf_op jit(solution)/shard_map/ppermute | solution.py:545
  43.8 6.7 %copy-start.4 = (f32[3,8,896]{2,1,0:T(8,128)S(1)}, f32[3,8,896]{2,1,0:T(8,128)}, u32[]{:S(2)}) copy-start(f32[3,8,896]{2,1,0:T(8,128)} %constant.24.clone) | copy-start | bytes 258052
  43.8 7.7 %copy-start.2 = (s32[16]{0:T(128)S(1)}, s32[16]{0:T(128)}, u32[]{:S(2)}) copy-start(s32[16]{0:T(128)} %dest_ref.7) | copy-start | bytes 196
  43.8 7.7 %copy-start.3 = (s32[16]{0:T(128)S(1)}, s32[16]{0:T(128)}, u32[]{:S(2)}) copy-start(s32[16]{0:T(128)} %parent_ref.3) | copy-start | bytes 196
  43.8 7.7 %collective-permute-start.6 = (f32[8,14,8,256]{3,2,1,0:T(8,128)S(1)}, f32[8,14,8,256]{3,2,1,0:T(8,128)S(1)}, u32[]{:S(2)}, u32[]{:S(2)}) collective-permute-start(f32[8,14,8,256]{3,2,1,0:T(8,128)S(1)} %get-tuple-element.26.now_ref.own_ref), channel_id=1, source_target_pairs={{0,1},{1,0},{2,3},{3,2},{4,5},{5,4},{6,7},{7,6},{8,9},{9,8},{10,11... | collective-permute-start | bytes 2752520 | tf_op jit(solution)/shard_map/ppermute | solution.py:556
  44.6 5.1 %collective-permute-start.7 = (f32[8,12,256]{2,1,0:T(8,128)S(1)}, f32[8,12,256]{2,1,0:T(8,128)S(1)}, u32[]{:S(2)}, u32[]{:S(2)}) collective-permute-start(f32[8,12,256]{2,1,0:T(8,128)S(1)} %get-tuple-element.27), channel_id=1, source_target_pairs={{0,2},{2,0},{1,3},{3,1},{4,6},{6,4},{5,7},{7,5},{8,10},{10,8},{9,1... | collective-permute-start | bytes 294920 | tf_op jit(solution)/shard_map/ppermute | solution.py:563
  49.7 1.8 %collective-permute-start.8 = (f32[8,12,256]{2,1,0:T(8,128)S(1)}, f32[8,12,256]{2,1,0:T(8,128)S(1)}, u32[]{:S(2)}, u32[]{:S(2)}) collective-permute-start(f32[8,12,256]{2,1,0:T(8,128)S(1)} %collective-permute-done.7.own_low.own_high), channel_id=1, source_target_pairs={{0,1},{1,0},{2,3},{3,2},{4,5},{5,4},{6,7},{7,6},{8,9},{9,8},{10,11... | collective-permute-start | bytes 294920 | tf_op jit(solution)/shard_map/ppermute | solution.py:567

commit v15 on v14

--- a/solution.py
+++ b/solution.py
@@ -283,7 +283,7 @@
                 now_ref[2 * source + k, fields + f // planes, f % planes : f % planes + 1] = values
             for edge_ref, plane in zip(edges, faced):
                 for f in range(fields):
-                    edge_ref[2 * source + k, f : f + 1] = now_ref[2 * source + k, f, pl.ds(plane, 1)]
+                    edge_ref[pl.ds((2 * source + k) * fields + f, 1)] = now_ref[2 * source + k, f, pl.ds(plane, 1)]
 
     for turn in range(1, box_count):
         source = source_of(own, turn, box_count)
@@ -304,7 +304,7 @@
     slots = 2 * box_count
     sides = 1 if slabs == 2 else 2
     vmem, hbm = pl.BlockSpec(memory_space=pltpu.VMEM), pl.BlockSpec(memory_space=pltpu.HBM)
-    shapes = [(slots, fields + ROWS // planes, planes, cross), moved.shape] + [(slots, fields, cross)] * sides
+    shapes = [(slots, fields + ROWS // planes, planes, cross), moved.shape] + [(slots * fields, cross)] * sides
     return pl.pallas_call(
         functools.partial(arrive_kernel, box_count, slabs, fields),
         out_shape=[jax.ShapeDtypeStruct(shape, jnp.float32) for shape in shapes],
@@ -485,15 +485,19 @@
             stack[base : base + 2 * ROWS] = x_face
             stack[base + 2 * ROWS : base + 4 * ROWS] = x_face
 
+            def set_halo(at, refs):
+                for n, ref in enumerate(refs):
+                    for f in range(fields):
+                        row = at + n * ROWS + f
+                        stack[row : row + 1] = ref[pl.ds(step * fields + f, 1)]
+
             @pl.when(slab > 0)
             def _():
-                stack[base : base + fields] = own_low[step]
-                stack[base + ROWS : base + ROWS + fields] = other_low[step]
+                set_halo(6 * rows, (own_low, other_low))
 
             @pl.when(slab < slabs - 1)
             def _():
-                stack[base + 2 * ROWS : base + 2 * ROWS + fields] = own_high[step]
-                stack[base + 3 * ROWS : base + 3 * ROWS + fields] = other_high[step]
+                set_halo(6 * rows + 2 * ROWS, (own_high, other_high))
 
             base += 4 * ROWS
             for n in range(2 * coarse_planes):
@@ -596,8 +600,8 @@
             flops=3 * slots * weight.size * cross, bytes_accessed=12 * now.size, transcendentals=0
         ),
     )(move_dest, parent, now, now_other, low[0], low[1], high[0], high[1], rim, spread, weight)
-    moved = settle(tuple(range(2, box_count - 1)), middle, moved, token)
-    return settle((1, box_count - 1), near, moved, token), slope
+    later_arrived = [near[0]] + middle + [near[1]]
+    return settle(tuple(range(1, box_count)), later_arrived, moved, token), slope
 
 
 def solution(mesh):

time: 60.6 us -> 60.7 us (level)
  waiting for transfers between devices: 33.3 us -> 35.3 us
  Pallas kernels: 15.9 us -> 14.1 us
    ppermute x6, waiting for transfers between devices: 29.4 us -> 32.1 us  [send(): lax.ppermute(piece, 'box', [(s, (s + turn) % box_count) for s in range(bo...]
    pallas_call x1, Pallas kernels: 4.77 us -> 3.63 us  [body(): pl.pallas_call(functools.partial(slope_kernel, edge, planes, fields, coar...]
    ppermute x1, waiting for transfers between devices: 3.01 us -> 2.31 us  [shifted(): return lax.ppermute(values, 'slab', swap if slabs == 2 else pairs)]
    pallas_call x2 -> x1, Pallas kernels: 1.66 us -> 1.03 us  [settle(): pl.pallas_call(functools.partial(settle_kernel, turns), out_shape=jax.Sha...]
  transfers between devices with their start and end apart: 9 -> 9, of which waited for: 5 -> 6; matrix products, arithmetic and copies ran while one was open for 1% -> 1% of each run, Pallas kernels for 21% -> 18%
where the time goes in v15:
time: 60.7 us; the launch traced here: 60.5 us
  waiting for transfers between devices  35.3 us (58%)
  Pallas kernels  14.1 us (23%)
  starting transfers between devices  9.73 us (16%)
  between operations  0.8 us (1%)
    ppermute x6, waiting for transfers between devices, send(): lax.ppermute(piece, 'box', [(s, (s + turn) % box_count) for s in range(bo...  32.1 us
    ppermute x6, starting transfers between devices, send(): lax.ppermute(piece, 'box', [(s, (s + turn) % box_count) for s in range(bo...  7.03 us
    pallas_call x2, Pallas kernels, pack_later(): pl.pallas_call(functools.partial(later_kernel, turns, per_device, box_cou...  5.49 us
    pallas_call x1, Pallas kernels, body(): pl.pallas_call(functools.partial(slope_kernel, edge, planes, fields, coar...  3.63 us
    pallas_call x1, Pallas kernels, pack_first(): pl.pallas_call(functools.partial(first_kernel, per_device, box_count, edg...  2.33 us
    ppermute x1, waiting for transfers between devices, shifted(): return lax.ppermute(values, 'slab', swap if slabs == 2 else pairs)  2.31 us
    ppermute x1, starting transfers between devices, shifted(): return lax.ppermute(values, 'slab', swap if slabs == 2 else pairs)  1.22 us
  transfers between devices with their start and end apart: 9, of which 6 were waited for; matrix products, arithmetic and copies ran while one was open for 1% of the time, Pallas kernels for 18%

profile of v15, /device:TPU:9, one launch (start us, length us, event | category | flops | bytes accessed | tf_op | source)
XLA Modules:
  0.0 60.5 jit_solution(3503352798462294563)
XLA Ops:
  0.6 2.3 %shard_map.115 = (f32[27,8,256]{2,1,0:T(8,128)}, f32[27,8,256]{2,1,0:T(8,128)}, f32[27,8,256]{2,1,0:T(8,128)}, f32[27,8,256]{2,1,0:T(8,128)}) custom-call(s32[16]{0:T(128)} %dest_ref.7, s32[16]{0:T(128)} %parent_ref.3, f32[3,4,12,8,256]{4,3,2,1,0:T(8,128)} %boxes_ref.5, f32[12,8,1000]{2,1,0:T(8,128)} %bitcast.11), custom_call_target="tpu_custom_call" | custom-call | flops 147456000 | bytes 2743296 | tf_op jit(solution)/shard_map/pallas_call | solution.py:132
  3.0 0.0 copy-start.1
  3.0 1.3 %collective-permute-start.3 = (f32[27,8,256]{2,1,0:T(8,128)}, f32[27,8,256]{2,1,0:T(8,128)S(1)}, u32[]{:S(2)}, u32[]{:S(2)}) collective-permute-start(f32[27,8,256]{2,1,0:T(8,128)} %get-tuple-element.21), channel_id=1, source_target_pairs={{0,4},{4,8},{8,12},{12,0},{1,5},{5,9},{9,13},{13,1},{2,6},{6,10},{... | collective-permute-start | bytes 663560 | tf_op jit(solution)/shard_map/ppermute | solution.py:549
  4.3 1.1 %collective-permute-start.4 = (f32[27,8,256]{2,1,0:T(8,128)}, f32[27,8,256]{2,1,0:T(8,128)S(1)}, u32[]{:S(2)}, u32[]{:S(2)}) collective-permute-start(f32[27,8,256]{2,1,0:T(8,128)} %get-tuple-element.22), channel_id=1, source_target_pairs={{0,8},{4,12},{8,0},{12,4},{1,9},{5,13},{9,1},{13,5},{2,10},{6,14},... | collective-permute-start | bytes 663560 | tf_op jit(solution)/shard_map/ppermute | solution.py:549
  5.4 1.4 %collective-permute-start.5 = (f32[27,8,256]{2,1,0:T(8,128)}, f32[27,8,256]{2,1,0:T(8,128)S(1)}, u32[]{:S(2)}, u32[]{:S(2)}) collective-permute-start(f32[27,8,256]{2,1,0:T(8,128)} %get-tuple-element.23), channel_id=1, source_target_pairs={{0,12},{4,0},{8,4},{12,8},{1,13},{5,1},{9,5},{13,9},{2,14},{6,2},{... | collective-permute-start | bytes 663560 | tf_op jit(solution)/shard_map/ppermute | solution.py:549
  6.8 2.5 %shard_map.114 = (f32[3,8,12,8,256]{4,3,2,1,0:T(8,128)}, f32[2,2,12,8,256]{4,3,2,1,0:T(8,128)}) custom-call(s32[16]{0:T(128)} %dest_ref.7, f32[3,4,12,8,256]{4,3,2,1,0:T(8,128)} %boxes_ref.5), custom_call_target="tpu_custom_call" | custom-call | bytes 2359296 | tf_op jit(solution)/shard_map/pallas_call | solution.py:206
  9.3 0.0 copy-start.6
  9.4 0.0 copy-start.7
  9.4 0.0 copy-start.8
  9.4 0.0 copy-start.5
  9.4 0.0 copy-start
  9.4 1.1 %collective-permute-start.1 = (f32[2,2,12,8,256]{4,3,2,1,0:T(8,128)}, f32[2,2,12,8,256]{4,3,2,1,0:T(8,128)S(1)}, u32[]{:S(2)}, u32[]{:S(2)}) collective-permute-start(f32[2,2,12,8,256]{4,3,2,1,0:T(8,128)} %get-tuple-element.18), channel_id=1, source_target_pairs={{0,8},{4,12},{8,0},{12,4},{1,9},{5,13},{9,1},{13,5},{2,10},{6,14},... | collective-permute-start | bytes 1179656 | tf_op jit(solution)/shard_map/ppermute | solution.py:549
  10.5 3.0 %shard_map.113 = (f32[2,2,12,8,256]{4,3,2,1,0:T(8,128)}, f32[2,2,12,8,256]{4,3,2,1,0:T(8,128)}) custom-call(s32[16]{0:T(128)} %dest_ref.7, f32[3,4,12,8,256]{4,3,2,1,0:T(8,128)} %boxes_ref.5), custom_call_target="tpu_custom_call" | custom-call | bytes 2359296 | tf_op jit(solution)/shard_map/pallas_call | solution.py:206
  13.5 2.1 %collective-permute-start = (f32[2,2,12,8,256]{4,3,2,1,0:T(8,128)}, f32[2,2,12,8,256]{4,3,2,1,0:T(8,128)S(1)}, u32[]{:S(2)}, u32[]{:S(2)}) collective-permute-start(f32[2,2,12,8,256]{4,3,2,1,0:T(8,128)} %get-tuple-element.17), channel_id=1, source_target_pairs={{0,4},{4,8},{8,12},{12,0},{1,5},{5,9},{9,13},{13,1},{2,6},{6,10},{... | collective-permute-start | bytes 1179656 | tf_op jit(solution)/shard_map/ppermute | solution.py:549
  15.6 0.0 collective-permute-done.3.refs_1_
  15.6 0.0 collective-permute-start.2
  15.6 15.8 %collective-permute-done.4.refs_2_ = f32[27,8,256]{2,1,0:T(8,128)S(1)} collective-permute-done((f32[27,8,256]{2,1,0:T(8,128)}, f32[27,8,256]{2,1,0:T(8,128)S(1)}, u32[]{:S(2)}, u32[]{:S(2)}) %collective-permute-start.4) | collective-permute-done | bytes 221216 | tf_op jit(solution)/shard_map/ppermute | solution.py:549
  31.4 11.2 %collective-permute-done.5.refs_3_ = f32[27,8,256]{2,1,0:T(8,128)S(1)} collective-permute-done((f32[27,8,256]{2,1,0:T(8,128)}, f32[27,8,256]{2,1,0:T(8,128)S(1)}, u32[]{:S(2)}, u32[]{:S(2)}) %collective-permute-start.5) | collective-permute-done | bytes 221216 | tf_op jit(solution)/shard_map/ppermute | solution.py:549
  42.6 0.0 copy-done.1
  42.6 1.1 %shard_map.116 = (f32[8,14,8,256]{3,2,1,0:T(8,128)S(1)}, f32[3,8,12,8,256]{4,3,2,1,0:T(8,128)}, f32[96,256]{1,0:T(8,128)S(1)}) custom-call(f32[27,8,256]{2,1,0:T(8,128)S(1)} %copy-done.1, f32[27,8,256]{2,1,0:T(8,128)S(1)} %collective-permute-done.3.refs_1_, f32[27,8,256]{2,1,0:T(8,128)S(1)} %collective-permute-done.4.refs_2_, ...), custom_call_target="tpu_custom_call", output_to_operand_aliasing={{1}: (4, {})} | custom-call | bytes 2654208 | tf_op jit(solution)/shard_map/pallas_call | solution.py:308
  43.8 0.0 copy-start.4
  43.8 0.0 copy-start.2
  43.8 0.0 copy-start.3
  43.8 0.7 %collective-permute-start.6 = (f32[8,14,8,256]{3,2,1,0:T(8,128)S(1)}, f32[8,14,8,256]{3,2,1,0:T(8,128)S(1)}, u32[]{:S(2)}, u32[]{:S(2)}) collective-permute-start(f32[8,14,8,256]{3,2,1,0:T(8,128)S(1)} %get-tuple-element.26.now_ref.own_ref), channel_id=1, source_target_pairs={{0,1},{1,0},{2,3},{3,2},{4,5},{5,4},{6,7},{7,6},{8,9},{9,8},{10,11... | collective-permute-start | bytes 2752520 | tf_op jit(solution)/shard_map/ppermute | solution.py:560
  44.4 0.0 copy-done.6
  44.4 0.0 copy-done.7
  44.4 0.0 copy-done.8
  44.5 0.1 fusion.7
  44.6 1.2 %collective-permute-start.7 = (f32[96,256]{1,0:T(8,128)S(1)}, f32[96,256]{1,0:T(8,128)S(1)}, u32[]{:S(2)}, u32[]{:S(2)}) collective-permute-start(f32[96,256]{1,0:T(8,128)S(1)} %get-tuple-element.27), channel_id=1, source_target_pairs={{0,2},{2,0},{1,3},{3,1},{4,6},{6,4},{5,7},{7,5},{8,10},{10,8},{9,1... | collective-permute-start | bytes 294920 | tf_op jit(solution)/shard_map/ppermute | solution.py:567
  45.8 0.0 copy-done.5
  45.8 0.4 fusion.2
  46.1 0.0 copy-done
  46.2 0.5 shard_map.117.own_rim
  46.6 2.3 %collective-permute-done.7.own_low.own_high = f32[96,256]{1,0:T(8,128)S(1)} collective-permute-done((f32[96,256]{1,0:T(8,128)S(1)}, f32[96,256]{1,0:T(8,128)S(1)}, u32[]{:S(2)}, u32[]{:S(2)}) %collective-permute-start.7) | collective-permute-done | bytes 98336 | tf_op jit(solution)/shard_map/ppermute | solution.py:567
  49.0 0.8 %collective-permute-start.8 = (f32[96,256]{1,0:T(8,128)S(1)}, f32[96,256]{1,0:T(8,128)S(1)}, u32[]{:S(2)}, u32[]{:S(2)}) collective-permute-start(f32[96,256]{1,0:T(8,128)S(1)} %collective-permute-done.7.own_low.own_high), channel_id=1, source_target_pairs={{0,1},{1,0},{2,3},{3,2},{4,5},{5,4},{6,7},{7,6},{8,9},{9,8},{10,11... | collective-permute-start | bytes 294920 | tf_op jit(solution)/shard_map/ppermute | solution.py:571
  49.8 0.0 copy-done.4
  49.8 0.1 multiply_reduce_fusion
  49.9 0.9 %collective-permute-done.8.other_low.other_high = f32[96,256]{1,0:T(8,128)S(1)} collective-permute-done((f32[96,256]{1,0:T(8,128)S(1)}, f32[96,256]{1,0:T(8,128)S(1)}, u32[]{:S(2)}, u32[]{:S(2)}) %collective-permute-start.8) | collective-permute-done | bytes 98336 | tf_op jit(solution)/shard_map/ppermute | solution.py:571
  50.7 0.0 collective-permute-done.6.other_ref
  50.7 0.0 copy-done.2
  50.7 0.0 copy-done.3
  50.7 3.6 %shard_map.118 = (f32[8,12,8,256]{3,2,1,0:T(8,128)}, f32[8,128]{1,0:T(8,128)S(1)}) custom-call(s32[16]{0:T(128)S(1)} %copy-done.2, s32[16]{0:T(128)S(1)} %copy-done.3, f32[8,14,8,256]{3,2,1,0:T(8,128)S(1)} %get-tuple-element.26.now_ref.own_ref, f32[8,14,8,256]{3,2,1,0:T(8,128)S(1)} %collective-permute-done.6.other_ref, ...), custom_call_target="tpu_custom_call" | custom-call | flops 528482304 | bytes 2752512 | tf_op jit(solution)/shard_map/pallas_call | solution.py:579
  54.4 0.0 collective-permute-done.1.refs_1_
  54.4 2.3 %collective-permute-done.refs_0_ = f32[2,2,12,8,256]{4,3,2,1,0:T(8,128)S(1)} collective-permute-done((f32[2,2,12,8,256]{4,3,2,1,0:T(8,128)}, f32[2,2,12,8,256]{4,3,2,1,0:T(8,128)S(1)}, u32[]{:S(2)}, u32[]{:S(2)}) %collective-permute-start) | collective-permute-done | bytes 393248 | tf_op jit(solution)/shard_map/ppermute | solution.py:549
  56.7 2.8 %collective-permute-done.2.refs_2_ = f32[2,2,12,8,256]{4,3,2,1,0:T(8,128)S(1)} collective-permute-done((f32[2,2,12,8,256]{4,3,2,1,0:T(8,128)}, f32[2,2,12,8,256]{4,3,2,1,0:T(8,128)S(1)}, u32[]{:S(2)}, u32[]{:S(2)}) %collective-permute-start.2) | collective-permute-done | bytes 393248 | tf_op jit(solution)/shard_map/ppermute | solution.py:549
  59.5 1.0 %shard_map.119 = f32[3,8,12,8,256]{4,3,2,1,0:T(8,128)} custom-call(f32[2,2,12,8,256]{4,3,2,1,0:T(8,128)S(1)} %collective-permute-done.refs_0_, f32[2,2,12,8,256]{4,3,2,1,0:T(8,128)S(1)} %collective-permute-done.1.refs_1_, f32[2,2,12,8,256]{4,3,2,1,0:T(8,128)S(1)} %collective-permute-done.2.refs_2_, ...), custom_call_target="tpu_custom_call", output_to_operand_aliasing={{}: (3, {})} | custom-call | bytes 2359296 | tf_op jit(solution)/shard_map/pallas_call | solution.py:242
  (2 shorter events, 0.0 us)
Async XLA Ops:
  3.0 39.6 %copy-start.1 = (f32[27,8,256]{2,1,0:T(8,128)S(1)}, f32[27,8,256]{2,1,0:T(8,128)}, u32[]{:S(2)}) copy-start(f32[27,8,256]{2,1,0:T(8,128)} %get-tuple-element.20.refs_0_) | copy-start | bytes 663556
  3.0 12.6 %collective-permute-start.3 = (f32[27,8,256]{2,1,0:T(8,128)}, f32[27,8,256]{2,1,0:T(8,128)S(1)}, u32[]{:S(2)}, u32[]{:S(2)}) collective-permute-start(f32[27,8,256]{2,1,0:T(8,128)} %get-tuple-element.21), channel_id=1, source_target_pairs={{0,4},{4,8},{8,12},{12,0},{1,5},{5,9},{9,13},{13,1},{2,6},{6,10},{... | collective-permute-start | bytes 663560 | tf_op jit(solution)/shard_map/ppermute | solution.py:549
  4.3 27.1 %collective-permute-start.4 = (f32[27,8,256]{2,1,0:T(8,128)}, f32[27,8,256]{2,1,0:T(8,128)S(1)}, u32[]{:S(2)}, u32[]{:S(2)}) collective-permute-start(f32[27,8,256]{2,1,0:T(8,128)} %get-tuple-element.22), channel_id=1, source_target_pairs={{0,8},{4,12},{8,0},{12,4},{1,9},{5,13},{9,1},{13,5},{2,10},{6,14},... | collective-permute-start | bytes 663560 | tf_op jit(solution)/shard_map/ppermute | solution.py:549
  5.4 37.2 %collective-permute-start.5 = (f32[27,8,256]{2,1,0:T(8,128)}, f32[27,8,256]{2,1,0:T(8,128)S(1)}, u32[]{:S(2)}, u32[]{:S(2)}) collective-permute-start(f32[27,8,256]{2,1,0:T(8,128)} %get-tuple-element.23), channel_id=1, source_target_pairs={{0,12},{4,0},{8,4},{12,8},{1,13},{5,1},{9,5},{13,9},{2,14},{6,2},{... | collective-permute-start | bytes 663560 | tf_op jit(solution)/shard_map/ppermute | solution.py:549
  9.3 35.1 %copy-start.6 = (f32[24,24]{1,0:T(8,128)S(1)}, f32[24,24]{1,0:T(8,128)}, u32[]{:S(2)}) copy-start(f32[24,24]{1,0:T(8,128)} %param.14) | copy-start | bytes 6916
  9.4 35.1 %copy-start.7 = (f32[24,24]{1,0:T(8,128)S(1)}, f32[24,24]{1,0:T(8,128)}, u32[]{:S(2)}) copy-start(f32[24,24]{1,0:T(8,128)} %param.15) | copy-start | bytes 6916
  9.4 35.1 %copy-start.8 = (f32[24,24]{1,0:T(8,128)S(1)}, f32[24,24]{1,0:T(8,128)}, u32[]{:S(2)}) copy-start(f32[24,24]{1,0:T(8,128)} %param.16) | copy-start | bytes 6916
  9.4 36.4 %copy-start.5 = (f32[24,896,1]{1,0,2:T(8,128)S(1)}, f32[24,896,1]{1,0,2:T(8,128)}, u32[]{:S(2)}) copy-start(f32[24,896,1]{1,0,2:T(8,128)} %constant.27) | copy-start | bytes 258052
  9.4 36.7 %copy-start = (bf16[256,2304]{1,0:T(8,128)(2,1)S(1)}, bf16[256,2304]{1,0:T(8,128)(2,1)}, u32[]{:S(2)}) copy-start(bf16[256,2304]{1,0:T(8,128)(2,1)} %constant.26.spread_ref) | copy-start | bytes 3538948
  9.4 45.0 %collective-permute-start.1 = (f32[2,2,12,8,256]{4,3,2,1,0:T(8,128)}, f32[2,2,12,8,256]{4,3,2,1,0:T(8,128)S(1)}, u32[]{:S(2)}, u32[]{:S(2)}) collective-permute-start(f32[2,2,12,8,256]{4,3,2,1,0:T(8,128)} %get-tuple-element.18), channel_id=1, source_target_pairs={{0,8},{4,12},{8,0},{12,4},{1,9},{5,13},{9,1},{13,5},{2,10},{6,14},... | collective-permute-start | bytes 1179656 | tf_op jit(solution)/shard_map/ppermute | solution.py:549
  13.5 43.2 %collective-permute-start = (f32[2,2,12,8,256]{4,3,2,1,0:T(8,128)}, f32[2,2,12,8,256]{4,3,2,1,0:T(8,128)S(1)}, u32[]{:S(2)}, u32[]{:S(2)}) collective-permute-start(f32[2,2,12,8,256]{4,3,2,1,0:T(8,128)} %get-tuple-element.17), channel_id=1, source_target_pairs={{0,4},{4,8},{8,12},{12,0},{1,5},{5,9},{9,13},{13,1},{2,6},{6,10},{... | collective-permute-start | bytes 1179656 | tf_op jit(solution)/shard_map/ppermute | solution.py:549
  15.6 43.9 %collective-permute-start.2 = (f32[2,2,12,8,256]{4,3,2,1,0:T(8,128)}, f32[2,2,12,8,256]{4,3,2,1,0:T(8,128)S(1)}, u32[]{:S(2)}, u32[]{:S(2)}) collective-permute-start(f32[2,2,12,8,256]{4,3,2,1,0:T(8,128)} %get-tuple-element.19), channel_id=1, source_target_pairs={{0,12},{4,0},{8,4},{12,8},{1,13},{5,1},{9,5},{13,9},{2,14},{6,2},{... | collective-permute-start | bytes 1179656 | tf_op jit(solution)/shard_map/ppermute | solution.py:549
  43.8 6.0 %copy-start.4 = (f32[3,8,896]{2,1,0:T(8,128)S(1)}, f32[3,8,896]{2,1,0:T(8,128)}, u32[]{:S(2)}) copy-start(f32[3,8,896]{2,1,0:T(8,128)} %constant.24.clone) | copy-start | bytes 258052
  43.8 7.0 %copy-start.2 = (s32[16]{0:T(128)S(1)}, s32[16]{0:T(128)}, u32[]{:S(2)}) copy-start(s32[16]{0:T(128)} %dest_ref.7) | copy-start | bytes 196
  43.8 7.0 %copy-start.3 = (s32[16]{0:T(128)S(1)}, s32[16]{0:T(128)}, u32[]{:S(2)}) copy-start(s32[16]{0:T(128)} %parent_ref.3) | copy-start | bytes 196
  43.8 6.9 %collective-permute-start.6 = (f32[8,14,8,256]{3,2,1,0:T(8,128)S(1)}, f32[8,14,8,256]{3,2,1,0:T(8,128)S(1)}, u32[]{:S(2)}, u32[]{:S(2)}) collective-permute-start(f32[8,14,8,256]{3,2,1,0:T(8,128)S(1)} %get-tuple-element.26.now_ref.own_ref), channel_id=1, source_target_pairs={{0,1},{1,0},{2,3},{3,2},{4,5},{5,4},{6,7},{7,6},{8,9},{9,8},{10,11... | collective-permute-start | bytes 2752520 | tf_op jit(solution)/shard_map/ppermute | solution.py:560
  44.6 4.4 %collective-permute-start.7 = (f32[96,256]{1,0:T(8,128)S(1)}, f32[96,256]{1,0:T(8,128)S(1)}, u32[]{:S(2)}, u32[]{:S(2)}) collective-permute-start(f32[96,256]{1,0:T(8,128)S(1)} %get-tuple-element.27), channel_id=1, source_target_pairs={{0,2},{2,0},{1,3},{3,1},{4,6},{6,4},{5,7},{7,5},{8,10},{10,8},{9,1... | collective-permute-start | bytes 294920 | tf_op jit(solution)/shard_map/ppermute | solution.py:567
  49.0 1.8 %collective-permute-start.8 = (f32[96,256]{1,0:T(8,128)S(1)}, f32[96,256]{1,0:T(8,128)S(1)}, u32[]{:S(2)}, u32[]{:S(2)}) collective-permute-start(f32[96,256]{1,0:T(8,128)S(1)} %collective-permute-done.7.own_low.own_high), channel_id=1, source_target_pairs={{0,1},{1,0},{2,3},{3,2},{4,5},{5,4},{6,7},{7,6},{8,9},{9,8},{10,11... | collective-permute-start | bytes 294920 | tf_op jit(solution)/shard_map/ppermute | solution.py:571

commit v16 on v15

--- a/solution.py
+++ b/solution.py
@@ -600,8 +600,8 @@
             flops=3 * slots * weight.size * cross, bytes_accessed=12 * now.size, transcendentals=0
         ),
     )(move_dest, parent, now, now_other, low[0], low[1], high[0], high[1], rim, spread, weight)
-    later_arrived = [near[0]] + middle + [near[1]]
-    return settle(tuple(range(1, box_count)), later_arrived, moved, token), slope
+    moved = settle(tuple(range(2, box_count - 1)), middle, moved, token)
+    return settle((1, box_count - 1), near, moved, token), slope
 
 
 def solution(mesh):

time: 60.7 us -> 60.6 us (level)
  Pallas kernels: 14.1 us -> 16.9 us
  starting transfers between devices: 9.73 us -> 8.17 us
  waiting for transfers between devices: 35.3 us -> 33.9 us
    ppermute x6, starting transfers between devices: 7.03 us -> 5.47 us  [send(): lax.ppermute(piece, 'box', [(s, (s + turn) % box_count) for s in range(bo...]
    ppermute x6, waiting for transfers between devices: 32.1 us -> 30.7 us  [send(): lax.ppermute(piece, 'box', [(s, (s + turn) % box_count) for s in range(bo...]
    pallas_call x1, Pallas kernels: 3.63 us -> 4.87 us  [body(): pl.pallas_call(functools.partial(slope_kernel, edge, planes, fields, coar...]
    pallas_call x2, Pallas kernels: 5.49 us -> 6.42 us  [pack_later(): pl.pallas_call(functools.partial(later_kernel, turns, per_device, box_cou...]
    pallas_call x1 -> x2, Pallas kernels: 1.03 us -> 1.66 us  [settle(): pl.pallas_call(functools.partial(settle_kernel, turns), out_shape=jax.Sha...]
  transfers between devices with their start and end apart: 9 -> 9, of which waited for: 6 -> 6; matrix products, arithmetic and copies ran while one was open for 1% -> 1% of each run, Pallas kernels for 18% -> 23%
where the time goes in v16:
time: 60.6 us; the launch traced here: 60.3 us
  waiting for transfers between devices  33.9 us (56%)
  Pallas kernels  16.9 us (28%)
  starting transfers between devices  8.17 us (13%)
  between operations  0.81 us (1%)
    ppermute x6, waiting for transfers between devices, send(): lax.ppermute(piece, 'box', [(s, (s + turn) % box_count) for s in range(bo...  30.7 us
    pallas_call x2, Pallas kernels, pack_later(): pl.pallas_call(functools.partial(later_kernel, turns, per_device, box_cou...  6.42 us
    ppermute x6, starting transfers between devices, send(): lax.ppermute(piece, 'box', [(s, (s + turn) % box_count) for s in range(bo...  5.47 us
    pallas_call x1, Pallas kernels, body(): pl.pallas_call(functools.partial(slope_kernel, edge, planes, fields, coar...  4.87 us
    pallas_call x1, Pallas kernels, pack_first(): pl.pallas_call(functools.partial(first_kernel, per_device, box_count, edg...  2.33 us
    ppermute x1, waiting for transfers between devices, shifted(): return lax.ppermute(values, 'slab', swap if slabs == 2 else pairs)  2.31 us
    pallas_call x2, Pallas kernels, settle(): pl.pallas_call(functools.partial(settle_kernel, turns), out_shape=jax.Sha...  1.66 us
    ppermute x1, starting transfers between devices, shifted(): return lax.ppermute(values, 'slab', swap if slabs == 2 else pairs)  1.22 us
  transfers between devices with their start and end apart: 9, of which 6 were waited for; matrix products, arithmetic and copies ran while one was open for 1% of the time, Pallas kernels for 23%

profile of v16, /device:TPU:9, one launch (start us, length us, event | category | flops | bytes accessed | tf_op | source)
XLA Modules:
  0.0 60.3 jit_solution(8087885716545354408)
XLA Ops:
  0.6 2.3 %shard_map.115 = (f32[27,8,256]{2,1,0:T(8,128)}, f32[27,8,256]{2,1,0:T(8,128)}, f32[27,8,256]{2,1,0:T(8,128)}, f32[27,8,256]{2,1,0:T(8,128)}) custom-call(s32[16]{0:T(128)} %dest_ref.7, s32[16]{0:T(128)} %parent_ref.3, f32[3,4,12,8,256]{4,3,2,1,0:T(8,128)} %boxes_ref.5, f32[12,8,1000]{2,1,0:T(8,128)} %bitcast.11), custom_call_target="tpu_custom_call" | custom-call | flops 147456000 | bytes 2743296 | tf_op jit(solution)/shard_map/pallas_call | solution.py:132
  3.0 0.0 copy-start.1
  3.0 1.3 %collective-permute-start.3 = (f32[27,8,256]{2,1,0:T(8,128)}, f32[27,8,256]{2,1,0:T(8,128)S(1)}, u32[]{:S(2)}, u32[]{:S(2)}) collective-permute-start(f32[27,8,256]{2,1,0:T(8,128)} %get-tuple-element.21), channel_id=1, source_target_pairs={{0,4},{4,8},{8,12},{12,0},{1,5},{5,9},{9,13},{13,1},{2,6},{6,10},{... | collective-permute-start | bytes 663560 | tf_op jit(solution)/shard_map/ppermute | solution.py:549
  4.3 1.1 %collective-permute-start.4 = (f32[27,8,256]{2,1,0:T(8,128)}, f32[27,8,256]{2,1,0:T(8,128)S(1)}, u32[]{:S(2)}, u32[]{:S(2)}) collective-permute-start(f32[27,8,256]{2,1,0:T(8,128)} %get-tuple-element.22), channel_id=1, source_target_pairs={{0,8},{4,12},{8,0},{12,4},{1,9},{5,13},{9,1},{13,5},{2,10},{6,14},... | collective-permute-start | bytes 663560 | tf_op jit(solution)/shard_map/ppermute | solution.py:549
  5.4 1.4 %collective-permute-start.5 = (f32[27,8,256]{2,1,0:T(8,128)}, f32[27,8,256]{2,1,0:T(8,128)S(1)}, u32[]{:S(2)}, u32[]{:S(2)}) collective-permute-start(f32[27,8,256]{2,1,0:T(8,128)} %get-tuple-element.23), channel_id=1, source_target_pairs={{0,12},{4,0},{8,4},{12,8},{1,13},{5,1},{9,5},{13,9},{2,14},{6,2},{... | collective-permute-start | bytes 663560 | tf_op jit(solution)/shard_map/ppermute | solution.py:549
  6.8 3.5 %shard_map.114 = (f32[3,8,12,8,256]{4,3,2,1,0:T(8,128)}, f32[2,2,12,8,256]{4,3,2,1,0:T(8,128)}) custom-call(s32[16]{0:T(128)} %dest_ref.7, f32[3,4,12,8,256]{4,3,2,1,0:T(8,128)} %boxes_ref.5), custom_call_target="tpu_custom_call" | custom-call | bytes 2359296 | tf_op jit(solution)/shard_map/pallas_call | solution.py:206
  10.3 0.0 copy-start.6
  10.3 0.0 copy-start.7
  10.3 0.0 copy-start.8
  10.4 0.0 copy-start.5
  10.4 0.0 copy-start
  10.4 0.1 collective-permute-start.2
  10.5 2.9 %shard_map.113 = (f32[2,2,12,8,256]{4,3,2,1,0:T(8,128)}, f32[2,2,12,8,256]{4,3,2,1,0:T(8,128)}) custom-call(s32[16]{0:T(128)} %dest_ref.7, f32[3,4,12,8,256]{4,3,2,1,0:T(8,128)} %boxes_ref.5), custom_call_target="tpu_custom_call" | custom-call | bytes 2359296 | tf_op jit(solution)/shard_map/pallas_call | solution.py:206
  13.4 1.2 %collective-permute-start = (f32[2,2,12,8,256]{4,3,2,1,0:T(8,128)}, f32[2,2,12,8,256]{4,3,2,1,0:T(8,128)S(1)}, u32[]{:S(2)}, u32[]{:S(2)}) collective-permute-start(f32[2,2,12,8,256]{4,3,2,1,0:T(8,128)} %get-tuple-element.17), channel_id=1, source_target_pairs={{0,4},{4,8},{8,12},{12,0},{1,5},{5,9},{9,13},{13,1},{2,6},{6,10},{... | collective-permute-start | bytes 1179656 | tf_op jit(solution)/shard_map/ppermute | solution.py:549
  14.6 0.0 collective-permute-done.3.refs_1_
  14.6 0.3 collective-permute-start.1
  14.9 16.5 %collective-permute-done.4.refs_2_ = f32[27,8,256]{2,1,0:T(8,128)S(1)} collective-permute-done((f32[27,8,256]{2,1,0:T(8,128)}, f32[27,8,256]{2,1,0:T(8,128)S(1)}, u32[]{:S(2)}, u32[]{:S(2)}) %collective-permute-start.4) | collective-permute-done | bytes 221216 | tf_op jit(solution)/shard_map/ppermute | solution.py:549
  31.4 11.2 %collective-permute-done.5.refs_3_ = f32[27,8,256]{2,1,0:T(8,128)S(1)} collective-permute-done((f32[27,8,256]{2,1,0:T(8,128)}, f32[27,8,256]{2,1,0:T(8,128)S(1)}, u32[]{:S(2)}, u32[]{:S(2)}) %collective-permute-start.5) | collective-permute-done | bytes 221216 | tf_op jit(solution)/shard_map/ppermute | solution.py:549
  42.6 0.0 copy-done.1
  42.6 1.1 %shard_map.116 = (f32[8,14,8,256]{3,2,1,0:T(8,128)S(1)}, f32[3,8,12,8,256]{4,3,2,1,0:T(8,128)}, f32[96,256]{1,0:T(8,128)S(1)}) custom-call(f32[27,8,256]{2,1,0:T(8,128)S(1)} %copy-done.1, f32[27,8,256]{2,1,0:T(8,128)S(1)} %collective-permute-done.3.refs_1_, f32[27,8,256]{2,1,0:T(8,128)S(1)} %collective-permute-done.4.refs_2_, ...), custom_call_target="tpu_custom_call", output_to_operand_aliasing={{1}: (4, {})} | custom-call | bytes 2654208 | tf_op jit(solution)/shard_map/pallas_call | solution.py:308
  43.8 0.0 copy-start.4
  43.8 0.0 copy-start.2
  43.8 0.0 copy-start.3
  43.8 0.7 %collective-permute-start.6 = (f32[8,14,8,256]{3,2,1,0:T(8,128)S(1)}, f32[8,14,8,256]{3,2,1,0:T(8,128)S(1)}, u32[]{:S(2)}, u32[]{:S(2)}) collective-permute-start(f32[8,14,8,256]{3,2,1,0:T(8,128)S(1)} %get-tuple-element.26.now_ref.own_ref), channel_id=1, source_target_pairs={{0,1},{1,0},{2,3},{3,2},{4,5},{5,4},{6,7},{7,6},{8,9},{9,8},{10,11... | collective-permute-start | bytes 2752520 | tf_op jit(solution)/shard_map/ppermute | solution.py:560
  44.4 0.0 copy-done.6
  44.4 0.0 copy-done.7
  44.4 0.0 copy-done.8
  44.5 0.1 fusion.7
  44.6 1.2 %collective-permute-start.7 = (f32[96,256]{1,0:T(8,128)S(1)}, f32[96,256]{1,0:T(8,128)S(1)}, u32[]{:S(2)}, u32[]{:S(2)}) collective-permute-start(f32[96,256]{1,0:T(8,128)S(1)} %get-tuple-element.27), channel_id=1, source_target_pairs={{0,2},{2,0},{1,3},{3,1},{4,6},{6,4},{5,7},{7,5},{8,10},{10,8},{9,1... | collective-permute-start | bytes 294920 | tf_op jit(solution)/shard_map/ppermute | solution.py:567
  45.8 0.0 copy-done.5
  45.8 0.4 fusion.2
  46.1 0.0 copy-done
  46.2 0.5 shard_map.117.own_rim
  46.6 2.3 %collective-permute-done.7.own_low.own_high = f32[96,256]{1,0:T(8,128)S(1)} collective-permute-done((f32[96,256]{1,0:T(8,128)S(1)}, f32[96,256]{1,0:T(8,128)S(1)}, u32[]{:S(2)}, u32[]{:S(2)}) %collective-permute-start.7) | collective-permute-done | bytes 98336 | tf_op jit(solution)/shard_map/ppermute | solution.py:567
  49.0 0.8 %collective-permute-start.8 = (f32[96,256]{1,0:T(8,128)S(1)}, f32[96,256]{1,0:T(8,128)S(1)}, u32[]{:S(2)}, u32[]{:S(2)}) collective-permute-start(f32[96,256]{1,0:T(8,128)S(1)} %collective-permute-done.7.own_low.own_high), channel_id=1, source_target_pairs={{0,1},{1,0},{2,3},{3,2},{4,5},{5,4},{6,7},{7,6},{8,9},{9,8},{10,11... | collective-permute-start | bytes 294920 | tf_op jit(solution)/shard_map/ppermute | solution.py:571
  49.8 0.0 copy-done.4
  49.8 0.1 multiply_reduce_fusion
  49.9 0.9 %collective-permute-done.8.other_low.other_high = f32[96,256]{1,0:T(8,128)S(1)} collective-permute-done((f32[96,256]{1,0:T(8,128)S(1)}, f32[96,256]{1,0:T(8,128)S(1)}, u32[]{:S(2)}, u32[]{:S(2)}) %collective-permute-start.8) | collective-permute-done | bytes 98336 | tf_op jit(solution)/shard_map/ppermute | solution.py:571
  50.7 0.0 collective-permute-done.6.other_ref
  50.7 0.0 copy-done.2
  50.7 0.0 copy-done.3
  50.7 4.9 %shard_map.118 = (f32[8,12,8,256]{3,2,1,0:T(8,128)}, f32[8,128]{1,0:T(8,128)S(1)}) custom-call(s32[16]{0:T(128)S(1)} %copy-done.2, s32[16]{0:T(128)S(1)} %copy-done.3, f32[8,14,8,256]{3,2,1,0:T(8,128)S(1)} %get-tuple-element.26.now_ref.own_ref, f32[8,14,8,256]{3,2,1,0:T(8,128)S(1)} %collective-permute-done.6.other_ref, ...), custom_call_target="tpu_custom_call" | custom-call | flops 528482304 | bytes 2752512 | tf_op jit(solution)/shard_map/pallas_call | solution.py:579
  55.6 0.0 collective-permute-done.2.refs_0_
  55.6 0.8 %shard_map.119.refs_2_ = f32[3,8,12,8,256]{4,3,2,1,0:T(8,128)} custom-call(f32[2,2,12,8,256]{4,3,2,1,0:T(8,128)S(1)} %collective-permute-done.2.refs_0_, f32[3,8,12,8,256]{4,3,2,1,0:T(8,128)} %get-tuple-element.25.refs_1_, f32[8,128]{1,0:T(8,128)S(1)} %get-tuple-element.30.refs_2_.refs_3_), custom_call_target="tpu_custom_call", output_to_operand_aliasing={{}: (1, {})} | custom-call | bytes 786432 | tf_op jit(solution)/shard_map/pallas_call | solution.py:242
  56.4 0.3 collective-permute-done.refs_0_
  56.7 2.8 %collective-permute-done.1.refs_1_ = f32[2,2,12,8,256]{4,3,2,1,0:T(8,128)S(1)} collective-permute-done((f32[2,2,12,8,256]{4,3,2,1,0:T(8,128)}, f32[2,2,12,8,256]{4,3,2,1,0:T(8,128)S(1)}, u32[]{:S(2)}, u32[]{:S(2)}) %collective-permute-start.1) | collective-permute-done | bytes 393248 | tf_op jit(solution)/shard_map/ppermute | solution.py:549
  59.5 0.9 %shard_map.120 = f32[3,8,12,8,256]{4,3,2,1,0:T(8,128)} custom-call(f32[2,2,12,8,256]{4,3,2,1,0:T(8,128)S(1)} %collective-permute-done.refs_0_, f32[2,2,12,8,256]{4,3,2,1,0:T(8,128)S(1)} %collective-permute-done.1.refs_1_, f32[3,8,12,8,256]{4,3,2,1,0:T(8,128)} %shard_map.119.refs_2_, ...), custom_call_target="tpu_custom_call", output_to_operand_aliasing={{}: (2, {})} | custom-call | bytes 1572864 | tf_op jit(solution)/shard_map/pallas_call | solution.py:242
  (2 shorter events, 0.0 us)
Async XLA Ops:
  3.0 39.6 %copy-start.1 = (f32[27,8,256]{2,1,0:T(8,128)S(1)}, f32[27,8,256]{2,1,0:T(8,128)}, u32[]{:S(2)}) copy-start(f32[27,8,256]{2,1,0:T(8,128)} %get-tuple-element.20.refs_0_) | copy-start | bytes 663556
  3.0 11.6 %collective-permute-start.3 = (f32[27,8,256]{2,1,0:T(8,128)}, f32[27,8,256]{2,1,0:T(8,128)S(1)}, u32[]{:S(2)}, u32[]{:S(2)}) collective-permute-start(f32[27,8,256]{2,1,0:T(8,128)} %get-tuple-element.21), channel_id=1, source_target_pairs={{0,4},{4,8},{8,12},{12,0},{1,5},{5,9},{9,13},{13,1},{2,6},{6,10},{... | collective-permute-start | bytes 663560 | tf_op jit(solution)/shard_map/ppermute | solution.py:549
  4.3 27.1 %collective-permute-start.4 = (f32[27,8,256]{2,1,0:T(8,128)}, f32[27,8,256]{2,1,0:T(8,128)S(1)}, u32[]{:S(2)}, u32[]{:S(2)}) collective-permute-start(f32[27,8,256]{2,1,0:T(8,128)} %get-tuple-element.22), channel_id=1, source_target_pairs={{0,8},{4,12},{8,0},{12,4},{1,9},{5,13},{9,1},{13,5},{2,10},{6,14},... | collective-permute-start | bytes 663560 | tf_op jit(solution)/shard_map/ppermute | solution.py:549
  5.4 37.2 %collective-permute-start.5 = (f32[27,8,256]{2,1,0:T(8,128)}, f32[27,8,256]{2,1,0:T(8,128)S(1)}, u32[]{:S(2)}, u32[]{:S(2)}) collective-permute-start(f32[27,8,256]{2,1,0:T(8,128)} %get-tuple-element.23), channel_id=1, source_target_pairs={{0,12},{4,0},{8,4},{12,8},{1,13},{5,1},{9,5},{13,9},{2,14},{6,2},{... | collective-permute-start | bytes 663560 | tf_op jit(solution)/shard_map/ppermute | solution.py:549
  10.3 34.1 %copy-start.6 = (f32[24,24]{1,0:T(8,128)S(1)}, f32[24,24]{1,0:T(8,128)}, u32[]{:S(2)}) copy-start(f32[24,24]{1,0:T(8,128)} %param.14) | copy-start | bytes 6916
  10.3 34.1 %copy-start.7 = (f32[24,24]{1,0:T(8,128)S(1)}, f32[24,24]{1,0:T(8,128)}, u32[]{:S(2)}) copy-start(f32[24,24]{1,0:T(8,128)} %param.15) | copy-start | bytes 6916
  10.3 34.1 %copy-start.8 = (f32[24,24]{1,0:T(8,128)S(1)}, f32[24,24]{1,0:T(8,128)}, u32[]{:S(2)}) copy-start(f32[24,24]{1,0:T(8,128)} %param.16) | copy-start | bytes 6916
  10.4 35.4 %copy-start.5 = (f32[24,896,1]{1,0,2:T(8,128)S(1)}, f32[24,896,1]{1,0,2:T(8,128)}, u32[]{:S(2)}) copy-start(f32[24,896,1]{1,0,2:T(8,128)} %constant.27) | copy-start | bytes 258052
  10.4 35.8 %copy-start = (bf16[256,2304]{1,0:T(8,128)(2,1)S(1)}, bf16[256,2304]{1,0:T(8,128)(2,1)}, u32[]{:S(2)}) copy-start(bf16[256,2304]{1,0:T(8,128)(2,1)} %constant.26.spread_ref) | copy-start | bytes 3538948
  10.4 45.2 %collective-permute-start.2 = (f32[2,2,12,8,256]{4,3,2,1,0:T(8,128)}, f32[2,2,12,8,256]{4,3,2,1,0:T(8,128)S(1)}, u32[]{:S(2)}, u32[]{:S(2)}) collective-permute-start(f32[2,2,12,8,256]{4,3,2,1,0:T(8,128)} %get-tuple-element.19), channel_id=1, source_target_pairs={{0,8},{4,12},{8,0},{12,4},{1,9},{5,13},{9,1},{13,5},{2,10},{6,14},... | collective-permute-start | bytes 1179656 | tf_op jit(solution)/shard_map/ppermute | solution.py:549
  13.4 43.3 %collective-permute-start = (f32[2,2,12,8,256]{4,3,2,1,0:T(8,128)}, f32[2,2,12,8,256]{4,3,2,1,0:T(8,128)S(1)}, u32[]{:S(2)}, u32[]{:S(2)}) collective-permute-start(f32[2,2,12,8,256]{4,3,2,1,0:T(8,128)} %get-tuple-element.17), channel_id=1, source_target_pairs={{0,4},{4,8},{8,12},{12,0},{1,5},{5,9},{9,13},{13,1},{2,6},{6,10},{... | collective-permute-start | bytes 1179656 | tf_op jit(solution)/shard_map/ppermute | solution.py:549
  14.6 44.9 %collective-permute-start.1 = (f32[2,2,12,8,256]{4,3,2,1,0:T(8,128)}, f32[2,2,12,8,256]{4,3,2,1,0:T(8,128)S(1)}, u32[]{:S(2)}, u32[]{:S(2)}) collective-permute-start(f32[2,2,12,8,256]{4,3,2,1,0:T(8,128)} %get-tuple-element.18), channel_id=1, source_target_pairs={{0,12},{4,0},{8,4},{12,8},{1,13},{5,1},{9,5},{13,9},{2,14},{6,2},{... | collective-permute-start | bytes 1179656 | tf_op jit(solution)/shard_map/ppermute | solution.py:549
  43.8 6.0 %copy-start.4 = (f32[3,8,896]{2,1,0:T(8,128)S(1)}, f32[3,8,896]{2,1,0:T(8,128)}, u32[]{:S(2)}) copy-start(f32[3,8,896]{2,1,0:T(8,128)} %constant.24.clone) | copy-start | bytes 258052
  43.8 7.0 %copy-start.2 = (s32[16]{0:T(128)S(1)}, s32[16]{0:T(128)}, u32[]{:S(2)}) copy-start(s32[16]{0:T(128)} %dest_ref.7) | copy-start | bytes 196
  43.8 7.0 %copy-start.3 = (s32[16]{0:T(128)S(1)}, s32[16]{0:T(128)}, u32[]{:S(2)}) copy-start(s32[16]{0:T(128)} %parent_ref.3) | copy-start | bytes 196
  43.8 6.9 %collective-permute-start.6 = (f32[8,14,8,256]{3,2,1,0:T(8,128)S(1)}, f32[8,14,8,256]{3,2,1,0:T(8,128)S(1)}, u32[]{:S(2)}, u32[]{:S(2)}) collective-permute-start(f32[8,14,8,256]{3,2,1,0:T(8,128)S(1)} %get-tuple-element.26.now_ref.own_ref), channel_id=1, source_target_pairs={{0,1},{1,0},{2,3},{3,2},{4,5},{5,4},{6,7},{7,6},{8,9},{9,8},{10,11... | collective-permute-start | bytes 2752520 | tf_op jit(solution)/shard_map/ppermute | solution.py:560
  44.6 4.4 %collective-permute-start.7 = (f32[96,256]{1,0:T(8,128)S(1)}, f32[96,256]{1,0:T(8,128)S(1)}, u32[]{:S(2)}, u32[]{:S(2)}) collective-permute-start(f32[96,256]{1,0:T(8,128)S(1)} %get-tuple-element.27), channel_id=1, source_target_pairs={{0,2},{2,0},{1,3},{3,1},{4,6},{6,4},{5,7},{7,5},{8,10},{10,8},{9,1... | collective-permute-start | bytes 294920 | tf_op jit(solution)/shard_map/ppermute | solution.py:567
  49.0 1.8 %collective-permute-start.8 = (f32[96,256]{1,0:T(8,128)S(1)}, f32[96,256]{1,0:T(8,128)S(1)}, u32[]{:S(2)}, u32[]{:S(2)}) collective-permute-start(f32[96,256]{1,0:T(8,128)S(1)} %collective-permute-done.7.own_low.own_high), channel_id=1, source_target_pairs={{0,1},{1,0},{2,3},{3,2},{4,5},{5,4},{6,7},{7,6},{8,9},{9,8},{10,11... | collective-permute-start | bytes 294920 | tf_op jit(solution)/shard_map/ppermute | solution.py:571

commit v17 on v16

--- a/solution.py
+++ b/solution.py
@@ -548,12 +548,12 @@
     def send(piece, turn):
         return lax.ppermute(piece, "box", [(s, (s + turn) % box_count) for s in range(box_count)])
 
-    near = pack_later((1, box_count - 1), boxes, move_dest, box_count)
-    near = [send(near[0], 1), send(near[1], box_count - 1)]
+    last = box_count - 1
     first = pack_first(boxes, coarse, move_dest, parent, edge, box_count)
     arrived = [first[0]] + [send(first[turn], turn) for turn in range(1, box_count)]
-    moved, *middle = pack_later((0,) + tuple(range(2, box_count - 1)), boxes, move_dest, box_count)
-    middle = [send(piece, n + 2) for n, piece in enumerate(middle)]
+    moved, *later = pack_later((0, 1), boxes, move_dest, box_count)
+    later += pack_later((last,) + tuple(range(2, last)), boxes, move_dest, box_count)
+    next_one, last_one, *middle = [send(piece, turn) for piece, turn in zip(later, [1, last, *range(2, last)])]
     now, moved, *facing = arrive(arrived, moved, slabs)
 
     swap = [(0, 1), (1, 0)]
@@ -600,8 +600,8 @@
             flops=3 * slots * weight.size * cross, bytes_accessed=12 * now.size, transcendentals=0
         ),
     )(move_dest, parent, now, now_other, low[0], low[1], high[0], high[1], rim, spread, weight)
-    moved = settle(tuple(range(2, box_count - 1)), middle, moved, token)
-    return settle((1, box_count - 1), near, moved, token), slope
+    moved = settle((1, last), [next_one, last_one], moved, token)
+    return settle(tuple(range(2, last)), middle, moved, token), slope
 
 
 def solution(mesh):

time: 60.6 us -> 62.7 us (1.035)
  the two profiles are of different devices: /device:TPU:9 before, /device:TPU:0 now
where the time goes in v17:
time: 62.7 us; the launch traced here: 62.5 us
  waiting for transfers between devices  26.9 us (43%)
  starting transfers between devices  18.1 us (29%)
  Pallas kernels  16 us (26%)
  between operations  0.85 us (1%)
    ppermute x6, waiting for transfers between devices, send(): lax.ppermute(piece, 'box', [(s, (s + turn) % box_count) for s in range(bo...  22.9 us
    ppermute x6, starting transfers between devices, send(): lax.ppermute(piece, 'box', [(s, (s + turn) % box_count) for s in range(bo...  16.5 us
    pallas_call x2, Pallas kernels, pack_later(): pl.pallas_call(functools.partial(later_kernel, turns, per_device, box_cou...  5.53 us
    pallas_call x1, Pallas kernels, body(): pl.pallas_call(functools.partial(slope_kernel, edge, planes, fields, coar...  4.87 us
    ppermute x1, waiting for transfers between devices, shifted(): return lax.ppermute(values, 'slab', swap if slabs == 2 else pairs)  2.83 us
    pallas_call x1, Pallas kernels, pack_first(): pl.pallas_call(functools.partial(first_kernel, per_device, box_count, edg...  2.33 us
    pallas_call x2, Pallas kernels, settle(): pl.pallas_call(functools.partial(settle_kernel, turns), out_shape=jax.Sha...  1.64 us
    ppermute x1, starting transfers between devices, shifted(): return lax.ppermute(values, 'slab', swap if slabs == 2 else pairs)  1.5 us
  transfers between devices with their start and end apart: 9, of which 4 were waited for; matrix products, arithmetic and copies ran while one was open for 1% of the time, Pallas kernels for 21%

profile of v17, /device:TPU:0, one launch (start us, length us, event | category | flops | bytes accessed | tf_op | source)
XLA Modules:
  0.0 62.5 jit_solution(7452806761812936193)
XLA Ops:
  0.6 2.3 %shard_map.115 = (f32[27,8,256]{2,1,0:T(8,128)}, f32[27,8,256]{2,1,0:T(8,128)}, f32[27,8,256]{2,1,0:T(8,128)}, f32[27,8,256]{2,1,0:T(8,128)}) custom-call(s32[16]{0:T(128)} %dest_ref.7, s32[16]{0:T(128)} %parent_ref.3, f32[3,4,12,8,256]{4,3,2,1,0:T(8,128)} %boxes_ref.5, f32[12,8,1000]{2,1,0:T(8,128)} %bitcast.11), custom_call_target="tpu_custom_call" | custom-call | flops 147456000 | bytes 2743296 | tf_op jit(solution)/shard_map/pallas_call | solution.py:132
  3.0 0.0 copy-start.1
  3.0 3.1 %collective-permute-start.3 = (f32[27,8,256]{2,1,0:T(8,128)}, f32[27,8,256]{2,1,0:T(8,128)S(1)}, u32[]{:S(2)}, u32[]{:S(2)}) collective-permute-start(f32[27,8,256]{2,1,0:T(8,128)} %get-tuple-element.21), channel_id=1, source_target_pairs={{0,4},{4,8},{8,12},{12,0},{1,5},{5,9},{9,13},{13,1},{2,6},{6,10},{... | collective-permute-start | bytes 663560 | tf_op jit(solution)/shard_map/ppermute | solution.py:549
  6.1 2.6 %collective-permute-start.4 = (f32[27,8,256]{2,1,0:T(8,128)}, f32[27,8,256]{2,1,0:T(8,128)S(1)}, u32[]{:S(2)}, u32[]{:S(2)}) collective-permute-start(f32[27,8,256]{2,1,0:T(8,128)} %get-tuple-element.22), channel_id=1, source_target_pairs={{0,8},{4,12},{8,0},{12,4},{1,9},{5,13},{9,1},{13,5},{2,10},{6,14},... | collective-permute-start | bytes 663560 | tf_op jit(solution)/shard_map/ppermute | solution.py:549
  8.6 1.3 %collective-permute-start.5 = (f32[27,8,256]{2,1,0:T(8,128)}, f32[27,8,256]{2,1,0:T(8,128)S(1)}, u32[]{:S(2)}, u32[]{:S(2)}) collective-permute-start(f32[27,8,256]{2,1,0:T(8,128)} %get-tuple-element.23), channel_id=1, source_target_pairs={{0,12},{4,0},{8,4},{12,8},{1,13},{5,1},{9,5},{13,9},{2,14},{6,2},{... | collective-permute-start | bytes 663560 | tf_op jit(solution)/shard_map/ppermute | solution.py:549
  10.0 3.7 %shard_map.114 = (f32[3,8,12,8,256]{4,3,2,1,0:T(8,128)}, f32[2,2,12,8,256]{4,3,2,1,0:T(8,128)}) custom-call(s32[16]{0:T(128)} %dest_ref.7, f32[3,4,12,8,256]{4,3,2,1,0:T(8,128)} %boxes_ref.5), custom_call_target="tpu_custom_call" | custom-call | bytes 2359296 | tf_op jit(solution)/shard_map/pallas_call | solution.py:206
  13.7 0.0 copy-start.6
  13.7 0.0 copy-start.7
  13.7 0.0 copy-start.8
  13.7 0.0 copy-start.5
  13.7 0.0 copy-start
  13.8 0.7 %collective-permute-start.1 = (f32[2,2,12,8,256]{4,3,2,1,0:T(8,128)}, f32[2,2,12,8,256]{4,3,2,1,0:T(8,128)S(1)}, u32[]{:S(2)}, u32[]{:S(2)}) collective-permute-start(f32[2,2,12,8,256]{4,3,2,1,0:T(8,128)} %get-tuple-element.18), channel_id=1, source_target_pairs={{0,4},{4,8},{8,12},{12,0},{1,5},{5,9},{9,13},{13,1},{2,6},{6,10},{... | collective-permute-start | bytes 1179656 | tf_op jit(solution)/shard_map/ppermute | solution.py:549
  14.5 1.8 %shard_map.113 = (f32[2,2,12,8,256]{4,3,2,1,0:T(8,128)}, f32[2,2,12,8,256]{4,3,2,1,0:T(8,128)}) custom-call(s32[16]{0:T(128)} %dest_ref.7, f32[3,4,12,8,256]{4,3,2,1,0:T(8,128)} %boxes_ref.5), custom_call_target="tpu_custom_call" | custom-call | bytes 2359296 | tf_op jit(solution)/shard_map/pallas_call | solution.py:206
  16.3 4.2 %collective-permute-start.2 = (f32[2,2,12,8,256]{4,3,2,1,0:T(8,128)}, f32[2,2,12,8,256]{4,3,2,1,0:T(8,128)S(1)}, u32[]{:S(2)}, u32[]{:S(2)}) collective-permute-start(f32[2,2,12,8,256]{4,3,2,1,0:T(8,128)} %get-tuple-element.19), channel_id=1, source_target_pairs={{0,12},{4,0},{8,4},{12,8},{1,13},{5,1},{9,5},{13,9},{2,14},{6,2},{... | collective-permute-start | bytes 1179656 | tf_op jit(solution)/shard_map/ppermute | solution.py:549
  20.5 0.0 collective-permute-done.3.refs_1_
  20.5 4.6 %collective-permute-start = (f32[2,2,12,8,256]{4,3,2,1,0:T(8,128)}, f32[2,2,12,8,256]{4,3,2,1,0:T(8,128)S(1)}, u32[]{:S(2)}, u32[]{:S(2)}) collective-permute-start(f32[2,2,12,8,256]{4,3,2,1,0:T(8,128)} %get-tuple-element.17), channel_id=1, source_target_pairs={{0,8},{4,12},{8,0},{12,4},{1,9},{5,13},{9,1},{13,5},{2,10},{6,14},... | collective-permute-start | bytes 1179656 | tf_op jit(solution)/shard_map/ppermute | solution.py:549
  25.1 0.0 collective-permute-done.4.refs_2_
  25.1 0.0 collective-permute-done.5.refs_3_
  25.1 0.0 copy-done.1
  25.1 1.2 %shard_map.116 = (f32[8,14,8,256]{3,2,1,0:T(8,128)S(1)}, f32[3,8,12,8,256]{4,3,2,1,0:T(8,128)}, f32[96,256]{1,0:T(8,128)S(1)}) custom-call(f32[27,8,256]{2,1,0:T(8,128)S(1)} %copy-done.1, f32[27,8,256]{2,1,0:T(8,128)S(1)} %collective-permute-done.3.refs_1_, f32[27,8,256]{2,1,0:T(8,128)S(1)} %collective-permute-done.4.refs_2_, ...), custom_call_target="tpu_custom_call", output_to_operand_aliasing={{1}: (4, {})} | custom-call | bytes 2654208 | tf_op jit(solution)/shard_map/pallas_call | solution.py:308
  26.3 0.0 copy-start.4
  26.3 0.0 copy-start.2
  26.3 0.0 copy-start.3
  26.4 0.1 collective-permute-start.6
  26.4 0.0 copy-done.6
  26.4 0.0 copy-done.7
  26.5 0.0 copy-done.8
  26.5 0.1 fusion.7
  26.6 1.5 %collective-permute-start.7 = (f32[96,256]{1,0:T(8,128)S(1)}, f32[96,256]{1,0:T(8,128)S(1)}, u32[]{:S(2)}, u32[]{:S(2)}) collective-permute-start(f32[96,256]{1,0:T(8,128)S(1)} %get-tuple-element.27), channel_id=1, source_target_pairs={{0,2},{2,0},{1,3},{3,1},{4,6},{6,4},{5,7},{7,5},{8,10},{10,8},{9,1... | collective-permute-start | bytes 294920 | tf_op jit(solution)/shard_map/ppermute | solution.py:567
  28.1 0.0 copy-done.5
  28.1 0.3 fusion.2
  28.4 0.0 copy-done
  28.4 0.5 shard_map.117.own_rim
  28.9 2.8 %collective-permute-done.7.own_low.own_high = f32[96,256]{1,0:T(8,128)S(1)} collective-permute-done((f32[96,256]{1,0:T(8,128)S(1)}, f32[96,256]{1,0:T(8,128)S(1)}, u32[]{:S(2)}, u32[]{:S(2)}) %collective-permute-start.7) | collective-permute-done | bytes 98336 | tf_op jit(solution)/shard_map/ppermute | solution.py:567
  31.8 0.0 collective-permute-start.8
  31.8 0.0 copy-done.4
  31.8 0.1 multiply_reduce_fusion
  31.9 1.2 %collective-permute-done.8.other_low.other_high = f32[96,256]{1,0:T(8,128)S(1)} collective-permute-done((f32[96,256]{1,0:T(8,128)S(1)}, f32[96,256]{1,0:T(8,128)S(1)}, u32[]{:S(2)}, u32[]{:S(2)}) %collective-permute-start.8) | collective-permute-done | bytes 98336 | tf_op jit(solution)/shard_map/ppermute | solution.py:571
  33.1 0.0 collective-permute-done.6.other_ref
  33.1 0.0 copy-done.2
  33.1 0.0 copy-done.3
  33.1 4.9 %shard_map.118 = (f32[8,12,8,256]{3,2,1,0:T(8,128)}, f32[8,128]{1,0:T(8,128)S(1)}) custom-call(s32[16]{0:T(128)S(1)} %copy-done.2, s32[16]{0:T(128)S(1)} %copy-done.3, f32[8,14,8,256]{3,2,1,0:T(8,128)S(1)} %get-tuple-element.26.now_ref.own_ref, f32[8,14,8,256]{3,2,1,0:T(8,128)S(1)} %collective-permute-done.6.other_ref, ...), custom_call_target="tpu_custom_call" | custom-call | flops 528482304 | bytes 2752512 | tf_op jit(solution)/shard_map/pallas_call | solution.py:579
  38.0 0.0 collective-permute-done.1.refs_0_
  38.0 2.1 %collective-permute-done.2.refs_1_ = f32[2,2,12,8,256]{4,3,2,1,0:T(8,128)S(1)} collective-permute-done((f32[2,2,12,8,256]{4,3,2,1,0:T(8,128)}, f32[2,2,12,8,256]{4,3,2,1,0:T(8,128)S(1)}, u32[]{:S(2)}, u32[]{:S(2)}) %collective-permute-start.2) | collective-permute-done | bytes 393248 | tf_op jit(solution)/shard_map/ppermute | solution.py:549
  40.0 0.9 %shard_map.119.refs_1_ = f32[3,8,12,8,256]{4,3,2,1,0:T(8,128)} custom-call(f32[2,2,12,8,256]{4,3,2,1,0:T(8,128)S(1)} %collective-permute-done.1.refs_0_, f32[2,2,12,8,256]{4,3,2,1,0:T(8,128)S(1)} %collective-permute-done.2.refs_1_, f32[3,8,12,8,256]{4,3,2,1,0:T(8,128)} %get-tuple-element.25.refs_2_, ...), custom_call_target="tpu_custom_call", output_to_operand_aliasing={{}: (2, {})} | custom-call | bytes 1572864 | tf_op jit(solution)/shard_map/pallas_call | solution.py:242
  40.9 20.8 %collective-permute-done.refs_0_ = f32[2,2,12,8,256]{4,3,2,1,0:T(8,128)S(1)} collective-permute-done((f32[2,2,12,8,256]{4,3,2,1,0:T(8,128)}, f32[2,2,12,8,256]{4,3,2,1,0:T(8,128)S(1)}, u32[]{:S(2)}, u32[]{:S(2)}) %collective-permute-start) | collective-permute-done | bytes 393248 | tf_op jit(solution)/shard_map/ppermute | solution.py:549
  61.7 0.8 %shard_map.120 = f32[3,8,12,8,256]{4,3,2,1,0:T(8,128)} custom-call(f32[2,2,12,8,256]{4,3,2,1,0:T(8,128)S(1)} %collective-permute-done.refs_0_, f32[3,8,12,8,256]{4,3,2,1,0:T(8,128)} %shard_map.119.refs_1_, f32[8,128]{1,0:T(8,128)S(1)} %get-tuple-element.30.refs_3_.refs_2_), custom_call_target="tpu_custom_call", output_to_operand_aliasing={{}: (1, {})} | custom-call | bytes 786432 | tf_op jit(solution)/shard_map/pallas_call | solution.py:242
  (2 shorter events, 0.0 us)
Async XLA Ops:
  3.0 22.2 %copy-start.1 = (f32[27,8,256]{2,1,0:T(8,128)S(1)}, f32[27,8,256]{2,1,0:T(8,128)}, u32[]{:S(2)}) copy-start(f32[27,8,256]{2,1,0:T(8,128)} %get-tuple-element.20.refs_0_) | copy-start | bytes 663556
  3.0 17.5 %collective-permute-start.3 = (f32[27,8,256]{2,1,0:T(8,128)}, f32[27,8,256]{2,1,0:T(8,128)S(1)}, u32[]{:S(2)}, u32[]{:S(2)}) collective-permute-start(f32[27,8,256]{2,1,0:T(8,128)} %get-tuple-element.21), channel_id=1, source_target_pairs={{0,4},{4,8},{8,12},{12,0},{1,5},{5,9},{9,13},{13,1},{2,6},{6,10},{... | collective-permute-start | bytes 663560 | tf_op jit(solution)/shard_map/ppermute | solution.py:549
  6.1 19.1 %collective-permute-start.4 = (f32[27,8,256]{2,1,0:T(8,128)}, f32[27,8,256]{2,1,0:T(8,128)S(1)}, u32[]{:S(2)}, u32[]{:S(2)}) collective-permute-start(f32[27,8,256]{2,1,0:T(8,128)} %get-tuple-element.22), channel_id=1, source_target_pairs={{0,8},{4,12},{8,0},{12,4},{1,9},{5,13},{9,1},{13,5},{2,10},{6,14},... | collective-permute-start | bytes 663560 | tf_op jit(solution)/shard_map/ppermute | solution.py:549
  8.6 16.5 %collective-permute-start.5 = (f32[27,8,256]{2,1,0:T(8,128)}, f32[27,8,256]{2,1,0:T(8,128)S(1)}, u32[]{:S(2)}, u32[]{:S(2)}) collective-permute-start(f32[27,8,256]{2,1,0:T(8,128)} %get-tuple-element.23), channel_id=1, source_target_pairs={{0,12},{4,0},{8,4},{12,8},{1,13},{5,1},{9,5},{13,9},{2,14},{6,2},{... | collective-permute-start | bytes 663560 | tf_op jit(solution)/shard_map/ppermute | solution.py:549
  13.7 12.7 %copy-start.6 = (f32[24,24]{1,0:T(8,128)S(1)}, f32[24,24]{1,0:T(8,128)}, u32[]{:S(2)}) copy-start(f32[24,24]{1,0:T(8,128)} %param.14) | copy-start | bytes 6916
  13.7 12.7 %copy-start.7 = (f32[24,24]{1,0:T(8,128)S(1)}, f32[24,24]{1,0:T(8,128)}, u32[]{:S(2)}) copy-start(f32[24,24]{1,0:T(8,128)} %param.15) | copy-start | bytes 6916
  13.7 12.7 %copy-start.8 = (f32[24,24]{1,0:T(8,128)S(1)}, f32[24,24]{1,0:T(8,128)}, u32[]{:S(2)}) copy-start(f32[24,24]{1,0:T(8,128)} %param.16) | copy-start | bytes 6916
  13.7 14.3 %copy-start.5 = (f32[24,896,1]{1,0,2:T(8,128)S(1)}, f32[24,896,1]{1,0,2:T(8,128)}, u32[]{:S(2)}) copy-start(f32[24,896,1]{1,0,2:T(8,128)} %constant.27) | copy-start | bytes 258052
  13.7 14.7 %copy-start = (bf16[256,2304]{1,0:T(8,128)(2,1)S(1)}, bf16[256,2304]{1,0:T(8,128)(2,1)}, u32[]{:S(2)}) copy-start(bf16[256,2304]{1,0:T(8,128)(2,1)} %constant.26.spread_ref) | copy-start | bytes 3538948
  13.8 24.2 %collective-permute-start.1 = (f32[2,2,12,8,256]{4,3,2,1,0:T(8,128)}, f32[2,2,12,8,256]{4,3,2,1,0:T(8,128)S(1)}, u32[]{:S(2)}, u32[]{:S(2)}) collective-permute-start(f32[2,2,12,8,256]{4,3,2,1,0:T(8,128)} %get-tuple-element.18), channel_id=1, source_target_pairs={{0,4},{4,8},{8,12},{12,0},{1,5},{5,9},{9,13},{13,1},{2,6},{6,10},{... | collective-permute-start | bytes 1179656 | tf_op jit(solution)/shard_map/ppermute | solution.py:549
  16.3 23.7 %collective-permute-start.2 = (f32[2,2,12,8,256]{4,3,2,1,0:T(8,128)}, f32[2,2,12,8,256]{4,3,2,1,0:T(8,128)S(1)}, u32[]{:S(2)}, u32[]{:S(2)}) collective-permute-start(f32[2,2,12,8,256]{4,3,2,1,0:T(8,128)} %get-tuple-element.19), channel_id=1, source_target_pairs={{0,12},{4,0},{8,4},{12,8},{1,13},{5,1},{9,5},{13,9},{2,14},{6,2},{... | collective-permute-start | bytes 1179656 | tf_op jit(solution)/shard_map/ppermute | solution.py:549
  20.5 41.2 %collective-permute-start = (f32[2,2,12,8,256]{4,3,2,1,0:T(8,128)}, f32[2,2,12,8,256]{4,3,2,1,0:T(8,128)S(1)}, u32[]{:S(2)}, u32[]{:S(2)}) collective-permute-start(f32[2,2,12,8,256]{4,3,2,1,0:T(8,128)} %get-tuple-element.17), channel_id=1, source_target_pairs={{0,8},{4,12},{8,0},{12,4},{1,9},{5,13},{9,1},{13,5},{2,10},{6,14},... | collective-permute-start | bytes 1179656 | tf_op jit(solution)/shard_map/ppermute | solution.py:549
  26.3 5.4 %copy-start.4 = (f32[3,8,896]{2,1,0:T(8,128)S(1)}, f32[3,8,896]{2,1,0:T(8,128)}, u32[]{:S(2)}) copy-start(f32[3,8,896]{2,1,0:T(8,128)} %constant.24.clone) | copy-start | bytes 258052
  26.3 6.7 %copy-start.2 = (s32[16]{0:T(128)S(1)}, s32[16]{0:T(128)}, u32[]{:S(2)}) copy-start(s32[16]{0:T(128)} %dest_ref.7) | copy-start | bytes 196
  26.3 6.7 %copy-start.3 = (s32[16]{0:T(128)S(1)}, s32[16]{0:T(128)}, u32[]{:S(2)}) copy-start(s32[16]{0:T(128)} %parent_ref.3) | copy-start | bytes 196
  26.4 6.7 %collective-permute-start.6 = (f32[8,14,8,256]{3,2,1,0:T(8,128)S(1)}, f32[8,14,8,256]{3,2,1,0:T(8,128)S(1)}, u32[]{:S(2)}, u32[]{:S(2)}) collective-permute-start(f32[8,14,8,256]{3,2,1,0:T(8,128)S(1)} %get-tuple-element.26.now_ref.own_ref), channel_id=1, source_target_pairs={{0,1},{1,0},{2,3},{3,2},{4,5},{5,4},{6,7},{7,6},{8,9},{9,8},{10,11... | collective-permute-start | bytes 2752520 | tf_op jit(solution)/shard_map/ppermute | solution.py:560
  26.6 5.2 %collective-permute-start.7 = (f32[96,256]{1,0:T(8,128)S(1)}, f32[96,256]{1,0:T(8,128)S(1)}, u32[]{:S(2)}, u32[]{:S(2)}) collective-permute-start(f32[96,256]{1,0:T(8,128)S(1)} %get-tuple-element.27), channel_id=1, source_target_pairs={{0,2},{2,0},{1,3},{3,1},{4,6},{6,4},{5,7},{7,5},{8,10},{10,8},{9,1... | collective-permute-start | bytes 294920 | tf_op jit(solution)/shard_map/ppermute | solution.py:567
  31.8 1.3 %collective-permute-start.8 = (f32[96,256]{1,0:T(8,128)S(1)}, f32[96,256]{1,0:T(8,128)S(1)}, u32[]{:S(2)}, u32[]{:S(2)}) collective-permute-start(f32[96,256]{1,0:T(8,128)S(1)} %collective-permute-done.7.own_low.own_high), channel_id=1, source_target_pairs={{0,1},{1,0},{2,3},{3,2},{4,5},{5,4},{6,7},{7,6},{8,9},{9,8},{10,11... | collective-permute-start | bytes 294920 | tf_op jit(solution)/shard_map/ppermute | solution.py:571

commit v18 on v17

--- a/solution.py
+++ b/solution.py
@@ -548,12 +548,11 @@
     def send(piece, turn):
         return lax.ppermute(piece, "box", [(s, (s + turn) % box_count) for s in range(box_count)])
 
-    last = box_count - 1
     first = pack_first(boxes, coarse, move_dest, parent, edge, box_count)
     arrived = [first[0]] + [send(first[turn], turn) for turn in range(1, box_count)]
     moved, *later = pack_later((0, 1), boxes, move_dest, box_count)
-    later += pack_later((last,) + tuple(range(2, last)), boxes, move_dest, box_count)
-    next_one, last_one, *middle = [send(piece, turn) for piece, turn in zip(later, [1, last, *range(2, last)])]
+    later += pack_later(tuple(range(2, box_count)), boxes, move_dest, box_count)
+    next_one, *middle, last_one = [send(piece, n + 1) for n, piece in enumerate(later)]
     now, moved, *facing = arrive(arrived, moved, slabs)
 
     swap = [(0, 1), (1, 0)]
@@ -600,8 +599,8 @@
             flops=3 * slots * weight.size * cross, bytes_accessed=12 * now.size, transcendentals=0
         ),
     )(move_dest, parent, now, now_other, low[0], low[1], high[0], high[1], rim, spread, weight)
-    moved = settle((1, last), [next_one, last_one], moved, token)
-    return settle(tuple(range(2, last)), middle, moved, token), slope
+    moved = settle(tuple(range(2, box_count - 1)), middle, moved, token)
+    return settle((1, box_count - 1), [next_one, last_one], moved, token), slope
 
 
 def solution(mesh):

time: 62.7 us -> 60.6 us (0.967)
  the two profiles are of different devices: /device:TPU:0 before, /device:TPU:9 now
where the time goes in v18:
time: 60.6 us; the launch traced here: 60.3 us
  waiting for transfers between devices  31.2 us (51%)
  Pallas kernels  19.4 us (32%)
  starting transfers between devices  8.35 us (14%)
  between operations  0.82 us (1%)
    ppermute x6, waiting for transfers between devices, send(): lax.ppermute(piece, 'box', [(s, (s + turn) % box_count) for s in range(bo...  28 us
    pallas_call x1, Pallas kernels, body(): pl.pallas_call(functools.partial(slope_kernel, edge, planes, fields, coar...  7.37 us
    pallas_call x2, Pallas kernels, pack_later(): pl.pallas_call(functools.partial(later_kernel, turns, per_device, box_cou...  6.45 us
    ppermute x6, starting transfers between devices, send(): lax.ppermute(piece, 'box', [(s, (s + turn) % box_count) for s in range(bo...  5.65 us
    pallas_call x1, Pallas kernels, pack_first(): pl.pallas_call(functools.partial(first_kernel, per_device, box_count, edg...  2.33 us
    ppermute x1, waiting for transfers between devices, shifted(): return lax.ppermute(values, 'slab', swap if slabs == 2 else pairs)  2.31 us
    pallas_call x2, Pallas kernels, settle(): pl.pallas_call(functools.partial(settle_kernel, turns), out_shape=jax.Sha...  1.66 us
    ppermute x1, starting transfers between devices, shifted(): return lax.ppermute(values, 'slab', swap if slabs == 2 else pairs)  1.22 us
  transfers between devices with their start and end apart: 9, of which 5 were waited for; matrix products, arithmetic and copies ran while one was open for 1% of the time, Pallas kernels for 27%

profile of v18, /device:TPU:9, one launch (start us, length us, event | category | flops | bytes accessed | tf_op | source)
XLA Modules:
  0.0 60.3 jit_solution(7944432730256633742)
XLA Ops:
  0.6 2.3 %shard_map.115 = (f32[27,8,256]{2,1,0:T(8,128)}, f32[27,8,256]{2,1,0:T(8,128)}, f32[27,8,256]{2,1,0:T(8,128)}, f32[27,8,256]{2,1,0:T(8,128)}) custom-call(s32[16]{0:T(128)} %dest_ref.7, s32[16]{0:T(128)} %parent_ref.3, f32[3,4,12,8,256]{4,3,2,1,0:T(8,128)} %boxes_ref.5, f32[12,8,1000]{2,1,0:T(8,128)} %bitcast.11), custom_call_target="tpu_custom_call" | custom-call | flops 147456000 | bytes 2743296 | tf_op jit(solution)/shard_map/pallas_call | solution.py:132
  3.0 0.0 copy-start.1
  3.0 1.3 %collective-permute-start.3 = (f32[27,8,256]{2,1,0:T(8,128)}, f32[27,8,256]{2,1,0:T(8,128)S(1)}, u32[]{:S(2)}, u32[]{:S(2)}) collective-permute-start(f32[27,8,256]{2,1,0:T(8,128)} %get-tuple-element.21), channel_id=1, source_target_pairs={{0,4},{4,8},{8,12},{12,0},{1,5},{5,9},{9,13},{13,1},{2,6},{6,10},{... | collective-permute-start | bytes 663560 | tf_op jit(solution)/shard_map/ppermute | solution.py:549
  4.3 1.1 %collective-permute-start.4 = (f32[27,8,256]{2,1,0:T(8,128)}, f32[27,8,256]{2,1,0:T(8,128)S(1)}, u32[]{:S(2)}, u32[]{:S(2)}) collective-permute-start(f32[27,8,256]{2,1,0:T(8,128)} %get-tuple-element.22), channel_id=1, source_target_pairs={{0,8},{4,12},{8,0},{12,4},{1,9},{5,13},{9,1},{13,5},{2,10},{6,14},... | collective-permute-start | bytes 663560 | tf_op jit(solution)/shard_map/ppermute | solution.py:549
  5.4 1.4 %collective-permute-start.5 = (f32[27,8,256]{2,1,0:T(8,128)}, f32[27,8,256]{2,1,0:T(8,128)S(1)}, u32[]{:S(2)}, u32[]{:S(2)}) collective-permute-start(f32[27,8,256]{2,1,0:T(8,128)} %get-tuple-element.23), channel_id=1, source_target_pairs={{0,12},{4,0},{8,4},{12,8},{1,13},{5,1},{9,5},{13,9},{2,14},{6,2},{... | collective-permute-start | bytes 663560 | tf_op jit(solution)/shard_map/ppermute | solution.py:549
  6.8 2.8 %shard_map.114 = (f32[2,2,12,8,256]{4,3,2,1,0:T(8,128)}, f32[2,2,12,8,256]{4,3,2,1,0:T(8,128)}) custom-call(s32[16]{0:T(128)} %dest_ref.7, f32[3,4,12,8,256]{4,3,2,1,0:T(8,128)} %boxes_ref.5), custom_call_target="tpu_custom_call" | custom-call | bytes 2359296 | tf_op jit(solution)/shard_map/pallas_call | solution.py:206
  9.6 0.0 copy-start.6
  9.6 0.0 copy-start.7
  9.6 0.0 copy-start.8
  9.6 0.0 copy-start.5
  9.6 0.0 copy-start
  9.6 0.3 collective-permute-start.2
  9.9 3.7 %shard_map.113 = (f32[3,8,12,8,256]{4,3,2,1,0:T(8,128)}, f32[2,2,12,8,256]{4,3,2,1,0:T(8,128)}) custom-call(s32[16]{0:T(128)} %dest_ref.7, f32[3,4,12,8,256]{4,3,2,1,0:T(8,128)} %boxes_ref.5), custom_call_target="tpu_custom_call" | custom-call | bytes 2359296 | tf_op jit(solution)/shard_map/pallas_call | solution.py:206
  13.6 0.9 %collective-permute-start = (f32[2,2,12,8,256]{4,3,2,1,0:T(8,128)}, f32[2,2,12,8,256]{4,3,2,1,0:T(8,128)S(1)}, u32[]{:S(2)}, u32[]{:S(2)}) collective-permute-start(f32[2,2,12,8,256]{4,3,2,1,0:T(8,128)} %get-tuple-element.17), channel_id=1, source_target_pairs={{0,4},{4,8},{8,12},{12,0},{1,5},{5,9},{9,13},{13,1},{2,6},{6,10},{... | collective-permute-start | bytes 1179656 | tf_op jit(solution)/shard_map/ppermute | solution.py:549
  14.5 0.0 collective-permute-done.3.refs_1_
  14.6 0.6 %collective-permute-start.1 = (f32[2,2,12,8,256]{4,3,2,1,0:T(8,128)}, f32[2,2,12,8,256]{4,3,2,1,0:T(8,128)S(1)}, u32[]{:S(2)}, u32[]{:S(2)}) collective-permute-start(f32[2,2,12,8,256]{4,3,2,1,0:T(8,128)} %get-tuple-element.18), channel_id=1, source_target_pairs={{0,12},{4,0},{8,4},{12,8},{1,13},{5,1},{9,5},{13,9},{2,14},{6,2},{... | collective-permute-start | bytes 1179656 | tf_op jit(solution)/shard_map/ppermute | solution.py:549
  15.2 16.3 %collective-permute-done.4.refs_2_ = f32[27,8,256]{2,1,0:T(8,128)S(1)} collective-permute-done((f32[27,8,256]{2,1,0:T(8,128)}, f32[27,8,256]{2,1,0:T(8,128)S(1)}, u32[]{:S(2)}, u32[]{:S(2)}) %collective-permute-start.4) | collective-permute-done | bytes 221216 | tf_op jit(solution)/shard_map/ppermute | solution.py:549
  31.4 11.2 %collective-permute-done.5.refs_3_ = f32[27,8,256]{2,1,0:T(8,128)S(1)} collective-permute-done((f32[27,8,256]{2,1,0:T(8,128)}, f32[27,8,256]{2,1,0:T(8,128)S(1)}, u32[]{:S(2)}, u32[]{:S(2)}) %collective-permute-start.5) | collective-permute-done | bytes 221216 | tf_op jit(solution)/shard_map/ppermute | solution.py:549
  42.6 0.0 copy-done.1
  42.6 1.1 %shard_map.116 = (f32[8,14,8,256]{3,2,1,0:T(8,128)S(1)}, f32[3,8,12,8,256]{4,3,2,1,0:T(8,128)}, f32[96,256]{1,0:T(8,128)S(1)}) custom-call(f32[27,8,256]{2,1,0:T(8,128)S(1)} %copy-done.1, f32[27,8,256]{2,1,0:T(8,128)S(1)} %collective-permute-done.3.refs_1_, f32[27,8,256]{2,1,0:T(8,128)S(1)} %collective-permute-done.4.refs_2_, ...), custom_call_target="tpu_custom_call", output_to_operand_aliasing={{1}: (4, {})} | custom-call | bytes 2654208 | tf_op jit(solution)/shard_map/pallas_call | solution.py:308
  43.8 0.0 copy-start.4
  43.8 0.0 copy-start.2
  43.8 0.0 copy-start.3
  43.8 0.7 %collective-permute-start.6 = (f32[8,14,8,256]{3,2,1,0:T(8,128)S(1)}, f32[8,14,8,256]{3,2,1,0:T(8,128)S(1)}, u32[]{:S(2)}, u32[]{:S(2)}) collective-permute-start(f32[8,14,8,256]{3,2,1,0:T(8,128)S(1)} %get-tuple-element.26.now_ref.own_ref), channel_id=1, source_target_pairs={{0,1},{1,0},{2,3},{3,2},{4,5},{5,4},{6,7},{7,6},{8,9},{9,8},{10,11... | collective-permute-start | bytes 2752520 | tf_op jit(solution)/shard_map/ppermute | solution.py:559
  44.4 0.0 copy-done.6
  44.4 0.0 copy-done.7
  44.4 0.0 copy-done.8
  44.5 0.1 fusion.7
  44.6 1.2 %collective-permute-start.7 = (f32[96,256]{1,0:T(8,128)S(1)}, f32[96,256]{1,0:T(8,128)S(1)}, u32[]{:S(2)}, u32[]{:S(2)}) collective-permute-start(f32[96,256]{1,0:T(8,128)S(1)} %get-tuple-element.27), channel_id=1, source_target_pairs={{0,2},{2,0},{1,3},{3,1},{4,6},{6,4},{5,7},{7,5},{8,10},{10,8},{9,1... | collective-permute-start | bytes 294920 | tf_op jit(solution)/shard_map/ppermute | solution.py:566
  45.8 0.0 copy-done.5
  45.8 0.4 fusion.2
  46.1 0.0 copy-done
  46.2 0.5 shard_map.117.own_rim
  46.6 2.3 %collective-permute-done.7.own_low.own_high = f32[96,256]{1,0:T(8,128)S(1)} collective-permute-done((f32[96,256]{1,0:T(8,128)S(1)}, f32[96,256]{1,0:T(8,128)S(1)}, u32[]{:S(2)}, u32[]{:S(2)}) %collective-permute-start.7) | collective-permute-done | bytes 98336 | tf_op jit(solution)/shard_map/ppermute | solution.py:566
  49.0 0.8 %collective-permute-start.8 = (f32[96,256]{1,0:T(8,128)S(1)}, f32[96,256]{1,0:T(8,128)S(1)}, u32[]{:S(2)}, u32[]{:S(2)}) collective-permute-start(f32[96,256]{1,0:T(8,128)S(1)} %collective-permute-done.7.own_low.own_high), channel_id=1, source_target_pairs={{0,1},{1,0},{2,3},{3,2},{4,5},{5,4},{6,7},{7,6},{8,9},{9,8},{10,11... | collective-permute-start | bytes 294920 | tf_op jit(solution)/shard_map/ppermute | solution.py:570
  49.8 0.0 copy-done.4
  49.8 0.1 multiply_reduce_fusion
  49.9 0.9 %collective-permute-done.8.other_low.other_high = f32[96,256]{1,0:T(8,128)S(1)} collective-permute-done((f32[96,256]{1,0:T(8,128)S(1)}, f32[96,256]{1,0:T(8,128)S(1)}, u32[]{:S(2)}, u32[]{:S(2)}) %collective-permute-start.8) | collective-permute-done | bytes 98336 | tf_op jit(solution)/shard_map/ppermute | solution.py:570
  50.7 0.0 collective-permute-done.6.other_ref
  50.7 0.0 copy-done.2
  50.7 0.0 copy-done.3
  50.7 7.4 %shard_map.118 = (f32[8,12,8,256]{3,2,1,0:T(8,128)}, f32[8,128]{1,0:T(8,128)S(1)}) custom-call(s32[16]{0:T(128)S(1)} %copy-done.2, s32[16]{0:T(128)S(1)} %copy-done.3, f32[8,14,8,256]{3,2,1,0:T(8,128)S(1)} %get-tuple-element.26.now_ref.own_ref, f32[8,14,8,256]{3,2,1,0:T(8,128)S(1)} %collective-permute-done.6.other_ref, ...), custom_call_target="tpu_custom_call" | custom-call | flops 528482304 | bytes 2752512 | tf_op jit(solution)/shard_map/pallas_call | solution.py:578
  58.1 0.0 collective-permute-done.2.refs_0_
  58.1 0.8 %shard_map.119.refs_2_ = f32[3,8,12,8,256]{4,3,2,1,0:T(8,128)} custom-call(f32[2,2,12,8,256]{4,3,2,1,0:T(8,128)S(1)} %collective-permute-done.2.refs_0_, f32[3,8,12,8,256]{4,3,2,1,0:T(8,128)} %get-tuple-element.25.refs_1_, f32[8,128]{1,0:T(8,128)S(1)} %get-tuple-element.30.refs_2_.refs_3_), custom_call_target="tpu_custom_call", output_to_operand_aliasing={{}: (1, {})} | custom-call | bytes 786432 | tf_op jit(solution)/shard_map/pallas_call | solution.py:242
  58.9 0.0 collective-permute-done.refs_0_
  58.9 0.5 collective-permute-done.1.refs_1_
  59.5 0.9 %shard_map.120 = f32[3,8,12,8,256]{4,3,2,1,0:T(8,128)} custom-call(f32[2,2,12,8,256]{4,3,2,1,0:T(8,128)S(1)} %collective-permute-done.refs_0_, f32[2,2,12,8,256]{4,3,2,1,0:T(8,128)S(1)} %collective-permute-done.1.refs_1_, f32[3,8,12,8,256]{4,3,2,1,0:T(8,128)} %shard_map.119.refs_2_, ...), custom_call_target="tpu_custom_call", output_to_operand_aliasing={{}: (2, {})} | custom-call | bytes 1572864 | tf_op jit(solution)/shard_map/pallas_call | solution.py:242
  (2 shorter events, 0.0 us)
Async XLA Ops:
  3.0 39.6 %copy-start.1 = (f32[27,8,256]{2,1,0:T(8,128)S(1)}, f32[27,8,256]{2,1,0:T(8,128)}, u32[]{:S(2)}) copy-start(f32[27,8,256]{2,1,0:T(8,128)} %get-tuple-element.20.refs_0_) | copy-start | bytes 663556
  3.0 11.6 %collective-permute-start.3 = (f32[27,8,256]{2,1,0:T(8,128)}, f32[27,8,256]{2,1,0:T(8,128)S(1)}, u32[]{:S(2)}, u32[]{:S(2)}) collective-permute-start(f32[27,8,256]{2,1,0:T(8,128)} %get-tuple-element.21), channel_id=1, source_target_pairs={{0,4},{4,8},{8,12},{12,0},{1,5},{5,9},{9,13},{13,1},{2,6},{6,10},{... | collective-permute-start | bytes 663560 | tf_op jit(solution)/shard_map/ppermute | solution.py:549
  4.3 27.1 %collective-permute-start.4 = (f32[27,8,256]{2,1,0:T(8,128)}, f32[27,8,256]{2,1,0:T(8,128)S(1)}, u32[]{:S(2)}, u32[]{:S(2)}) collective-permute-start(f32[27,8,256]{2,1,0:T(8,128)} %get-tuple-element.22), channel_id=1, source_target_pairs={{0,8},{4,12},{8,0},{12,4},{1,9},{5,13},{9,1},{13,5},{2,10},{6,14},... | collective-permute-start | bytes 663560 | tf_op jit(solution)/shard_map/ppermute | solution.py:549
  5.4 37.2 %collective-permute-start.5 = (f32[27,8,256]{2,1,0:T(8,128)}, f32[27,8,256]{2,1,0:T(8,128)S(1)}, u32[]{:S(2)}, u32[]{:S(2)}) collective-permute-start(f32[27,8,256]{2,1,0:T(8,128)} %get-tuple-element.23), channel_id=1, source_target_pairs={{0,12},{4,0},{8,4},{12,8},{1,13},{5,1},{9,5},{13,9},{2,14},{6,2},{... | collective-permute-start | bytes 663560 | tf_op jit(solution)/shard_map/ppermute | solution.py:549
  9.6 34.9 %copy-start.6 = (f32[24,24]{1,0:T(8,128)S(1)}, f32[24,24]{1,0:T(8,128)}, u32[]{:S(2)}) copy-start(f32[24,24]{1,0:T(8,128)} %param.14) | copy-start | bytes 6916
  9.6 34.9 %copy-start.7 = (f32[24,24]{1,0:T(8,128)S(1)}, f32[24,24]{1,0:T(8,128)}, u32[]{:S(2)}) copy-start(f32[24,24]{1,0:T(8,128)} %param.15) | copy-start | bytes 6916
  9.6 34.8 %copy-start.8 = (f32[24,24]{1,0:T(8,128)S(1)}, f32[24,24]{1,0:T(8,128)}, u32[]{:S(2)}) copy-start(f32[24,24]{1,0:T(8,128)} %param.16) | copy-start | bytes 6916
  9.6 36.2 %copy-start.5 = (f32[24,896,1]{1,0,2:T(8,128)S(1)}, f32[24,896,1]{1,0,2:T(8,128)}, u32[]{:S(2)}) copy-start(f32[24,896,1]{1,0,2:T(8,128)} %constant.27) | copy-start | bytes 258052
  9.6 36.5 %copy-start = (bf16[256,2304]{1,0:T(8,128)(2,1)S(1)}, bf16[256,2304]{1,0:T(8,128)(2,1)}, u32[]{:S(2)}) copy-start(bf16[256,2304]{1,0:T(8,128)(2,1)} %constant.26.spread_ref) | copy-start | bytes 3538948
  9.6 48.5 %collective-permute-start.2 = (f32[2,2,12,8,256]{4,3,2,1,0:T(8,128)}, f32[2,2,12,8,256]{4,3,2,1,0:T(8,128)S(1)}, u32[]{:S(2)}, u32[]{:S(2)}) collective-permute-start(f32[2,2,12,8,256]{4,3,2,1,0:T(8,128)} %get-tuple-element.19), channel_id=1, source_target_pairs={{0,8},{4,12},{8,0},{12,4},{1,9},{5,13},{9,1},{13,5},{2,10},{6,14},... | collective-permute-start | bytes 1179656 | tf_op jit(solution)/shard_map/ppermute | solution.py:549
  13.6 45.3 %collective-permute-start = (f32[2,2,12,8,256]{4,3,2,1,0:T(8,128)}, f32[2,2,12,8,256]{4,3,2,1,0:T(8,128)S(1)}, u32[]{:S(2)}, u32[]{:S(2)}) collective-permute-start(f32[2,2,12,8,256]{4,3,2,1,0:T(8,128)} %get-tuple-element.17), channel_id=1, source_target_pairs={{0,4},{4,8},{8,12},{12,0},{1,5},{5,9},{9,13},{13,1},{2,6},{6,10},{... | collective-permute-start | bytes 1179656 | tf_op jit(solution)/shard_map/ppermute | solution.py:549
  14.6 44.9 %collective-permute-start.1 = (f32[2,2,12,8,256]{4,3,2,1,0:T(8,128)}, f32[2,2,12,8,256]{4,3,2,1,0:T(8,128)S(1)}, u32[]{:S(2)}, u32[]{:S(2)}) collective-permute-start(f32[2,2,12,8,256]{4,3,2,1,0:T(8,128)} %get-tuple-element.18), channel_id=1, source_target_pairs={{0,12},{4,0},{8,4},{12,8},{1,13},{5,1},{9,5},{13,9},{2,14},{6,2},{... | collective-permute-start | bytes 1179656 | tf_op jit(solution)/shard_map/ppermute | solution.py:549
  43.8 6.0 %copy-start.4 = (f32[3,8,896]{2,1,0:T(8,128)S(1)}, f32[3,8,896]{2,1,0:T(8,128)}, u32[]{:S(2)}) copy-start(f32[3,8,896]{2,1,0:T(8,128)} %constant.24.clone) | copy-start | bytes 258052
  43.8 7.0 %copy-start.2 = (s32[16]{0:T(128)S(1)}, s32[16]{0:T(128)}, u32[]{:S(2)}) copy-start(s32[16]{0:T(128)} %dest_ref.7) | copy-start | bytes 196
  43.8 7.0 %copy-start.3 = (s32[16]{0:T(128)S(1)}, s32[16]{0:T(128)}, u32[]{:S(2)}) copy-start(s32[16]{0:T(128)} %parent_ref.3) | copy-start | bytes 196
  43.8 6.9 %collective-permute-start.6 = (f32[8,14,8,256]{3,2,1,0:T(8,128)S(1)}, f32[8,14,8,256]{3,2,1,0:T(8,128)S(1)}, u32[]{:S(2)}, u32[]{:S(2)}) collective-permute-start(f32[8,14,8,256]{3,2,1,0:T(8,128)S(1)} %get-tuple-element.26.now_ref.own_ref), channel_id=1, source_target_pairs={{0,1},{1,0},{2,3},{3,2},{4,5},{5,4},{6,7},{7,6},{8,9},{9,8},{10,11... | collective-permute-start | bytes 2752520 | tf_op jit(solution)/shard_map/ppermute | solution.py:559
  44.6 4.4 %collective-permute-start.7 = (f32[96,256]{1,0:T(8,128)S(1)}, f32[96,256]{1,0:T(8,128)S(1)}, u32[]{:S(2)}, u32[]{:S(2)}) collective-permute-start(f32[96,256]{1,0:T(8,128)S(1)} %get-tuple-element.27), channel_id=1, source_target_pairs={{0,2},{2,0},{1,3},{3,1},{4,6},{6,4},{5,7},{7,5},{8,10},{10,8},{9,1... | collective-permute-start | bytes 294920 | tf_op jit(solution)/shard_map/ppermute | solution.py:566
  49.0 1.8 %collective-permute-start.8 = (f32[96,256]{1,0:T(8,128)S(1)}, f32[96,256]{1,0:T(8,128)S(1)}, u32[]{:S(2)}, u32[]{:S(2)}) collective-permute-start(f32[96,256]{1,0:T(8,128)S(1)} %collective-permute-done.7.own_low.own_high), channel_id=1, source_target_pairs={{0,1},{1,0},{2,3},{3,2},{4,5},{5,4},{6,7},{7,6},{8,9},{9,8},{10,11... | collective-permute-start | bytes 294920 | tf_op jit(solution)/shard_map/ppermute | solution.py:570

commit v19 on v18

--- a/solution.py
+++ b/solution.py
@@ -221,15 +221,17 @@
     )(move_dest, boxes)
 
 
-def settle_later(piece, turn, moved_ref, sem):
-    source = source_of(lax.axis_index("box"), turn, moved_ref.shape[1] // 2)
-    to = moved_ref.at[pl.ds(1, moved_ref.shape[0] - 1), pl.ds(2 * source, 2)]
-    return pltpu.make_async_copy(piece, to, sem)
-
-
 def settle_kernel(turns, *refs):
     out_ref, sems = refs[-2:]
-    copies = [settle_later(refs[n], turn, out_ref, sems.at[n]) for n, turn in enumerate(turns)]
+    own = lax.axis_index("box")
+    levels, slots = out_ref.shape[:2]
+    copies = []
+    for n, turn in enumerate(turns):
+        source = source_of(own, turn, slots // 2)
+        for level in range(levels - 1):
+            for k in range(2):
+                to = out_ref.at[level + 1, 2 * source + k]
+                copies.append(pltpu.make_async_copy(refs[n].at[level, k], to, sems.at[n, level, k]))
     for copy in copies:
         copy.start()
     for copy in copies:
@@ -244,7 +246,7 @@
         out_shape=jax.ShapeDtypeStruct(moved.shape, jnp.float32),
         in_specs=[vmem] * count + [hbm, vmem],
         out_specs=hbm,
-        scratch_shapes=[pltpu.SemaphoreType.DMA((count,))],
+        scratch_shapes=[pltpu.SemaphoreType.DMA((count, moved.shape[0] - 1, 2))],
         input_output_aliases={count: 0},
         compiler_params=pltpu.CompilerParams(vmem_limit_bytes=48 * 2 ** 20),
         cost_estimate=pl.CostEstimate(

time: 60.6 us -> 60.6 us (level)
  no operation moved by 1% of the time
where the time goes in v19:
time: 60.6 us; the launch traced here: 60.4 us
  waiting for transfers between devices  31.1 us (51%)
  Pallas kernels  19.5 us (32%)
  starting transfers between devices  8.35 us (14%)
  between operations  0.82 us (1%)
    ppermute x6, waiting for transfers between devices, send(): lax.ppermute(piece, 'box', [(s, (s + turn) % box_count) for s in range(bo...  28 us
    pallas_call x1, Pallas kernels, body(): pl.pallas_call(functools.partial(slope_kernel, edge, planes, fields, coar...  7.37 us
    pallas_call x2, Pallas kernels, pack_later(): pl.pallas_call(functools.partial(later_kernel, turns, per_device, box_cou...  6.45 us
    ppermute x6, starting transfers between devices, send(): lax.ppermute(piece, 'box', [(s, (s + turn) % box_count) for s in range(bo...  5.65 us
    pallas_call x1, Pallas kernels, pack_first(): pl.pallas_call(functools.partial(first_kernel, per_device, box_count, edg...  2.33 us
    ppermute x1, waiting for transfers between devices, shifted(): return lax.ppermute(values, 'slab', swap if slabs == 2 else pairs)  2.31 us
    pallas_call x2, Pallas kernels, settle(): pl.pallas_call(functools.partial(settle_kernel, turns), out_shape=jax.Sha...  1.73 us
    ppermute x1, starting transfers between devices, shifted(): return lax.ppermute(values, 'slab', swap if slabs == 2 else pairs)  1.22 us
  transfers between devices with their start and end apart: 9, of which 5 were waited for; matrix products, arithmetic and copies ran while one was open for 1% of the time, Pallas kernels for 27%

profile of v19, /device:TPU:9, one launch (start us, length us, event | category | flops | bytes accessed | tf_op | source)
XLA Modules:
  0.0 60.4 jit_solution(13055832719952485344)
XLA Ops:
  0.6 2.3 %shard_map.115 = (f32[27,8,256]{2,1,0:T(8,128)}, f32[27,8,256]{2,1,0:T(8,128)}, f32[27,8,256]{2,1,0:T(8,128)}, f32[27,8,256]{2,1,0:T(8,128)}) custom-call(s32[16]{0:T(128)} %dest_ref.7, s32[16]{0:T(128)} %parent_ref.3, f32[3,4,12,8,256]{4,3,2,1,0:T(8,128)} %boxes_ref.5, f32[12,8,1000]{2,1,0:T(8,128)} %bitcast.11), custom_call_target="tpu_custom_call" | custom-call | flops 147456000 | bytes 2743296 | tf_op jit(solution)/shard_map/pallas_call | solution.py:132
  3.0 0.0 copy-start.1
  3.0 1.3 %collective-permute-start.3 = (f32[27,8,256]{2,1,0:T(8,128)}, f32[27,8,256]{2,1,0:T(8,128)S(1)}, u32[]{:S(2)}, u32[]{:S(2)}) collective-permute-start(f32[27,8,256]{2,1,0:T(8,128)} %get-tuple-element.21), channel_id=1, source_target_pairs={{0,4},{4,8},{8,12},{12,0},{1,5},{5,9},{9,13},{13,1},{2,6},{6,10},{... | collective-permute-start | bytes 663560 | tf_op jit(solution)/shard_map/ppermute | solution.py:551
  4.3 1.1 %collective-permute-start.4 = (f32[27,8,256]{2,1,0:T(8,128)}, f32[27,8,256]{2,1,0:T(8,128)S(1)}, u32[]{:S(2)}, u32[]{:S(2)}) collective-permute-start(f32[27,8,256]{2,1,0:T(8,128)} %get-tuple-element.22), channel_id=1, source_target_pairs={{0,8},{4,12},{8,0},{12,4},{1,9},{5,13},{9,1},{13,5},{2,10},{6,14},... | collective-permute-start | bytes 663560 | tf_op jit(solution)/shard_map/ppermute | solution.py:551
  5.4 1.4 %collective-permute-start.5 = (f32[27,8,256]{2,1,0:T(8,128)}, f32[27,8,256]{2,1,0:T(8,128)S(1)}, u32[]{:S(2)}, u32[]{:S(2)}) collective-permute-start(f32[27,8,256]{2,1,0:T(8,128)} %get-tuple-element.23), channel_id=1, source_target_pairs={{0,12},{4,0},{8,4},{12,8},{1,13},{5,1},{9,5},{13,9},{2,14},{6,2},{... | collective-permute-start | bytes 663560 | tf_op jit(solution)/shard_map/ppermute | solution.py:551
  6.8 2.8 %shard_map.114 = (f32[2,2,12,8,256]{4,3,2,1,0:T(8,128)}, f32[2,2,12,8,256]{4,3,2,1,0:T(8,128)}) custom-call(s32[16]{0:T(128)} %dest_ref.7, f32[3,4,12,8,256]{4,3,2,1,0:T(8,128)} %boxes_ref.5), custom_call_target="tpu_custom_call" | custom-call | bytes 2359296 | tf_op jit(solution)/shard_map/pallas_call | solution.py:206
  9.6 0.0 copy-start.6
  9.6 0.0 copy-start.7
  9.6 0.0 copy-start.8
  9.6 0.0 copy-start.5
  9.6 0.0 copy-start
  9.6 0.3 collective-permute-start.2
  9.9 3.7 %shard_map.113 = (f32[3,8,12,8,256]{4,3,2,1,0:T(8,128)}, f32[2,2,12,8,256]{4,3,2,1,0:T(8,128)}) custom-call(s32[16]{0:T(128)} %dest_ref.7, f32[3,4,12,8,256]{4,3,2,1,0:T(8,128)} %boxes_ref.5), custom_call_target="tpu_custom_call" | custom-call | bytes 2359296 | tf_op jit(solution)/shard_map/pallas_call | solution.py:206
  13.6 0.9 %collective-permute-start = (f32[2,2,12,8,256]{4,3,2,1,0:T(8,128)}, f32[2,2,12,8,256]{4,3,2,1,0:T(8,128)S(1)}, u32[]{:S(2)}, u32[]{:S(2)}) collective-permute-start(f32[2,2,12,8,256]{4,3,2,1,0:T(8,128)} %get-tuple-element.17), channel_id=1, source_target_pairs={{0,4},{4,8},{8,12},{12,0},{1,5},{5,9},{9,13},{13,1},{2,6},{6,10},{... | collective-permute-start | bytes 1179656 | tf_op jit(solution)/shard_map/ppermute | solution.py:551
  14.5 0.0 collective-permute-done.3.refs_1_
  14.6 0.6 collective-permute-start.1
  15.2 16.3 %collective-permute-done.4.refs_2_ = f32[27,8,256]{2,1,0:T(8,128)S(1)} collective-permute-done((f32[27,8,256]{2,1,0:T(8,128)}, f32[27,8,256]{2,1,0:T(8,128)S(1)}, u32[]{:S(2)}, u32[]{:S(2)}) %collective-permute-start.4) | collective-permute-done | bytes 221216 | tf_op jit(solution)/shard_map/ppermute | solution.py:551
  31.4 11.2 %collective-permute-done.5.refs_3_ = f32[27,8,256]{2,1,0:T(8,128)S(1)} collective-permute-done((f32[27,8,256]{2,1,0:T(8,128)}, f32[27,8,256]{2,1,0:T(8,128)S(1)}, u32[]{:S(2)}, u32[]{:S(2)}) %collective-permute-start.5) | collective-permute-done | bytes 221216 | tf_op jit(solution)/shard_map/ppermute | solution.py:551
  42.6 0.0 copy-done.1
  42.6 1.1 %shard_map.116 = (f32[8,14,8,256]{3,2,1,0:T(8,128)S(1)}, f32[3,8,12,8,256]{4,3,2,1,0:T(8,128)}, f32[96,256]{1,0:T(8,128)S(1)}) custom-call(f32[27,8,256]{2,1,0:T(8,128)S(1)} %copy-done.1, f32[27,8,256]{2,1,0:T(8,128)S(1)} %collective-permute-done.3.refs_1_, f32[27,8,256]{2,1,0:T(8,128)S(1)} %collective-permute-done.4.refs_2_, ...), custom_call_target="tpu_custom_call", output_to_operand_aliasing={{1}: (4, {})} | custom-call | bytes 2654208 | tf_op jit(solution)/shard_map/pallas_call | solution.py:310
  43.8 0.0 copy-start.4
  43.8 0.0 copy-start.2
  43.8 0.0 copy-start.3
  43.8 0.7 %collective-permute-start.6 = (f32[8,14,8,256]{3,2,1,0:T(8,128)S(1)}, f32[8,14,8,256]{3,2,1,0:T(8,128)S(1)}, u32[]{:S(2)}, u32[]{:S(2)}) collective-permute-start(f32[8,14,8,256]{3,2,1,0:T(8,128)S(1)} %get-tuple-element.26.now_ref.own_ref), channel_id=1, source_target_pairs={{0,1},{1,0},{2,3},{3,2},{4,5},{5,4},{6,7},{7,6},{8,9},{9,8},{10,11... | collective-permute-start | bytes 2752520 | tf_op jit(solution)/shard_map/ppermute | solution.py:561
  44.4 0.0 copy-done.6
  44.4 0.0 copy-done.7
  44.4 0.0 copy-done.8
  44.5 0.1 fusion.7
  44.6 1.2 %collective-permute-start.7 = (f32[96,256]{1,0:T(8,128)S(1)}, f32[96,256]{1,0:T(8,128)S(1)}, u32[]{:S(2)}, u32[]{:S(2)}) collective-permute-start(f32[96,256]{1,0:T(8,128)S(1)} %get-tuple-element.27), channel_id=1, source_target_pairs={{0,2},{2,0},{1,3},{3,1},{4,6},{6,4},{5,7},{7,5},{8,10},{10,8},{9,1... | collective-permute-start | bytes 294920 | tf_op jit(solution)/shard_map/ppermute | solution.py:568
  45.8 0.0 copy-done.5
  45.8 0.4 fusion.2
  46.1 0.0 copy-done
  46.2 0.5 shard_map.117.own_rim
  46.6 2.3 %collective-permute-done.7.own_low.own_high = f32[96,256]{1,0:T(8,128)S(1)} collective-permute-done((f32[96,256]{1,0:T(8,128)S(1)}, f32[96,256]{1,0:T(8,128)S(1)}, u32[]{:S(2)}, u32[]{:S(2)}) %collective-permute-start.7) | collective-permute-done | bytes 98336 | tf_op jit(solution)/shard_map/ppermute | solution.py:568
  49.0 0.8 %collective-permute-start.8 = (f32[96,256]{1,0:T(8,128)S(1)}, f32[96,256]{1,0:T(8,128)S(1)}, u32[]{:S(2)}, u32[]{:S(2)}) collective-permute-start(f32[96,256]{1,0:T(8,128)S(1)} %collective-permute-done.7.own_low.own_high), channel_id=1, source_target_pairs={{0,1},{1,0},{2,3},{3,2},{4,5},{5,4},{6,7},{7,6},{8,9},{9,8},{10,11... | collective-permute-start | bytes 294920 | tf_op jit(solution)/shard_map/ppermute | solution.py:572
  49.8 0.0 copy-done.4
  49.8 0.1 multiply_reduce_fusion
  49.9 0.9 %collective-permute-done.8.other_low.other_high = f32[96,256]{1,0:T(8,128)S(1)} collective-permute-done((f32[96,256]{1,0:T(8,128)S(1)}, f32[96,256]{1,0:T(8,128)S(1)}, u32[]{:S(2)}, u32[]{:S(2)}) %collective-permute-start.8) | collective-permute-done | bytes 98336 | tf_op jit(solution)/shard_map/ppermute | solution.py:572
  50.7 0.0 collective-permute-done.6.other_ref
  50.7 0.0 copy-done.2
  50.7 0.0 copy-done.3
  50.7 7.4 %shard_map.118 = (f32[8,12,8,256]{3,2,1,0:T(8,128)}, f32[8,128]{1,0:T(8,128)S(1)}) custom-call(s32[16]{0:T(128)S(1)} %copy-done.2, s32[16]{0:T(128)S(1)} %copy-done.3, f32[8,14,8,256]{3,2,1,0:T(8,128)S(1)} %get-tuple-element.26.now_ref.own_ref, f32[8,14,8,256]{3,2,1,0:T(8,128)S(1)} %collective-permute-done.6.other_ref, ...), custom_call_target="tpu_custom_call" | custom-call | flops 528482304 | bytes 2752512 | tf_op jit(solution)/shard_map/pallas_call | solution.py:580
  58.1 0.0 collective-permute-done.2.refs_0_
  58.1 0.8 %shard_map.119.refs_2_ = f32[3,8,12,8,256]{4,3,2,1,0:T(8,128)} custom-call(f32[2,2,12,8,256]{4,3,2,1,0:T(8,128)S(1)} %collective-permute-done.2.refs_0_, f32[3,8,12,8,256]{4,3,2,1,0:T(8,128)} %get-tuple-element.25.refs_1_, f32[8,128]{1,0:T(8,128)S(1)} %get-tuple-element.30.refs_2_.refs_3_), custom_call_target="tpu_custom_call", output_to_operand_aliasing={{}: (1, {})} | custom-call | bytes 786432 | tf_op jit(solution)/shard_map/pallas_call | solution.py:244
  58.9 0.0 collective-permute-done.refs_0_
  58.9 0.5 collective-permute-done.1.refs_1_
  59.5 0.9 %shard_map.120 = f32[3,8,12,8,256]{4,3,2,1,0:T(8,128)} custom-call(f32[2,2,12,8,256]{4,3,2,1,0:T(8,128)S(1)} %collective-permute-done.refs_0_, f32[2,2,12,8,256]{4,3,2,1,0:T(8,128)S(1)} %collective-permute-done.1.refs_1_, f32[3,8,12,8,256]{4,3,2,1,0:T(8,128)} %shard_map.119.refs_2_, ...), custom_call_target="tpu_custom_call", output_to_operand_aliasing={{}: (2, {})} | custom-call | bytes 1572864 | tf_op jit(solution)/shard_map/pallas_call | solution.py:244
  (2 shorter events, 0.0 us)
Async XLA Ops:
  3.0 39.6 %copy-start.1 = (f32[27,8,256]{2,1,0:T(8,128)S(1)}, f32[27,8,256]{2,1,0:T(8,128)}, u32[]{:S(2)}) copy-start(f32[27,8,256]{2,1,0:T(8,128)} %get-tuple-element.20.refs_0_) | copy-start | bytes 663556
  3.0 11.6 %collective-permute-start.3 = (f32[27,8,256]{2,1,0:T(8,128)}, f32[27,8,256]{2,1,0:T(8,128)S(1)}, u32[]{:S(2)}, u32[]{:S(2)}) collective-permute-start(f32[27,8,256]{2,1,0:T(8,128)} %get-tuple-element.21), channel_id=1, source_target_pairs={{0,4},{4,8},{8,12},{12,0},{1,5},{5,9},{9,13},{13,1},{2,6},{6,10},{... | collective-permute-start | bytes 663560 | tf_op jit(solution)/shard_map/ppermute | solution.py:551
  4.3 27.1 %collective-permute-start.4 = (f32[27,8,256]{2,1,0:T(8,128)}, f32[27,8,256]{2,1,0:T(8,128)S(1)}, u32[]{:S(2)}, u32[]{:S(2)}) collective-permute-start(f32[27,8,256]{2,1,0:T(8,128)} %get-tuple-element.22), channel_id=1, source_target_pairs={{0,8},{4,12},{8,0},{12,4},{1,9},{5,13},{9,1},{13,5},{2,10},{6,14},... | collective-permute-start | bytes 663560 | tf_op jit(solution)/shard_map/ppermute | solution.py:551
  5.4 37.2 %collective-permute-start.5 = (f32[27,8,256]{2,1,0:T(8,128)}, f32[27,8,256]{2,1,0:T(8,128)S(1)}, u32[]{:S(2)}, u32[]{:S(2)}) collective-permute-start(f32[27,8,256]{2,1,0:T(8,128)} %get-tuple-element.23), channel_id=1, source_target_pairs={{0,12},{4,0},{8,4},{12,8},{1,13},{5,1},{9,5},{13,9},{2,14},{6,2},{... | collective-permute-start | bytes 663560 | tf_op jit(solution)/shard_map/ppermute | solution.py:551
  9.6 34.9 %copy-start.6 = (f32[24,24]{1,0:T(8,128)S(1)}, f32[24,24]{1,0:T(8,128)}, u32[]{:S(2)}) copy-start(f32[24,24]{1,0:T(8,128)} %param.14) | copy-start | bytes 6916
  9.6 34.9 %copy-start.7 = (f32[24,24]{1,0:T(8,128)S(1)}, f32[24,24]{1,0:T(8,128)}, u32[]{:S(2)}) copy-start(f32[24,24]{1,0:T(8,128)} %param.15) | copy-start | bytes 6916
  9.6 34.8 %copy-start.8 = (f32[24,24]{1,0:T(8,128)S(1)}, f32[24,24]{1,0:T(8,128)}, u32[]{:S(2)}) copy-start(f32[24,24]{1,0:T(8,128)} %param.16) | copy-start | bytes 6916
  9.6 36.2 %copy-start.5 = (f32[24,896,1]{1,0,2:T(8,128)S(1)}, f32[24,896,1]{1,0,2:T(8,128)}, u32[]{:S(2)}) copy-start(f32[24,896,1]{1,0,2:T(8,128)} %constant.27) | copy-start | bytes 258052
  9.6 36.5 %copy-start = (bf16[256,2304]{1,0:T(8,128)(2,1)S(1)}, bf16[256,2304]{1,0:T(8,128)(2,1)}, u32[]{:S(2)}) copy-start(bf16[256,2304]{1,0:T(8,128)(2,1)} %constant.26.spread_ref) | copy-start | bytes 3538948
  9.6 48.5 %collective-permute-start.2 = (f32[2,2,12,8,256]{4,3,2,1,0:T(8,128)}, f32[2,2,12,8,256]{4,3,2,1,0:T(8,128)S(1)}, u32[]{:S(2)}, u32[]{:S(2)}) collective-permute-start(f32[2,2,12,8,256]{4,3,2,1,0:T(8,128)} %get-tuple-element.19), channel_id=1, source_target_pairs={{0,8},{4,12},{8,0},{12,4},{1,9},{5,13},{9,1},{13,5},{2,10},{6,14},... | collective-permute-start | bytes 1179656 | tf_op jit(solution)/shard_map/ppermute | solution.py:551
  13.6 45.3 %collective-permute-start = (f32[2,2,12,8,256]{4,3,2,1,0:T(8,128)}, f32[2,2,12,8,256]{4,3,2,1,0:T(8,128)S(1)}, u32[]{:S(2)}, u32[]{:S(2)}) collective-permute-start(f32[2,2,12,8,256]{4,3,2,1,0:T(8,128)} %get-tuple-element.17), channel_id=1, source_target_pairs={{0,4},{4,8},{8,12},{12,0},{1,5},{5,9},{9,13},{13,1},{2,6},{6,10},{... | collective-permute-start | bytes 1179656 | tf_op jit(solution)/shard_map/ppermute | solution.py:551
  14.6 44.9 %collective-permute-start.1 = (f32[2,2,12,8,256]{4,3,2,1,0:T(8,128)}, f32[2,2,12,8,256]{4,3,2,1,0:T(8,128)S(1)}, u32[]{:S(2)}, u32[]{:S(2)}) collective-permute-start(f32[2,2,12,8,256]{4,3,2,1,0:T(8,128)} %get-tuple-element.18), channel_id=1, source_target_pairs={{0,12},{4,0},{8,4},{12,8},{1,13},{5,1},{9,5},{13,9},{2,14},{6,2},{... | collective-permute-start | bytes 1179656 | tf_op jit(solution)/shard_map/ppermute | solution.py:551
  43.8 6.0 %copy-start.4 = (f32[3,8,896]{2,1,0:T(8,128)S(1)}, f32[3,8,896]{2,1,0:T(8,128)}, u32[]{:S(2)}) copy-start(f32[3,8,896]{2,1,0:T(8,128)} %constant.24.clone) | copy-start | bytes 258052
  43.8 7.0 %copy-start.2 = (s32[16]{0:T(128)S(1)}, s32[16]{0:T(128)}, u32[]{:S(2)}) copy-start(s32[16]{0:T(128)} %dest_ref.7) | copy-start | bytes 196
  43.8 7.0 %copy-start.3 = (s32[16]{0:T(128)S(1)}, s32[16]{0:T(128)}, u32[]{:S(2)}) copy-start(s32[16]{0:T(128)} %parent_ref.3) | copy-start | bytes 196
  43.8 6.9 %collective-permute-start.6 = (f32[8,14,8,256]{3,2,1,0:T(8,128)S(1)}, f32[8,14,8,256]{3,2,1,0:T(8,128)S(1)}, u32[]{:S(2)}, u32[]{:S(2)}) collective-permute-start(f32[8,14,8,256]{3,2,1,0:T(8,128)S(1)} %get-tuple-element.26.now_ref.own_ref), channel_id=1, source_target_pairs={{0,1},{1,0},{2,3},{3,2},{4,5},{5,4},{6,7},{7,6},{8,9},{9,8},{10,11... | collective-permute-start | bytes 2752520 | tf_op jit(solution)/shard_map/ppermute | solution.py:561
  44.6 4.4 %collective-permute-start.7 = (f32[96,256]{1,0:T(8,128)S(1)}, f32[96,256]{1,0:T(8,128)S(1)}, u32[]{:S(2)}, u32[]{:S(2)}) collective-permute-start(f32[96,256]{1,0:T(8,128)S(1)} %get-tuple-element.27), channel_id=1, source_target_pairs={{0,2},{2,0},{1,3},{3,1},{4,6},{6,4},{5,7},{7,5},{8,10},{10,8},{9,1... | collective-permute-start | bytes 294920 | tf_op jit(solution)/shard_map/ppermute | solution.py:568
  49.0 1.8 %collective-permute-start.8 = (f32[96,256]{1,0:T(8,128)S(1)}, f32[96,256]{1,0:T(8,128)S(1)}, u32[]{:S(2)}, u32[]{:S(2)}) collective-permute-start(f32[96,256]{1,0:T(8,128)S(1)} %collective-permute-done.7.own_low.own_high), channel_id=1, source_target_pairs={{0,1},{1,0},{2,3},{3,2},{4,5},{5,4},{6,7},{7,6},{8,9},{9,8},{10,11... | collective-permute-start | bytes 294920 | tf_op jit(solution)/shard_map/ppermute | solution.py:572
